TPU v7x, 32 devices: a whole 2x2x4 slice. The times are simulated.
32 devices in a mesh: section: 2 (over y), row: 4 (over x, core), col: 4 (over z).
Axes of the slice: x: 2, y: 2, z: 4, core: 2. Of those that a mesh axis runs over, the one named last changes fastest.
Arguments:
- inputs: bfloat16 [2, 4096, 2048], P(None, 'row', 'col'), may hold values from -6 to 6
- cotangent: bfloat16 [2, 4096, 2048], P(None, 'row', 'col'), may hold values from -6 to 6
- block_ids: int32 [2, 4096], replicated, may hold values from 0 to 31, never falling along the last dimension, each value on 1 to 256 neighbouring positions
- norm_gains: float32 [2, 2, 2048], P('section', None, 'col'), may hold values from 0.5 to 1.5
- norm_shifts: float32 [2, 2, 2048], P('section', None, 'col'), may hold values from -1 to 1
- qkv_weight: bfloat16 [2, 2048, 3, 2048], P('section', 'row', None, 'col'), may hold values from -0.125 to 0.125
- qkv_bias: float32 [2, 3, 2048], P('section', None, 'col'), may hold values from -3 to 3
- out_weight: bfloat16 [2, 2048, 2048], P('section', 'row', 'col'), may hold values from -0.375 to 0.375
- gate_up_weight: bfloat16 [2, 2048, 2, 5632], P('section', 'row', None, 'col'), may hold values from -0.125 to 0.125
- down_weight: bfloat16 [2, 2048, 5632], P('section', 'row', 'col'), may hold values from -0.109375 to 0.109375
Outputs:
- hidden_states: bfloat16 [2, 2, 4096, 2048], P('section', None, 'row', 'col')
- input_grads: float32 [2, 2, 4096, 2048], P('section', None, 'row', 'col')
- norm_gain_grads: float32 [2, 2, 2048], P('section', None, 'col')
- norm_shift_grads: float32 [2, 2, 2048], P('section', None, 'col')
- qkv_weight_grad: float32 [2, 2048, 3, 2048], P('section', 'row', None, 'col')
- qkv_bias_grad: float32 [2, 3, 2048], P('section', None, 'col')
- out_weight_grad: float32 [2, 2048, 2048], P('section', 'row', 'col')
- gate_up_grad: float32 [2, 2048, 2, 5632], P('section', 'row', None, 'col')
- down_grad: float32 [2, 2048, 5632], P('section', 'row', 'col')
Inputs may be any that keep to these rules, and one draw needn't show every extreme that they name: `block_ids`: along each sequence the block ids never fall; a block holds 1 to 256 tokens, and some block exactly 256.
All inputs are finite; a program needn't handle non-finite values.
Results may differ from a plain program's by a relative error of at most 0.013.
Values may be sent and summed in bfloat16 or wider, within the bound.
A program may use at most 576 MiB of HBM per device.

v0:
```python
import jax
import jax.numpy as jnp
from jax import lax
from jax.sharding import PartitionSpec as P

D = 2048
HEADS = 32
HEAD_DIM = 64
ROT = 16


epsilon = 1e-05


def passed_along(block, axis, distance):
    devices = range(lax.axis_size(axis))
    route = [(i - distance, i) for i in devices if i - distance in devices]
    return lax.ppermute(block, axis, route)


def rotary_tables(positions):
    half_dims = ROT // 2
    inverse_freq = 1.0 / 10000.0 ** (jnp.arange(half_dims, dtype=jnp.float32) * 2.0 / ROT)
    angles = positions.astype(jnp.float32)[:, None] * inverse_freq[None, :]
    return (jnp.cos(angles)[:, None, :], jnp.sin(angles)[:, None, :])


def rotate(values, cosine_table, sine_table):
    half_dims = ROT // 2
    first_half = values[..., :half_dims]
    second_half = values[..., half_dims:ROT]
    return jnp.concatenate(
        [
            first_half * cosine_table - second_half * sine_table,
            second_half * cosine_table + first_half * sine_table,
            values[..., ROT:],
        ],
        axis=-1,
    )


def unrotate(values, cosine_table, sine_table):
    half_dims = ROT // 2
    first_half = values[..., :half_dims]
    second_half = values[..., half_dims:ROT]
    return jnp.concatenate(
        [
            first_half * cosine_table + second_half * sine_table,
            second_half * cosine_table - first_half * sine_table,
            values[..., ROT:],
        ],
        axis=-1,
    )


def dot_last(left, right):
    return lax.dot_general(
        left, right, (((1,), (1,)), ((), ())), preferred_element_type=jnp.float32
    )


def dot_first(left, right):
    return lax.dot_general(
        left, right, (((0,), (0,)), ((), ())), preferred_element_type=jnp.float32
    )


def gather_weights(qkv_weight, out_weight, gate_up_weight, down_weight):
    return (
        lax.all_gather(qkv_weight[0], "row", axis=0, tiled=True),
        lax.all_gather(out_weight[0], "row", axis=0, tiled=True),
        lax.all_gather(gate_up_weight[0], "row", axis=0, tiled=True),
        lax.all_gather(down_weight[0], "row", axis=0, tiled=True),
    )


def col_totals(first_sum, second_sum):
    return lax.psum((first_sum, second_sum), "col")


def norm_forward(values, norm_gain, offset):
    totals, squares = col_totals(jnp.sum(values, axis=-1), jnp.sum(values * values, axis=-1))
    mean_value = totals / D
    inv_std = lax.rsqrt(squares / D - mean_value * mean_value + epsilon)
    centred = (values - mean_value[:, None]) * inv_std[:, None]
    normed = (centred * norm_gain + offset).astype(jnp.bfloat16)
    whole = lax.all_gather(normed, "col", axis=1, tiled=True)
    return (whole, mean_value, inv_std)


def norm_backward(grad_rows, centred, inv_std, norm_gain):
    scaled = grad_rows * norm_gain
    totals, weighted = col_totals(jnp.sum(scaled, axis=-1), jnp.sum(scaled * centred, axis=-1))
    return inv_std[:, None] * (scaled - totals[:, None] / D - centred * (weighted[:, None] / D))


def branch_sum(partial_value):
    return lax.psum_scatter(partial_value, "col", scatter_dimension=1, tiled=True)


def norm_grad_sum(partial_value):
    return lax.psum_scatter(partial_value, "col", scatter_dimension=1, tiled=True)


def gather_grad(values):
    return lax.all_gather(values.astype(jnp.bfloat16), "col", axis=1, tiled=True)


def attend(queries, keys_all, values_all, visible, score_scale):
    scores = (
        jnp.einsum("qhd,khd->hqk", queries, keys_all, preferred_element_type=jnp.float32)
        * score_scale
    )
    scores = jnp.where(visible[None], scores, -1e30)
    row_max = jnp.max(scores, axis=-1, keepdims=True)
    weights = jnp.exp(scores - row_max)
    totals = jnp.sum(weights, axis=-1, keepdims=True)
    chances = (weights / totals).astype(jnp.bfloat16)
    outcome = jnp.einsum(
        "hqk,khd->qhd", chances, values_all, preferred_element_type=jnp.float32
    ).astype(jnp.bfloat16)
    return (outcome, (row_max + jnp.log(totals))[..., 0])


def attend_back(queries, keys_all, values_all, d_mix, log_total, visible, score_scale):

    def one_head(pieces):
        query_head, key_head, value_head, grad_head, log_head = pieces
        scores = jnp.where(visible, dot_last(query_head, key_head) * score_scale, -1e30)
        chances = jnp.exp(scores - log_head[:, None])
        d_value = dot_first(chances.astype(jnp.bfloat16), grad_head)
        d_chance = dot_last(grad_head, value_head)
        d_scores = (
            chances * (d_chance - jnp.sum(chances * d_chance, axis=-1, keepdims=True))
        ).astype(jnp.bfloat16)
        d_query = jnp.dot(d_scores, key_head, preferred_element_type=jnp.float32) * score_scale
        d_key = dot_first(d_scores, query_head) * score_scale
        return (d_query, d_key, d_value)

    per_head = lax.map(
        one_head,
        (
            queries.transpose(1, 0, 2),
            keys_all.transpose(1, 0, 2),
            values_all.transpose(1, 0, 2),
            d_mix.transpose(1, 0, 2),
            log_total,
        ),
    )
    return tuple((array.transpose(1, 0, 2) for array in per_head))


def forward_step(
    current,
    weights,
    gains,
    shifts,
    bias_rows,
    block_all,
    visible,
    cosine_table,
    sine_table,
    local_heads,
):
    qkv_full, out_full, gate_up_full, down_full = weights
    row_count = current.shape[0]
    score_scale = HEAD_DIM ** (-0.5)
    normed, mean_one, inv_one = norm_forward(current.astype(jnp.float32), gains[0], shifts[0])
    qkv_rows = (
        jnp.einsum("td,dsk->tsk", normed, qkv_full, preferred_element_type=jnp.float32) + bias_rows
    )
    queries = rotate(
        qkv_rows[:, 0].reshape(row_count, local_heads, HEAD_DIM), cosine_table, sine_table
    ).astype(jnp.bfloat16)
    keys_rot = rotate(
        qkv_rows[:, 1].reshape(row_count, local_heads, HEAD_DIM), cosine_table, sine_table
    ).astype(jnp.bfloat16)
    values = qkv_rows[:, 2].astype(jnp.bfloat16)
    keys_all, values_all = (
        lax.all_gather(keys_rot.reshape(row_count, -1), "row", axis=0, tiled=True),
        lax.all_gather(values, "row", axis=0, tiled=True),
    )
    keys_all = keys_all.reshape(-1, local_heads, HEAD_DIM)
    values_all = values_all.reshape(-1, local_heads, HEAD_DIM)
    outcome, log_total = attend(queries, keys_all, values_all, visible, score_scale)
    attn_mix = outcome.reshape(row_count, -1)
    after_attn = current.astype(jnp.float32) + branch_sum(dot_last(attn_mix, out_full))
    after_low = after_attn.astype(jnp.bfloat16)
    normed_two, mean_two, inv_two = norm_forward(after_low.astype(jnp.float32), gains[1], shifts[1])
    gate_up = jnp.einsum(
        "td,dsf->tsf", normed_two, gate_up_full, preferred_element_type=jnp.float32
    )
    hidden = (jax.nn.silu(gate_up[:, 0]) * gate_up[:, 1]).astype(jnp.bfloat16)
    result = (after_attn + branch_sum(dot_last(hidden, down_full))).astype(jnp.bfloat16)
    stored = (
        current,
        mean_one,
        inv_one,
        normed,
        queries,
        keys_all,
        values_all,
        log_total,
        attn_mix,
        after_low,
        mean_two,
        inv_two,
        normed_two,
        gate_up,
        hidden,
        visible,
        block_all,
    )
    return (result, stored)


def backward_step(incoming_grad, weights, stored, gains, cosine_table, sine_table):
    (
        current,
        mean_one,
        inv_one,
        normed,
        queries,
        keys_all,
        values_all,
        log_total,
        attn_mix,
        after_low,
        mean_two,
        inv_two,
        normed_two,
        gate_up,
        hidden,
        visible,
        block_all,
    ) = stored
    qkv_full, out_full, gate_up_full, down_full = weights
    row_count = current.shape[0]
    score_scale = HEAD_DIM ** (-0.5)
    grad_branch = gather_grad(incoming_grad)
    d_hidden = jnp.dot(grad_branch, down_full, preferred_element_type=jnp.float32)
    grad_down = dot_first(grad_branch, hidden)
    gate_part = gate_up[:, 0]
    up_part = gate_up[:, 1]
    sigmoid_gate = jax.nn.sigmoid(gate_part)
    d_gate = d_hidden * up_part * sigmoid_gate * (1.0 + gate_part * (1.0 - sigmoid_gate))
    d_up = d_hidden * gate_part * sigmoid_gate
    d_gate_up = jnp.stack([d_gate, d_up], axis=1).astype(jnp.bfloat16)
    grad_gate_up = jnp.einsum(
        "td,tsf->dsf", normed_two, d_gate_up, preferred_element_type=jnp.float32
    )
    d_normed_two = norm_grad_sum(
        jnp.einsum("tsf,dsf->td", d_gate_up, gate_up_full, preferred_element_type=jnp.float32)
    )
    centred_two = (after_low.astype(jnp.float32) - mean_two[:, None]) * inv_two[:, None]
    d_after = incoming_grad + norm_backward(d_normed_two, centred_two, inv_two, gains[1])
    grad_attn = gather_grad(d_after)
    d_mix = jnp.dot(grad_attn, out_full, preferred_element_type=jnp.float32).astype(jnp.bfloat16)
    grad_out = dot_first(grad_attn, attn_mix)
    local_heads = queries.shape[1]
    mix_heads = d_mix.reshape(row_count, local_heads, HEAD_DIM)
    d_query, d_key_part, d_value_part = attend_back(
        queries, keys_all, values_all, mix_heads, log_total, visible, score_scale
    )
    d_key, d_value = (
        lax.psum_scatter(
            d_key_part.reshape(d_key_part.shape[0], -1), "row", scatter_dimension=0, tiled=True
        ),
        lax.psum_scatter(
            d_value_part.reshape(d_value_part.shape[0], -1), "row", scatter_dimension=0, tiled=True
        ),
    )
    d_query = unrotate(d_query, cosine_table, sine_table).reshape(row_count, -1)
    d_key = unrotate(
        d_key.reshape(row_count, local_heads, HEAD_DIM), cosine_table, sine_table
    ).reshape(row_count, -1)
    d_qkv = jnp.stack([d_query, d_key, d_value], axis=1).astype(jnp.bfloat16)
    bias_sum = jnp.sum(d_qkv.astype(jnp.float32), axis=0)
    grad_qkv = jnp.einsum("td,tsk->dsk", normed, d_qkv, preferred_element_type=jnp.float32)
    d_normed = norm_grad_sum(
        jnp.einsum("tsk,dsk->td", d_qkv, qkv_full, preferred_element_type=jnp.float32)
    )
    centred_one = (current.astype(jnp.float32) - mean_one[:, None]) * inv_one[:, None]
    d_input = d_after + norm_backward(d_normed, centred_one, inv_one, gains[0])
    gain_sum = jnp.stack(
        [jnp.sum(d_normed * centred_one, axis=0), jnp.sum(d_normed_two * centred_two, axis=0)]
    )
    shift_sum = jnp.stack([jnp.sum(d_normed, axis=0), jnp.sum(d_normed_two, axis=0)])
    return (d_input, (grad_qkv, grad_out, grad_gate_up, grad_down), (bias_sum, gain_sum, shift_sum))


def per_device(
    inputs,
    cotangent,
    block_ids,
    norm_gains,
    norm_shifts,
    qkv_weight,
    qkv_bias,
    out_weight,
    gate_up_weight,
    down_weight,
):
    section_index = lax.axis_index("section")
    micro_count = inputs.shape[0]
    row_count = inputs.shape[1]
    local_width = inputs.shape[2]
    local_heads = HEADS // lax.axis_size("col")
    row_start = lax.axis_index("row") * row_count
    positions = row_start + jnp.arange(row_count, dtype=jnp.int32)
    cosine_table, sine_table = rotary_tables(positions)
    gains = norm_gains[0]
    shifts = norm_shifts[0]
    bias_rows = qkv_bias[0]

    def fetch():
        return gather_weights(qkv_weight, out_weight, gate_up_weight, down_weight)

    received = jnp.zeros((row_count, local_width), jnp.bfloat16)
    results = []
    stored_all = []
    for moment in range(micro_count + 1):
        batch_first = min(moment, micro_count - 1)
        batch_second = max(moment - 1, 0)
        current = jnp.where(section_index == 0, inputs[batch_first], received)
        block_all = jnp.where(section_index == 0, block_ids[batch_first], block_ids[batch_second])
        block_rows = lax.dynamic_slice_in_dim(block_all, row_start, row_count)
        visible = block_all[None, :] <= block_rows[:, None]
        result, stored = forward_step(
            current,
            fetch(),
            gains,
            shifts,
            bias_rows,
            block_all,
            visible,
            cosine_table,
            sine_table,
            local_heads,
        )
        results.append(result)
        stored_all.append(stored)
        if moment < micro_count:
            received = passed_along(result, "section", 1)
    hidden_states = jnp.stack(
        [
            jnp.where(section_index == 0, results[batch], results[batch + 1])
            for batch in range(micro_count)
        ]
    )
    returned = jnp.zeros((row_count, local_width), jnp.float32)
    weight_totals = None
    small_totals = None
    d_inputs = []
    for moment in range(micro_count + 1):
        valid_flag = 1.0 if moment < micro_count else 0.0
        outside = cotangent[min(moment, micro_count - 1)].astype(jnp.float32) * valid_flag
        incoming_grad = jnp.where(section_index == 1, outside, returned)
        later_step = min(moment + 1, micro_count)
        early_step = max(moment - 1, 0)
        stored = jax.tree.map(
            lambda later_item, early_item: jnp.where(section_index == 1, later_item, early_item),
            stored_all[later_step],
            stored_all[early_step],
        )
        d_input, weight_terms, small_terms = backward_step(
            incoming_grad, fetch(), stored, gains, cosine_table, sine_table
        )
        if weight_totals is None:
            weight_totals = weight_terms
            small_totals = small_terms
        else:
            weight_totals = tuple(
                (total + term for total, term in zip(weight_totals, weight_terms))
            )
            small_totals = tuple((total + term for total, term in zip(small_totals, small_terms)))
        d_inputs.append(d_input)
        if moment < micro_count:
            returned = passed_along(d_input, "section", -1)
    input_grads = jnp.stack(
        [
            jnp.where(section_index == 1, d_inputs[batch], d_inputs[batch + 1])
            for batch in range(micro_count)
        ]
    )
    grad_qkv, grad_out, grad_gate_up, grad_down = lax.psum_scatter(
        weight_totals, "row", scatter_dimension=0, tiled=True
    )
    bias_sum, gain_sum, shift_sum = lax.psum(small_totals, "row")
    return (
        hidden_states[None],
        input_grads[None],
        gain_sum[None],
        shift_sum[None],
        grad_qkv[None],
        bias_sum[None],
        grad_out[None],
        grad_gate_up[None],
        grad_down[None],
    )


def solution(mesh):
    in_specs = (
        P(None, "row", "col"),
        P(None, "row", "col"),
        P(),
        P("section", None, "col"),
        P("section", None, "col"),
        P("section", "row", None, "col"),
        P("section", None, "col"),
        P("section", "row", "col"),
        P("section", "row", None, "col"),
        P("section", "row", "col"),
    )
    out_specs = (
        P("section", None, "row", "col"),
        P("section", None, "row", "col"),
        P("section", None, "col"),
        P("section", None, "col"),
        P("section", "row", None, "col"),
        P("section", None, "col"),
        P("section", "row", "col"),
        P("section", "row", None, "col"),
        P("section", "row", "col"),
    )
    return jax.shard_map(
        per_device, mesh=mesh, in_specs=in_specs, out_specs=out_specs, check_vma=False
    )
```

profile of v0, /device:TPU:0, one launch (start us, length us, event | category | flops | bytes accessed | tf_op | source)
XLA Modules:
  0.0 5625.6 jit_solution(12639422043506676072)
XLA Ops:
  30.7 77.1 %all-gather.30.cloned.1.call-done = bf16[1024,2048]{1,0:T(8,128)(2,1)} async-done(((bf16[1024,512]{1,0:T(8,128)(2,1)}), bf16[1024,2048]{1,0:T(8,128)(2,1)}) %all-gather.30.cloned.1.call-update) | async-done | bytes 4194320 | tf_op jit(solution)/shard_map/all_gather | solution.py:87
  372.4 128.5 %reduce-scatter.23.cloned.1.call-done = f32[1024,512]{1,0:T(8,128)} async-done(((f32[1024,2048]{1,0:T(8,128)}), f32[1024,512]{1,0:T(8,128)}) %reduce-scatter.23.cloned.1.call-update) | async-done | bytes 2097168 | tf_op jit(solution)/shard_map/reduce_scatter | solution.py:98
  579.9 82.9 %all-gather.34.cloned.1.call-done = bf16[1024,2048]{1,0:T(8,128)(2,1)} async-done(((bf16[1024,512]{1,0:T(8,128)(2,1)}), bf16[1024,2048]{1,0:T(8,128)(2,1)}) %all-gather.34.cloned.1.call-update) | async-done | bytes 4194320 | tf_op jit(solution)/shard_map/all_gather | solution.py:87
  718.0 144.5 %reduce-scatter.25.cloned.1.call-done = f32[1024,512]{1,0:T(8,128)} async-done(((f32[1024,2048]{1,0:T(8,128)}), f32[1024,512]{1,0:T(8,128)}) %reduce-scatter.25.cloned.1.call-update) | async-done | bytes 2097168 | tf_op jit(solution)/shard_map/reduce_scatter | solution.py:98
  905.6 81.4 %all-gather.36.cloned.1.call-done = bf16[1024,2048]{1,0:T(8,128)(2,1)} async-done(((bf16[1024,512]{1,0:T(8,128)(2,1)}), bf16[1024,2048]{1,0:T(8,128)(2,1)}) %all-gather.36.cloned.1.call-update) | async-done | bytes 4194320 | tf_op jit(solution)/shard_map/all_gather | solution.py:87
  1184.0 144.5 %reduce-scatter.27.cloned.1.call-done = f32[1024,512]{1,0:T(8,128)} async-done(((f32[1024,2048]{1,0:T(8,128)}), f32[1024,512]{1,0:T(8,128)}) %reduce-scatter.27.cloned.1.call-update) | async-done | bytes 2097168 | tf_op jit(solution)/shard_map/reduce_scatter | solution.py:98
  1347.4 78.0 %all-gather.40.cloned.1.call-done = bf16[1024,2048]{1,0:T(8,128)(2,1)} async-done(((bf16[1024,512]{1,0:T(8,128)(2,1)}), bf16[1024,2048]{1,0:T(8,128)(2,1)}) %all-gather.40.cloned.1.call-update) | async-done | bytes 4194320 | tf_op jit(solution)/shard_map/all_gather | solution.py:87
  1540.4 111.6 %reduce-scatter.29.cloned.1.call-done = f32[1024,512]{1,0:T(8,128)} async-done(((f32[1024,2048]{1,0:T(8,128)}), f32[1024,512]{1,0:T(8,128)}) %reduce-scatter.29.cloned.1.call-update) | async-done | bytes 2097168 | tf_op jit(solution)/shard_map/reduce_scatter | solution.py:98
  1660.1 139.4 %reduce-scatter.35.cloned.1.call-done = f32[1024,512]{1,0:T(8,128)} async-done(((f32[1024,2048]{1,0:T(8,128)}), f32[1024,512]{1,0:T(8,128)}) %reduce-scatter.35.cloned.1.call-update) | async-done | bytes 2097168 | tf_op jit(solution)/shard_map/reduce_scatter | solution.py:102
  1828.6 76.2 %all-gather.42.cloned.1.call-done = bf16[1024,2048]{1,0:T(8,128)(2,1)} async-done(((bf16[1024,512]{1,0:T(8,128)(2,1)}), bf16[1024,2048]{1,0:T(8,128)(2,1)}) %all-gather.42.cloned.1.call-update) | async-done | bytes 4194320 | tf_op jit(solution)/shard_map/all_gather | solution.py:87
  2147.1 314.3 %while.45 = (s32[]{:T(128)}, f32[8,1024,64]{1,2,0:T(8,128)}, f32[8,4096,64]{1,2,0:T(8,128)}, f32[8,4096,64]{1,2,0:T(8,128)}, bf16[8,1024,64]{1,2,0:T(8,128)(2,1)...) while((s32[]{:T(128)}, f32[8,1024,64]{1,2,0:T(8,128)}, ...), condition=%wide.region_43.44_spmd.clone, body=%wide.region_41.43_spmd.clone.sunk | while | flops 2735012864 | bytes 130614936 | solution.py:140
  2621.9 133.2 %reduce-scatter.31.cloned.1.call-done = f32[1024,512]{1,0:T(8,128)} async-done(((f32[1024,2048]{1,0:T(8,128)}), f32[1024,512]{1,0:T(8,128)}) %reduce-scatter.31.cloned.1.call-update) | async-done | bytes 2097168 | tf_op jit(solution)/shard_map/reduce_scatter | solution.py:98
  2757.2 145.4 %reduce-scatter.41.cloned.1.call-done = f32[1024,512]{1,0:T(8,128)} async-done(((f32[1024,2048]{1,0:T(8,128)}), f32[1024,512]{1,0:T(8,128)}) %reduce-scatter.41.cloned.1.call-update) | async-done | bytes 2097168 | tf_op jit(solution)/shard_map/reduce_scatter | solution.py:102
  3121.9 142.5 %reduce-scatter.43.cloned.1.call-done = f32[1024,512]{1,0:T(8,128)} async-done(((f32[1024,2048]{1,0:T(8,128)}), f32[1024,512]{1,0:T(8,128)}) %reduce-scatter.43.cloned.1.call-update) | async-done | bytes 2097168 | tf_op jit(solution)/shard_map/reduce_scatter | solution.py:102
  3284.2 78.8 %all-gather.54.cloned.1.call-done = bf16[1024,2048]{1,0:T(8,128)(2,1)} async-done(((bf16[1024,512]{1,0:T(8,128)(2,1)}), bf16[1024,2048]{1,0:T(8,128)(2,1)}) %all-gather.54.cloned.1.call-update) | async-done | bytes 4194320 | tf_op jit(solution)/shard_map/all_gather | solution.py:106
  3379.4 320.2 %while.46 = (s32[]{:T(128)}, f32[8,1024,64]{1,2,0:T(8,128)}, f32[8,4096,64]{1,2,0:T(8,128)}, f32[8,4096,64]{1,2,0:T(8,128)}, bf16[8,1024,64]{1,2,0:T(8,128)(2,1)...) while((s32[]{:T(128)}, f32[8,1024,64]{1,2,0:T(8,128)}, ...), condition=%wide.region_58.59_spmd.clone, body=%wide.region_56.58_spmd.clone.sunk | while | flops 2735012864 | bytes 130614936 | solution.py:140
  3858.6 144.0 %reduce-scatter.49.cloned.1.call-done = f32[1024,512]{1,0:T(8,128)} async-done(((f32[1024,2048]{1,0:T(8,128)}), f32[1024,512]{1,0:T(8,128)}) %reduce-scatter.49.cloned.1.call-update) | async-done | bytes 2097168 | tf_op jit(solution)/shard_map/reduce_scatter | solution.py:102
  4073.5 78.2 %all-gather.56.cloned.1.call-done = bf16[1024,2048]{1,0:T(8,128)(2,1)} async-done(((bf16[1024,512]{1,0:T(8,128)(2,1)}), bf16[1024,2048]{1,0:T(8,128)(2,1)}) %all-gather.56.cloned.1.call-update) | async-done | bytes 4194320 | tf_op jit(solution)/shard_map/all_gather | solution.py:106
  4185.1 143.1 %reduce-scatter.51.cloned.1.call-done = f32[1024,512]{1,0:T(8,128)} async-done(((f32[1024,2048]{1,0:T(8,128)}), f32[1024,512]{1,0:T(8,128)}) %reduce-scatter.51.cloned.1.call-update) | async-done | bytes 2097168 | tf_op jit(solution)/shard_map/reduce_scatter | solution.py:102
  4347.6 78.8 %all-gather.58.cloned.1.call-done = bf16[1024,2048]{1,0:T(8,128)(2,1)} async-done(((bf16[1024,512]{1,0:T(8,128)(2,1)}), bf16[1024,2048]{1,0:T(8,128)(2,1)}) %all-gather.58.cloned.1.call-update) | async-done | bytes 4194320 | tf_op jit(solution)/shard_map/all_gather | solution.py:106
  4443.0 320.6 %while.47 = (s32[]{:T(128)}, f32[8,1024,64]{1,2,0:T(8,128)}, f32[8,4096,64]{1,2,0:T(8,128)}, f32[8,4096,64]{1,2,0:T(8,128)}, bf16[8,1024,64]{1,2,0:T(8,128)(2,1)...) while((s32[]{:T(128)}, f32[8,1024,64]{1,2,0:T(8,128)}, ...), condition=%wide.region_73.74_spmd.clone, body=%wide.region_71.73_spmd.clone.sunk | while | flops 2735012864 | bytes 130614936 | solution.py:140
  5061.3 164.1 %reduce-scatter.63.cloned.1.call-done = f32[512,2,1408]{2,0,1:T(8,128)} async-done(((f32[2048,2,1408]{2,0,1:T(8,128)}), f32[512,2,1408]{2,0,1:T(8,128)}) %reduce-scatter.63.cloned.1.call-update) | async-done | bytes 5767184 | tf_op jit(solution)/shard_map/reduce_scatter | solution.py:386
  5235.4 137.0 %reduce-scatter.57.cloned.1.call-done = f32[1024,512]{1,0:T(8,128)} async-done(((f32[1024,2048]{1,0:T(8,128)}), f32[1024,512]{1,0:T(8,128)}) %reduce-scatter.57.cloned.1.call-update) | async-done | bytes 2097168 | tf_op jit(solution)/shard_map/reduce_scatter | solution.py:102
  5516.4 102.2 %reduce-scatter.59.cloned.1.call-done = f32[512,3,512]{2,0,1:T(8,128)} async-done(((f32[2048,3,512]{2,0,1:T(8,128)}), f32[512,3,512]{2,0,1:T(8,128)}) %reduce-scatter.59.cloned.1.call-update) | async-done | bytes 3145744 | tf_op jit(solution)/shard_map/reduce_scatter | solution.py:386
  (877 shorter events, 3195.9 us)
Async XLA Ops:
  172.4 328.4 %reduce-scatter.23.cloned.1.call-start = ((), (), s32[]{:S(2)}) async-start(), calls=%async_computation.24 | async-start | bytes 10485760 | tf_op jit(solution)/shard_map/reduce_scatter | solution.py:98
  360.2 302.7 %all-gather.34.cloned.1.call-start = ((), (), s32[]{:S(2)}) async-start(), calls=%async_computation.25 | async-start | bytes 5242880 | tf_op jit(solution)/shard_map/all_gather | solution.py:87
  517.1 345.5 %reduce-scatter.25.cloned.1.call-start = ((), (), s32[]{:S(2)}) async-start(), calls=%async_computation.26 | async-start | bytes 10485760 | tf_op jit(solution)/shard_map/reduce_scatter | solution.py:98
  718.0 269.0 %all-gather.36.cloned.1.call-start = ((), (), s32[]{:S(2)}) async-start(), calls=%async_computation.27 | async-start | bytes 5242880 | tf_op jit(solution)/shard_map/all_gather | solution.py:87
  1009.7 318.8 %reduce-scatter.27.cloned.1.call-start = ((), (), s32[]{:S(2)}) async-start(), calls=%async_computation.29 | async-start | bytes 10485760 | tf_op jit(solution)/shard_map/reduce_scatter | solution.py:98
  1347.4 304.6 %reduce-scatter.29.cloned.1.call-start = ((), (), s32[]{:S(2)}) async-start(), calls=%async_computation.31 | async-start | bytes 10485760 | tf_op jit(solution)/shard_map/reduce_scatter | solution.py:98
  1466.3 333.2 %reduce-scatter.35.cloned.1.call-start = ((), (), s32[]{:S(2)}) async-start(), calls=%async_computation.38 | async-start | bytes 10485760 | tf_op jit(solution)/shard_map/reduce_scatter | solution.py:102
  1540.4 364.4 %all-gather.42.cloned.1.call-start = ((), (), s32[]{:S(2)}) async-start(), calls=%async_computation.32 | async-start | bytes 5242880 | tf_op jit(solution)/shard_map/all_gather | solution.py:87
  1994.5 539.3 %reduce-scatter.37.cloned.1.call-start = ((), (), s32[]{:S(2)}) async-start(), calls=%async_computation.40 | async-start | bytes 10485760 | tf_op jit(solution)/shard_map/reduce_scatter | solution.py:266
  2471.1 284.0 %reduce-scatter.31.cloned.1.call-start = ((), (), s32[]{:S(2)}) async-start(), calls=%async_computation.34 | async-start | bytes 10485760 | tf_op jit(solution)/shard_map/reduce_scatter | solution.py:98
  2530.3 372.3 %reduce-scatter.41.cloned.1.call-start = ((), (), s32[]{:S(2)}) async-start(), calls=%async_computation.42 | async-start | bytes 10485760 | tf_op jit(solution)/shard_map/reduce_scatter | solution.py:102
  2621.8 384.5 %all-gather.46.cloned.1.call-start = ((), (), s32[]{:S(2)}) async-start(), calls=%async_computation.35 | async-start | bytes 5242880 | tf_op jit(solution)/shard_map/all_gather | solution.py:87
  2980.0 284.4 %reduce-scatter.43.cloned.1.call-start = ((), (), s32[]{:S(2)}) async-start(), calls=%async_computation.44 | async-start | bytes 10485760 | tf_op jit(solution)/shard_map/reduce_scatter | solution.py:102
  3284.2 485.9 %reduce-scatter.45.cloned.1.call-start = ((), (), s32[]{:S(2)}) async-start(), calls=%async_computation.46 | async-start | bytes 10485760 | tf_op jit(solution)/shard_map/reduce_scatter | solution.py:266
  3709.4 293.2 %reduce-scatter.49.cloned.1.call-start = ((), (), s32[]{:S(2)}) async-start(), calls=%async_computation.48 | async-start | bytes 10485760 | tf_op jit(solution)/shard_map/reduce_scatter | solution.py:102
  3858.0 293.7 %all-gather.56.cloned.1.call-start = ((), (), s32[]{:S(2)}) async-start(), calls=%async_computation.49 | async-start | bytes 5242880 | tf_op jit(solution)/shard_map/all_gather | solution.py:106
  4073.5 254.7 %reduce-scatter.51.cloned.1.call-start = ((), (), s32[]{:S(2)}) async-start(), calls=%async_computation.50 | async-start | bytes 10485760 | tf_op jit(solution)/shard_map/reduce_scatter | solution.py:102
  4347.6 517.0 %reduce-scatter.53.cloned.1.call-start = ((), (), s32[]{:S(2)}) async-start(), calls=%async_computation.52 | async-start | bytes 10485760 | tf_op jit(solution)/shard_map/reduce_scatter | solution.py:266
  4773.5 281.9 %reduce-scatter.33.cloned.1.call-start = ((), (), s32[]{:S(2)}) async-start(), calls=%async_computation.36 | async-start | bytes 10485760 | tf_op jit(solution)/shard_map/reduce_scatter | solution.py:98
  4790.9 434.6 %reduce-scatter.63.cloned.1.call-start = ((), (), s32[]{:S(2)}) async-start(), calls=%async_computation.57 | async-start | bytes 28835840 | tf_op jit(solution)/shard_map/reduce_scatter | solution.py:386
  4862.0 510.5 %reduce-scatter.57.cloned.1.call-start = ((), (), s32[]{:S(2)}) async-start(), calls=%async_computation.54 | async-start | bytes 10485760 | tf_op jit(solution)/shard_map/reduce_scatter | solution.py:102
  4921.4 547.3 %reduce-scatter.65.cloned.1.call-start = ((), (), s32[]{:S(2)}) async-start(), calls=%async_computation.58 | async-start | bytes 14417920 | tf_op jit(solution)/shard_map/reduce_scatter | solution.py:386
  4959.7 556.7 %reduce-scatter.61.cloned.1.call-start = ((), (), s32[]{:S(2)}) async-start(), calls=%async_computation.56 | async-start | bytes 5242880 | tf_op jit(solution)/shard_map/reduce_scatter | solution.py:386
  4981.4 637.3 %reduce-scatter.59.cloned.1.call-start = ((), (), s32[]{:S(2)}) async-start(), calls=%async_computation.55 | async-start | bytes 15728640 | tf_op jit(solution)/shard_map/reduce_scatter | solution.py:386
  (220 other events, 16041.8 us)
Sparse Core Ops, SparseCore 0:
  28.8 78.9 all-gather.29
  356.3 144.4 reduce-scatter.22
  582.0 80.7 all-gather.33
  718.0 144.4 reduce-scatter.24
  905.7 81.2 all-gather.35
  1184.0 144.4 reduce-scatter.26
  1346.2 79.1 all-gather.39
  1427.4 79.2 all-gather.47
  1509.0 143.0 reduce-scatter.28
  1654.2 145.1 reduce-scatter.34
  1824.4 80.3 all-gather.41
  1906.8 79.2 all-gather.49
  2610.6 144.4 reduce-scatter.30
  2757.3 145.2 reduce-scatter.40
  2927.1 79.1 all-gather.45
  3008.4 79.2 all-gather.51
  3121.4 142.9 reduce-scatter.42
  3858.1 144.4 reduce-scatter.48
  4185.1 142.9 reduce-scatter.50
  4910.8 144.4 reduce-scatter.32
  5058.0 167.4 reduce-scatter.62
  5228.0 144.4 reduce-scatter.56
  5375.8 92.9 reduce-scatter.64
  5519.6 99.0 reduce-scatter.58
  (20 shorter events, 1097.0 us)
where the time goes:
time: 5640 us; the launch traced here: 5630 us
  waiting for transfers between devices  3280 us (58%)
  matrix products  1520 us (27%)
  other arithmetic  474 us (8%)
  local copies, waits for them, and re-layouts  166 us (3%)
  blocking collectives  140 us (2%)
    reduce_scatter x6, waiting for transfers between devices, norm_grad_sum(): lax.psum_scatter(partial_value, 'col', scatter_dimension=1, tiled=True)  851 us
    reduce_scatter x6, waiting for transfers between devices, branch_sum(): lax.psum_scatter(partial_value, 'col', scatter_dimension=1, tiled=True)  692 us
    dot_general x54, matrix products, dot_last(): lax.dot_general(left, right, (((1,), (1,)), ((), ())), preferred_element_...  553 us
    all_gather x6, waiting for transfers between devices, norm_forward(): whole = lax.all_gather(normed, 'col', axis=1, tiled=True)  422 us
    all_gather x6, waiting for transfers between devices, gather_grad(): lax.all_gather(values.astype(jnp.bfloat16), 'col', axis=1, tiled=True)  385 us
    reduce_scatter x4, waiting for transfers between devices, per_device(): lax.psum_scatter(weight_totals, 'row', scatter_dimension=0, tiled=True)  380 us
    dot_general x54, matrix products, dot_first(): lax.dot_general(left, right, (((0,), (0,)), ((), ())), preferred_element_...  201 us
    convert_element_type x24, other arithmetic, one_head(): d_scores = (chances * (d_chance - jnp.sum(chances * d_chance, axis=-1, ke...  187 us
  transfers between devices with their start and end apart: 48, of which 42 were waited for; matrix products, arithmetic and copies ran while one was open for 16% of the time, Pallas kernels for 0%

commit v1 on v0

v1 whole, which is shorter than its diff:
```python
import functools

import jax
import jax.numpy as jnp
from jax import lax
from jax.experimental import pallas as pl
from jax.experimental.pallas import tpu as pltpu
from jax.sharding import PartitionSpec as P

D = 2048
HEADS = 32
HEAD_DIM = 64
ROT = 16
LANES = 128
REACH = 256


epsilon = 1e-05

def dot_last(a,b):
    return lax.dot_general(a,b,(((1,),(1,)),((),())),preferred_element_type=jnp.float32)
def dot_first(a,b):
    return lax.dot_general(a,b,(((0,),(0,)),((),())),preferred_element_type=jnp.float32)

def lanes_of(rows, head):
    lane = lax.broadcasted_iota(jnp.int32, (rows,128), 1)
    return (lane//HEAD_DIM)==head

def attend_kernel(heads, bq, bk, bid_q, bid_k, q_ref, k_ref, v_ref, o_ref, lse_ref, vone, scores):
    i = pl.program_id(0)
    seq = k_ref.shape[0]
    @pl.when(i==0)
    def _():
        for h in range(heads):
            vone[h] = jnp.where(lanes_of(seq,h), v_ref[...], jnp.ones((),jnp.bfloat16))
    q = q_ref[...]
    free = i*(bq//bk)
    last = jnp.minimum(((i+1)*bq+REACH+bk-1)//bk, seq//bk)
    qs = [jnp.where(lanes_of(bq,h), q, jnp.zeros((),jnp.bfloat16)) for h in range(heads)]
    def fold(s, m):
        for c in range(bk//128):
            m = jnp.maximum(m, s[:, c*128:(c+1)*128])
        return m
    def plain(t, ms):
        keys = k_ref[pl.ds(t*bk,bk),:]
        out=[]
        for h in range(heads):
            s=dot_last(qs[h], keys)
            scores[h,:,pl.ds(t*bk,bk)] = s
            out.append(fold(s, ms[h]))
        return tuple(out)
    def masked(t, ms):
        keys = k_ref[pl.ds(t*bk,bk),:]
        vis = bid_k[:, pl.ds(t*bk,bk)] <= bid_q[...]
        out=[]
        for h in range(heads):
            s=jnp.where(vis, dot_last(qs[h], keys), -1e30)
            scores[h,:,pl.ds(t*bk,bk)] = s
            out.append(fold(s, ms[h]))
        return tuple(out)
    ms = tuple(jnp.full((bq,128),-1e30,jnp.float32) for _ in range(heads))
    ms = lax.fori_loop(0, free, plain, ms)
    ms = lax.fori_loop(free, last, masked, ms)
    ms = [jnp.max(m,axis=1,keepdims=True) for m in ms]
    def mix(t, accs):
        out=[]
        for h in range(heads):
            p=jnp.exp(scores[h,:,pl.ds(t*bk,bk)]-ms[h]).astype(jnp.bfloat16)
            out.append(accs[h]+jnp.dot(p, vone[h,pl.ds(t*bk,bk),:], preferred_element_type=jnp.float32))
        return tuple(out)
    accs = lax.fori_loop(0, last, mix, tuple(jnp.zeros((bq,128),jnp.float32) for _ in range(heads)))
    total=None
    lse=None
    for h in range(heads):
        sums = pltpu.roll(accs[h], HEAD_DIM, 1)
        o = accs[h]/sums
        l = ms[h] + jnp.log(sums)
        mine = lanes_of(bq,h)
        total = jnp.where(mine, o, 0.0 if total is None else total)
        lse = jnp.where(mine, l, 0.0 if lse is None else lse)
    o_ref[...] = total.astype(jnp.bfloat16)
    lse_ref[...] = lse.T

def attend(q,k,v,block_all,heads,bq=512,bk=512):
    seq=q.shape[0]
    vm=pl.BlockSpec(memory_space=pltpu.VMEM)
    return pl.pallas_call(
        functools.partial(attend_kernel, heads,bq,bk),
        grid=(seq//bq,),
        in_specs=[pl.BlockSpec((bq,1),lambda i:(i,0)), pl.BlockSpec((1,seq),lambda i:(0,0)),
                  pl.BlockSpec((bq,128),lambda i:(i,0)), pl.BlockSpec((seq,128),lambda i:(0,0)), pl.BlockSpec((seq,128),lambda i:(0,0))],
        out_specs=[pl.BlockSpec((bq,128),lambda i:(i,0)), pl.BlockSpec((128,bq),lambda i:(0,i))],
        out_shape=[jax.ShapeDtypeStruct((seq,128),jnp.bfloat16), jax.ShapeDtypeStruct((128,seq),jnp.float32)],
        scratch_shapes=[pltpu.VMEM((heads,seq,128),jnp.bfloat16), pltpu.VMEM((heads,bq,seq),jnp.float32)],
        compiler_params=pltpu.CompilerParams(vmem_limit_bytes=56*2**20),
        cost_estimate=pl.CostEstimate(flops=heads*seq*seq*256,bytes_accessed=seq*128*12,transcendentals=heads*seq*seq//2),
    )(block_all.reshape(seq,1), block_all.reshape(1,seq), q,k,v)

def spin(x, cosines, sines):
    lane = lax.broadcasted_iota(jnp.int32, x.shape, 1)
    other = jnp.where(lane % ROT < ROT//2, pltpu.roll(x, 128-ROT//2, 1), pltpu.roll(x, ROT//2, 1))
    return x*cosines + other*sines

def attend_back_kernel(heads, bq, bk, bid_q, bid_k, q_ref, k_ref, v_ref, g_ref, o_ref, lse_ref, cos_ref, sin_ref,
                       dq_ref, dk_ref, dv_ref, kone, dk_acc, dv_acc):
    i = pl.program_id(0)
    seq = k_ref.shape[0]
    zero = jnp.zeros((),jnp.bfloat16)
    @pl.when(i==0)
    def _():
        for h in range(heads):
            kone[h] = jnp.where(lanes_of(seq,h), k_ref[...], zero)
        dk_acc[...] = jnp.zeros_like(dk_acc)
        dv_acc[...] = jnp.zeros_like(dv_acc)
    q = q_ref[...]; g = g_ref[...]
    prod = (g.astype(jnp.float32)*o_ref[...].astype(jnp.float32)).T
    deltas = [jnp.sum(prod[h*HEAD_DIM:(h+1)*HEAD_DIM],axis=0,keepdims=True) for h in range(heads)]
    lses = [lse_ref[h*HEAD_DIM:h*HEAD_DIM+1,:] for h in range(heads)]
    qs = [jnp.where(lanes_of(bq,h), q, zero) for h in range(heads)]
    gs = [jnp.where(lanes_of(bq,h), g, zero) for h in range(heads)]
    free = i*(bq//bk)
    last = jnp.minimum(((i+1)*bq+REACH+bk-1)//bk, seq//bk)
    def tile(t, dq, hide):
        here = pl.ds(t*bk,bk)
        keys = k_ref[here,:]; vals = v_ref[here,:]
        dv = dv_acc[here,:]; dk = dk_acc[here,:]
        if hide: vis = bid_k[here,:] <= bid_q[...]
        for h in range(heads):
            s = dot_last(keys, qs[h])
            if hide: s = jnp.where(vis, s, -1e30)
            p = jnp.exp(s - lses[h])
            dp = dot_last(vals, gs[h])
            ds = (p*(dp-deltas[h])).astype(jnp.bfloat16)
            dv = dv + jnp.dot(p.astype(jnp.bfloat16), gs[h], preferred_element_type=jnp.float32)
            dk = dk + jnp.dot(ds, qs[h], preferred_element_type=jnp.float32)
            dq = dq + dot_first(ds, kone[h,here,:])
        dv_acc[here,:] = dv; dk_acc[here,:] = dk
        return dq
    dq = jnp.zeros((bq,128),jnp.float32)
    dq = lax.fori_loop(0, free, lambda t,c: tile(t,c,False), dq)
    dq = lax.fori_loop(free, last, lambda t,c: tile(t,c,True), dq)
    rows = pl.ds(i*bq,bq)
    dq_ref[...] = spin(dq*(HEAD_DIM**-0.5), cos_ref[rows,:], -sin_ref[rows,:]).astype(jnp.bfloat16)
    @pl.when(i==pl.num_programs(0)-1)
    def _():
        dk_ref[...] = spin(dk_acc[...], cos_ref[...], -sin_ref[...]).astype(jnp.bfloat16)
        dv_ref[...] = dv_acc[...].astype(jnp.bfloat16)

def attend_back(q,k,v,g,o,lse,block_all,cosines,sines,heads,bq=512,bk=512):
    seq=q.shape[0]
    row=pl.BlockSpec((bq,128),lambda i:(i,0)); whole=pl.BlockSpec((seq,128),lambda i:(0,0))
    return pl.pallas_call(
        functools.partial(attend_back_kernel, heads,bq,bk),
        grid=(seq//bq,),
        in_specs=[pl.BlockSpec((1,bq),lambda i:(0,i)), pl.BlockSpec((seq,1),lambda i:(0,0)), row, whole, whole, row, row,
                  pl.BlockSpec((128,bq),lambda i:(0,i)), whole, whole],
        out_specs=[row, whole, whole],
        out_shape=[jax.ShapeDtypeStruct((seq,128),jnp.bfloat16)]*3,
        scratch_shapes=[pltpu.VMEM((heads,seq,128),jnp.bfloat16), pltpu.VMEM((seq,128),jnp.float32), pltpu.VMEM((seq,128),jnp.float32)],
        compiler_params=pltpu.CompilerParams(vmem_limit_bytes=56*2**20),
        cost_estimate=pl.CostEstimate(flops=heads*seq*seq*640,bytes_accessed=seq*128*20,transcendentals=heads*seq*seq//2),
    )(block_all.reshape(1,seq), block_all.reshape(seq,1), q,k,v,g,o,lse,cosines,sines)


def lanes_padded(values):
    width = values.shape[-1]
    if width == LANES:
        return values
    return jnp.pad(values, ((0, 0), (0, LANES - width)))


def rotary_lanes(positions, width):
    half_dims = ROT // 2
    inverse_freq = 1.0 / 10000.0 ** (jnp.arange(half_dims, dtype=jnp.float32) * 2.0 / ROT)
    angles = positions.astype(jnp.float32)[:, None] * inverse_freq[None, :]
    cosine, sine = jnp.cos(angles), jnp.sin(angles)
    rest = jnp.zeros((positions.shape[0], HEAD_DIM - ROT), jnp.float32)
    cosines = jnp.concatenate([cosine, cosine, rest + 1.0], axis=1)
    sines = jnp.concatenate([-sine, sine, rest], axis=1)
    return jnp.tile(cosines, (1, width // HEAD_DIM)), jnp.tile(sines, (1, width // HEAD_DIM))


def rotate(values, cosines, sines):
    lane = lax.broadcasted_iota(jnp.int32, values.shape, 1)
    other = jnp.where(
        lane % ROT < ROT // 2, jnp.roll(values, -(ROT // 2), axis=1), jnp.roll(values, ROT // 2, axis=1)
    )
    return values * cosines + other * sines


def statistics(values):
    mean = jnp.mean(values, axis=-1, keepdims=True)
    spread = jnp.mean(values * values, axis=-1, keepdims=True) - mean * mean
    return mean, lax.rsqrt(spread + epsilon)


def layer_norm(values, gain, shift):
    values = values.astype(jnp.float32)
    mean, inverse = statistics(values)
    return ((values - mean) * inverse * gain + shift).astype(jnp.bfloat16)


def norm_back(grads, values, gain):
    values = values.astype(jnp.float32)
    grads = grads.astype(jnp.float32)
    mean, inverse = statistics(values)
    centred = (values - mean) * inverse
    scaled = grads * gain
    back = inverse * (
        scaled
        - jnp.mean(scaled, axis=-1, keepdims=True)
        - centred * jnp.mean(scaled * centred, axis=-1, keepdims=True)
    )
    return back, jnp.stack([jnp.sum(grads * centred, axis=0), jnp.sum(grads, axis=0)])


def summed_rows(partial):
    return lax.psum_scatter(partial.astype(jnp.bfloat16), "col", scatter_dimension=0, tiled=True)


def gathered_rows(own):
    return lax.all_gather(own, "col", axis=0, tiled=True)


def product(left, right):
    return jnp.dot(left, right, preferred_element_type=jnp.float32)


def per_device(
    inputs,
    cotangent,
    block_ids,
    norm_gains,
    norm_shifts,
    qkv_weight,
    qkv_bias,
    out_weight,
    gate_up_weight,
    down_weight,
):
    section = lax.axis_index("section")
    row = lax.axis_index("row")
    col = lax.axis_index("col")
    rows_axis = lax.axis_size("row")
    cols_axis = lax.axis_size("col")
    tokens, width = inputs.shape[1:]
    owned = tokens // cols_axis
    units = down_weight.shape[2]
    seq = tokens * rows_axis
    copies = max(1, rows_axis * HEAD_DIM // width)
    head_width = width * copies // rows_axis
    heads = head_width // HEAD_DIM
    both = ("section", "row")

    def weights_of(block):
        block = block[0].reshape(block.shape[1], -1)
        return lax.all_gather(block, both, axis=0, tiled=True).reshape(2, D, -1)

    qkv_w = weights_of(qkv_weight)
    out_w = weights_of(out_weight)
    gate_up_w = weights_of(gate_up_weight)
    down_w = weights_of(down_weight)
    small = lax.all_gather(
        jnp.concatenate([norm_gains, norm_shifts], axis=1), "section", axis=0, tiled=True
    )
    small = lax.all_gather(small, "col", axis=2, tiled=True)
    gains, shifts = small[:, :2], small[:, 2:]
    bias = lax.all_gather(qkv_bias, "section", axis=0, tiled=True).reshape(2, -1)

    ids = lax.dynamic_index_in_dim(block_ids, section, 0, keepdims=False)
    positions = row * tokens + jnp.arange(tokens, dtype=jnp.int32)
    cosines, sines = rotary_lanes(positions, width)
    cos_all, sin_all = rotary_lanes(jnp.arange(seq, dtype=jnp.int32), LANES)

    def mine(values):
        return lax.dynamic_slice_in_dim(values, col * owned, owned, 0)

    def my_features(values):
        return lax.dynamic_slice_in_dim(values, col * width, width, 1)

    def to_heads(values):
        if copies > 1:
            whole = values.reshape(values.shape[:-1] + (-1, HEAD_DIM))
            values = jnp.repeat(whole, copies, axis=-2).reshape(values.shape[:-1] + (-1,))
        return lax.all_to_all(values, "row", values.ndim - 1, 0, tiled=True)

    def from_heads(values):
        values = lax.all_to_all(values, "row", 0, values.ndim - 1, tiled=True)
        if copies > 1:
            whole = values.reshape(values.shape[:-1] + (-1, copies, HEAD_DIM))
            values = whole[..., 0, :].reshape(values.shape[:-1] + (-1,))
        return values

    def by_features(values):
        return lax.all_to_all(values, "col", 1, 0, tiled=True)

    stream = lax.all_gather(
        lax.dynamic_index_in_dim(inputs, section, 0, keepdims=False), "col", axis=1, tiled=True
    )
    kept = []
    hidden_out = []
    for layer in range(2):
        normed = layer_norm(stream, gains[layer, 0], shifts[layer, 0])
        qkv = product(normed, qkv_w[layer]) + bias[layer]
        query = rotate(qkv[:, :width], cosines, sines).astype(jnp.bfloat16) * (HEAD_DIM**-0.5)
        key = rotate(qkv[:, width : 2 * width], cosines, sines).astype(jnp.bfloat16)
        value = qkv[:, 2 * width :].astype(jnp.bfloat16)
        spread = to_heads(jnp.stack([query.astype(jnp.bfloat16), key, value]).transpose(1, 0, 2))
        query, key, value = (lanes_padded(spread[:, i]) for i in range(3))
        mixed, log_sums = attend(query, key, value, ids, heads)
        attn_mix = from_heads(mixed[:, :head_width])
        after = mine(stream).astype(jnp.float32) + summed_rows(
            product(attn_mix, out_w[layer].T)
        ).astype(jnp.float32)
        after_low = after.astype(jnp.bfloat16)
        normed_two = gathered_rows(layer_norm(after_low, gains[layer, 1], shifts[layer, 1]))
        gate_up = product(normed_two, gate_up_w[layer])
        gate, up = gate_up[:, :units], gate_up[:, units:]
        hidden = (jax.nn.silu(gate) * up).astype(jnp.bfloat16)
        result = (
            after + summed_rows(product(hidden, down_w[layer].T)).astype(jnp.float32)
        ).astype(jnp.bfloat16)
        kept.append(
            (stream, normed, query, key, value, mixed, log_sums, attn_mix, after_low, normed_two, gate_up, hidden)
        )
        if layer == 0:
            stream = gathered_rows(result)
            hidden_out.append(my_features(stream))
        else:
            hidden_out.append(by_features(result))

    branch = lax.all_gather(
        lax.dynamic_index_in_dim(cotangent, section, 0, keepdims=False), "col", axis=1, tiled=True
    )
    grad = mine(branch).astype(jnp.float32)
    weight_grads = [None, None]
    small_grads = [None, None]
    bias_grads = [None, None]
    input_out = [None, None]
    for layer in (1, 0):
        (
            stream, normed, query, key, value, mixed, log_sums, attn_mix, after_low, normed_two, gate_up, hidden
        ) = kept[layer]
        gate, up = gate_up[:, :units], gate_up[:, units:]
        down_term = dot_first(branch, hidden)
        d_hidden = product(branch, down_w[layer])
        sig = jax.nn.sigmoid(gate)
        d_gate = d_hidden * up * sig * (1.0 + gate * (1.0 - sig))
        d_up = d_hidden * gate * sig
        d_gate_up = jnp.concatenate([d_gate, d_up], axis=1).astype(jnp.bfloat16)
        gate_up_term = dot_first(normed_two, d_gate_up)
        d_normed_two = summed_rows(dot_last(d_gate_up, gate_up_w[layer]))
        back, sums_two = norm_back(d_normed_two, after_low, gains[layer, 1])
        d_after = grad + back
        grad_attn = gathered_rows(d_after.astype(jnp.bfloat16))
        d_mix = product(grad_attn, out_w[layer]).astype(jnp.bfloat16)
        out_term = dot_first(grad_attn, attn_mix)
        d_mixed = lanes_padded(to_heads(d_mix))
        d_query, d_key, d_value = attend_back(
            query, key, value, d_mixed, mixed, log_sums, ids, cos_all, sin_all, heads
        )
        d_spread = jnp.stack([d[:, :head_width] for d in (d_query, d_key, d_value)])
        d_qkv = from_heads(d_spread.transpose(1, 0, 2)).reshape(tokens, -1)
        bias_grads[layer] = jnp.sum(d_qkv.astype(jnp.float32), axis=0)
        qkv_term = dot_first(normed, d_qkv)
        d_normed = summed_rows(dot_last(d_qkv, qkv_w[layer]))
        back, sums_one = norm_back(d_normed, mine(stream), gains[layer, 0])
        d_input = (d_after + back)
        small_grads[layer] = jnp.stack([sums_one, sums_two], axis=1)
        weight_grads[layer] = (qkv_term, out_term, gate_up_term, down_term)
        if layer == 1:
            grad = d_input
            branch = gathered_rows(d_input.astype(jnp.bfloat16))
            input_out[1] = my_features(branch)
        else:
            input_out[0] = by_features(d_input.astype(jnp.bfloat16))

    def by_section(first, second):
        keep = jnp.where(section == 0, first, second)
        give = jnp.where(section == 0, second, first)
        got = lax.ppermute(give, "section", [(0, 1), (1, 0)])
        return jnp.stack([jnp.where(section == 0, keep, got), jnp.where(section == 0, got, keep)])

    hidden_states = by_section(*hidden_out)
    input_grads = by_section(*input_out).astype(jnp.float32)

    def summed_weights(first, second):
        terms = jnp.concatenate([first, second], axis=0).astype(jnp.bfloat16)
        return lax.psum_scatter(terms, both, scatter_dimension=0, tiled=True).astype(jnp.float32)

    qkv_grad, out_grad, gate_up_grad, down_grad = (
        summed_weights(first, second) for first, second in zip(*weight_grads)
    )
    bias_sum = lax.psum(jnp.stack(bias_grads), both)
    bias_sum = lax.dynamic_index_in_dim(bias_sum, section, 0, keepdims=True)
    small_sum = lax.psum(jnp.stack(small_grads), ("section", "row", "col"))
    small_sum = lax.dynamic_index_in_dim(small_sum, section, 0, keepdims=False)
    small_sum = lax.dynamic_slice_in_dim(small_sum, col * width, width, 2)
    return (
        hidden_states[None],
        input_grads[None],
        small_sum[0][None],
        small_sum[1][None],
        qkv_grad.reshape(qkv_weight.shape),
        bias_sum.reshape(qkv_bias.shape),
        out_grad[None],
        gate_up_grad.reshape(gate_up_weight.shape),
        down_grad[None],
    )


def solution(mesh):
    in_specs = (
        P(None, "row", "col"),
        P(None, "row", "col"),
        P(),
        P("section", None, "col"),
        P("section", None, "col"),
        P("section", "row", None, "col"),
        P("section", None, "col"),
        P("section", "row", "col"),
        P("section", "row", None, "col"),
        P("section", "row", "col"),
    )
    out_specs = (
        P("section", None, "row", "col"),
        P("section", None, "row", "col"),
        P("section", None, "col"),
        P("section", None, "col"),
        P("section", "row", None, "col"),
        P("section", None, "col"),
        P("section", "row", "col"),
        P("section", "row", None, "col"),
        P("section", "row", "col"),
    )
    return jax.shard_map(
        per_device, mesh=mesh, in_specs=in_specs, out_specs=out_specs, check_vma=False
    )
```

time: 5640 us -> 2930 us (0.52)
  waiting for transfers between devices: 3280 us -> 1820 us
  matrix products: 1520 us -> 265 us
  other arithmetic: 474 us -> 136 us
  Pallas kernels: 0 us -> 259 us
  blocking collectives: 140 us -> 240 us
    reduce_scatter x22 -> x12, waiting for transfers between devices: 2160 us -> 764 us  [the longest x8 518 us: summed_rows(): lax.psum_scatter(partial.astype(jnp.bfloat16), 'col', scatter_dimension=0...]
    dot_general x162 -> x24, matrix products: 1520 us -> 265 us  [the longest x12 132 us: product(): return jnp.dot(left, right, preferred_element_type=jnp.float32)]
    pallas_call x0 -> x4, Pallas kernels: none -> 259 us  [the longest x2 157 us: attend_back(): pl.pallas_call(functools.partial(attend_back_kernel, heads, bq, bk), grid...]
    convert_element_type x41 -> x10, other arithmetic: 232 us -> 23.8 us  [the longest x2 7.85 us: per_device(): grad_attn = gathered_rows(d_after.astype(jnp.bfloat16))]
    all_to_all x0 -> x5, blocking collectives: none -> 190 us  [the longest x3 119 us: from_heads(): values = lax.all_to_all(values, 'row', 0, values.ndim - 1, tiled=True)]
    all_gather x22 -> x12, waiting for transfers between devices: 1010 us -> 822 us  [the longest x6 480 us: gathered_rows(): return lax.all_gather(own, 'col', axis=0, tiled=True)]
    reduce_sum x18 -> x13, other arithmetic: 167 us -> 34.4 us  [the longest x4 11 us: norm_back(): jnp.sum(grads * centred, axis=0)]
    psum x0 -> x1, waiting for transfers between devices: none -> 123 us  [per_device(): small_sum = lax.psum(jnp.stack(small_grads), ('section', 'row', 'col'))]
  transfers between devices with their start and end apart: 48 -> 32, of which waited for: 42 -> 27; matrix products, arithmetic and copies ran while one was open for 16% -> 10% of each run, Pallas kernels for 0% -> 2%
where the time goes in v1:
time: 2930 us; the launch traced here: 2920 us
  waiting for transfers between devices  1820 us (62%)
  matrix products  265 us (9%)
  Pallas kernels  259 us (9%)
  blocking collectives  240 us (8%)
  local copies, waits for them, and re-layouts  161 us (5%)
  other arithmetic  136 us (5%)
    reduce_scatter x8, waiting for transfers between devices, summed_rows(): lax.psum_scatter(partial.astype(jnp.bfloat16), 'col', scatter_dimension=0...  518 us
    all_gather x6, waiting for transfers between devices, gathered_rows(): return lax.all_gather(own, 'col', axis=0, tiled=True)  480 us
    reduce_scatter x4, waiting for transfers between devices, summed_weights(): lax.psum_scatter(terms, both, scatter_dimension=0, tiled=True)  245 us
    all_gather x4, waiting for transfers between devices, weights_of(): return lax.all_gather(block, both, axis=0, tiled=True).reshape(2, D, -1)  234 us
    pallas_call x2, Pallas kernels, attend_back(): pl.pallas_call(functools.partial(attend_back_kernel, heads, bq, bk), grid...  157 us
    dot_general x12, matrix products, product(): return jnp.dot(left, right, preferred_element_type=jnp.float32)  132 us
    psum x1, waiting for transfers between devices, per_device(): small_sum = lax.psum(jnp.stack(small_grads), ('section', 'row', 'col'))  123 us
    all_to_all x3, blocking collectives, from_heads(): values = lax.all_to_all(values, 'row', 0, values.ndim - 1, tiled=True)  119 us
  transfers between devices with their start and end apart: 32, of which 27 were waited for; matrix products, arithmetic and copies ran while one was open for 10% of the time, Pallas kernels for 2%

profile of v1, /device:TPU:0, one launch (start us, length us, event | category | flops | bytes accessed | tf_op | source)
XLA Modules:
  0.0 2920.8 jit_solution(8074197788734358743)
XLA Ops:
  99.0 71.2 %all-gather.17.cloned.1.call-done = bf16[4096,1536]{0,1:T(8,128)(2,1)} async-done(((bf16[512,1536]{0,1:T(8,128)(2,1)}), bf16[4096,1536]{0,1:T(8,128)(2,1)}) %all-gather.17.cloned.1.call-update) | async-done | bytes 12582928 | tf_op jit(solution)/shard_map/all_gather | solution.py:257
  263.1 51.0 %shard_map.169 = (bf16[4096,128]{1,0:T(8,128)(2,1)}, f32[128,4096]{1,0:T(8,128)}) custom-call(s32[4096,1]{1,0:T(8,128)} %copy.95.bid_q.bid_k, s32[1,4096]{1,0:T(1,128)} %constant_dynamic-slice_fusion.2.bid_k.bid_q, bf16[4096,128]{1,0:T(8,128)(2,1)} %get-tuple-element.139.q_ref, bf16[4096,128]{1,0:T(8,128)(2,1)} %get-tuple-element.138.k_ref, ...), custom_call_target="tpu_custom_call" | custom-call | flops 8589934592 | bytes 6291456 | tf_op jit(solution)/shard_map/pallas_call | solution.py:87
  340.8 76.9 %reduce-scatter.13.cloned.1.call-done = bf16[256,2048]{1,0:T(8,128)(2,1)} async-done(((bf16[1024,2048]{1,0:T(8,128)(2,1)}), bf16[256,2048]{1,0:T(8,128)(2,1)}) %reduce-scatter.13.cloned.1.call-update) | async-done | bytes 1048592 | tf_op jit(solution)/shard_map/reduce_scatter | solution.py:218
  426.8 76.7 %all-gather.19.cloned.1.call-done = bf16[1024,2048]{1,0:T(8,128)(2,1)} async-done(((bf16[256,2048]{1,0:T(8,128)(2,1)}), bf16[1024,2048]{1,0:T(8,128)(2,1)}) %all-gather.19.cloned.1.call-update) | async-done | bytes 4194320 | tf_op jit(solution)/shard_map/all_gather | solution.py:222
  503.6 117.5 %all-gather.21.cloned.1.call-done = bf16[4096,2816]{1,0:T(8,128)(2,1)} async-done(((bf16[512,2816]{1,0:T(8,128)(2,1)}), bf16[4096,2816]{1,0:T(8,128)(2,1)}) %all-gather.21.cloned.1.call-update) | async-done | bytes 23068688 | tf_op jit(solution)/shard_map/all_gather | solution.py:257
  701.8 76.9 %reduce-scatter.15.cloned.1.call-done = bf16[256,2048]{1,0:T(8,128)(2,1)} async-done(((bf16[1024,2048]{1,0:T(8,128)(2,1)}), bf16[256,2048]{1,0:T(8,128)(2,1)}) %reduce-scatter.15.cloned.1.call-update) | async-done | bytes 1048592 | tf_op jit(solution)/shard_map/reduce_scatter | solution.py:218
  782.5 81.2 %all-gather.23.cloned.1.call-done = bf16[1024,2048]{1,0:T(8,128)(2,1)} async-done(((bf16[256,2048]{1,0:T(8,128)(2,1)}), bf16[1024,2048]{1,0:T(8,128)(2,1)}) %all-gather.23.cloned.1.call-update) | async-done | bytes 4194320 | tf_op jit(solution)/shard_map/all_gather | solution.py:222
  894.2 54.1 %all_to_all.180 = bf16[1024,3,512]{0,1,2:T(4,128)(2,1)} all-to-all(bf16[1024,3,512]{0,1,2:T(4,128)(2,1)} %copy.101), channel_id=1, replica_groups=mesh['section'=2,'row'=4,'col'=4] {'row'}, dimensions={2} | all-to-all | bytes 6291456 | tf_op jit(solution)/shard_map/all_to_all | solution.py:285
  1035.1 74.5 %reduce-scatter.17.cloned.1.call-done = bf16[256,2048]{1,0:T(8,128)(2,1)} async-done(((bf16[1024,2048]{1,0:T(8,128)(2,1)}), bf16[256,2048]{1,0:T(8,128)(2,1)}) %reduce-scatter.17.cloned.1.call-update) | async-done | bytes 1048592 | tf_op jit(solution)/shard_map/reduce_scatter | solution.py:218
  1116.9 78.6 %all-gather.25.cloned.1.call-done = bf16[1024,2048]{1,0:T(8,128)(2,1)} async-done(((bf16[256,2048]{1,0:T(8,128)(2,1)}), bf16[1024,2048]{1,0:T(8,128)(2,1)}) %all-gather.25.cloned.1.call-update) | async-done | bytes 4194320 | tf_op jit(solution)/shard_map/all_gather | solution.py:222
  1214.1 62.2 %all-gather.39.cloned.1.call-done = bf16[1,1024,2048]{2,1,0:T(8,128)(2,1)} async-done(((bf16[1,1024,512]{2,1,0:T(8,128)(2,1)}), bf16[1,1024,2048]{2,1,0:T(8,128)(2,1)}) %all-gather.39.cloned.1.call-update) | async-done | bytes 4194320 | tf_op jit(solution)/shard_map/all_gather | solution.py:332
  1310.9 75.2 %reduce-scatter.21.cloned.1.call-done = bf16[256,2048]{1,0:T(8,128)(2,1)} async-done(((bf16[1024,2048]{1,0:T(8,128)(2,1)}), bf16[256,2048]{1,0:T(8,128)(2,1)}) %reduce-scatter.21.cloned.1.call-update) | async-done | bytes 1048592 | tf_op jit(solution)/shard_map/reduce_scatter | solution.py:218
  1393.1 80.9 %all-gather.27.cloned.1.call-done = bf16[1024,2048]{1,0:T(8,128)(2,1)} async-done(((bf16[256,2048]{1,0:T(8,128)(2,1)}), bf16[1024,2048]{1,0:T(8,128)(2,1)}) %all-gather.27.cloned.1.call-update) | async-done | bytes 4194320 | tf_op jit(solution)/shard_map/all_gather | solution.py:222
  1499.4 78.5 %shard_map.171 = (bf16[4096,128]{1,0:T(8,128)(2,1)}, bf16[4096,128]{1,0:T(8,128)(2,1)}, bf16[4096,128]{1,0:T(8,128)(2,1)}) custom-call(s32[1,4096]{1,0:T(1,128)} %constant_dynamic-slice_fusion.2.bid_k.bid_q, s32[4096,1]{1,0:T(8,128)} %copy.95.bid_q.bid_k, bf16[4096,128]{1,0:T(8,128)(2,1)} %get-tuple-element.136.q_ref, ...), custom_call_target="tpu_custom_call" | custom-call | flops 21474836480 | bytes 10485760 | tf_op jit(solution)/shard_map/pallas_call | solution.py:152
  1681.7 62.5 %reduce-scatter.23.cloned.1.call-done = bf16[256,2048]{1,0:T(8,128)(2,1)} async-done(((bf16[1024,2048]{1,0:T(8,128)(2,1)}), bf16[256,2048]{1,0:T(8,128)(2,1)}) %reduce-scatter.23.cloned.1.call-update) | async-done | bytes 1048592 | tf_op jit(solution)/shard_map/reduce_scatter | solution.py:218
  1747.4 77.0 %reduce-scatter.19.cloned.1.call-done = bf16[256,2048]{1,0:T(8,128)(2,1)} async-done(((bf16[1024,2048]{1,0:T(8,128)(2,1)}), bf16[256,2048]{1,0:T(8,128)(2,1)}) %reduce-scatter.19.cloned.1.call-update) | async-done | bytes 1048592 | tf_op jit(solution)/shard_map/reduce_scatter | solution.py:218
  1829.6 81.4 %all-gather.29.cloned.1.call-done = bf16[1024,2048]{1,0:T(8,128)(2,1)} async-done(((bf16[256,2048]{1,0:T(8,128)(2,1)}), bf16[1024,2048]{1,0:T(8,128)(2,1)}) %all-gather.29.cloned.1.call-update) | async-done | bytes 4194320 | tf_op jit(solution)/shard_map/all_gather | solution.py:222
  1943.9 75.2 %reduce-scatter.25.cloned.1.call-done = bf16[256,2048]{1,0:T(8,128)(2,1)} async-done(((bf16[1024,2048]{1,0:T(8,128)(2,1)}), bf16[256,2048]{1,0:T(8,128)(2,1)}) %reduce-scatter.25.cloned.1.call-update) | async-done | bytes 1048592 | tf_op jit(solution)/shard_map/reduce_scatter | solution.py:218
  2025.9 81.4 %all-gather.31.cloned.1.call-done = bf16[1024,2048]{1,0:T(8,128)(2,1)} async-done(((bf16[256,2048]{1,0:T(8,128)(2,1)}), bf16[1024,2048]{1,0:T(8,128)(2,1)}) %all-gather.31.cloned.1.call-update) | async-done | bytes 4194320 | tf_op jit(solution)/shard_map/all_gather | solution.py:222
  2130.8 78.4 %shard_map.172 = (bf16[4096,128]{1,0:T(8,128)(2,1)}, bf16[4096,128]{1,0:T(8,128)(2,1)}, bf16[4096,128]{1,0:T(8,128)(2,1)}) custom-call(s32[1,4096]{1,0:T(1,128)} %constant_dynamic-slice_fusion.2.bid_k.bid_q, s32[4096,1]{1,0:T(8,128)} %copy.95.bid_q.bid_k, bf16[4096,128]{1,0:T(8,128)(2,1)} %get-tuple-element.139.q_ref, ...), custom_call_target="tpu_custom_call" | custom-call | flops 21474836480 | bytes 10485760 | tf_op jit(solution)/shard_map/pallas_call | solution.py:152
  2231.4 51.1 %all_to_all.184 = bf16[4096,3,128]{2,1,0:T(4,128)(2,1)S(1)} all-to-all(bf16[4096,3,128]{2,1,0:T(4,128)(2,1)S(1)} %copy.117), channel_id=1, replica_groups=mesh['section'=2,'row'=4,'col'=4] {'row'}, dimensions={0} | all-to-all | bytes 6291456 | tf_op jit(solution)/shard_map/all_to_all | solution.py:288
  2537.6 122.5 %all-reduce.2.cloned.1.call-done = f32[2,2,2,2048]{3,2,1,0:T(2,128)} async-done(((f32[2,2,2,2048]{3,2,1,0:T(2,128)}), f32[2,2,2,2048]{3,2,1,0:T(2,128)}) %all-reduce.2.cloned.1.call-update) | async-done | bytes 65552 | tf_op jit(solution)/shard_map/psum | solution.py:396
  2665.5 145.3 %reduce-scatter.33.cloned.1.call-done = bf16[512,2816]{1,0:T(8,128)(2,1)} async-done(((bf16[4096,2816]{1,0:T(8,128)(2,1)}), bf16[512,2816]{1,0:T(8,128)(2,1)}) %reduce-scatter.33.cloned.1.call-update) | async-done | bytes 2883600 | tf_op jit(solution)/shard_map/reduce_scatter | solution.py:389
  2817.9 89.2 %reduce-scatter.29.cloned.1.call-done = bf16[512,1536]{1,0:T(8,128)(2,1)} async-done(((bf16[4096,1536]{1,0:T(8,128)(2,1)}), bf16[512,1536]{1,0:T(8,128)(2,1)}) %reduce-scatter.29.cloned.1.call-update) | async-done | bytes 1572880 | tf_op jit(solution)/shard_map/reduce_scatter | solution.py:389
  (385 shorter events, 986.0 us)
Async XLA Ops:
  9.8 160.3 %all-gather.17.cloned.1.call-start = ((), (), s32[]{:S(2)}) async-start(), calls=%async_computation.22 | async-start | bytes 14155776 | tf_op jit(solution)/shard_map/all_gather | solution.py:257
  12.5 307.4 %all-gather.35.cloned.1.call-start = ((), (), s32[]{:S(2)}) async-start(), calls=%async_computation.44 | async-start | bytes 4718592 | tf_op jit(solution)/shard_map/all_gather | solution.py:257
  340.7 162.9 %all-gather.19.cloned.1.call-start = ((), (), s32[]{:S(2)}) async-start(), calls=%async_computation.24 | async-start | bytes 5242880 | tf_op jit(solution)/shard_map/all_gather | solution.py:222
  422.1 198.9 %all-gather.21.cloned.1.call-start = ((), (), s32[]{:S(2)}) async-start(), calls=%async_computation.25 | async-start | bytes 25952256 | tf_op jit(solution)/shard_map/all_gather | solution.py:257
  426.0 264.8 %all-gather.37.cloned.1.call-start = ((), (), s32[]{:S(2)}) async-start(), calls=%async_computation.45 | async-start | bytes 12976128 | tf_op jit(solution)/shard_map/all_gather | solution.py:257
  426.8 351.9 %reduce-scatter.15.cloned.1.call-start = ((), (), s32[]{:S(2)}) async-start(), calls=%async_computation.26 | async-start | bytes 5242880 | tf_op jit(solution)/shard_map/reduce_scatter | solution.py:218
  701.8 162.0 %all-gather.23.cloned.1.call-start = ((), (), s32[]{:S(2)}) async-start(), calls=%async_computation.27 | async-start | bytes 5242880 | tf_op jit(solution)/shard_map/all_gather | solution.py:222
  782.3 327.3 %reduce-scatter.17.cloned.1.call-start = ((), (), s32[]{:S(2)}) async-start(), calls=%async_computation.28 | async-start | bytes 5242880 | tf_op jit(solution)/shard_map/reduce_scatter | solution.py:218
  1035.0 160.5 %all-gather.25.cloned.1.call-start = ((), (), s32[]{:S(2)}) async-start(), calls=%async_computation.29 | async-start | bytes 5242880 | tf_op jit(solution)/shard_map/all_gather | solution.py:222
  1114.1 162.2 %all-gather.39.cloned.1.call-start = ((), (), s32[]{:S(2)}) async-start(), calls=%async_computation.46 | async-start | bytes 5242880 | tf_op jit(solution)/shard_map/all_gather | solution.py:332
  1116.4 269.7 %reduce-scatter.21.cloned.1.call-start = ((), (), s32[]{:S(2)}) async-start(), calls=%async_computation.31 | async-start | bytes 5242880 | tf_op jit(solution)/shard_map/reduce_scatter | solution.py:218
  1310.7 163.3 %all-gather.27.cloned.1.call-start = ((), (), s32[]{:S(2)}) async-start(), calls=%async_computation.32 | async-start | bytes 5242880 | tf_op jit(solution)/shard_map/all_gather | solution.py:222
  1484.0 260.2 %reduce-scatter.23.cloned.1.call-start = ((), (), s32[]{:S(2)}) async-start(), calls=%async_computation.33 | async-start | bytes 5242880 | tf_op jit(solution)/shard_map/reduce_scatter | solution.py:218
  1669.7 154.7 %reduce-scatter.19.cloned.1.call-start = ((), (), s32[]{:S(2)}) async-start(), calls=%async_computation.30 | async-start | bytes 5242880 | tf_op jit(solution)/shard_map/reduce_scatter | solution.py:218
  1681.1 229.8 %all-gather.29.cloned.1.call-start = ((), (), s32[]{:S(2)}) async-start(), calls=%async_computation.34 | async-start | bytes 5242880 | tf_op jit(solution)/shard_map/all_gather | solution.py:222
  1829.5 189.5 %reduce-scatter.25.cloned.1.call-start = ((), (), s32[]{:S(2)}) async-start(), calls=%async_computation.35 | async-start | bytes 5242880 | tf_op jit(solution)/shard_map/reduce_scatter | solution.py:218
  1943.6 163.6 %all-gather.31.cloned.1.call-start = ((), (), s32[]{:S(2)}) async-start(), calls=%async_computation.36 | async-start | bytes 5242880 | tf_op jit(solution)/shard_map/all_gather | solution.py:222
  2025.8 352.3 %reduce-scatter.27.cloned.1.call-start = ((), (), s32[]{:S(2)}) async-start(), calls=%async_computation.37 | async-start | bytes 5242880 | tf_op jit(solution)/shard_map/reduce_scatter | solution.py:218
  2301.3 196.3 %reduce-scatter.35.cloned.1.call-start = ((), (), s32[]{:S(2)}) async-start(), calls=%async_computation.42 | async-start | bytes 12976128 | tf_op jit(solution)/shard_map/reduce_scatter | solution.py:389
  2333.4 202.1 %reduce-scatter.31.cloned.1.call-start = ((), (), s32[]{:S(2)}) async-start(), calls=%async_computation.40 | async-start | bytes 4718592 | tf_op jit(solution)/shard_map/reduce_scatter | solution.py:389
  2344.6 315.5 %all-reduce.2.cloned.1.call-start = ((), (), s32[]{:S(2)}) async-start(), calls=%async_computation.38 | async-start | bytes 131072 | tf_op jit(solution)/shard_map/psum | solution.py:396
  2381.5 429.3 %reduce-scatter.33.cloned.1.call-start = ((), (), s32[]{:S(2)}) async-start(), calls=%async_computation.41 | async-start | bytes 25952256 | tf_op jit(solution)/shard_map/reduce_scatter | solution.py:389
  2402.9 504.2 %reduce-scatter.29.cloned.1.call-start = ((), (), s32[]{:S(2)}) async-start(), calls=%async_computation.39 | async-start | bytes 14155776 | tf_op jit(solution)/shard_map/reduce_scatter | solution.py:389
  2497.1 164.4 %collective-permute-start.1 = (bf16[1024,512]{1,0:T(8,128)(2,1)S(1)}, bf16[1024,512]{1,0:T(8,128)(2,1)S(1)}, u32[]{:S(2)}, u32[]{:S(2)}) collective-permute-start(bf16[1024,512]{1,0:T(8,128)(2,1)S(1)} %bitcast_select_fusion), channel_id=1, source_target_pairs={{0,16},{16,0},{1,17},{17,1},{2,18},{18,2},{3,19},{19,3},{4,20},{20... | collective-permute-start | bytes 3145736 | tf_op jit(solution)/shard_map/ppermute | solution.py:381
  (87 other events, 3677.5 us)
Sparse Core Ops, SparseCore 0:
  10.2 84.4 all-gather.32
  97.1 73.0 all-gather.16
  340.8 76.7 reduce-scatter.12
  422.3 81.2 all-gather.18
  506.0 114.9 all-gather.20
  623.1 67.6 all-gather.36
  701.9 76.7 reduce-scatter.14
  782.4 81.2 all-gather.22
  1035.1 74.3 reduce-scatter.16
  1114.2 81.2 all-gather.24
  1197.0 79.2 all-gather.38
  1310.8 75.2 reduce-scatter.20
  1392.6 81.2 all-gather.26
  1669.8 74.3 reduce-scatter.22
  1747.0 77.2 reduce-scatter.18
  1829.6 81.2 all-gather.28
  1943.8 75.2 reduce-scatter.24
  2025.9 81.2 all-gather.30
  2301.4 74.3 reduce-scatter.26
  2379.4 87.2 reduce-scatter.34
  2470.6 64.7 reduce-scatter.30
  2542.6 117.5 all-reduce.1
  2664.0 146.6 reduce-scatter.32
  2814.7 92.4 reduce-scatter.28
  (1 shorter events, 38.5 us)

commit v2 on v1

v2 whole, which is shorter than its diff:
```python
import functools

import jax
import jax.numpy as jnp
from jax import lax
from jax.experimental import pallas as pl
from jax.experimental.pallas import tpu as pltpu
from jax.sharding import PartitionSpec as P

D = 2048
HEADS = 32
HEAD_DIM = 64
ROT = 16
LANES = 128
REACH = 256
RELAY_ROWS = 16


epsilon = 1e-05


def dot_last(a, b):
    return lax.dot_general(a, b, (((1,), (1,)), ((), ())), preferred_element_type=jnp.float32)


def dot_first(a, b):
    return lax.dot_general(a, b, (((0,), (0,)), ((), ())), preferred_element_type=jnp.float32)


def lanes_of(rows, head):
    lane = lax.broadcasted_iota(jnp.int32, (rows, LANES), 1)
    return lane // HEAD_DIM == head


def spin(x, cosines, sines):
    lane = lax.broadcasted_iota(jnp.int32, x.shape, 1)
    ahead, behind = pltpu.roll(x, LANES - ROT // 2, 1), pltpu.roll(x, ROT // 2, 1)
    return x * cosines + jnp.where(lane % ROT < ROT // 2, ahead, behind) * sines


def meet(axis, n):
    me = lax.axis_index(axis)
    barrier = pltpu.get_barrier_semaphore()
    for d in range(1, n):
        pl.semaphore_signal(
            barrier, 1, device_id={axis: lax.rem(me + d, n)}, device_id_type=pl.DeviceIdType.MESH
        )
    pl.semaphore_wait(barrier, n - 1)


def remote(source, target, sent, got, axis, device):
    return pltpu.make_async_remote_copy(
        src_ref=source,
        dst_ref=target,
        send_sem=sent,
        recv_sem=got,
        device_id={axis: device},
        device_id_type=pl.DeviceIdType.MESH,
    )


def columns(which, size=LANES):
    return pl.ds(pl.multiple_of(which * size, size), size)


def attend_kernel(
    heads, n, bq, bk, bid_q, bid_k, qkv, cosines, sines,
    spread, mixed, lse_ref, mix, vone, scores, leaving, qkv_sent, qkv_got, mix_sent, mix_got,
):
    me = lax.axis_index("row")
    tokens = qkv.shape[0]
    seq = n * tokens
    here = pl.ds(pl.multiple_of(me * tokens, tokens), tokens)
    low = jnp.bfloat16
    meet("row", n)

    def parts(t):
        cos, sin = cosines[...], sines[...]
        query = spin(qkv[:, columns(t)], cos, sin).astype(low) * jnp.asarray(HEAD_DIM**-0.5, low)
        key = spin(qkv[:, columns(n + t)], cos, sin).astype(low)
        return query.astype(low), key, qkv[:, columns(2 * n + t)].astype(low)

    def leave(d):
        to = lax.rem(me + d, n)
        return remote(leaving.at[d - 1], spread.at[:, here], qkv_sent.at[d - 1], qkv_got.at[me], "row", to)

    for d in range(1, n):
        for k, part in enumerate(parts(lax.rem(me + d, n))):
            leaving[d - 1, k] = part
        leave(d).start()
    for k, part in enumerate(parts(me)):
        spread[k, here, :] = part

    def come(row):
        @pl.when(row != me)
        def _():
            there = pl.ds(row * tokens, tokens)
            remote(leaving.at[0], spread.at[:, there], qkv_sent.at[0], qkv_got.at[row], "row", me).wait_recv()

        there = pl.ds(row * tokens, tokens)
        for h in range(heads):
            vone[h, there, :] = jnp.where(lanes_of(tokens, h), spread[2, there, :], jnp.ones((), low))

    def mix_copy(i, device):
        rows = pl.ds(lax.rem(i, tokens // bq) * bq, bq)
        return remote(
            mixed.at[pl.ds(i * bq, bq)], mix.at[rows, columns(me)], mix_sent.at[i], mix_got.at[me, lax.rem(i, tokens // bq)], "row", device
        )

    def block(i, carry):
        rows = pl.ds(pl.multiple_of(i * bq, bq), bq)
        q = spread[0, rows, :]
        bid = bid_q[rows, :]
        free = i * (bq // bk)
        last = jnp.minimum(((i + 1) * bq + REACH + bk - 1) // bk, seq // bk)
        qs = [jnp.where(lanes_of(bq, h), q, jnp.zeros((), low)) for h in range(heads)]

        def score(t, tops, hide):
            span = pl.ds(pl.multiple_of(t * bk, bk), bk)
            keys = spread[1, span, :]
            if hide:
                visible = bid_k[:, span] <= bid
            found = []
            for h in range(heads):
                s = dot_last(qs[h], keys)
                if hide:
                    s = jnp.where(visible, s, -1e30)
                scores[h, :, span] = s
                top = tops[h]
                for c in range(bk // LANES):
                    top = jnp.maximum(top, s[:, c * LANES : (c + 1) * LANES])
                found.append(top)
            return tuple(found)

        tops = tuple(jnp.full((bq, LANES), -1e30, jnp.float32) for _ in range(heads))
        tops = lax.fori_loop(0, free, lambda t, c: score(t, c, False), tops)
        tops = lax.fori_loop(free, last, lambda t, c: score(t, c, True), tops)
        tops = [jnp.max(top, axis=1, keepdims=True) for top in tops]

        def gather(t, sums):
            span = pl.ds(pl.multiple_of(t * bk, bk), bk)
            found = []
            for h in range(heads):
                p = jnp.exp(scores[h, :, span] - tops[h]).astype(low)
                found.append(sums[h] + jnp.dot(p, vone[h, span, :], preferred_element_type=jnp.float32))
            return tuple(found)

        sums = tuple(jnp.zeros((bq, LANES), jnp.float32) for _ in range(heads))
        sums = lax.fori_loop(0, last, gather, sums)
        outcome = jnp.zeros((bq, LANES), jnp.float32)
        lse = jnp.zeros((bq, LANES), jnp.float32)
        for h in range(heads):
            totals = pltpu.roll(sums[h], HEAD_DIM, 1)
            outcome = jnp.where(lanes_of(bq, h), sums[h] / totals, outcome)
            lse = jnp.where(lanes_of(bq, h), tops[h] + jnp.log(totals), lse)
        mixed[rows, :] = outcome.astype(low)
        lse_ref[:, rows] = lse.T
        return carry

    per_row = tokens // bq
    for row in range(n):
        if row == 0:
            come(0)
        if row + 1 < n:
            come(row + 1)

        def run(half, carry, row=row):
            i = row * per_row + half
            block(i, 0)

            @pl.when(row == me)
            def _():
                mix[pl.ds(pl.multiple_of(half * bq, bq), bq), columns(me)] = mixed[pl.ds(pl.multiple_of(i * bq, bq), bq), :]

            @pl.when(row != me)
            def _():
                mix_copy(i, row).start()

            return carry

        lax.fori_loop(0, per_row, run, 0)

    for d in range(1, n):
        leave(d).wait_send()
    for i in range(n * per_row):
        @pl.when(i // per_row != me)
        def _(i=i):
            mix_copy(i, me).wait_send()

    for row in range(n):
        @pl.when(row != me)
        def _(row=row):
            for half in range(per_row):
                rows = pl.ds(half * bq, bq)
                remote(
                    mixed.at[pl.ds(0, bq)], mix.at[rows, columns(row)], mix_sent.at[0], mix_got.at[row, half], "row", me
                ).wait_recv()


def attend(number, qkv, block_all, cosines, sines, heads, n, bq=512, bk=512):
    tokens = qkv.shape[0]
    bq, bk = min(bq, tokens), min(bk, tokens)
    seq = n * tokens
    vmem = pl.BlockSpec(memory_space=pltpu.VMEM)
    low = jnp.bfloat16
    return pl.pallas_call(
        functools.partial(attend_kernel, heads, n, bq, bk),
        in_specs=[vmem] * 5,
        out_specs=[vmem] * 4,
        out_shape=[
            jax.ShapeDtypeStruct((3, seq, LANES), low),
            jax.ShapeDtypeStruct((seq, LANES), low),
            jax.ShapeDtypeStruct((LANES, seq), jnp.float32),
            jax.ShapeDtypeStruct((tokens, n * LANES), low),
        ],
        scratch_shapes=[
            pltpu.VMEM((heads, seq, LANES), low),
            pltpu.VMEM((heads, bq, seq), jnp.float32),
            pltpu.VMEM((n - 1, 3, tokens, LANES), low),
            pltpu.SemaphoreType.DMA((n - 1,)),
            pltpu.SemaphoreType.DMA((n,)),
            pltpu.SemaphoreType.DMA((seq // bq,)),
            pltpu.SemaphoreType.DMA((n, tokens // bq)),
        ],
        compiler_params=pltpu.CompilerParams(
            collective_id=number, has_side_effects=True, vmem_limit_bytes=58 * 2**20
        ),
        cost_estimate=pl.CostEstimate(flops=10**10, bytes_accessed=2 * 10**8, transcendentals=0),
    )(block_all.reshape(seq, 1), block_all.reshape(1, seq), qkv, cosines, sines)


def attend_back_kernel(
    heads, n, bq, bk, bid_q, bid_k, d_mix, spread, mixed, lse_ref, cosines, sines,
    d_qkv, grads, kone, dk_acc, dv_acc, leaving, g_sent, g_got, back_sent, back_got,
):
    me = lax.axis_index("row")
    tokens = d_mix.shape[0]
    seq = n * tokens
    per_row = tokens // bq
    blocks = n * per_row
    low = jnp.bfloat16
    zero = jnp.zeros((), low)
    here = pl.ds(pl.multiple_of(me * tokens, tokens), tokens)
    meet("row", n)

    def give(d):
        to = lax.rem(me + d, n)
        return remote(d_mix.at[:, columns(to)], grads.at[here], g_sent.at[d - 1], g_got.at[me], "row", to)

    for d in range(1, n):
        give(d).start()
    grads[here, :] = d_mix[:, columns(me)]
    for h in range(heads):
        kone[h] = jnp.where(lanes_of(seq, h), spread[1], zero)
    dk_acc[...] = jnp.zeros_like(dk_acc)
    dv_acc[...] = jnp.zeros_like(dv_acc)

    def tile(t, dq, hide, stuff):
        qs, gs, lses, deltas, bid = stuff
        span = pl.ds(pl.multiple_of(t * bk, bk), bk)
        keys, values = spread[1, span, :], spread[2, span, :]
        dv, dk = dv_acc[span, :], dk_acc[span, :]
        if hide:
            visible = bid_k[span, :] <= bid
        for h in range(heads):
            s = dot_last(keys, qs[h])
            if hide:
                s = jnp.where(visible, s, -1e30)
            p = jnp.exp(s - lses[h])
            dp = dot_last(values, gs[h])
            ds = (p * (dp - deltas[h])).astype(low)
            dv = dv + jnp.dot(p.astype(low), gs[h], preferred_element_type=jnp.float32)
            dk = dk + jnp.dot(ds, qs[h], preferred_element_type=jnp.float32)
            dq = dq + dot_first(ds, kone[h, span, :])
        dv_acc[span, :] = dv
        dk_acc[span, :] = dk
        return dq

    def block(i):
        rows = pl.ds(pl.multiple_of(i * bq, bq), bq)
        q, g = spread[0, rows, :], grads[rows, :]
        product = (g.astype(jnp.float32) * mixed[rows, :].astype(jnp.float32)).T
        span = lambda h: slice(h * HEAD_DIM, (h + 1) * HEAD_DIM)
        deltas = [jnp.sum(product[span(h)], axis=0, keepdims=True) for h in range(heads)]
        lses = [lse_ref[h * HEAD_DIM : h * HEAD_DIM + 1, rows] for h in range(heads)]
        qs = [jnp.where(lanes_of(bq, h), q, zero) for h in range(heads)]
        gs = [jnp.where(lanes_of(bq, h), g, zero) for h in range(heads)]
        stuff = (qs, gs, lses, deltas, bid_q[:, rows])
        free = i * (bq // bk)
        last = jnp.minimum(((i + 1) * bq + REACH + bk - 1) // bk, seq // bk)
        dq = jnp.zeros((bq, LANES), jnp.float32)
        dq = lax.fori_loop(0, free, lambda t, c: tile(t, c, False, stuff), dq)
        dq = lax.fori_loop(free, last, lambda t, c: tile(t, c, True, stuff), dq)
        return spin(dq * (HEAD_DIM**-0.5), cosines[rows, :], -sines[rows, :]).astype(low)

    def back_copy(k, i, device):
        half = lax.rem(i, per_row)
        rows = pl.ds(pl.multiple_of(half * bq, bq), bq)
        return remote(
            leaving.at[k, pl.ds(pl.multiple_of(i * bq, bq), bq)],
            d_qkv.at[rows, columns(k * n + me)],
            back_sent.at[k, i],
            back_got.at[k, me, half],
            "row",
            device,
        )

    def send(k, i, values):
        row = i // per_row
        half = lax.rem(i, per_row)

        @pl.when(row == me)
        def _():
            d_qkv[pl.ds(pl.multiple_of(half * bq, bq), bq), columns(k * n + me)] = values

        @pl.when(row != me)
        def _():
            leaving[k, pl.ds(pl.multiple_of(i * bq, bq), bq), :] = values
            back_copy(k, i, row).start()

    def keys_done(i):
        rows = pl.ds(pl.multiple_of(i * bq, bq), bq)
        send(1, i, spin(dk_acc[rows, :], cosines[rows, :], -sines[rows, :]).astype(low))
        send(2, i, dv_acc[rows, :].astype(low))

    for row in range(n - 1, -1, -1):
        @pl.when(row != me)
        def _(row=row):
            there = pl.ds(row * tokens, tokens)
            remote(d_mix.at[:, columns(0)], grads.at[there], g_sent.at[0], g_got.at[row], "row", me).wait_recv()

        def run(step, carry, row=row):
            i = row * per_row + per_row - 1 - step
            send(0, i, block(i))

            @pl.when(i + 1 < blocks)
            def _():
                keys_done(i + 1)

            return carry

        lax.fori_loop(0, per_row, run, 0)
    keys_done(0)

    for d in range(1, n):
        give(d).wait_send()

    def settle(i, carry):
        @pl.when(i // per_row != me)
        def _():
            half = lax.rem(i, per_row)
            rows = pl.ds(pl.multiple_of(half * bq, bq), bq)
            for k in range(3):
                back_copy(k, i, me).wait_send()
                remote(
                    leaving.at[k, pl.ds(0, bq)],
                    d_qkv.at[rows, columns(k * n + i // per_row)],
                    back_sent.at[k, 0],
                    back_got.at[k, i // per_row, half],
                    "row",
                    me,
                ).wait_recv()

        return carry

    lax.fori_loop(0, blocks, settle, 0)


def attend_back(number, d_mix, spread, mixed, lse, block_all, cosines, sines, heads, n, bq=512, bk=512):
    tokens = d_mix.shape[0]
    bq, bk = min(bq, tokens), min(bk, tokens)
    seq = n * tokens
    vmem = pl.BlockSpec(memory_space=pltpu.VMEM)
    low = jnp.bfloat16
    return pl.pallas_call(
        functools.partial(attend_back_kernel, heads, n, bq, bk),
        in_specs=[vmem] * 8,
        out_specs=vmem,
        out_shape=jax.ShapeDtypeStruct((tokens, 3 * n * LANES), low),
        scratch_shapes=[
            pltpu.VMEM((seq, LANES), low),
            pltpu.VMEM((heads, seq, LANES), low),
            pltpu.VMEM((seq, LANES), jnp.float32),
            pltpu.VMEM((seq, LANES), jnp.float32),
            pltpu.VMEM((3, seq, LANES), low),
            pltpu.SemaphoreType.DMA((n - 1,)),
            pltpu.SemaphoreType.DMA((n,)),
            pltpu.SemaphoreType.DMA((3, seq // bq)),
            pltpu.SemaphoreType.DMA((3, n, tokens // bq)),
        ],
        compiler_params=pltpu.CompilerParams(
            collective_id=number, has_side_effects=True, vmem_limit_bytes=58 * 2**20
        ),
        cost_estimate=pl.CostEstimate(flops=10**10, bytes_accessed=3 * 10**8, transcendentals=0),
    )(block_all.reshape(1, seq), block_all.reshape(seq, 1), d_mix, spread, mixed, lse, cosines, sines)


def norm_parts(values):
    mean = jnp.mean(values, axis=-1, keepdims=True)
    spread = jnp.mean(values * values, axis=-1, keepdims=True) - mean * mean
    return mean, lax.rsqrt(spread + epsilon)


def after_attention(total, c, ins, outs):
    stream, gain, shift = ins
    (after_ref,) = outs
    after = stream[c].astype(jnp.float32) + total
    after_ref[c] = after
    values = after.astype(jnp.bfloat16).astype(jnp.float32)
    mean, inverse = norm_parts(values)
    return ((values - mean) * inverse * gain[...] + shift[...]).astype(jnp.bfloat16)


def after_hidden(total, c, ins, outs):
    (after,) = ins
    return (after[c] + total).astype(jnp.bfloat16)


def behind_norm(total, c, ins, outs):
    grad, values_ref, gain = ins
    grad_ref, sums = outs
    values = values_ref[c].astype(jnp.bfloat16).astype(jnp.float32)
    mean, inverse = norm_parts(values)
    centred = (values - mean) * inverse
    scaled = total * gain[...]
    back = inverse * (
        scaled
        - jnp.mean(scaled, axis=-1, keepdims=True)
        - centred * jnp.mean(scaled * centred, axis=-1, keepdims=True)
    )
    given = grad[c] + back
    grad_ref[c] = given
    here = [jnp.sum(total * centred, axis=0, keepdims=True), jnp.sum(total, axis=0, keepdims=True)]

    @pl.when(c == 0)
    def _():
        sums[...] = jnp.zeros_like(sums)

    sums[...] += jnp.concatenate(here, axis=0)
    return given.astype(jnp.bfloat16)


def relay_kernel(middle, n_ins, n_outs, n, chunks, lag, spread, partial, *refs):
    ins, refs = refs[:n_ins], refs[n_ins:]
    whole, outs, refs = refs[0], refs[1 : 1 + n_outs], refs[1 + n_outs :]
    arrived, outgoing, total, sum_sent, sum_got, block_sent, block_got = refs
    i = lax.axis_index("col")
    width = whole.shape[-1]
    first, last = i == 0, i == n - 1

    barrier = pltpu.get_barrier_semaphore()
    if spread:
        for d in range(1, n):
            pl.semaphore_signal(barrier, 1, device_id={"col": lax.rem(i + d, n)}, device_id_type=pl.DeviceIdType.MESH)
        pl.semaphore_wait(barrier, n - 1)
    else:
        @pl.when(i > 0)
        def _():
            pl.semaphore_signal(barrier, 1, device_id={"col": i - 1}, device_id_type=pl.DeviceIdType.MESH)

        @pl.when(i < n - 1)
        def _():
            pl.semaphore_signal(barrier, 1, device_id={"col": i + 1}, device_id_type=pl.DeviceIdType.MESH)

        @pl.when(first | last)
        def _():
            pl.semaphore_wait(barrier, 1)

        @pl.when((i > 0) & (i < n - 1))
        def _():
            pl.semaphore_wait(barrier, 2)

    def remote_col(source, target, sent, got, device):
        return remote(source, target, sent, got, "col", device)

    def sum_copy(c, j, right):
        slot = j + 1 if right else j
        return remote_col(
            outgoing.at[c, j], arrived.at[c, slot], sum_sent.at[c, j], sum_got.at[c, slot], i + 1 if right else i - 1
        )

    def block_copy(c, o, right, own=False):
        sent = n if own and not right else o
        return remote_col(whole.at[c, o], whole.at[c, o], block_sent.at[c, sent], block_got.at[c, o], i + 1 if right else i - 1)

    def slice_copy(c, d):
        to = lax.rem(i + d, n)
        source = outgoing.at[c, i, :, pl.ds(pl.multiple_of(to * width, 128), width)]
        return remote_col(source, whole.at[c, i], block_sent.at[c, d], block_got.at[c, i], to)

    def arrive(c, slot):
        remote_col(outgoing.at[c, 0], arrived.at[c, slot], sum_sent.at[c, 0], sum_got.at[c, slot], i).wait_recv()

    def middle_slot(k):
        return jnp.maximum(lag * k + n - 1 - k, lag * (n - 1 - k) + k)

    def at(now, slot, allowed):
        since = now - slot
        c = jnp.maximum(since, 0) // n
        return c, allowed & (since >= 0) & (lax.rem(jnp.maximum(since, 0), n) == 0) & (since < n * chunks)

    def step(now, carry):
        for j in range(n - 1, 0, -1):
            c, due = at(now, lag * i + n - 1 - j, i < j)

            @pl.when(due & first)
            def _(c=c, j=j):
                outgoing[c, j] = partial[c, j]

            @pl.when(due & (i > 0))
            def _(c=c, j=j):
                arrive(c, j + 1)
                both = arrived[c, j + 1].astype(jnp.float32) + partial[c, j].astype(jnp.float32)
                outgoing[c, j] = both.astype(jnp.bfloat16)

            @pl.when(due)
            def _(c=c, j=j):
                sum_copy(c, j, True).start()

        for j in range(n - 1):
            c, due = at(now, lag * (n - 1 - i) + j, i > j)

            @pl.when(due & last)
            def _(c=c, j=j):
                outgoing[c, j] = partial[c, j]

            @pl.when(due & (i < n - 1))
            def _(c=c, j=j):
                arrive(c, j)
                both = arrived[c, j].astype(jnp.float32) + partial[c, j].astype(jnp.float32)
                outgoing[c, j] = both.astype(jnp.bfloat16)

            @pl.when(due)
            def _(c=c, j=j):
                sum_copy(c, j, False).start()

        c, due = at(now, middle_slot(i), i >= 0)

        @pl.when(due)
        def _():
            total[...] = partial[c, i].astype(jnp.float32)

        @pl.when(due & (i > 0))
        def _():
            arrive(c, i + 1)
            total[...] += arrived[c, i + 1].astype(jnp.float32)

        @pl.when(due & (i < n - 1))
        def _():
            arrive(c, i)
            total[...] += arrived[c, i].astype(jnp.float32)

        @pl.when(due)
        def _():
            block = middle(total[...], c, ins, outs)
            if spread:
                outgoing[c, i] = block
                for d in range(1, n):
                    slice_copy(c, d).start()
                whole[c, i] = outgoing[c, i, :, pl.ds(pl.multiple_of(i * width, 128), width)]
            else:
                whole[c, i] = block

        if spread:
            return carry

        @pl.when(due & (i < n - 1))
        def _():
            block_copy(c, i, True, own=True).start()

        @pl.when(due & (i > 0))
        def _():
            block_copy(c, i, False, own=True).start()

        for o in range(n - 1):
            c, due = at(now, middle_slot(o) + lag * (i - o), i > o)

            @pl.when(due)
            def _(c=c, o=o):
                block_copy(c, o, True).wait_recv()

            @pl.when(due & (i < n - 1))
            def _(c=c, o=o):
                block_copy(c, o, True).start()

        for o in range(1, n):
            c, due = at(now, middle_slot(o) + lag * (o - i), i < o)

            @pl.when(due)
            def _(c=c, o=o):
                block_copy(c, o, False).wait_recv()

            @pl.when(due & (i > 0))
            def _(c=c, o=o):
                block_copy(c, o, False).start()

        return carry

    lax.fori_loop(0, n * (chunks - 1) + 2 * lag * (n - 1) + 1, step, 0)

    def settle(c, carry):
        for j in range(n):
            @pl.when(j != i)
            def _(j=j):
                sum_copy(c, j, True).wait_send()
                if spread:
                    remote_col(outgoing.at[c, j, :, pl.ds(0, width)], whole.at[c, j], block_sent.at[c, 0], block_got.at[c, j], i).wait_recv()

        if spread:
            for d in range(1, n):
                slice_copy(c, d).wait_send()
            return carry
        for o in range(n):
            @pl.when((o <= i) & (i < n - 1))
            def _(o=o):
                block_copy(c, o, True).wait_send()

            @pl.when((o > i) & (i > 0))
            def _(o=o):
                block_copy(c, o, True).wait_send()

        @pl.when(i > 0)
        def _():
            block_copy(c, i, False, own=True).wait_send()

        return carry

    lax.fori_loop(0, chunks, settle, 0)


def relay(middle, number, partial, ins, outs, n, spread=False, lag=3, rows=RELAY_ROWS):
    tokens, features = partial.shape
    owned = tokens // n
    chunks = owned // rows
    blocks = lambda values: values.reshape(chunks, rows, features) if values.shape[0] == owned else values
    ins = [blocks(values) for values in ins]
    out_shapes = [
        jax.ShapeDtypeStruct((chunks, n, rows, features // n if spread else features), jnp.bfloat16)
    ] + [
        jax.ShapeDtypeStruct((chunks, rows, features) if shape[0] == owned else shape, jnp.float32) for shape in outs
    ]
    vmem = pl.BlockSpec(memory_space=pltpu.VMEM)
    whole, *rest = pl.pallas_call(
        functools.partial(relay_kernel, middle, len(ins), len(outs), n, chunks, lag, spread),
        in_specs=[vmem] * (1 + len(ins)),
        out_specs=[vmem] * len(out_shapes),
        out_shape=out_shapes,
        scratch_shapes=[
            pltpu.VMEM((chunks, n + 1, rows, features), jnp.bfloat16),
            pltpu.VMEM((chunks, n, rows, features), jnp.bfloat16),
            pltpu.VMEM((rows, features), jnp.float32),
            pltpu.SemaphoreType.DMA((chunks, n)),
            pltpu.SemaphoreType.DMA((chunks, n + 1)),
            pltpu.SemaphoreType.DMA((chunks, n + 1)),
            pltpu.SemaphoreType.DMA((chunks, n)),
        ],
        compiler_params=pltpu.CompilerParams(
            collective_id=number, has_side_effects=True, vmem_limit_bytes=56 * 2**20
        ),
        cost_estimate=pl.CostEstimate(flops=0, bytes_accessed=35 * 10**7, transcendentals=0),
    )(partial.reshape(chunks, n, rows, features), *ins)
    rest = [values.reshape(owned, features) if values.ndim == 3 else values for values in rest]
    return [whole.reshape(tokens, -1)] + rest


def gather_kernel(n, chunks, lag, own, small, whole, smalls, sent, got, small_sent, small_got):
    section, i = lax.axis_index("section"), lax.axis_index("col")
    rows, width = own.shape[0] // chunks, own.shape[1]
    others = [(s, d) for s in range(2) for d in range(n) if (s, d) != (0, 0)]
    place = lambda s, d: {"section": lax.rem(section + s, 2), "col": lax.rem(i + d, n)}
    barrier = pltpu.get_barrier_semaphore()
    for s, d in others:
        pl.semaphore_signal(barrier, 1, device_id=place(s, d), device_id_type=pl.DeviceIdType.MESH)
    pl.semaphore_wait(barrier, len(others))

    def small_copy(s, d):
        return pltpu.make_async_remote_copy(
            src_ref=small,
            dst_ref=smalls.at[section, i],
            send_sem=small_sent.at[s, d],
            recv_sem=small_got.at[section, i],
            device_id=place(s, d),
            device_id_type=pl.DeviceIdType.MESH,
        )

    for s, d in others:
        small_copy(s, d).start()
    smalls[section, i] = small[...]

    def block(c, o, right, mine=False):
        part = whole.at[pl.ds(pl.multiple_of(c * rows, rows), rows), columns(o, width)]
        return remote(
            part, part, sent.at[c, n if mine and not right else o], got.at[c, o], "col", i + 1 if right else i - 1
        )

    def at(now, slot, allowed):
        since = jnp.maximum(now - slot, 0)
        return since // (n - 1), allowed & (now >= slot) & (lax.rem(since, n - 1) == 0) & (since < (n - 1) * chunks)

    def step(now, carry):
        c, due = at(now, 0, i >= 0)

        @pl.when(due)
        def _():
            here = pl.ds(pl.multiple_of(c * rows, rows), rows)
            whole[here, columns(i, width)] = own[here, :]

        @pl.when(due & (i < n - 1))
        def _():
            block(c, i, True, True).start()

        @pl.when(due & (i > 0))
        def _():
            block(c, i, False, True).start()

        for o in range(n):
            c, due = at(now, lag * jnp.abs(i - o), i != o)

            @pl.when(due)
            def _(c=c, o=o):
                block(c, o, True).wait_recv()

            @pl.when(due & (i > o) & (i < n - 1))
            def _(c=c, o=o):
                block(c, o, True).start()

            @pl.when(due & (i < o) & (i > 0))
            def _(c=c, o=o):
                block(c, o, False).start()

        return carry

    lax.fori_loop(0, (n - 1) * (chunks - 1) + lag * (n - 1) + 1, step, 0)

    def settle(c, carry):
        for o in range(n):
            @pl.when(((o <= i) & (i < n - 1)) | ((o > i) & (i > 0)))
            def _(o=o):
                block(c, o, True).wait_send()

        @pl.when(i > 0)
        def _():
            block(c, i, False, True).wait_send()

        return carry

    lax.fori_loop(0, chunks, settle, 0)
    for s, d in others:
        small_copy(s, d).wait_send()
        from_s, from_d = lax.rem(section + s, 2), lax.rem(i + d, n)
        pltpu.make_async_remote_copy(
            src_ref=small,
            dst_ref=smalls.at[from_s, from_d],
            send_sem=small_sent.at[s, d],
            recv_sem=small_got.at[from_s, from_d],
            device_id=place(s, d),
            device_id_type=pl.DeviceIdType.MESH,
        ).wait_recv()


def gathered(number, own, small, n, lag=3, rows=64):
    tokens, width = own.shape
    chunks = tokens // rows
    vmem = pl.BlockSpec(memory_space=pltpu.VMEM)
    return pl.pallas_call(
        functools.partial(gather_kernel, n, chunks, lag),
        in_specs=[vmem] * 2,
        out_specs=[vmem] * 2,
        out_shape=[
            jax.ShapeDtypeStruct((tokens, n * width), own.dtype),
            jax.ShapeDtypeStruct((2, n) + small.shape, small.dtype),
        ],
        scratch_shapes=[
            pltpu.SemaphoreType.DMA((chunks, n + 1)),
            pltpu.SemaphoreType.DMA((chunks, n)),
            pltpu.SemaphoreType.DMA((2, n)),
            pltpu.SemaphoreType.DMA((2, n)),
        ],
        compiler_params=pltpu.CompilerParams(
            collective_id=number, has_side_effects=True, vmem_limit_bytes=40 * 2**20
        ),
        cost_estimate=pl.CostEstimate(flops=0, bytes_accessed=25 * 10**7, transcendentals=0),
    )(own, small)


def layer_norm(values, gain, shift):
    values = values.astype(jnp.float32)
    mean, inverse = norm_parts(values)
    return ((values - mean) * inverse * gain + shift).astype(jnp.bfloat16)


def rotary_lanes(positions):
    half_dims = ROT // 2
    inverse_freq = 1.0 / 10000.0 ** (jnp.arange(half_dims, dtype=jnp.float32) * 2.0 / ROT)
    angles = positions.astype(jnp.float32)[:, None] * inverse_freq[None, :]
    cosine, sine = jnp.cos(angles), jnp.sin(angles)
    rest = jnp.zeros((positions.shape[0], HEAD_DIM - ROT), jnp.float32)
    cosines = jnp.concatenate([cosine, cosine, rest + 1.0], axis=1)
    sines = jnp.concatenate([-sine, sine, rest], axis=1)
    return jnp.tile(cosines, (1, LANES // HEAD_DIM)), jnp.tile(sines, (1, LANES // HEAD_DIM))


def product(left, right):
    return jnp.dot(left, right, preferred_element_type=jnp.float32)


def per_device(
    inputs,
    cotangent,
    block_ids,
    norm_gains,
    norm_shifts,
    qkv_weight,
    qkv_bias,
    out_weight,
    gate_up_weight,
    down_weight,
):
    section = lax.axis_index("section")
    row = lax.axis_index("row")
    col = lax.axis_index("col")
    rows_axis = lax.axis_size("row")
    cols_axis = lax.axis_size("col")
    tokens, width = inputs.shape[1:]
    owned = tokens // cols_axis
    units = down_weight.shape[2]
    seq = tokens * rows_axis
    both = ("section", "row")
    whole_lanes = width == rows_axis * LANES
    heads = LANES // HEAD_DIM if whole_lanes else 1
    copies = 1 if whole_lanes else rows_axis * HEAD_DIM // width

    def expand(values):
        if whole_lanes:
            return values
        values = values.reshape(tokens, -1, width // HEAD_DIM, HEAD_DIM)
        values = jnp.pad(jnp.repeat(values, copies, axis=2), ((0, 0), (0, 0), (0, 0), (0, LANES - HEAD_DIM)))
        return values.reshape(tokens, -1)

    def contract(values):
        if whole_lanes:
            return values
        values = values.reshape(tokens, -1, rows_axis, LANES)[:, :, ::copies, :HEAD_DIM]
        return values.reshape(tokens, -1)

    def weights_of(block):
        block = block[0].reshape(block.shape[1], -1)
        return lax.all_gather(block, both, axis=0, tiled=True).reshape(2, D, -1)

    def mine(values):
        blocks = values.reshape(owned // RELAY_ROWS, cols_axis, RELAY_ROWS, -1)
        return lax.dynamic_index_in_dim(blocks, col, 1, keepdims=False).reshape(owned, -1)

    def my_features(values):
        return lax.dynamic_slice_in_dim(values, col * width, width, 1)

    own_small = jnp.concatenate([norm_gains[0], norm_shifts[0], qkv_bias[0], jnp.zeros((1, width), jnp.float32)])
    stream, small = gathered(6, lax.dynamic_index_in_dim(inputs, section, 0, keepdims=False), own_small, cols_axis)
    whole_small = small.transpose(0, 2, 1, 3).reshape(2, own_small.shape[0], D)
    gains, shifts = whole_small[:, :2], whole_small[:, 2:4]
    bias = lax.dynamic_index_in_dim(small, col, 1, keepdims=False)[:, 4:7].reshape(2, -1)

    qkv_w = weights_of(qkv_weight)
    out_w = weights_of(out_weight)
    gate_up_w = weights_of(gate_up_weight)
    down_w = weights_of(down_weight)

    ids = lax.dynamic_index_in_dim(block_ids, section, 0, keepdims=False)
    cos_all, sin_all = rotary_lanes(jnp.arange(seq, dtype=jnp.int32))
    cosines, sines = (lax.dynamic_slice_in_dim(table, row * tokens, tokens, 0) for table in (cos_all, sin_all))
    branch = lax.all_gather(
        lax.dynamic_index_in_dim(cotangent, section, 0, keepdims=False), "col", axis=1, tiled=True
    )

    kept = []
    hidden_out = []
    for layer in range(2):
        normed = layer_norm(stream, gains[layer, 0], shifts[layer, 0])
        qkv = product(normed, qkv_w[layer]) + bias[layer]
        spread, mixed, log_sums, attn_mix = attend(7, expand(qkv), ids, cosines, sines, heads, rows_axis)
        attn_mix = contract(attn_mix)
        normed_two, after = relay(
            after_attention,
            0,
            product(attn_mix, out_w[layer].T).astype(jnp.bfloat16),
            [mine(stream), gains[layer, 1:], shifts[layer, 1:]],
            [(owned, D)],
            cols_axis,
        )
        gate_up = product(normed_two, gate_up_w[layer])
        gate, up = gate_up[:, :units], gate_up[:, units:]
        hidden = (jax.nn.silu(gate) * up).astype(jnp.bfloat16)
        kept.append((stream, normed, spread, mixed, log_sums, attn_mix, after, normed_two, gate_up, hidden))
        partial = product(hidden, down_w[layer].T)
        if layer == 0:
            (stream,) = relay(after_hidden, 1, partial.astype(jnp.bfloat16), [after], [], cols_axis)
            hidden_out.append(my_features(stream))
        else:
            blocks = partial.reshape(owned // RELAY_ROWS, cols_axis, RELAY_ROWS, D)
            owner = lax.broadcasted_iota(jnp.int32, blocks.shape, 1) == col
            blocks = blocks + jnp.where(owner, after.reshape(-1, 1, RELAY_ROWS, D), 0.0)
            result = blocks.reshape(tokens, D).astype(jnp.bfloat16)
            hidden_out.append(lax.psum_scatter(result, "col", scatter_dimension=1, tiled=True))

    grad = mine(branch).astype(jnp.float32)
    weight_grads = [[], []]
    small_grads = [None, None]
    bias_grads = [None, None]
    input_out = [None, None]

    def collect(layer, term):
        term = lax.psum_scatter(term, "row", scatter_dimension=0, tiled=True)
        got = lax.ppermute(term, "section", [(1 - layer, layer)])
        weight_grads[layer].append(term.astype(jnp.float32) + got.astype(jnp.float32))

    def together(*values):
        return lax.optimization_barrier(values)

    for layer in (1, 0):
        stream, normed, spread, mixed, log_sums, attn_mix, after, normed_two, gate_up, hidden = kept[layer]
        gate, up = gate_up[:, :units], gate_up[:, units:]
        d_hidden = product(branch, down_w[layer])
        sig = jax.nn.sigmoid(gate)
        d_gate = d_hidden * up * sig * (1.0 + gate * (1.0 - sig))
        d_up = d_hidden * gate * sig
        d_gate_up = jnp.concatenate([d_gate, d_up], axis=1).astype(jnp.bfloat16)
        partial, down_term, gate_up_term = together(
            dot_last(d_gate_up, gate_up_w[layer]).astype(jnp.bfloat16),
            dot_first(branch, hidden).astype(jnp.bfloat16),
            dot_first(normed_two, d_gate_up).astype(jnp.bfloat16),
        )
        collect(layer, down_term)
        collect(layer, gate_up_term)
        grad_attn, d_after, sums_two = relay(
            behind_norm, 3, partial, [grad, after, gains[layer, 1:]], [(owned, D), (2, D)], cols_axis
        )
        d_mix, out_term = together(
            product(grad_attn, out_w[layer]).astype(jnp.bfloat16), dot_first(grad_attn, attn_mix).astype(jnp.bfloat16)
        )
        collect(layer, out_term)
        d_qkv = contract(
            attend_back(8, expand(d_mix), spread, mixed, log_sums, ids, cos_all, sin_all, heads, rows_axis)
        )
        partial, qkv_term, bias_grads[layer] = together(
            dot_last(d_qkv, qkv_w[layer]).astype(jnp.bfloat16),
            dot_first(normed, d_qkv).astype(jnp.bfloat16),
            jnp.sum(d_qkv.astype(jnp.float32), axis=0),
        )
        collect(layer, qkv_term)
        branch, grad, sums_one = relay(
            behind_norm,
            4 + layer,
            partial,
            [d_after, mine(stream), gains[layer, :1]],
            [(owned, D), (2, D)],
            cols_axis,
            spread=layer == 0,
        )
        small_grads[layer] = jnp.stack([sums_one, sums_two], axis=1)
        input_out[layer] = my_features(branch) if layer == 1 else branch

    def by_section(first, second):
        keep = jnp.where(section == 0, first, second)
        give = jnp.where(section == 0, second, first)
        got = lax.ppermute(give, "section", [(0, 1), (1, 0)])
        return jnp.stack([jnp.where(section == 0, keep, got), jnp.where(section == 0, got, keep)])

    hidden_states = by_section(*hidden_out)
    input_grads = by_section(*input_out).astype(jnp.float32)
    down_grad, gate_up_grad, out_grad, qkv_grad = (
        jnp.where(section == 0, first, second) for first, second in zip(*weight_grads)
    )
    bias_sum = lax.psum(jnp.stack(bias_grads), both)
    bias_sum = lax.dynamic_index_in_dim(bias_sum, section, 0, keepdims=True)
    small_sum = lax.psum_scatter(jnp.stack(small_grads), "col", scatter_dimension=3, tiled=True)
    small_sum = lax.psum(small_sum, both)
    small_sum = lax.dynamic_index_in_dim(small_sum, section, 0, keepdims=False)
    return (
        hidden_states[None],
        input_grads[None],
        small_sum[0][None],
        small_sum[1][None],
        qkv_grad.reshape(qkv_weight.shape),
        bias_sum.reshape(qkv_bias.shape),
        out_grad[None],
        gate_up_grad.reshape(gate_up_weight.shape),
        down_grad[None],
    )


def solution(mesh):
    in_specs = (
        P(None, "row", "col"),
        P(None, "row", "col"),
        P(),
        P("section", None, "col"),
        P("section", None, "col"),
        P("section", "row", None, "col"),
        P("section", None, "col"),
        P("section", "row", "col"),
        P("section", "row", None, "col"),
        P("section", "row", "col"),
    )
    out_specs = (
        P("section", None, "row", "col"),
        P("section", None, "row", "col"),
        P("section", None, "col"),
        P("section", None, "col"),
        P("section", "row", None, "col"),
        P("section", None, "col"),
        P("section", "row", "col"),
        P("section", "row", None, "col"),
        P("section", "row", "col"),
    )
    return jax.shard_map(
        per_device, mesh=mesh, in_specs=in_specs, out_specs=out_specs, check_vma=False
    )
```

time: 2930 us -> 2170 us (0.74)
  waiting for transfers between devices: 1820 us -> 359 us
  Pallas kernels: 259 us -> 1350 us
  blocking collectives: 240 us -> 24.9 us
  local copies, waits for them, and re-layouts: 161 us -> 73 us
  other arithmetic: 136 us -> 54.6 us
    pallas_call x4 -> x12, Pallas kernels: 259 us -> 1350 us  [the longest x7 865 us: relay(): pl.pallas_call(functools.partial(relay_kernel, middle, len(ins), len(outs...]
    all_gather x7 -> x0, waiting for transfers between devices: 526 us -> none  [the longest x6 480 us: gathered_rows(): return lax.all_gather(own, 'col', axis=0, tiled=True)]
    reduce_scatter x12 -> x9, waiting for transfers between devices: 764 us -> 323 us  [the longest x8 323 us: collect(): term = lax.psum_scatter(term, 'row', scatter_dimension=0, tiled=True)]
    all_gather x4, waiting for transfers between devices: 234 us -> 0.06 us  [weights_of(): return lax.all_gather(block, both, axis=0, tiled=True).reshape(2, D, -1)]
    all_to_all x5 -> x0, blocking collectives: 190 us -> none  [the longest x3 119 us: from_heads(): values = lax.all_to_all(values, 'row', 0, values.ndim - 1, tiled=True)]
    psum x1 -> x0, waiting for transfers between devices: 123 us -> none  [per_device(): small_sum = lax.psum(jnp.stack(small_grads), ('section', 'row', 'col'))]
    all_to_all x5 -> x0, waiting for transfers between devices: 88.1 us -> none  [the longest x2 52.1 us: to_heads(): return lax.all_to_all(values, 'row', values.ndim - 1, 0, tiled=True)]
    all_gather x1, waiting for transfers between devices: 62.2 us -> 0.01 us  [per_device(): lax.all_gather(lax.dynamic_index_in_dim(cotangent, section, 0, keepdims=F...]
  transfers between devices with their start and end apart: 32 -> 25, of which waited for: 27 -> 7; matrix products, arithmetic and copies ran while one was open for 10% -> 14% of each run, Pallas kernels for 2% -> 62%
where the time goes in v2:
time: 2170 us
  Pallas kernels  1350 us (62%)
  waiting for transfers between devices  359 us (17%)
  matrix products  274 us (13%)
  local copies, waits for them, and re-layouts  73 us (3%)
  other arithmetic  54.6 us (3%)
  starting transfers between devices  25.1 us (1%)
  blocking collectives  24.9 us (1%)
    pallas_call x7, Pallas kernels, relay(): pl.pallas_call(functools.partial(relay_kernel, middle, len(ins), len(outs...  865 us
    reduce_scatter x8, waiting for transfers between devices, collect(): term = lax.psum_scatter(term, 'row', scatter_dimension=0, tiled=True)  323 us
    pallas_call x2, Pallas kernels, attend_back(): pl.pallas_call(functools.partial(attend_back_kernel, heads, n, bq, bk), i...  223 us
    pallas_call x2, Pallas kernels, attend(): pl.pallas_call(functools.partial(attend_kernel, heads, n, bq, bk), in_spe...  179 us
    dot_general x12, matrix products, product(): return jnp.dot(left, right, preferred_element_type=jnp.float32)  138 us
    pallas_call x1, Pallas kernels, gathered(): pl.pallas_call(functools.partial(gather_kernel, n, chunks, lag), in_specs...  78.8 us
    dot_general x8, matrix products, dot_first(): lax.dot_general(a, b, (((0,), (0,)), ((), ())), preferred_element_type=jn...  76.9 us
    dot_general x4, matrix products, dot_last(): lax.dot_general(a, b, (((1,), (1,)), ((), ())), preferred_element_type=jn...  59.8 us
  transfers between devices with their start and end apart: 25, of which 7 were waited for; matrix products, arithmetic and copies ran while one was open for 14% of the time, Pallas kernels for 62%

profile of v2, /device:TPU:0, one launch (start us, length us, event | category | flops | bytes accessed | tf_op | source)
XLA Modules:
  0.0 2171.1 jit_solution(12863670418790150671)
XLA Ops:
  34.6 78.8 %shard_map.169 = (bf16[1024,2048]{1,0:T(8,128)(2,1)S(1)}, f32[2,4,8,512]{3,2,1,0:T(8,128)S(1)}) custom-call(bf16[1024,512]{1,0:T(8,128)(2,1)S(1)} %dynamic-slice_bitcast_fusion.2.own, f32[8,512]{1,0:T(8,128)S(1)} %maximum_maximum_fusion.2.small), custom_call_target="tpu_custom_call" | custom-call | bytes 250000000 | tf_op jit(solution)/shard_map/pallas_call | solution.py:765
  132.8 102.9 %shard_map.170 = (bf16[3,4096,128]{2,1,0:T(8,128)(2,1)}, bf16[4096,128]{1,0:T(8,128)(2,1)}, f32[128,4096]{1,0:T(8,128)}, bf16[1024,512]{1,0:T(8,128)(2,1)}) custom-call(s32[4096,1]{1,0:T(8,128)} %copy.43.bid_q.bid_k, s32[1,4096]{1,0:T(1,128)} %constant_dynamic-slice_fusion.4.bid_k.bid_q, f32[1024,1536]{1,0:T(8,128)} %fusion.28.qkv, ...), custom_call_target="tpu_custom_call" | custom-call | flops 10000000000 | bytes 200000000 | tf_op jit(solution)/shard_map/pallas_call | solution.py:206
  242.0 104.4 %shard_map.171 = (bf16[16,4,16,2048]{3,2,1,0:T(8,128)(2,1)}, f32[16,16,2048]{2,1,0:T(8,128)}) custom-call(bf16[16,4,16,2048]{3,2,1,0:T(8,128)(2,1)} %bitcast.179, bf16[16,16,2048]{2,1,0:T(8,128)(2,1)} %dynamic-slice_bitcast_fusion.1.refs_0_.refs_1_, f32[1,2048]{1,0:T(1,128)} %get-tuple-element.140.refs_1_.refs_2_, f32[1,2048]{1,0:T(1,128)} %get-tuple-element.139.refs_2_), custom_call_target="tpu_custom_call" | custom-call | bytes 350000000 | tf_op jit(solution)/shard_map/pallas_call | solution.py:643
  346.4 17.3 fusion.6
  381.7 154.6 %shard_map.172 = bf16[16,4,16,2048]{3,2,1,0:T(8,128)(2,1)} custom-call(bf16[16,4,16,2048]{3,2,1,0:T(8,128)(2,1)} %bitcast.184, f32[16,16,2048]{2,1,0:T(8,128)} %get-tuple-element.54.refs_0_.refs_1_), custom_call_target="tpu_custom_call" | custom-call | bytes 350000000 | tf_op jit(solution)/shard_map/pallas_call | solution.py:643
  558.2 76.6 %shard_map.173 = (bf16[3,4096,128]{2,1,0:T(8,128)(2,1)}, bf16[4096,128]{1,0:T(8,128)(2,1)}, f32[128,4096]{1,0:T(8,128)}, bf16[1024,512]{1,0:T(8,128)(2,1)}) custom-call(s32[4096,1]{1,0:T(8,128)} %copy.43.bid_q.bid_k, s32[1,4096]{1,0:T(1,128)} %constant_dynamic-slice_fusion.4.bid_k.bid_q, f32[1024,1536]{1,0:T(8,128)} %fusion.31.qkv, ...), custom_call_target="tpu_custom_call" | custom-call | flops 10000000000 | bytes 200000000 | tf_op jit(solution)/shard_map/pallas_call | solution.py:206
  641.1 110.4 %shard_map.174 = (bf16[16,4,16,2048]{3,2,1,0:T(8,128)(2,1)}, f32[16,16,2048]{2,1,0:T(8,128)}) custom-call(bf16[16,4,16,2048]{3,2,1,0:T(8,128)(2,1)} %bitcast.180, bf16[16,16,2048]{2,1,0:T(8,128)(2,1)} %dynamic-slice_bitcast_fusion.refs_0_.refs_1_, f32[1,2048]{1,0:T(1,128)} %get-tuple-element.136.refs_1_.refs_2_, f32[1,2048]{1,0:T(1,128)} %get-tuple-element.135.refs_2_), custom_call_target="tpu_custom_call" | custom-call | bytes 350000000 | tf_op jit(solution)/shard_map/pallas_call | solution.py:643
  751.5 18.7 fusion.2
  770.2 15.7 multiply_convert_fusion.3
  803.0 18.4 fusion.39
  845.5 181.4 %shard_map.175 = (bf16[16,4,16,2048]{3,2,1,0:T(8,128)(2,1)}, f32[16,16,2048]{2,1,0:T(8,128)}, f32[2,2048]{1,0:T(2,128)}) custom-call(bf16[16,4,16,2048]{3,2,1,0:T(8,128)(2,1)} %bitcast.177, f32[16,16,2048]{2,1,0:T(8,128)} %bitcast_convert_fusion.refs_0_, f32[16,16,2048]{2,1,0:T(8,128)} %get-tuple-element.57.refs_1_, f32[1,2048]{1,0:T(1,128)} %get-tuple-element.136.refs_1_.refs_2_), custom_call_target="tpu_custom_call" | custom-call | bytes 350000000 | tf_op jit(solution)/shard_map/pallas_call | solution.py:643
  1039.0 110.8 %shard_map.176 = bf16[1024,1536]{1,0:T(8,128)(2,1)} custom-call(s32[1,4096]{1,0:T(1,128)} %constant_dynamic-slice_fusion.4.bid_k.bid_q, s32[4096,1]{1,0:T(8,128)} %copy.43.bid_q.bid_k, bf16[1024,512]{1,0:T(8,128)(2,1)} %fusion.51.d_mix, bf16[3,4096,128]{2,1,0:T(8,128)(2,1)} %get-tuple-element.61.spread, bf16[4096,128]{1,0:T(8,128)(2,1)} %get-tuple-element.62.mixed, ...), custom_call_target="tpu_custom_call" | custom-call | flops 10000000000 | bytes 300000000 | tf_op jit(solution)/shard_map/pallas_call | solution.py:375
  1172.8 109.4 %shard_map.177 = (bf16[16,4,16,2048]{3,2,1,0:T(8,128)(2,1)}, f32[16,16,2048]{2,1,0:T(8,128)}, f32[2,2048]{1,0:T(2,128)}) custom-call(bf16[16,4,16,2048]{3,2,1,0:T(8,128)(2,1)} %bitcast.182, f32[16,16,2048]{2,1,0:T(8,128)} %get-tuple-element.65.refs_0_, bf16[16,16,2048]{2,1,0:T(8,128)(2,1)} %dynamic-slice_bitcast_fusion.refs_0_.refs_1_, ...), custom_call_target="tpu_custom_call" | custom-call | bytes 350000000 | tf_op jit(solution)/shard_map/pallas_call | solution.py:643
  1313.4 18.2 fusion.36
  1340.5 107.3 %shard_map.178 = (bf16[16,4,16,2048]{3,2,1,0:T(8,128)(2,1)}, f32[16,16,2048]{2,1,0:T(8,128)}, f32[2,2048]{1,0:T(2,128)}) custom-call(bf16[16,4,16,2048]{3,2,1,0:T(8,128)(2,1)} %bitcast.178, f32[16,16,2048]{2,1,0:T(8,128)} %get-tuple-element.68.refs_0_, f32[16,16,2048]{2,1,0:T(8,128)} %get-tuple-element.54.refs_0_.refs_1_, ...), custom_call_target="tpu_custom_call" | custom-call | bytes 350000000 | tf_op jit(solution)/shard_map/pallas_call | solution.py:643
  1459.9 112.1 %shard_map.179 = bf16[1024,1536]{1,0:T(8,128)(2,1)} custom-call(s32[1,4096]{1,0:T(1,128)} %constant_dynamic-slice_fusion.4.bid_k.bid_q, s32[4096,1]{1,0:T(8,128)} %copy.43.bid_q.bid_k, bf16[1024,512]{1,0:T(8,128)(2,1)} %fusion.52.d_mix, bf16[3,4096,128]{2,1,0:T(8,128)(2,1)} %get-tuple-element.71.spread, bf16[4096,128]{1,0:T(8,128)(2,1)} %get-tuple-element.72.mixed, ...), custom_call_target="tpu_custom_call" | custom-call | flops 10000000000 | bytes 300000000 | tf_op jit(solution)/shard_map/pallas_call | solution.py:375
  1596.2 96.9 %shard_map.180 = (bf16[16,4,16,512]{3,2,1,0:T(8,128)(2,1)}, f32[16,16,2048]{2,1,0:T(8,128)}, f32[2,2048]{1,0:T(2,128)}) custom-call(bf16[16,4,16,2048]{3,2,1,0:T(8,128)(2,1)} %bitcast.183, f32[16,16,2048]{2,1,0:T(8,128)} %get-tuple-element.75.refs_0_, bf16[16,16,2048]{2,1,0:T(8,128)(2,1)} %dynamic-slice_bitcast_fusion.1.refs_0_.refs_1_, ...), custom_call_target="tpu_custom_call" | custom-call | bytes 350000000 | tf_op jit(solution)/shard_map/pallas_call | solution.py:643
  1734.2 24.9 %all-reduce = (f32[2,2,2,512]{3,1,2,0:T(2,128)S(1)}, f32[2,1536]{1,0:T(2,128)S(1)}) all-reduce(f32[2,2,2,512]{3,1,2,0:T(2,128)S(1)} %copy.58, f32[2,1536]{1,0:T(2,128)S(1)} %pad_maximum_fusion.7), channel_id=1, replica_groups=mesh['section'=2,'row'=4,'col'=4] {'section','row'}, use_global_device_ids=true, to_apply=%region_8.9 | all-reduce | flops 7168 | bytes 57344 | tf_op jit(solution)/shard_map/psum | solution.py:976
  1759.7 28.3 %reduce-scatter.27.cloned.1.call-done = bf16[512,1408]{1,0:T(8,128)(2,1)} async-done(((bf16[2048,1408]{1,0:T(8,128)(2,1)}), bf16[512,1408]{1,0:T(8,128)(2,1)}) %reduce-scatter.27.cloned.1.call-update) | async-done | bytes 1441808 | tf_op jit(solution)/shard_map/reduce_scatter | solution.py:912
  1789.3 93.3 %reduce-scatter.23.cloned.1.call-done = bf16[512,2816]{1,0:T(8,128)(2,1)} async-done(((bf16[2048,2816]{1,0:T(8,128)(2,1)}), bf16[512,2816]{1,0:T(8,128)(2,1)}) %reduce-scatter.23.cloned.1.call-update) | async-done | bytes 2883600 | tf_op jit(solution)/shard_map/reduce_scatter | solution.py:912
  1883.9 93.5 %reduce-scatter.25.cloned.1.call-done = bf16[512,2816]{1,0:T(8,128)(2,1)} async-done(((bf16[2048,2816]{1,0:T(8,128)(2,1)}), bf16[512,2816]{1,0:T(8,128)(2,1)}) %reduce-scatter.25.cloned.1.call-update) | async-done | bytes 2883600 | tf_op jit(solution)/shard_map/reduce_scatter | solution.py:912
  1986.7 51.5 %reduce-scatter.17.cloned.1.call-done = bf16[512,1536]{1,0:T(8,128)(2,1)} async-done(((bf16[2048,1536]{1,0:T(8,128)(2,1)}), bf16[512,1536]{1,0:T(8,128)(2,1)}) %reduce-scatter.17.cloned.1.call-update) | async-done | bytes 1572880 | tf_op jit(solution)/shard_map/reduce_scatter | solution.py:912
  2042.8 56.4 %reduce-scatter.15.cloned.1.call-done = bf16[512,1536]{1,0:T(8,128)(2,1)} async-done(((bf16[2048,1536]{1,0:T(8,128)(2,1)}), bf16[512,1536]{1,0:T(8,128)(2,1)}) %reduce-scatter.15.cloned.1.call-update) | async-done | bytes 1572880 | tf_op jit(solution)/shard_map/reduce_scatter | solution.py:912
  2114.4 23.0 %collective-permute-done.2 = bf16[512,1536]{1,0:T(8,128)(2,1)S(1)} collective-permute-done((bf16[512,1536]{1,0:T(8,128)(2,1)}, bf16[512,1536]{1,0:T(8,128)(2,1)S(1)}, u32[]{:S(2)}, u32[]{:S(2)}) %collective-permute-start.2) | collective-permute-done | bytes 1572896 | tf_op jit(solution)/shard_map/ppermute | solution.py:913
  (244 shorter events, 351.6 us)
Async XLA Ops:
  7.2 112.6 %all-gather.9.cloned.1.call-start = ((), (), s32[]{:S(2)}) async-start(), calls=%async_computation.10 | async-start | bytes 14155776 | tf_op jit(solution)/shard_map/all_gather | solution.py:848
  10.0 225.7 %all-gather.13.cloned.1.call-start = ((), (), s32[]{:S(2)}) async-start(), calls=%async_computation.21 | async-start | bytes 4718592 | tf_op jit(solution)/shard_map/all_gather | solution.py:848
  10.7 335.7 %all-gather.11.cloned.1.call-start = ((), (), s32[]{:S(2)}) async-start(), calls=%async_computation.11 | async-start | bytes 25952256 | tf_op jit(solution)/shard_map/all_gather | solution.py:848
  14.6 356.2 %all-gather.15.cloned.1.call-start = ((), (), s32[]{:S(2)}) async-start(), calls=%async_computation.22 | async-start | bytes 12976128 | tf_op jit(solution)/shard_map/all_gather | solution.py:848
  15.2 755.0 %all-gather.17.cloned.1.call-start = ((), (), s32[]{:S(2)}) async-start(), calls=%async_computation.23 | async-start | bytes 5242880 | tf_op jit(solution)/shard_map/all_gather | solution.py:871
  16.4 1693.0 %reduce-scatter.29.cloned.1.call-start = ((), (), s32[]{:S(2)}) async-start(), calls=%async_computation.20 | async-start | bytes 7208960 | tf_op jit(solution)/shard_map/reduce_scatter | solution.py:912
  830.1 884.3 %reduce-scatter.13.cloned.1.call-start = ((), (), s32[]{:S(2)}) async-start(), calls=%async_computation.12 | async-start | bytes 5242880 | tf_op jit(solution)/shard_map/reduce_scatter | solution.py:903
  842.6 874.6 %reduce-scatter.21.cloned.1.call-start = ((), (), s32[]{:S(2)}) async-start(), calls=%async_computation.16 | async-start | bytes 2621440 | tf_op jit(solution)/shard_map/reduce_scatter | solution.py:912
  1172.8 549.1 %reduce-scatter.19.cloned.1.call-start = ((), (), s32[]{:S(2)}) async-start(), calls=%async_computation.15 | async-start | bytes 2621440 | tf_op jit(solution)/shard_map/reduce_scatter | solution.py:912
  1574.4 157.3 %reduce-scatter.31.cloned.1.call-start = ((), (), s32[]{:S(2)}) async-start(), calls=%async_computation.24 | async-start | bytes 1310720
  1703.8 84.1 %reduce-scatter.27.cloned.1.call-start = ((), (), s32[]{:S(2)}) async-start(), calls=%async_computation.19 | async-start | bytes 7208960 | tf_op jit(solution)/shard_map/reduce_scatter | solution.py:912
  1704.6 178.0 %reduce-scatter.23.cloned.1.call-start = ((), (), s32[]{:S(2)}) async-start(), calls=%async_computation.17 | async-start | bytes 14417920 | tf_op jit(solution)/shard_map/reduce_scatter | solution.py:912
  1705.1 272.3 %reduce-scatter.25.cloned.1.call-start = ((), (), s32[]{:S(2)}) async-start(), calls=%async_computation.18 | async-start | bytes 14417920 | tf_op jit(solution)/shard_map/reduce_scatter | solution.py:912
  1705.9 332.3 %reduce-scatter.17.cloned.1.call-start = ((), (), s32[]{:S(2)}) async-start(), calls=%async_computation.14 | async-start | bytes 7864320 | tf_op jit(solution)/shard_map/reduce_scatter | solution.py:912
  1706.5 392.7 %reduce-scatter.15.cloned.1.call-start = ((), (), s32[]{:S(2)}) async-start(), calls=%async_computation.13 | async-start | bytes 7864320 | tf_op jit(solution)/shard_map/reduce_scatter | solution.py:912
  1709.3 50.4 %collective-permute-start.1 = (bf16[1024,512]{1,0:T(8,128)(2,1)S(1)}, bf16[1024,512]{1,0:T(8,128)(2,1)}, u32[]{:S(2)}, u32[]{:S(2)}) collective-permute-start(bf16[1024,512]{1,0:T(8,128)(2,1)S(1)} %bitcast_select_fusion.1), channel_id=1, source_target_pairs={{0,16},{16,0},{1,17},{17,1},{2,18},{18,2},{3,19},{19,3},{4,20},{20... | collective-permute-start | bytes 3145736 | tf_op jit(solution)/shard_map/ppermute | solution.py:965
  1709.4 389.8 %collective-permute-start.9 = (bf16[512,1408]{1,0:T(8,128)(2,1)}, bf16[512,1408]{1,0:T(8,128)(2,1)}, u32[]{:S(2)}, u32[]{:S(2)}) collective-permute-start(bf16[512,1408]{1,0:T(8,128)(2,1)} %reduce-scatter.29.cloned.1.call-done), channel_id=1, source_target_pairs={{0,16},{1,17},{2,18},{3,19},{4,20},{5,21},{6,22},{7,23},{8,24},{9,... | collective-permute-start | bytes 4325384 | tf_op jit(solution)/shard_map/ppermute | solution.py:913
  1717.2 269.5 %collective-permute-start = (bf16[1024,512]{1,0:T(8,128)(2,1)}, bf16[1024,512]{1,0:T(8,128)(2,1)}, u32[]{:S(2)}, u32[]{:S(2)}) collective-permute-start(bf16[1024,512]{1,0:T(8,128)(2,1)} %broadcast_select_fusion), channel_id=1, source_target_pairs={{0,16},{16,0},{1,17},{17,1},{2,18},{18,2},{3,19},{19,3},{4,20},{20... | collective-permute-start | bytes 3145736 | tf_op jit(solution)/shard_map/ppermute | solution.py:965
  1717.2 72.1 %collective-permute-start.5 = (bf16[512,512]{1,0:T(8,128)(2,1)}, bf16[512,512]{1,0:T(8,128)(2,1)}, u32[]{:S(2)}, u32[]{:S(2)}) collective-permute-start(bf16[512,512]{1,0:T(8,128)(2,1)} %reduce-scatter.21.cloned.1.call-done), channel_id=1, source_target_pairs={{0,16},{1,17},{2,18},{3,19},{4,20},{5,21},{6,22},{7,23},{8,24},{9,... | collective-permute-start | bytes 1572872 | tf_op jit(solution)/shard_map/ppermute | solution.py:913
  1721.9 162.0 %collective-permute-start.4 = (bf16[512,512]{1,0:T(8,128)(2,1)}, bf16[512,512]{1,0:T(8,128)(2,1)}, u32[]{:S(2)}, u32[]{:S(2)}) collective-permute-start(bf16[512,512]{1,0:T(8,128)(2,1)} %reduce-scatter.19.cloned.1.call-done), channel_id=1, source_target_pairs={{16,0},{17,1},{18,2},{19,3},{20,4},{21,5},{22,6},{23,7},{24,8},{25... | collective-permute-start | bytes 1572872 | tf_op jit(solution)/shard_map/ppermute | solution.py:913
  1788.0 322.2 %collective-permute-start.8 = (bf16[512,1408]{1,0:T(8,128)(2,1)}, bf16[512,1408]{1,0:T(8,128)(2,1)}, u32[]{:S(2)}, u32[]{:S(2)}) collective-permute-start(bf16[512,1408]{1,0:T(8,128)(2,1)} %reduce-scatter.27.cloned.1.call-done), channel_id=1, source_target_pairs={{16,0},{17,1},{18,2},{19,3},{20,4},{21,5},{22,6},{23,7},{24,8},{25... | collective-permute-start | bytes 4325384 | tf_op jit(solution)/shard_map/ppermute | solution.py:913
  1882.6 265.7 %collective-permute-start.6 = (bf16[512,2816]{1,0:T(8,128)(2,1)}, bf16[512,2816]{1,0:T(8,128)(2,1)}, u32[]{:S(2)}, u32[]{:S(2)}) collective-permute-start(bf16[512,2816]{1,0:T(8,128)(2,1)} %reduce-scatter.23.cloned.1.call-done), channel_id=1, source_target_pairs={{16,0},{17,1},{18,2},{19,3},{20,4},{21,5},{22,6},{23,7},{24,8},{25... | collective-permute-start | bytes 8650760 | tf_op jit(solution)/shard_map/ppermute | solution.py:913
  1977.4 170.9 %collective-permute-start.7 = (bf16[512,2816]{1,0:T(8,128)(2,1)}, bf16[512,2816]{1,0:T(8,128)(2,1)}, u32[]{:S(2)}, u32[]{:S(2)}) collective-permute-start(bf16[512,2816]{1,0:T(8,128)(2,1)} %reduce-scatter.25.cloned.1.call-done), channel_id=1, source_target_pairs={{0,16},{1,17},{2,18},{3,19},{4,20},{5,21},{6,22},{7,23},{8,24},{9,... | collective-permute-start | bytes 8650760 | tf_op jit(solution)/shard_map/ppermute | solution.py:913
  2038.2 76.2 %collective-permute-start.3 = (bf16[512,1536]{1,0:T(8,128)(2,1)}, bf16[512,1536]{1,0:T(8,128)(2,1)}, u32[]{:S(2)}, u32[]{:S(2)}) collective-permute-start(bf16[512,1536]{1,0:T(8,128)(2,1)} %reduce-scatter.17.cloned.1.call-done), channel_id=1, source_target_pairs={{0,16},{1,17},{2,18},{3,19},{4,20},{5,21},{6,22},{7,23},{8,24},{9,... | collective-permute-start | bytes 4718600 | tf_op jit(solution)/shard_map/ppermute | solution.py:913
  (47 other events, 1270.7 us)
Sparse Core Ops, SparseCore 0:
  10.5 78.2 all-gather.8
  90.7 36.7 all-gather.12
  129.9 150.9 all-gather.10
  282.7 70.7 all-gather.14
  354.9 112.3 all-gather.16
  830.2 66.4 reduce-scatter.28
  899.1 110.4 reduce-scatter.12
  1172.9 29.3 reduce-scatter.20
  1574.5 28.7 reduce-scatter.18
  1704.0 27.6 reduce-scatter.30
  1734.4 53.5 reduce-scatter.26
  1790.4 92.1 reduce-scatter.22
  1885.2 92.1 reduce-scatter.24
  1979.8 58.3 reduce-scatter.16
  2040.8 58.3 reduce-scatter.14

commit v3 on v2

--- a/solution.py
+++ b/solution.py
@@ -64,9 +64,9 @@
 
 
 def attend_kernel(
-    heads, n, bq, bk, bid_q, bid_k, qkv, cosines, sines,
-    spread, mixed, lse_ref, mix, vone, scores, leaving, qkv_sent, qkv_got, mix_sent, mix_got,
+    heads, n, bq, bk, bid_q, bid_k, qkv, cosines, sines, *refs
 ):
+    spread, mixed, lse_ref, mix, vone, scores, leaving, qkv_sent, qkv_got, mix_sent, mix_got = refs[-11:]
     me = lax.axis_index("row")
     tokens = qkv.shape[0]
     seq = n * tokens
@@ -75,7 +75,7 @@
     meet("row", n)
 
     def parts(t):
-        cos, sin = cosines[...], sines[...]
+        cos, sin = cosines[here, :], sines[here, :]
         query = spin(qkv[:, columns(t)], cos, sin).astype(low) * jnp.asarray(HEAD_DIM**-0.5, low)
         key = spin(qkv[:, columns(n + t)], cos, sin).astype(low)
         return query.astype(low), key, qkv[:, columns(2 * n + t)].astype(low)
@@ -197,7 +197,7 @@
                 ).wait_recv()
 
 
-def attend(number, qkv, block_all, cosines, sines, heads, n, bq=512, bk=512):
+def attend(number, qkv, block_all, cosines, sines, heads, n, behind=(), bq=512, bk=512):
     tokens = qkv.shape[0]
     bq, bk = min(bq, tokens), min(bk, tokens)
     seq = n * tokens
@@ -205,7 +205,7 @@
     low = jnp.bfloat16
     return pl.pallas_call(
         functools.partial(attend_kernel, heads, n, bq, bk),
-        in_specs=[vmem] * 5,
+        in_specs=[vmem] * 5 + [pl.BlockSpec(memory_space=pl.ANY)] * len(behind),
         out_specs=[vmem] * 4,
         out_shape=[
             jax.ShapeDtypeStruct((3, seq, LANES), low),
@@ -226,13 +226,13 @@
             collective_id=number, has_side_effects=True, vmem_limit_bytes=58 * 2**20
         ),
         cost_estimate=pl.CostEstimate(flops=10**10, bytes_accessed=2 * 10**8, transcendentals=0),
-    )(block_all.reshape(seq, 1), block_all.reshape(1, seq), qkv, cosines, sines)
+    )(block_all.reshape(seq, 1), block_all.reshape(1, seq), qkv, cosines, sines, *behind)
 
 
 def attend_back_kernel(
-    heads, n, bq, bk, bid_q, bid_k, d_mix, spread, mixed, lse_ref, cosines, sines,
-    d_qkv, grads, kone, dk_acc, dv_acc, leaving, g_sent, g_got, back_sent, back_got,
+    heads, n, bq, bk, bid_q, bid_k, d_mix, spread, mixed, lse_ref, cosines, sines, *refs
 ):
+    d_qkv, grads, kone, dk_acc, dv_acc, leaving, g_sent, g_got, back_sent, back_got = refs[-10:]
     me = lax.axis_index("row")
     tokens = d_mix.shape[0]
     seq = n * tokens
@@ -366,7 +366,7 @@
     lax.fori_loop(0, blocks, settle, 0)
 
 
-def attend_back(number, d_mix, spread, mixed, lse, block_all, cosines, sines, heads, n, bq=512, bk=512):
+def attend_back(number, d_mix, spread, mixed, lse, block_all, cosines, sines, heads, n, behind=(), bq=512, bk=512):
     tokens = d_mix.shape[0]
     bq, bk = min(bq, tokens), min(bk, tokens)
     seq = n * tokens
@@ -374,7 +374,7 @@
     low = jnp.bfloat16
     return pl.pallas_call(
         functools.partial(attend_back_kernel, heads, n, bq, bk),
-        in_specs=[vmem] * 8,
+        in_specs=[vmem] * 8 + [pl.BlockSpec(memory_space=pl.ANY)] * len(behind),
         out_specs=vmem,
         out_shape=jax.ShapeDtypeStruct((tokens, 3 * n * LANES), low),
         scratch_shapes=[
@@ -392,7 +392,7 @@
             collective_id=number, has_side_effects=True, vmem_limit_bytes=58 * 2**20
         ),
         cost_estimate=pl.CostEstimate(flops=10**10, bytes_accessed=3 * 10**8, transcendentals=0),
-    )(block_all.reshape(1, seq), block_all.reshape(seq, 1), d_mix, spread, mixed, lse, cosines, sines)
+    )(block_all.reshape(1, seq), block_all.reshape(seq, 1), d_mix, spread, mixed, lse, cosines, sines, *behind)
 
 
 def norm_parts(values):
@@ -440,35 +440,55 @@
     return given.astype(jnp.bfloat16)
 
 
-def relay_kernel(middle, n_ins, n_outs, n, chunks, lag, spread, partial, *refs):
-    ins, refs = refs[:n_ins], refs[n_ins:]
+def relay_kernel(middle, n_ins, n_outs, layers, n_after, polish, n, chunks, lag, spread, partial, *refs):
+    ins, carry, refs = refs[:n_ins], refs[n_ins : n_ins + len(layers)], refs[n_ins + len(layers) + n_after :]
     whole, outs, refs = refs[0], refs[1 : 1 + n_outs], refs[1 + n_outs :]
-    arrived, outgoing, total, sum_sent, sum_got, block_sent, block_got = refs
-    i = lax.axis_index("col")
+    carried, refs = refs[: len(layers)], refs[len(layers) :]
+    if polish:
+        ins, (gain, shift) = ins[:-2], ins[-2:]
+        outs, polished = outs[:-1], outs[-1]
+    if spread:
+        outs, all_sums = outs[:-1], outs[-1]
+    arrived, outgoing, total, sum_sent, sum_got, block_sent, block_got, carry_sent, carry_got, last_sent, last_got = refs
+    section, i = lax.axis_index("section"), lax.axis_index("col")
     width = whole.shape[-1]
     first, last = i == 0, i == n - 1
 
     barrier = pltpu.get_barrier_semaphore()
+
+    def greet(**place):
+        pl.semaphore_signal(barrier, 1, device_id=place, device_id_type=pl.DeviceIdType.MESH)
+
     if spread:
-        for d in range(1, n):
-            pl.semaphore_signal(barrier, 1, device_id={"col": lax.rem(i + d, n)}, device_id_type=pl.DeviceIdType.MESH)
-        pl.semaphore_wait(barrier, n - 1)
+        for d in range(1, 2 * n):
+            greet(section=lax.rem(section + d // n, 2), col=lax.rem(i + d, n))
+        pl.semaphore_wait(barrier, 2 * n - 1)
     else:
+        greet(section=1 - section)
+
         @pl.when(i > 0)
         def _():
-            pl.semaphore_signal(barrier, 1, device_id={"col": i - 1}, device_id_type=pl.DeviceIdType.MESH)
+            greet(col=i - 1)
 
         @pl.when(i < n - 1)
         def _():
-            pl.semaphore_signal(barrier, 1, device_id={"col": i + 1}, device_id_type=pl.DeviceIdType.MESH)
+            greet(col=i + 1)
 
         @pl.when(first | last)
         def _():
-            pl.semaphore_wait(barrier, 1)
+            pl.semaphore_wait(barrier, 2)
 
         @pl.when((i > 0) & (i < n - 1))
         def _():
-            pl.semaphore_wait(barrier, 2)
+            pl.semaphore_wait(barrier, 3)
+
+    def carry_copy(k):
+        return remote(carry[k], carried[k], carry_sent.at[k], carry_got.at[k], "section", layers[k])
+
+    for k, layer in enumerate(layers):
+        @pl.when(section != layer)
+        def _(k=k):
+            carry_copy(k).start()
 
     def remote_col(source, target, sent, got, device):
         return remote(source, target, sent, got, "col", device)
@@ -481,15 +501,48 @@
 
     def block_copy(c, o, right, own=False):
         sent = n if own and not right else o
-        return remote_col(whole.at[c, o], whole.at[c, o], block_sent.at[c, sent], block_got.at[c, o], i + 1 if right else i - 1)
+        return remote_col(whole.at[c, o], whole.at[c, o], block_sent.at[c, sent], block_got.at[0, c, o], i + 1 if right else i - 1)
 
     def slice_copy(c, d):
         to = lax.rem(i + d, n)
-        source = outgoing.at[c, i, :, pl.ds(pl.multiple_of(to * width, 128), width)]
-        return remote_col(source, whole.at[c, i], block_sent.at[c, d], block_got.at[c, i], to)
+        return pltpu.make_async_remote_copy(
+            src_ref=outgoing.at[c, i, :, pl.ds(pl.multiple_of(to * width, 128), width)],
+            dst_ref=whole.at[section, c, i],
+            send_sem=block_sent.at[c, d],
+            recv_sem=block_got.at[section, c, i],
+            device_id={"section": 0, "col": to},
+            device_id_type=pl.DeviceIdType.MESH,
+        )
 
     def arrive(c, slot):
         remote_col(outgoing.at[c, 0], arrived.at[c, slot], sum_sent.at[c, 0], sum_got.at[c, slot], i).wait_recv()
+
+    def work(c, o):
+        if polish:
+            values = whole[c, o].astype(jnp.float32)
+            mean, inverse = norm_parts(values)
+            polished[c, o] = ((values - mean) * inverse * gain[...] + shift[...]).astype(jnp.bfloat16)
+
+    def sums_copy(d):
+        to = lax.rem(i + d, n)
+        return pltpu.make_async_remote_copy(
+            src_ref=outs[-1].at[:, pl.ds(pl.multiple_of(to * width, 128), width)],
+            dst_ref=all_sums.at[section, i],
+            send_sem=last_sent.at[d],
+            recv_sem=last_got.at[section, i],
+            device_id={"section": 0, "col": to},
+            device_id_type=pl.DeviceIdType.MESH,
+        )
+
+    def sums_arrive(s, o):
+        return pltpu.make_async_remote_copy(
+            src_ref=outs[-1].at[:, pl.ds(0, width)],
+            dst_ref=all_sums.at[s, o],
+            send_sem=last_sent.at[0],
+            recv_sem=last_got.at[s, o],
+            device_id={"section": 0, "col": o},
+            device_id_type=pl.DeviceIdType.MESH,
+        )
 
     def middle_slot(k):
         return jnp.maximum(lag * k + n - 1 - k, lag * (n - 1 - k) + k)
@@ -557,9 +610,18 @@
                 outgoing[c, i] = block
                 for d in range(1, n):
                     slice_copy(c, d).start()
-                whole[c, i] = outgoing[c, i, :, pl.ds(pl.multiple_of(i * width, 128), width)]
+
+                @pl.when(section == 0)
+                def _():
+                    whole[0, c, i] = outgoing[c, i, :, pl.ds(pl.multiple_of(i * width, 128), width)]
+
+                @pl.when(section != 0)
+                def _():
+                    slice_copy(c, 0).start()
+
             else:
                 whole[c, i] = block
+                work(c, i)
 
         if spread:
             return carry
@@ -583,6 +645,10 @@
             def _(c=c, o=o):
                 block_copy(c, o, True).start()
 
+            @pl.when(due)
+            def _(c=c, o=o):
+                work(c, o)
+
         for o in range(1, n):
             c, due = at(now, middle_slot(o) + lag * (o - i), i < o)
 
@@ -594,21 +660,56 @@
             def _(c=c, o=o):
                 block_copy(c, o, False).start()
 
+            @pl.when(due)
+            def _(c=c, o=o):
+                work(c, o)
+
         return carry
 
     lax.fori_loop(0, n * (chunks - 1) + 2 * lag * (n - 1) + 1, step, 0)
+
+    if spread:
+        for d in range(1, n):
+            sums_copy(d).start()
+
+        @pl.when(section == 0)
+        def _():
+            all_sums[0, i] = outs[-1][:, pl.ds(pl.multiple_of(i * width, 128), width)]
+
+        @pl.when(section != 0)
+        def _():
+            sums_copy(0).start()
+
+    def slice_arrives(c, s, o):
+        return pltpu.make_async_remote_copy(
+            src_ref=outgoing.at[c, 0, :, pl.ds(0, width)],
+            dst_ref=whole.at[s, c, o],
+            send_sem=block_sent.at[c, 0],
+            recv_sem=block_got.at[s, c, o],
+            device_id={"section": 0, "col": o},
+            device_id_type=pl.DeviceIdType.MESH,
+        )
 
     def settle(c, carry):
         for j in range(n):
             @pl.when(j != i)
             def _(j=j):
                 sum_copy(c, j, True).wait_send()
-                if spread:
-                    remote_col(outgoing.at[c, j, :, pl.ds(0, width)], whole.at[c, j], block_sent.at[c, 0], block_got.at[c, j], i).wait_recv()
 
         if spread:
             for d in range(1, n):
                 slice_copy(c, d).wait_send()
+
+            @pl.when(section != 0)
+            def _():
+                slice_copy(c, 0).wait_send()
+
+            for s in range(2):
+                for o in range(n):
+                    @pl.when((section == 0) & ((s == 1) | (o != i)))
+                    def _(s=s, o=o):
+                        slice_arrives(c, s, o).wait_recv()
+
             return carry
         for o in range(n):
             @pl.when((o <= i) & (i < n - 1))
@@ -626,25 +727,55 @@
         return carry
 
     lax.fori_loop(0, chunks, settle, 0)
-
-
-def relay(middle, number, partial, ins, outs, n, spread=False, lag=3, rows=RELAY_ROWS):
+    if spread:
+        for d in range(1, n):
+            sums_copy(d).wait_send()
+
+        @pl.when(section != 0)
+        def _():
+            sums_copy(0).wait_send()
+
+        for s in range(2):
+            for o in range(n):
+                @pl.when((section == 0) & ((s == 1) | (o != i)))
+                def _(s=s, o=o):
+                    sums_arrive(s, o).wait_recv()
+
+    for k, layer in enumerate(layers):
+        @pl.when(section != layer)
+        def _(k=k):
+            carry_copy(k).wait_send()
+
+        @pl.when(section == layer)
+        def _(k=k):
+            carry_copy(k).wait_recv()
+
+
+def relay(middle, number, partial, ins, outs, n, spread=False, carry=(), behind=(), polish=(), lag=3, rows=RELAY_ROWS):
     tokens, features = partial.shape
     owned = tokens // n
     chunks = owned // rows
     blocks = lambda values: values.reshape(chunks, rows, features) if values.shape[0] == owned else values
-    ins = [blocks(values) for values in ins]
+    ins = [blocks(values) for values in ins] + list(polish)
+    outs = list(outs) + ([(tokens, features)] if polish else []) + ([(2, n, 2, features // n)] if spread else [])
     out_shapes = [
-        jax.ShapeDtypeStruct((chunks, n, rows, features // n if spread else features), jnp.bfloat16)
+        jax.ShapeDtypeStruct(
+            (2, chunks, n, rows, features // n) if spread else (chunks, n, rows, features), jnp.bfloat16
+        )
     ] + [
-        jax.ShapeDtypeStruct((chunks, rows, features) if shape[0] == owned else shape, jnp.float32) for shape in outs
+        jax.ShapeDtypeStruct((chunks, n, rows, features), jnp.bfloat16)
+        if shape[0] == tokens
+        else jax.ShapeDtypeStruct((chunks, rows, features) if shape[0] == owned else shape, jnp.float32)
+        for shape in outs
     ]
-    vmem = pl.BlockSpec(memory_space=pltpu.VMEM)
+    vmem, anywhere = pl.BlockSpec(memory_space=pltpu.VMEM), pl.BlockSpec(memory_space=pl.ANY)
+    layers = tuple(layer for layer, _ in carry)
+    carry = [values for _, values in carry]
     whole, *rest = pl.pallas_call(
-        functools.partial(relay_kernel, middle, len(ins), len(outs), n, chunks, lag, spread),
-        in_specs=[vmem] * (1 + len(ins)),
-        out_specs=[vmem] * len(out_shapes),
-        out_shape=out_shapes,
+        functools.partial(relay_kernel, middle, len(ins), len(outs), layers, len(behind), bool(polish), n, chunks, lag, spread),
+        in_specs=[vmem] * (1 + len(ins)) + [anywhere] * (len(carry) + len(behind)),
+        out_specs=[vmem] * len(out_shapes) + [anywhere] * len(carry),
+        out_shape=out_shapes + [jax.ShapeDtypeStruct(values.shape, values.dtype) for values in carry],
         scratch_shapes=[
             pltpu.VMEM((chunks, n + 1, rows, features), jnp.bfloat16),
             pltpu.VMEM((chunks, n, rows, features), jnp.bfloat16),
@@ -652,18 +783,23 @@
             pltpu.SemaphoreType.DMA((chunks, n)),
             pltpu.SemaphoreType.DMA((chunks, n + 1)),
             pltpu.SemaphoreType.DMA((chunks, n + 1)),
-            pltpu.SemaphoreType.DMA((chunks, n)),
+            pltpu.SemaphoreType.DMA((2 if spread else 1, chunks, n)),
+            pltpu.SemaphoreType.DMA((max(1, len(carry)),)),
+            pltpu.SemaphoreType.DMA((max(1, len(carry)),)),
+            pltpu.SemaphoreType.DMA((n,)),
+            pltpu.SemaphoreType.DMA((2, n)),
         ],
         compiler_params=pltpu.CompilerParams(
             collective_id=number, has_side_effects=True, vmem_limit_bytes=56 * 2**20
         ),
         cost_estimate=pl.CostEstimate(flops=0, bytes_accessed=35 * 10**7, transcendentals=0),
-    )(partial.reshape(chunks, n, rows, features), *ins)
-    rest = [values.reshape(owned, features) if values.ndim == 3 else values for values in rest]
-    return [whole.reshape(tokens, -1)] + rest
-
-
-def gather_kernel(n, chunks, lag, own, small, whole, smalls, sent, got, small_sent, small_got):
+    )(partial.reshape(chunks, n, rows, features), *ins, *carry, *behind)
+    shapes = {(chunks, rows, features): (owned, features), (chunks, n, rows, features): (tokens, features)}
+    rest = [values.reshape(shapes.get(values.shape, values.shape)) for values in rest]
+    return [whole.reshape((2, tokens, -1) if spread else (tokens, -1))] + rest
+
+
+def gather_kernel(n, chunks, lag, own, small, angles, whole, smalls, normed, cosines, sines, sent, got, small_sent, small_got):
     section, i = lax.axis_index("section"), lax.axis_index("col")
     rows, width = own.shape[0] // chunks, own.shape[1]
     others = [(s, d) for s in range(2) for d in range(n) if (s, d) != (0, 0)]
@@ -687,88 +823,126 @@
         small_copy(s, d).start()
     smalls[section, i] = small[...]
 
-    def block(c, o, right, mine=False):
-        part = whole.at[pl.ds(pl.multiple_of(c * rows, rows), rows), columns(o, width)]
-        return remote(
-            part, part, sent.at[c, n if mine and not right else o], got.at[c, o], "col", i + 1 if right else i - 1
-        )
-
-    def at(now, slot, allowed):
-        since = jnp.maximum(now - slot, 0)
-        return since // (n - 1), allowed & (now >= slot) & (lax.rem(since, n - 1) == 0) & (since < (n - 1) * chunks)
-
-    def step(now, carry):
-        c, due = at(now, 0, i >= 0)
-
-        @pl.when(due)
-        def _():
-            here = pl.ds(pl.multiple_of(c * rows, rows), rows)
-            whole[here, columns(i, width)] = own[here, :]
-
-        @pl.when(due & (i < n - 1))
-        def _():
-            block(c, i, True, True).start()
-
-        @pl.when(due & (i > 0))
-        def _():
-            block(c, i, False, True).start()
-
-        for o in range(n):
-            c, due = at(now, lag * jnp.abs(i - o), i != o)
-
-            @pl.when(due)
-            def _(c=c, o=o):
-                block(c, o, True).wait_recv()
-
-            @pl.when(due & (i > o) & (i < n - 1))
-            def _(c=c, o=o):
-                block(c, o, True).start()
-
-            @pl.when(due & (i < o) & (i > 0))
-            def _(c=c, o=o):
-                block(c, o, False).start()
-
-        return carry
-
-    lax.fori_loop(0, (n - 1) * (chunks - 1) + lag * (n - 1) + 1, step, 0)
-
-    def settle(c, carry):
-        for o in range(n):
-            @pl.when(((o <= i) & (i < n - 1)) | ((o > i) & (i > 0)))
-            def _(o=o):
-                block(c, o, True).wait_send()
-
-        @pl.when(i > 0)
-        def _():
-            block(c, i, False, True).wait_send()
-
-        return carry
-
-    lax.fori_loop(0, chunks, settle, 0)
-    for s, d in others:
-        small_copy(s, d).wait_send()
+    def small_arrives(s, d):
         from_s, from_d = lax.rem(section + s, 2), lax.rem(i + d, n)
-        pltpu.make_async_remote_copy(
+        return pltpu.make_async_remote_copy(
             src_ref=small,
             dst_ref=smalls.at[from_s, from_d],
             send_sem=small_sent.at[s, d],
             recv_sem=small_got.at[from_s, from_d],
             device_id=place(s, d),
             device_id_type=pl.DeviceIdType.MESH,
-        ).wait_recv()
-
-
-def gathered(number, own, small, n, lag=3, rows=64):
+        )
+
+    def norm(c):
+        here = pl.ds(pl.multiple_of(c * rows, rows), rows)
+        values = whole[here, :].astype(jnp.float32)
+        mean, inverse = norm_parts(values)
+        for o in range(n):
+            part = slice(o * width, (o + 1) * width)
+            gain, shift = smalls[0, o, 0:1, :], smalls[0, o, 2:3, :]
+            normed[here, part] = ((values[:, part] - mean) * inverse * gain + shift).astype(jnp.bfloat16)
+
+    def block(c, o, right, mine=False):
+        part = whole.at[pl.ds(pl.multiple_of(c * rows, rows), rows), columns(o, width)]
+        return remote(
+            part, part, sent.at[c, n if mine and not right else o], got.at[c, o], "col", i + 1 if right else i - 1
+        )
+
+    def at(now, slot, allowed):
+        since = jnp.maximum(now - slot, 0)
+        return since // (n - 1), allowed & (now >= slot) & (lax.rem(since, n - 1) == 0) & (since < (n - 1) * chunks)
+
+    def step(now, carry):
+        c, due = at(now, 0, i >= 0)
+
+        @pl.when(due)
+        def _():
+            here = pl.ds(pl.multiple_of(c * rows, rows), rows)
+            whole[here, columns(i, width)] = own[here, :]
+
+        @pl.when(due & (i < n - 1))
+        def _():
+            block(c, i, True, True).start()
+
+        @pl.when(due & (i > 0))
+        def _():
+            block(c, i, False, True).start()
+
+        for o in range(n):
+            c, due = at(now, lag * jnp.abs(i - o), i != o)
+
+            @pl.when(due)
+            def _(c=c, o=o):
+                block(c, o, True).wait_recv()
+
+            @pl.when(due & (i > o) & (i < n - 1))
+            def _(c=c, o=o):
+                block(c, o, True).start()
+
+            @pl.when(due & (i < o) & (i > 0))
+            def _(c=c, o=o):
+                block(c, o, False).start()
+
+        c, due = at(now, lag * (n - 1), i >= 0)
+
+        @pl.when(due)
+        def _():
+            norm(c)
+
+        return carry
+
+    turns = angles.shape[0] // 2
+    lane = lax.broadcasted_iota(jnp.int32, (turns, LANES), 1)
+    place_of = lax.broadcasted_iota(jnp.int32, (turns, LANES), 0)
+    turned = lane % HEAD_DIM < 2 * turns
+    picked = jnp.where(turned & (lane % turns == place_of), 1.0, 0.0)
+    sign = jnp.where(lane % HEAD_DIM < turns, -1.0, 1.0)
+
+    def spread_out(table, pick):
+        return lax.dot_general(
+            table, pick, (((0,), (0,)), ((), ())), precision=lax.Precision.HIGHEST, preferred_element_type=jnp.float32
+        )
+
+    still = jnp.where(turned[:1], 0.0, 1.0)
+    cosines[...] = spread_out(angles[:turns, :], picked) + still
+    sines[...] = spread_out(angles[turns:, :], picked * sign)
+    for s, d in others:
+        small_arrives(s, d).wait_recv()
+
+    lax.fori_loop(0, (n - 1) * (chunks - 1) + lag * (n - 1) + 1, step, 0)
+
+    def settle(c, carry):
+        for o in range(n):
+            @pl.when(((o <= i) & (i < n - 1)) | ((o > i) & (i > 0)))
+            def _(o=o):
+                block(c, o, True).wait_send()
+
+        @pl.when(i > 0)
+        def _():
+            block(c, i, False, True).wait_send()
+
+        return carry
+
+    lax.fori_loop(0, chunks, settle, 0)
+    for s, d in others:
+        small_copy(s, d).wait_send()
+
+
+def gathered(number, own, small, angles, n, lag=3, rows=64):
     tokens, width = own.shape
     chunks = tokens // rows
     vmem = pl.BlockSpec(memory_space=pltpu.VMEM)
     return pl.pallas_call(
         functools.partial(gather_kernel, n, chunks, lag),
-        in_specs=[vmem] * 2,
-        out_specs=[vmem] * 2,
+        in_specs=[vmem] * 3,
+        out_specs=[vmem] * 5,
         out_shape=[
             jax.ShapeDtypeStruct((tokens, n * width), own.dtype),
             jax.ShapeDtypeStruct((2, n) + small.shape, small.dtype),
+            jax.ShapeDtypeStruct((tokens, n * width), own.dtype),
+            jax.ShapeDtypeStruct((angles.shape[1], LANES), jnp.float32),
+            jax.ShapeDtypeStruct((angles.shape[1], LANES), jnp.float32),
         ],
         scratch_shapes=[
             pltpu.SemaphoreType.DMA((chunks, n + 1)),
@@ -780,24 +954,14 @@
             collective_id=number, has_side_effects=True, vmem_limit_bytes=40 * 2**20
         ),
         cost_estimate=pl.CostEstimate(flops=0, bytes_accessed=25 * 10**7, transcendentals=0),
-    )(own, small)
-
-
-def layer_norm(values, gain, shift):
-    values = values.astype(jnp.float32)
-    mean, inverse = norm_parts(values)
-    return ((values - mean) * inverse * gain + shift).astype(jnp.bfloat16)
-
-
-def rotary_lanes(positions):
+    )(own, small, angles)
+
+
+def rotary_angles(positions):
     half_dims = ROT // 2
     inverse_freq = 1.0 / 10000.0 ** (jnp.arange(half_dims, dtype=jnp.float32) * 2.0 / ROT)
-    angles = positions.astype(jnp.float32)[:, None] * inverse_freq[None, :]
-    cosine, sine = jnp.cos(angles), jnp.sin(angles)
-    rest = jnp.zeros((positions.shape[0], HEAD_DIM - ROT), jnp.float32)
-    cosines = jnp.concatenate([cosine, cosine, rest + 1.0], axis=1)
-    sines = jnp.concatenate([-sine, sine, rest], axis=1)
-    return jnp.tile(cosines, (1, LANES // HEAD_DIM)), jnp.tile(sines, (1, LANES // HEAD_DIM))
+    angles = positions.astype(jnp.float32)[None, :] * inverse_freq[:, None]
+    return jnp.concatenate([jnp.cos(angles), jnp.sin(angles)])
 
 
 def product(left, right):
@@ -855,7 +1019,10 @@
         return lax.dynamic_slice_in_dim(values, col * width, width, 1)
 
     own_small = jnp.concatenate([norm_gains[0], norm_shifts[0], qkv_bias[0], jnp.zeros((1, width), jnp.float32)])
-    stream, small = gathered(6, lax.dynamic_index_in_dim(inputs, section, 0, keepdims=False), own_small, cols_axis)
+    angles = rotary_angles(jnp.arange(seq, dtype=jnp.int32))
+    stream, small, normed, cosines, sines = gathered(
+        7, lax.dynamic_index_in_dim(inputs, section, 0, keepdims=False), own_small, angles, cols_axis
+    )
     whole_small = small.transpose(0, 2, 1, 3).reshape(2, own_small.shape[0], D)
     gains, shifts = whole_small[:, :2], whole_small[:, 2:4]
     bias = lax.dynamic_index_in_dim(small, col, 1, keepdims=False)[:, 4:7].reshape(2, -1)
@@ -866,26 +1033,27 @@
     down_w = weights_of(down_weight)
 
     ids = lax.dynamic_index_in_dim(block_ids, section, 0, keepdims=False)
-    cos_all, sin_all = rotary_lanes(jnp.arange(seq, dtype=jnp.int32))
-    cosines, sines = (lax.dynamic_slice_in_dim(table, row * tokens, tokens, 0) for table in (cos_all, sin_all))
-    branch = lax.all_gather(
-        lax.dynamic_index_in_dim(cotangent, section, 0, keepdims=False), "col", axis=1, tiled=True
-    )
-
     kept = []
     hidden_out = []
+    waited = []
     for layer in range(2):
-        normed = layer_norm(stream, gains[layer, 0], shifts[layer, 0])
         qkv = product(normed, qkv_w[layer]) + bias[layer]
-        spread, mixed, log_sums, attn_mix = attend(7, expand(qkv), ids, cosines, sines, heads, rows_axis)
+        if layer == 1:
+            here = section + jnp.where(hidden_out[0][0, 0] == hidden_out[0][0, 0], 0, 1)
+            branch = lax.all_gather(
+                lax.dynamic_index_in_dim(cotangent, here, 0, keepdims=False), "col", axis=1, tiled=True
+            )
+            waited = [branch]
+        spread, mixed, log_sums, attn_mix = attend(8, expand(qkv), ids, cosines, sines, heads, rows_axis)
         attn_mix = contract(attn_mix)
         normed_two, after = relay(
             after_attention,
-            0,
+            layer,
             product(attn_mix, out_w[layer].T).astype(jnp.bfloat16),
             [mine(stream), gains[layer, 1:], shifts[layer, 1:]],
             [(owned, D)],
             cols_axis,
+            behind=waited,
         )
         gate_up = product(normed_two, gate_up_w[layer])
         gate, up = gate_up[:, :units], gate_up[:, units:]
@@ -893,26 +1061,35 @@
         kept.append((stream, normed, spread, mixed, log_sums, attn_mix, after, normed_two, gate_up, hidden))
         partial = product(hidden, down_w[layer].T)
         if layer == 0:
-            (stream,) = relay(after_hidden, 1, partial.astype(jnp.bfloat16), [after], [], cols_axis)
+            stream, normed = relay(
+                after_hidden,
+                2,
+                partial.astype(jnp.bfloat16),
+                [after],
+                [],
+                cols_axis,
+                polish=(gains[1, :1], shifts[1, :1]),
+            )
             hidden_out.append(my_features(stream))
         else:
             blocks = partial.reshape(owned // RELAY_ROWS, cols_axis, RELAY_ROWS, D)
             owner = lax.broadcasted_iota(jnp.int32, blocks.shape, 1) == col
             blocks = blocks + jnp.where(owner, after.reshape(-1, 1, RELAY_ROWS, D), 0.0)
             result = blocks.reshape(tokens, D).astype(jnp.bfloat16)
-            hidden_out.append(lax.psum_scatter(result, "col", scatter_dimension=1, tiled=True))
 
     grad = mine(branch).astype(jnp.float32)
-    weight_grads = [[], []]
-    small_grads = [None, None]
+    weight_sums = [[], []]
+    small_sums = []
     bias_grads = [None, None]
     input_out = [None, None]
+    input_got = [None, None]
+    hidden_got = [None, None]
 
     def collect(layer, term):
-        term = lax.psum_scatter(term, "row", scatter_dimension=0, tiled=True)
-        got = lax.ppermute(term, "section", [(1 - layer, layer)])
-        weight_grads[layer].append(term.astype(jnp.float32) + got.astype(jnp.float32))
-
+        weight_sums[layer].append(lax.psum_scatter(term, "row", scatter_dimension=0, tiled=True))
+        return weight_sums[layer][-1]
+
+    arrived = [[None] * 4, [None] * 4]
     def together(*values):
         return lax.optimization_barrier(values)
 
@@ -929,57 +1106,89 @@
             dot_first(branch, hidden).astype(jnp.bfloat16),
             dot_first(normed_two, d_gate_up).astype(jnp.bfloat16),
         )
-        collect(layer, down_term)
-        collect(layer, gate_up_term)
-        grad_attn, d_after, sums_two = relay(
-            behind_norm, 3, partial, [grad, after, gains[layer, 1:]], [(owned, D), (2, D)], cols_axis
-        )
+        down_sum, gate_up_sum = collect(layer, down_term), collect(layer, gate_up_term)
+        grad_attn, d_after, sums_two, *got = relay(
+            behind_norm,
+            3 + layer,
+            partial,
+            [grad, after, gains[layer, 1:]],
+            [(owned, D), (2, D)],
+            cols_axis,
+            carry=[]
+            if layer == 1
+            else [(0, hidden_out[0]), (1, hidden_out[1]), (1, input_out[1]), (1, weight_sums[1][2]), (1, weight_sums[1][3])],
+            behind=[] if layer == 1 else [down_sum],
+        )
+        if layer == 1:
+            result = jnp.where(d_after[0, 0] == d_after[0, 0], result, 0)
+            hidden_out.append(lax.psum_scatter(result, "col", scatter_dimension=1, tiled=True))
+        else:
+            hidden_got[0], hidden_got[1], input_got[1], arrived[1][2], arrived[1][3] = got
+        small_sums += [sums_two]
         d_mix, out_term = together(
             product(grad_attn, out_w[layer]).astype(jnp.bfloat16), dot_first(grad_attn, attn_mix).astype(jnp.bfloat16)
         )
-        collect(layer, out_term)
+        out_sum = collect(layer, out_term)
         d_qkv = contract(
-            attend_back(8, expand(d_mix), spread, mixed, log_sums, ids, cos_all, sin_all, heads, rows_axis)
+            attend_back(
+                9,
+                expand(d_mix),
+                spread,
+                mixed,
+                log_sums,
+                ids,
+                cosines,
+                sines,
+                heads,
+                rows_axis,
+                behind=[down_sum, gate_up_sum],
+            )
         )
         partial, qkv_term, bias_grads[layer] = together(
             dot_last(d_qkv, qkv_w[layer]).astype(jnp.bfloat16),
             dot_first(normed, d_qkv).astype(jnp.bfloat16),
             jnp.sum(d_qkv.astype(jnp.float32), axis=0),
         )
-        collect(layer, qkv_term)
-        branch, grad, sums_one = relay(
+        qkv_sum = collect(layer, qkv_term)
+        if layer == 0:
+            early_sums = lax.psum_scatter(jnp.stack(small_sums), "col", scatter_dimension=2, tiled=True)
+            early = jnp.concatenate([early_sums.reshape(6, -1), bias_grads[1].reshape(3, -1), bias_grads[0].reshape(3, -1)])
+            early = jnp.sum(lax.all_gather(early, both, axis=0), axis=0)
+        branch, grad, sums_one, *got = relay(
             behind_norm,
-            4 + layer,
+            5 + layer,
             partial,
             [d_after, mine(stream), gains[layer, :1]],
             [(owned, D), (2, D)],
             cols_axis,
             spread=layer == 0,
-        )
-        small_grads[layer] = jnp.stack([sums_one, sums_two], axis=1)
+            carry=[(layer, down_sum), (layer, gate_up_sum)] + ([(0, out_sum)] if layer == 0 else []),
+            behind=[hidden_out[1]] if layer == 1 else [early_sums],
+        )
+        if layer == 0:
+            late_sums, *got = got
+        arrived[layer][: len(got)] = got
+        small_sums += [sums_one]
         input_out[layer] = my_features(branch) if layer == 1 else branch
 
-    def by_section(first, second):
-        keep = jnp.where(section == 0, first, second)
-        give = jnp.where(section == 0, second, first)
-        got = lax.ppermute(give, "section", [(0, 1), (1, 0)])
-        return jnp.stack([jnp.where(section == 0, keep, got), jnp.where(section == 0, got, keep)])
-
-    hidden_states = by_section(*hidden_out)
-    input_grads = by_section(*input_out).astype(jnp.float32)
+    arrived[0][3] = lax.ppermute(weight_sums[0][3], "section", [(1, 0)])
+    hidden_states = jnp.where(
+        section == 0, jnp.stack([hidden_out[0], hidden_got[0]]), jnp.stack([hidden_got[1], hidden_out[1]])
+    )
+    input_grads = jnp.where(section == 0, input_out[0], jnp.stack([input_got[1], input_out[1]])).astype(jnp.float32)
     down_grad, gate_up_grad, out_grad, qkv_grad = (
-        jnp.where(section == 0, first, second) for first, second in zip(*weight_grads)
+        jnp.where(section == 0, first, second).astype(jnp.float32)
+        + jnp.where(section == 0, first_got, second_got).astype(jnp.float32)
+        for first, second, first_got, second_got in zip(*weight_sums, *arrived)
     )
-    bias_sum = lax.psum(jnp.stack(bias_grads), both)
-    bias_sum = lax.dynamic_index_in_dim(bias_sum, section, 0, keepdims=True)
-    small_sum = lax.psum_scatter(jnp.stack(small_grads), "col", scatter_dimension=3, tiled=True)
-    small_sum = lax.psum(small_sum, both)
-    small_sum = lax.dynamic_index_in_dim(small_sum, section, 0, keepdims=False)
+    last = lax.psum(jnp.sum(late_sums, axis=(0, 1)), "row")
+    norm_sums = jnp.where(section == 0, jnp.stack([last, early[4:6]]), jnp.stack([early[2:4], early[0:2]]))
+    bias_sum = jnp.where(section == 0, early[9:12], early[6:9])
     return (
         hidden_states[None],
         input_grads[None],
-        small_sum[0][None],
-        small_sum[1][None],
+        norm_sums[:, 0][None],
+        norm_sums[:, 1][None],
         qkv_grad.reshape(qkv_weight.shape),
         bias_sum.reshape(qkv_bias.shape),
         out_grad[None],

time: 2170 us -> 1870 us (0.86)
  waiting for transfers between devices: 359 us -> 160 us
  Pallas kernels: 1350 us -> 1290 us
  starting transfers between devices: 25.1 us -> 2.03 us
  other arithmetic: 54.6 us -> 31.9 us
    reduce_scatter x8, waiting for transfers between devices: 323 us -> 126 us  [collect(): lax.psum_scatter(term, 'row', scatter_dimension=0, tiled=True)]
    pallas_call x7, Pallas kernels: 865 us -> 813 us  [relay(): pl.pallas_call(functools.partial(relay_kernel, middle, len(ins), len(outs...]
    ppermute x10 -> x1, starting transfers between devices: 24.5 us -> 1.42 us  [per_device(): arrived[0][3] = lax.ppermute(weight_sums[0][3], 'section', [(1, 0)])]
  transfers between devices with their start and end apart: 25 -> 16, of which waited for: 7 -> 5; matrix products, arithmetic and copies ran while one was open for 14% -> 14% of each run, Pallas kernels for 62% -> 57%
where the time goes in v3:
time: 1870 us; the launch traced here: 1860 us
  Pallas kernels  1290 us (69%)
  matrix products  278 us (15%)
  waiting for transfers between devices  160 us (9%)
  local copies, waits for them, and re-layouts  66.9 us (4%)
  other arithmetic  31.9 us (2%)
    pallas_call x7, Pallas kernels, relay(): pl.pallas_call(functools.partial(relay_kernel, middle, len(ins), len(outs...  813 us
    pallas_call x2, Pallas kernels, attend_back(): pl.pallas_call(functools.partial(attend_back_kernel, heads, n, bq, bk), i...  213 us
    pallas_call x2, Pallas kernels, attend(): pl.pallas_call(functools.partial(attend_kernel, heads, n, bq, bk), in_spe...  184 us
    dot_general x12, matrix products, product(): return jnp.dot(left, right, preferred_element_type=jnp.float32)  136 us
    reduce_scatter x8, waiting for transfers between devices, collect(): lax.psum_scatter(term, 'row', scatter_dimension=0, tiled=True)  126 us
    dot_general x8, matrix products, dot_first(): lax.dot_general(a, b, (((0,), (0,)), ((), ())), preferred_element_type=jn...  83.2 us
    pallas_call x1, Pallas kernels, gathered(): pl.pallas_call(functools.partial(gather_kernel, n, chunks, lag), in_specs...  81.9 us
    dot_general x4, matrix products, dot_last(): lax.dot_general(a, b, (((1,), (1,)), ((), ())), preferred_element_type=jn...  58.6 us
  transfers between devices with their start and end apart: 16, of which 5 were waited for; matrix products, arithmetic and copies ran while one was open for 14% of the time, Pallas kernels for 57%

profile of v3, /device:TPU:0, one launch (start us, length us, event | category | flops | bytes accessed | tf_op | source)
XLA Modules:
  0.0 1862.4 jit_solution(10177268062314954614)
XLA Ops:
  18.2 81.9 %shard_map.169 = (bf16[1024,2048]{1,0:T(8,128)(2,1)S(1)}, f32[2,4,8,512]{3,2,1,0:T(8,128)S(1)}, bf16[1024,2048]{1,0:T(8,128)(2,1)S(1)}, f32[4096,128]{1,0:T(8,128)S(1)}, f32[4096,128]{1,0:T(8,128)S(1)}) custom-call(bf16[1024,512]{1,0:T(8,128)(2,1)S(1)} %dynamic-slice_bitcast_fusion.2.own, f32[8,512]{1,0:T(8,128)S(1)} %maximum_maximum_fusion.small, ...), custom_call_target="tpu_custom_call" | custom-call | bytes 250000000 | tf_op jit(solution)/shard_map/pallas_call | solution.py:936
  122.8 84.3 %shard_map.170 = (bf16[3,4096,128]{2,1,0:T(8,128)(2,1)}, bf16[4096,128]{1,0:T(8,128)(2,1)}, f32[128,4096]{1,0:T(8,128)}, bf16[1024,512]{1,0:T(8,128)(2,1)}) custom-call(s32[4096,1]{1,0:T(8,128)} %copy.31.bid_q.bid_k, s32[1,4096]{1,0:T(1,128)} %constant_dynamic-slice_fusion.4.bid_k.bid_q, f32[1024,1536]{1,0:T(8,128)} %fusion.22.qkv, f32[4096,128]{1,0:T(8,128)} %copy-done.5, ...), custom_call_target="tpu_custom_call" | custom-call | flops 10000000000 | bytes 200000000 | tf_op jit(solution)/shard_map/pallas_call | solution.py:206
  214.3 104.9 %shard_map.171 = (bf16[16,4,16,2048]{3,2,1,0:T(8,128)(2,1)}, f32[16,16,2048]{2,1,0:T(8,128)}) custom-call(bf16[16,4,16,2048]{3,2,1,0:T(8,128)(2,1)} %bitcast.175, bf16[16,16,2048]{2,1,0:T(8,128)(2,1)} %dynamic-slice_bitcast_fusion.1.refs_0_.refs_1_, f32[1,2048]{1,0:T(1,128)} %get-tuple-element.159.refs_1_.refs_2_, f32[1,2048]{1,0:T(1,128)} %get-tuple-element.158.refs_2_), custom_call_target="tpu_custom_call" | custom-call | bytes 350000000 | tf_op jit(solution)/shard_map/pallas_call | solution.py:774
  319.3 17.4 fusion.6
  356.9 113.3 %shard_map.172 = (bf16[16,4,16,2048]{3,2,1,0:T(8,128)(2,1)}, bf16[16,4,16,2048]{3,2,1,0:T(8,128)(2,1)}) custom-call(bf16[16,4,16,2048]{3,2,1,0:T(8,128)(2,1)} %bitcast.176, f32[16,16,2048]{2,1,0:T(8,128)} %get-tuple-element.72.refs_0_.refs_1_, f32[1,2048]{1,0:T(1,128)} %get-tuple-element.157.refs_1_.refs_2_, f32[1,2048]{1,0:T(1,128)} %get-tuple-element.156.refs_2_), custom_call_target="tpu_custom_call" | custom-call | bytes 350000000 | tf_op jit(solution)/shard_map/pallas_call | solution.py:774
  487.6 99.3 %shard_map.173 = (bf16[3,4096,128]{2,1,0:T(8,128)(2,1)}, bf16[4096,128]{1,0:T(8,128)(2,1)}, f32[128,4096]{1,0:T(8,128)}, bf16[1024,512]{1,0:T(8,128)(2,1)}) custom-call(s32[4096,1]{1,0:T(8,128)} %copy.31.bid_q.bid_k, s32[1,4096]{1,0:T(1,128)} %constant_dynamic-slice_fusion.4.bid_k.bid_q, f32[1024,1536]{1,0:T(8,128)} %fusion.25.qkv, f32[4096,128]{1,0:T(8,128)} %copy-done.5, ...), custom_call_target="tpu_custom_call" | custom-call | flops 10000000000 | bytes 200000000 | tf_op jit(solution)/shard_map/pallas_call | solution.py:206
  593.2 110.0 %shard_map.174 = (bf16[16,4,16,2048]{3,2,1,0:T(8,128)(2,1)}, f32[16,16,2048]{2,1,0:T(8,128)}) custom-call(bf16[16,4,16,2048]{3,2,1,0:T(8,128)(2,1)} %bitcast.178, bf16[16,16,2048]{2,1,0:T(8,128)(2,1)} %dynamic-slice_bitcast_fusion.refs_0_.refs_1_, f32[1,2048]{1,0:T(1,128)} %get-tuple-element.155.refs_1_.refs_2_, f32[1,2048]{1,0:T(1,128)} %get-tuple-element.154.refs_2_, ...), custom_call_target="tpu_custom_call" | custom-call | bytes 350000000 | tf_op jit(solution)/shard_map/pallas_call | solution.py:774
  703.3 18.8 %fusion.2 = f32[1024,2816]{1,0:T(8,128)} fusion(bf16[1024,2048]{1,0:T(8,128)(2,1)} %bitcast.211, bf16[4096,2816]{1,0:T(8,128)(2,1)} %all-gather.13.cloned.1.call-done), kind=kOutput, calls=%fused_computation.4 | convolution fusion | flops 11811160064 | bytes 27262976 | tf_op jit(solution)/shard_map/dot_general | solution.py:968
  722.1 13.4 multiply_convert_fusion.4
  735.6 18.7 %convolution_convert_fusion.1 = bf16[2048,2816]{1,0:T(8,128)(2,1)} fusion(bf16[1024,2048]{1,0:T(8,128)(2,1)} %bitcast.212, bf16[1024,1408]{1,0:T(8,128)(2,1)} %get-tuple-element.151, bf16[1024,1408]{1,0:T(8,128)(2,1)} %get-tuple-element.150), kind=kOutput, calls=%fused_computation.1 | convolution fusion | flops 11828461568 | bytes 21495808 | tf_op jit(solution)/shard_map/dot_general | solution.py:27
  754.3 18.2 fusion.32
  785.1 115.2 %shard_map.175 = (bf16[16,4,16,2048]{3,2,1,0:T(8,128)(2,1)}, f32[16,16,2048]{2,1,0:T(8,128)}, f32[2,2048]{1,0:T(2,128)}) custom-call(bf16[16,4,16,2048]{3,2,1,0:T(8,128)(2,1)} %bitcast.174, f32[16,16,2048]{2,1,0:T(8,128)} %bitcast_convert_fusion.refs_0_, f32[16,16,2048]{2,1,0:T(8,128)} %get-tuple-element.78.refs_1_, f32[1,2048]{1,0:T(1,128)} %get-tuple-element.155.refs_1_.refs_2_), custom_call_target="tpu_custom_call" | custom-call | bytes 350000000 | tf_op jit(solution)/shard_map/pallas_call | solution.py:774
  927.3 17.4 reduce-scatter.15.cloned.1.call-done.refs_1_.refs_4_
  944.7 107.5 %shard_map.176 = bf16[1024,1536]{1,0:T(8,128)(2,1)} custom-call(s32[1,4096]{1,0:T(1,128)} %constant_dynamic-slice_fusion.4.bid_k.bid_q, s32[4096,1]{1,0:T(8,128)} %copy.31.bid_q.bid_k, bf16[1024,512]{1,0:T(8,128)(2,1)} %fusion.45.d_mix, bf16[3,4096,128]{2,1,0:T(8,128)(2,1)} %get-tuple-element.81.spread, bf16[4096,128]{1,0:T(8,128)(2,1)} %get-tuple-element.82.mixed, ...), custom_call_target="tpu_custom_call" | custom-call | flops 10000000000 | bytes 300000000 | tf_op jit(solution)/shard_map/pallas_call | solution.py:375
  1077.8 112.8 %shard_map.177 = (bf16[16,4,16,2048]{3,2,1,0:T(8,128)(2,1)}, f32[16,16,2048]{2,1,0:T(8,128)}, f32[2,2048]{1,0:T(2,128)}, bf16[512,1408]{1,0:T(8,128)(2,1)}, bf16[512,2816]{1,0:T(8,128)(2,1)}) custom-call(bf16[16,4,16,2048]{3,2,1,0:T(8,128)(2,1)} %bitcast.180, f32[16,16,2048]{2,1,0:T(8,128)} %get-tuple-element.87.refs_0_, ...), custom_call_target="tpu_custom_call" | custom-call | bytes 350000000 | tf_op jit(solution)/shard_map/pallas_call | solution.py:774
  1190.6 14.0 multiply_convert_fusion.1
  1207.2 14.6 convolution_convert_fusion
  1232.7 18.3 fusion.29
  1257.2 48.1 %reduce-scatter.23.cloned.1.call-done.refs_8_.refs_0_.refs_3_ = bf16[512,1408]{1,0:T(8,128)(2,1)} async-done(((bf16[2048,1408]{1,0:T(8,128)(2,1)}), bf16[512,1408]{1,0:T(8,128)(2,1)}) %reduce-scatter.23.cloned.1.call-update) | async-done | bytes 1441808 | tf_op jit(solution)/shard_map/reduce_scatter | solution.py:1089
  1305.2 60.9 %reduce-scatter.21.cloned.1.call-done.refs_7_ = bf16[512,1536]{1,0:T(8,128)(2,1)} async-done(((bf16[2048,1536]{1,0:T(8,128)(2,1)}), bf16[512,1536]{1,0:T(8,128)(2,1)}) %reduce-scatter.21.cloned.1.call-update) | async-done | bytes 1572880 | tf_op jit(solution)/shard_map/reduce_scatter | solution.py:1089
  1366.2 116.6 %shard_map.178 = (bf16[16,4,16,2048]{3,2,1,0:T(8,128)(2,1)}, f32[16,16,2048]{2,1,0:T(8,128)}, f32[2,2048]{1,0:T(2,128)}, bf16[1024,512]{1,0:T(8,128)(2,1)}, bf16...) custom-call(bf16[16,4,16,2048]{3,2,1,0:T(8,128)(2,1)} %bitcast.173, ...), custom_call_target="tpu_custom_call" | custom-call | bytes 350000000 | tf_op jit(solution)/shard_map/pallas_call | solution.py:774
  1502.2 105.5 %shard_map.179 = bf16[1024,1536]{1,0:T(8,128)(2,1)} custom-call(s32[1,4096]{1,0:T(1,128)} %constant_dynamic-slice_fusion.4.bid_k.bid_q, s32[4096,1]{1,0:T(8,128)} %copy.31.bid_q.bid_k, bf16[1024,512]{1,0:T(8,128)(2,1)} %fusion.46.d_mix, bf16[3,4096,128]{2,1,0:T(8,128)(2,1)} %get-tuple-element.98.spread, bf16[4096,128]{1,0:T(8,128)(2,1)} %get-tuple-element.99.mixed, ...), custom_call_target="tpu_custom_call" | custom-call | flops 10000000000 | bytes 300000000 | tf_op jit(solution)/shard_map/pallas_call | solution.py:375
  1647.9 140.4 %shard_map.180 = (bf16[2,16,4,16,512]{4,3,2,1,0:T(8,128)(2,1)}, f32[16,16,2048]{2,1,0:T(8,128)}, f32[2,2048]{1,0:T(2,128)}, f32[2,4,2,512]{3,2,1,0:T(2,128)}, bf...) custom-call(bf16[16,4,16,2048]{3,2,1,0:T(8,128)(2,1)} %bitcast.179, ...), custom_call_target="tpu_custom_call" | custom-call | bytes 350000000 | tf_op jit(solution)/shard_map/pallas_call | solution.py:774
  1817.7 28.3 %collective-permute-done = bf16[512,1536]{1,0:T(8,128)(2,1)S(1)} collective-permute-done((bf16[512,1536]{1,0:T(8,128)(2,1)}, bf16[512,1536]{1,0:T(8,128)(2,1)S(1)}, u32[]{:S(2)}, u32[]{:S(2)}) %collective-permute-start) | collective-permute-done | bytes 1572896 | tf_op jit(solution)/shard_map/ppermute | solution.py:1174
  (222 shorter events, 265.7 us)
Async XLA Ops:
  7.2 103.2 %all-gather.11.cloned.1.call-start = ((), (), s32[]{:S(2)}) async-start(), calls=%async_computation.10 | async-start | bytes 14155776 | tf_op jit(solution)/shard_map/all_gather | solution.py:1012
  10.0 197.1 %all-gather.15.cloned.1.call-start = ((), (), s32[]{:S(2)}) async-start(), calls=%async_computation.21 | async-start | bytes 4718592 | tf_op jit(solution)/shard_map/all_gather | solution.py:1012
  10.7 308.6 %all-gather.13.cloned.1.call-start = ((), (), s32[]{:S(2)}) async-start(), calls=%async_computation.11 | async-start | bytes 25952256 | tf_op jit(solution)/shard_map/all_gather | solution.py:1012
  14.7 331.4 %all-gather.17.cloned.1.call-start = ((), (), s32[]{:S(2)}) async-start(), calls=%async_computation.22 | async-start | bytes 12976128 | tf_op jit(solution)/shard_map/all_gather | solution.py:1012
  15.3 578.0 %all-gather.19.cloned.1.call-start = ((), (), s32[]{:S(2)}) async-start(), calls=%async_computation.23 | async-start | bytes 5242880 | tf_op jit(solution)/shard_map/all_gather | solution.py:1043
  356.9 115.3 %copy-start.27 = (bf16[2,1024,512]{2,1,0:T(8,128)(2,1)S(1)}, bf16[2,1024,512]{2,1,0:T(8,128)(2,1)}, u32[]{:S(2)}) copy-start(bf16[2,1024,512]{2,1,0:T(8,128)(2,1)} %param.11) | copy-start | bytes 6291460
  473.3 454.0 %reduce-scatter.13.cloned.1.call-start = ((), (), s32[]{:S(2)}) async-start(), calls=%async_computation.12 | async-start | bytes 7208960 | tf_op jit(solution)/shard_map/reduce_scatter | solution.py:1089
  593.2 128.9 %slice-start = ((s8[11534336]{0:T(1024)(128)(4,1)}), s8[3145728]{0:T(1024)(128)(4,1)S(1)}, s32[]{:S(2)}) async-start(s8[11534336]{0:T(1024)(128)(4,1)} %bitcast.201), calls=%async_computation.25 | async-start | bytes 6291456
  781.4 163.3 %reduce-scatter.15.cloned.1.call-start = ((), (), s32[]{:S(2)}) async-start(), calls=%async_computation.13 | async-start | bytes 14417920 | tf_op jit(solution)/shard_map/reduce_scatter | solution.py:1089
  782.1 295.6 %reduce-scatter.17.cloned.1.call-start = ((), (), s32[]{:S(2)}) async-start(), calls=%async_computation.14 | async-start | bytes 5242880 | tf_op jit(solution)/shard_map/reduce_scatter | solution.py:1124
  785.1 117.7 %copy-start.18 = (f32[16,16,2048]{2,1,0:T(8,128)S(1)}, f32[16,16,2048]{2,1,0:T(8,128)}, u32[]{:S(2)}) copy-start(f32[16,16,2048]{2,1,0:T(8,128)} %get-tuple-element.78.refs_1_) | copy-start | bytes 6291460
  785.1 117.7 %copy-start.42 = (bf16[1024,1408]{1,0:T(8,128)(2,1)S(1)}, bf16[1024,1408]{1,0:T(8,128)(2,1)}, u32[]{:S(2)}) copy-start(bf16[1024,1408]{1,0:T(8,128)(2,1)} %get-tuple-element.152) | copy-start | bytes 8650756
  913.8 343.4 %reduce-scatter.19.cloned.1.call-start = ((), (), s32[]{:S(2)}) async-start(), calls=%async_computation.15 | async-start | bytes 2621440 | tf_op jit(solution)/shard_map/reduce_scatter | solution.py:1089
  927.2 378.0 %reduce-scatter.23.cloned.1.call-start = ((), (), s32[]{:S(2)}) async-start(), calls=%async_computation.17 | async-start | bytes 7208960 | tf_op jit(solution)/shard_map/reduce_scatter | solution.py:1089
  1251.0 115.1 %reduce-scatter.21.cloned.1.call-start = ((), (), s32[]{:S(2)}) async-start(), calls=%async_computation.16 | async-start | bytes 7864320 | tf_op jit(solution)/shard_map/reduce_scatter | solution.py:1089
  1251.8 250.4 %reduce-scatter.25.cloned.1.call-start = ((), (), s32[]{:S(2)}) async-start(), calls=%async_computation.18 | async-start | bytes 14417920 | tf_op jit(solution)/shard_map/reduce_scatter | solution.py:1089
  1252.3 384.5 %reduce-scatter.31.cloned.1.call-start = ((), (), s32[]{:S(2)}) async-start(), calls=%async_computation.24 | async-start | bytes 1310720
  1366.2 116.7 %copy-start.34 = (f32[2,2048]{1,0:T(2,128)S(1)}, f32[2,2048]{1,0:T(2,128)}, u32[]{:S(2)}) copy-start(f32[2,2048]{1,0:T(2,128)} %get-tuple-element.105) | copy-start | bytes 49156
  1366.2 116.7 %copy-start.35 = (f32[2,2048]{1,0:T(2,128)S(1)}, f32[2,2048]{1,0:T(2,128)}, u32[]{:S(2)}) copy-start(f32[2,2048]{1,0:T(2,128)} %get-tuple-element.106) | copy-start | bytes 49156
  1491.9 155.9 %reduce-scatter.27.cloned.1.call-start = ((), (), s32[]{:S(2)}) async-start(), calls=%async_computation.19 | async-start | bytes 2621440 | tf_op jit(solution)/shard_map/reduce_scatter | solution.py:1089
  1502.1 306.3 %reduce-scatter.29.cloned.1.call-start = ((), (), s32[]{:S(2)}) async-start(), calls=%async_computation.20 | async-start | bytes 7864320 | tf_op jit(solution)/shard_map/reduce_scatter | solution.py:1089
  1647.9 140.4 %copy-start.8 = (bf16[512,2816]{1,0:T(8,128)(2,1)S(1)}, bf16[512,2816]{1,0:T(8,128)(2,1)}, u32[]{:S(2)}) copy-start(bf16[512,2816]{1,0:T(8,128)(2,1)} %reduce-scatter.15.cloned.1.call-done.refs_1_.refs_4_) | copy-start | bytes 8650756
  1647.9 140.4 %copy-start.9 = (bf16[512,2816]{1,0:T(8,128)(2,1)S(1)}, bf16[512,2816]{1,0:T(8,128)(2,1)}, u32[]{:S(2)}) copy-start(bf16[512,2816]{1,0:T(8,128)(2,1)} %reduce-scatter.25.cloned.1.call-done.refs_1_.refs_4_) | copy-start | bytes 8650756
  1808.4 37.6 %collective-permute-start = (bf16[512,1536]{1,0:T(8,128)(2,1)}, bf16[512,1536]{1,0:T(8,128)(2,1)S(1)}, u32[]{:S(2)}, u32[]{:S(2)}) collective-permute-start(bf16[512,1536]{1,0:T(8,128)(2,1)} %reduce-scatter.29.cloned.1.call-done), channel_id=1, source_target_pairs={{16,0},{17,1},{18,2},{19,3},{20,4},{21,5},{22,6},{23,7},{24,8},{25... | collective-permute-start | bytes 4718600 | tf_op jit(solution)/shard_map/ppermute | solution.py:1174
  (42 other events, 413.3 us)
Sparse Core Ops, SparseCore 0:
  10.5 78.1 all-gather.10
  90.5 36.6 all-gather.14
  129.7 144.1 all-gather.12
  275.7 70.2 all-gather.16
  473.4 104.0 all-gather.18
  781.5 68.1 reduce-scatter.12
  852.4 92.2 reduce-scatter.14
  947.1 76.7 reduce-scatter.16
  1026.4 33.5 reduce-scatter.18
  1251.1 54.0 reduce-scatter.22
  1307.8 58.3 reduce-scatter.20
  1368.8 92.1 reduce-scatter.24
  1492.1 25.0 reduce-scatter.30
  1520.1 30.0 reduce-scatter.26
  1630.3 56.1 reduce-scatter.28

commit v4 on v3

--- a/solution.py
+++ b/solution.py
@@ -64,9 +64,9 @@
 
 
 def attend_kernel(
-    heads, n, bq, bk, bid_q, bid_k, qkv, cosines, sines, *refs
+    heads, n, bq, bk, bid_q, bid_k, qkv, cosines, sines,
+    spread, mixed, lse_ref, mix, vone, scores, leaving, qkv_sent, qkv_got, mix_sent, mix_got,
 ):
-    spread, mixed, lse_ref, mix, vone, scores, leaving, qkv_sent, qkv_got, mix_sent, mix_got = refs[-11:]
     me = lax.axis_index("row")
     tokens = qkv.shape[0]
     seq = n * tokens
@@ -197,7 +197,7 @@
                 ).wait_recv()
 
 
-def attend(number, qkv, block_all, cosines, sines, heads, n, behind=(), bq=512, bk=512):
+def attend(number, qkv, block_all, cosines, sines, heads, n, bq=512, bk=512):
     tokens = qkv.shape[0]
     bq, bk = min(bq, tokens), min(bk, tokens)
     seq = n * tokens
@@ -205,7 +205,7 @@
     low = jnp.bfloat16
     return pl.pallas_call(
         functools.partial(attend_kernel, heads, n, bq, bk),
-        in_specs=[vmem] * 5 + [pl.BlockSpec(memory_space=pl.ANY)] * len(behind),
+        in_specs=[vmem] * 5,
         out_specs=[vmem] * 4,
         out_shape=[
             jax.ShapeDtypeStruct((3, seq, LANES), low),
@@ -226,13 +226,14 @@
             collective_id=number, has_side_effects=True, vmem_limit_bytes=58 * 2**20
         ),
         cost_estimate=pl.CostEstimate(flops=10**10, bytes_accessed=2 * 10**8, transcendentals=0),
-    )(block_all.reshape(seq, 1), block_all.reshape(1, seq), qkv, cosines, sines, *behind)
+    )(block_all.reshape(seq, 1), block_all.reshape(1, seq), qkv, cosines, sines)
 
 
 def attend_back_kernel(
-    heads, n, bq, bk, bid_q, bid_k, d_mix, spread, mixed, lse_ref, cosines, sines, *refs
+    heads, n, bq, bk, layer, bid_q, bid_k, d_mix, spread, mixed, lse_ref, cosines, sines, carry, *refs
 ):
-    d_qkv, grads, kone, dk_acc, dv_acc, leaving, g_sent, g_got, back_sent, back_got = refs[-10:]
+    d_qkv, carried, grads, kone, dk_acc, dv_acc, leaving, g_sent, g_got, back_sent, back_got, carry_sent, carry_got = refs
+    section = lax.axis_index("section")
     me = lax.axis_index("row")
     tokens = d_mix.shape[0]
     seq = n * tokens
@@ -241,7 +242,12 @@
     low = jnp.bfloat16
     zero = jnp.zeros((), low)
     here = pl.ds(pl.multiple_of(me * tokens, tokens), tokens)
-    meet("row", n)
+    barrier = pltpu.get_barrier_semaphore()
+    pl.semaphore_signal(barrier, 1, device_id={"section": 1 - section}, device_id_type=pl.DeviceIdType.MESH)
+    for d in range(1, n):
+        pl.semaphore_signal(barrier, 1, device_id={"row": lax.rem(me + d, n)}, device_id_type=pl.DeviceIdType.MESH)
+    pl.semaphore_wait(barrier, n)
+    carry_copy = remote(carry, carried, carry_sent, carry_got, "section", layer)
 
     def give(d):
         to = lax.rem(me + d, n)
@@ -249,6 +255,11 @@
 
     for d in range(1, n):
         give(d).start()
+
+    @pl.when(section != layer)
+    def _():
+        carry_copy.start()
+
     grads[here, :] = d_mix[:, columns(me)]
     for h in range(heads):
         kone[h] = jnp.where(lanes_of(seq, h), spread[1], zero)
@@ -365,18 +376,26 @@
 
     lax.fori_loop(0, blocks, settle, 0)
 
-
-def attend_back(number, d_mix, spread, mixed, lse, block_all, cosines, sines, heads, n, behind=(), bq=512, bk=512):
+    @pl.when(section != layer)
+    def _():
+        carry_copy.wait_send()
+
+    @pl.when(section == layer)
+    def _():
+        carry_copy.wait_recv()
+
+
+def attend_back(number, d_mix, spread, mixed, lse, block_all, cosines, sines, heads, n, layer, carry, bq=512, bk=512):
     tokens = d_mix.shape[0]
     bq, bk = min(bq, tokens), min(bk, tokens)
     seq = n * tokens
     vmem = pl.BlockSpec(memory_space=pltpu.VMEM)
     low = jnp.bfloat16
     return pl.pallas_call(
-        functools.partial(attend_back_kernel, heads, n, bq, bk),
-        in_specs=[vmem] * 8 + [pl.BlockSpec(memory_space=pl.ANY)] * len(behind),
-        out_specs=vmem,
-        out_shape=jax.ShapeDtypeStruct((tokens, 3 * n * LANES), low),
+        functools.partial(attend_back_kernel, heads, n, bq, bk, layer),
+        in_specs=[vmem] * 8 + [pl.BlockSpec(memory_space=pl.ANY)],
+        out_specs=[vmem, pl.BlockSpec(memory_space=pl.ANY)],
+        out_shape=[jax.ShapeDtypeStruct((tokens, 3 * n * LANES), low), jax.ShapeDtypeStruct(carry.shape, carry.dtype)],
         scratch_shapes=[
             pltpu.VMEM((seq, LANES), low),
             pltpu.VMEM((heads, seq, LANES), low),
@@ -387,12 +406,14 @@
             pltpu.SemaphoreType.DMA((n,)),
             pltpu.SemaphoreType.DMA((3, seq // bq)),
             pltpu.SemaphoreType.DMA((3, n, tokens // bq)),
+            pltpu.SemaphoreType.DMA,
+            pltpu.SemaphoreType.DMA,
         ],
         compiler_params=pltpu.CompilerParams(
             collective_id=number, has_side_effects=True, vmem_limit_bytes=58 * 2**20
         ),
         cost_estimate=pl.CostEstimate(flops=10**10, bytes_accessed=3 * 10**8, transcendentals=0),
-    )(block_all.reshape(1, seq), block_all.reshape(seq, 1), d_mix, spread, mixed, lse, cosines, sines, *behind)
+    )(block_all.reshape(1, seq), block_all.reshape(seq, 1), d_mix, spread, mixed, lse, cosines, sines, carry)
 
 
 def norm_parts(values):
@@ -1117,7 +1138,7 @@
             carry=[]
             if layer == 1
             else [(0, hidden_out[0]), (1, hidden_out[1]), (1, input_out[1]), (1, weight_sums[1][2]), (1, weight_sums[1][3])],
-            behind=[] if layer == 1 else [down_sum],
+            behind=[] if layer == 1 else [weight_sums[1][0]],
         )
         if layer == 1:
             result = jnp.where(d_after[0, 0] == d_after[0, 0], result, 0)
@@ -1129,21 +1150,21 @@
             product(grad_attn, out_w[layer]).astype(jnp.bfloat16), dot_first(grad_attn, attn_mix).astype(jnp.bfloat16)
         )
         out_sum = collect(layer, out_term)
-        d_qkv = contract(
-            attend_back(
-                9,
-                expand(d_mix),
-                spread,
-                mixed,
-                log_sums,
-                ids,
-                cosines,
-                sines,
-                heads,
-                rows_axis,
-                behind=[down_sum, gate_up_sum],
-            )
-        )
+        d_qkv, arrived[layer][1] = attend_back(
+            9 + layer,
+            expand(d_mix),
+            spread,
+            mixed,
+            log_sums,
+            ids,
+            cosines,
+            sines,
+            heads,
+            rows_axis,
+            layer,
+            gate_up_sum,
+        )
+        d_qkv = contract(d_qkv)
         partial, qkv_term, bias_grads[layer] = together(
             dot_last(d_qkv, qkv_w[layer]).astype(jnp.bfloat16),
             dot_first(normed, d_qkv).astype(jnp.bfloat16),
@@ -1162,12 +1183,11 @@
             [(owned, D), (2, D)],
             cols_axis,
             spread=layer == 0,
-            carry=[(layer, down_sum), (layer, gate_up_sum)] + ([(0, out_sum)] if layer == 0 else []),
+            carry=[] if layer == 1 else [(0, down_sum), (0, out_sum), (1, weight_sums[1][0])],
             behind=[hidden_out[1]] if layer == 1 else [early_sums],
         )
         if layer == 0:
-            late_sums, *got = got
-        arrived[layer][: len(got)] = got
+            late_sums, arrived[0][0], arrived[0][2], arrived[1][0] = got
         small_sums += [sums_one]
         input_out[layer] = my_features(branch) if layer == 1 else branch
 

time: 1870 us -> 1720 us (0.920)
  waiting for transfers between devices: 160 us -> 32.4 us
  Pallas kernels: 1290 us -> 1270 us
    reduce_scatter x8, waiting for transfers between devices: 126 us -> 0.07 us  [collect(): lax.psum_scatter(term, 'row', scatter_dimension=0, tiled=True)]
    pallas_call x7, Pallas kernels: 813 us -> 760 us  [relay(): pl.pallas_call(functools.partial(relay_kernel, middle, len(ins), len(outs...]
    pallas_call x2, Pallas kernels: 213 us -> 243 us  [attend_back(): pl.pallas_call(functools.partial(attend_back_kernel, heads, n, bq, bk, la...]
  transfers between devices with their start and end apart: 16 -> 16, of which waited for: 5 -> 2; matrix products, arithmetic and copies ran while one was open for 14% -> 15% of each run, Pallas kernels for 57% -> 61%
where the time goes in v4:
time: 1720 us
  Pallas kernels  1270 us (74%)
  matrix products  278 us (16%)
  local copies, waits for them, and re-layouts  65.7 us (4%)
  other arithmetic  36.7 us (2%)
  waiting for transfers between devices  32.4 us (2%)
    pallas_call x7, Pallas kernels, relay(): pl.pallas_call(functools.partial(relay_kernel, middle, len(ins), len(outs...  760 us
    pallas_call x2, Pallas kernels, attend_back(): pl.pallas_call(functools.partial(attend_back_kernel, heads, n, bq, bk, la...  243 us
    pallas_call x2, Pallas kernels, attend(): pl.pallas_call(functools.partial(attend_kernel, heads, n, bq, bk), in_spe...  186 us
    dot_general x12, matrix products, product(): return jnp.dot(left, right, preferred_element_type=jnp.float32)  136 us
    dot_general x8, matrix products, dot_first(): lax.dot_general(a, b, (((0,), (0,)), ((), ())), preferred_element_type=jn...  82.3 us
    pallas_call x1, Pallas kernels, gathered(): pl.pallas_call(functools.partial(gather_kernel, n, chunks, lag), in_specs...  82.3 us
    dot_general x4, matrix products, dot_last(): lax.dot_general(a, b, (((1,), (1,)), ((), ())), preferred_element_type=jn...  59.4 us
    unnamed x101, local copies, waits for them, and re-layouts  35.8 us
  transfers between devices with their start and end apart: 16, of which 2 were waited for; matrix products, arithmetic and copies ran while one was open for 15% of the time, Pallas kernels for 61%

profile of v4, /device:TPU:0, one launch (start us, length us, event | category | flops | bytes accessed | tf_op | source)
XLA Modules:
  0.0 1717.7 jit_solution(9151705751394631319)
XLA Ops:
  18.2 82.3 %shard_map.169 = (bf16[1024,2048]{1,0:T(8,128)(2,1)S(1)}, f32[2,4,8,512]{3,2,1,0:T(8,128)S(1)}, bf16[1024,2048]{1,0:T(8,128)(2,1)S(1)}, f32[4096,128]{1,0:T(8,128)S(1)}, f32[4096,128]{1,0:T(8,128)S(1)}) custom-call(bf16[1024,512]{1,0:T(8,128)(2,1)S(1)} %dynamic-slice_bitcast_fusion.2.own, f32[8,512]{1,0:T(8,128)S(1)} %maximum_maximum_fusion.small, ...), custom_call_target="tpu_custom_call" | custom-call | bytes 250000000 | tf_op jit(solution)/shard_map/pallas_call | solution.py:957
  110.7 12.5 fusion.22.qkv
  123.2 84.5 %shard_map.170 = (bf16[3,4096,128]{2,1,0:T(8,128)(2,1)}, bf16[4096,128]{1,0:T(8,128)(2,1)}, f32[128,4096]{1,0:T(8,128)}, bf16[1024,512]{1,0:T(8,128)(2,1)}) custom-call(s32[4096,1]{1,0:T(8,128)} %copy.31.bid_q.bid_k, s32[1,4096]{1,0:T(1,128)} %constant_dynamic-slice_fusion.4.bid_k.bid_q, f32[1024,1536]{1,0:T(8,128)} %fusion.22.qkv, f32[4096,128]{1,0:T(8,128)} %copy-done.5, ...), custom_call_target="tpu_custom_call" | custom-call | flops 10000000000 | bytes 200000000 | tf_op jit(solution)/shard_map/pallas_call | solution.py:206
  215.0 105.0 %shard_map.171 = (bf16[16,4,16,2048]{3,2,1,0:T(8,128)(2,1)}, f32[16,16,2048]{2,1,0:T(8,128)}) custom-call(bf16[16,4,16,2048]{3,2,1,0:T(8,128)(2,1)} %bitcast.176, bf16[16,16,2048]{2,1,0:T(8,128)(2,1)} %dynamic-slice_bitcast_fusion.1.refs_0_.refs_1_, f32[1,2048]{1,0:T(1,128)} %get-tuple-element.163.refs_1_.refs_2_, f32[1,2048]{1,0:T(1,128)} %get-tuple-element.162.refs_2_), custom_call_target="tpu_custom_call" | custom-call | bytes 350000000 | tf_op jit(solution)/shard_map/pallas_call | solution.py:795
  320.0 17.4 %fusion.6 = f32[1024,2816]{1,0:T(8,128)S(1)} fusion(bf16[1024,2048]{1,0:T(8,128)(2,1)} %bitcast.203, bf16[4096,2816]{1,0:T(8,128)(2,1)} %all-gather.13.cloned.1.call-done), kind=kOutput, calls=%fused_computation.8 | convolution fusion | flops 11811160064 | bytes 27262976 | tf_op jit(solution)/shard_map/dot_general | solution.py:989
  356.9 111.9 %shard_map.172 = (bf16[16,4,16,2048]{3,2,1,0:T(8,128)(2,1)}, bf16[16,4,16,2048]{3,2,1,0:T(8,128)(2,1)}) custom-call(bf16[16,4,16,2048]{3,2,1,0:T(8,128)(2,1)} %bitcast.177, f32[16,16,2048]{2,1,0:T(8,128)} %get-tuple-element.74.refs_0_.refs_1_, f32[1,2048]{1,0:T(1,128)} %get-tuple-element.161.refs_1_.refs_2_, f32[1,2048]{1,0:T(1,128)} %get-tuple-element.160.refs_2_), custom_call_target="tpu_custom_call" | custom-call | bytes 350000000 | tf_op jit(solution)/shard_map/pallas_call | solution.py:795
  474.1 12.0 fusion.25.qkv
  486.1 101.2 %shard_map.173 = (bf16[3,4096,128]{2,1,0:T(8,128)(2,1)}, bf16[4096,128]{1,0:T(8,128)(2,1)}, f32[128,4096]{1,0:T(8,128)}, bf16[1024,512]{1,0:T(8,128)(2,1)}) custom-call(s32[4096,1]{1,0:T(8,128)} %copy.31.bid_q.bid_k, s32[1,4096]{1,0:T(1,128)} %constant_dynamic-slice_fusion.4.bid_k.bid_q, f32[1024,1536]{1,0:T(8,128)} %fusion.25.qkv, f32[4096,128]{1,0:T(8,128)} %copy-done.5, ...), custom_call_target="tpu_custom_call" | custom-call | flops 10000000000 | bytes 200000000 | tf_op jit(solution)/shard_map/pallas_call | solution.py:206
  593.7 111.6 %shard_map.174 = (bf16[16,4,16,2048]{3,2,1,0:T(8,128)(2,1)}, f32[16,16,2048]{2,1,0:T(8,128)}) custom-call(bf16[16,4,16,2048]{3,2,1,0:T(8,128)(2,1)} %bitcast.180, bf16[16,16,2048]{2,1,0:T(8,128)(2,1)} %dynamic-slice_bitcast_fusion.refs_0_.refs_1_, f32[1,2048]{1,0:T(1,128)} %get-tuple-element.159.refs_1_.refs_2_, f32[1,2048]{1,0:T(1,128)} %get-tuple-element.158.refs_2_, ...), custom_call_target="tpu_custom_call" | custom-call | bytes 350000000 | tf_op jit(solution)/shard_map/pallas_call | solution.py:795
  705.3 18.8 %fusion.2 = f32[1024,2816]{1,0:T(8,128)} fusion(bf16[1024,2048]{1,0:T(8,128)(2,1)} %bitcast.211, bf16[4096,2816]{1,0:T(8,128)(2,1)} %all-gather.13.cloned.1.call-done), kind=kOutput, calls=%fused_computation.4 | convolution fusion | flops 11811160064 | bytes 27262976 | tf_op jit(solution)/shard_map/dot_general | solution.py:989
  724.2 13.4 multiply_convert_fusion.4
  737.6 18.5 %convolution_convert_fusion.1 = bf16[2048,2816]{1,0:T(8,128)(2,1)} fusion(bf16[1024,2048]{1,0:T(8,128)(2,1)} %bitcast.212, bf16[1024,1408]{1,0:T(8,128)(2,1)} %get-tuple-element.155, bf16[1024,1408]{1,0:T(8,128)(2,1)} %get-tuple-element.154), kind=kOutput, calls=%fused_computation.1 | convolution fusion | flops 11828461568 | bytes 21495808 | tf_op jit(solution)/shard_map/dot_general | solution.py:27
  756.1 18.2 %fusion.32 = bf16[1024,2048]{1,0:T(8,128)(2,1)} fusion(bf16[4096,2816]{1,0:T(8,128)(2,1)} %all-gather.13.cloned.1.call-done, bf16[1024,1408]{1,0:T(8,128)(2,1)} %get-tuple-element.155, bf16[1024,1408]{1,0:T(8,128)(2,1)} %get-tuple-element.154), kind=kOutput, calls=%fused_computation.48 | convolution fusion | flops 11824791552 | bytes 21495808 | tf_op jit(solution)/shard_map/dot_general | solution.py:23
  786.4 113.4 %shard_map.175 = (bf16[16,4,16,2048]{3,2,1,0:T(8,128)(2,1)}, f32[16,16,2048]{2,1,0:T(8,128)}, f32[2,2048]{1,0:T(2,128)}) custom-call(bf16[16,4,16,2048]{3,2,1,0:T(8,128)(2,1)} %bitcast.174, f32[16,16,2048]{2,1,0:T(8,128)} %bitcast_convert_fusion.refs_0_, f32[16,16,2048]{2,1,0:T(8,128)} %get-tuple-element.80.refs_1_, f32[1,2048]{1,0:T(1,128)} %get-tuple-element.159.refs_1_.refs_2_), custom_call_target="tpu_custom_call" | custom-call | bytes 350000000 | tf_op jit(solution)/shard_map/pallas_call | solution.py:795
  927.4 123.4 %shard_map.176 = (bf16[1024,1536]{1,0:T(8,128)(2,1)}, bf16[512,2816]{1,0:T(8,128)(2,1)}) custom-call(s32[1,4096]{1,0:T(1,128)} %constant_dynamic-slice_fusion.4.bid_k.bid_q, s32[4096,1]{1,0:T(8,128)} %copy.31.bid_q.bid_k, bf16[1024,512]{1,0:T(8,128)(2,1)} %fusion.45.d_mix, bf16[3,4096,128]{2,1,0:T(8,128)(2,1)} %get-tuple-element.83.spread, ...), custom_call_target="tpu_custom_call" | custom-call | flops 10000000000 | bytes 300000000 | tf_op jit(solution)/shard_map/pallas_call | solution.py:394
  1053.8 11.9 fusion.39
  1074.6 108.9 %shard_map.177 = (bf16[16,4,16,2048]{3,2,1,0:T(8,128)(2,1)}, f32[16,16,2048]{2,1,0:T(8,128)}, f32[2,2048]{1,0:T(2,128)}) custom-call(bf16[16,4,16,2048]{3,2,1,0:T(8,128)(2,1)} %bitcast.175, f32[16,16,2048]{2,1,0:T(8,128)} %get-tuple-element.89.refs_0_, bf16[16,16,2048]{2,1,0:T(8,128)(2,1)} %dynamic-slice_bitcast_fusion.refs_0_.refs_1_, ...), custom_call_target="tpu_custom_call" | custom-call | bytes 350000000 | tf_op jit(solution)/shard_map/pallas_call | solution.py:795
  1194.4 14.0 multiply_convert_fusion.1
  1211.0 14.6 convolution_convert_fusion
  1225.5 18.2 %fusion.29 = bf16[1024,2048]{1,0:T(8,128)(2,1)} fusion(bf16[4096,2816]{1,0:T(8,128)(2,1)} %all-gather.13.cloned.1.call-done, bf16[1024,1408]{1,0:T(8,128)(2,1)} %copy-done.42, bf16[1024,1408]{1,0:T(8,128)(2,1)} %copy-done.41), kind=kOutput, calls=%fused_computation.47 | convolution fusion | flops 11824791552 | bytes 21495808 | tf_op jit(solution)/shard_map/dot_general | solution.py:23
  1248.3 104.4 %shard_map.178 = (bf16[16,4,16,2048]{3,2,1,0:T(8,128)(2,1)}, f32[16,16,2048]{2,1,0:T(8,128)}, f32[2,2048]{1,0:T(2,128)}, bf16[1024,512]{1,0:T(8,128)(2,1)}, bf16...) custom-call(bf16[16,4,16,2048]{3,2,1,0:T(8,128)(2,1)} %bitcast.173, ...), custom_call_target="tpu_custom_call" | custom-call | bytes 350000000 | tf_op jit(solution)/shard_map/pallas_call | solution.py:795
  1375.2 119.6 %shard_map.179 = (bf16[1024,1536]{1,0:T(8,128)(2,1)}, bf16[512,2816]{1,0:T(8,128)(2,1)}) custom-call(s32[1,4096]{1,0:T(1,128)} %constant_dynamic-slice_fusion.4.bid_k.bid_q, s32[4096,1]{1,0:T(8,128)} %copy.31.bid_q.bid_k, bf16[1024,512]{1,0:T(8,128)(2,1)} %fusion.46.d_mix, bf16[3,4096,128]{2,1,0:T(8,128)(2,1)} %get-tuple-element.100.spread, ...), custom_call_target="tpu_custom_call" | custom-call | flops 10000000000 | bytes 300000000 | tf_op jit(solution)/shard_map/pallas_call | solution.py:394
  1551.7 104.4 %shard_map.180 = (bf16[2,16,4,16,512]{4,3,2,1,0:T(8,128)(2,1)}, f32[16,16,2048]{2,1,0:T(8,128)}, f32[2,2048]{1,0:T(2,128)}, f32[2,4,2,512]{3,2,1,0:T(2,128)}, bf...) custom-call(bf16[16,4,16,2048]{3,2,1,0:T(8,128)(2,1)} %bitcast.179, ...), custom_call_target="tpu_custom_call" | custom-call | bytes 350000000 | tf_op jit(solution)/shard_map/pallas_call | solution.py:795
  1673.2 28.0 %collective-permute-done = bf16[512,1536]{1,0:T(8,128)(2,1)S(1)} collective-permute-done((bf16[512,1536]{1,0:T(8,128)(2,1)}, bf16[512,1536]{1,0:T(8,128)(2,1)S(1)}, u32[]{:S(2)}, u32[]{:S(2)}) %collective-permute-start) | collective-permute-done | bytes 1572896 | tf_op jit(solution)/shard_map/ppermute | solution.py:1194
  (214 shorter events, 232.8 us)
Async XLA Ops:
  7.2 103.5 %all-gather.11.cloned.1.call-start = ((), (), s32[]{:S(2)}) async-start(), calls=%async_computation.10 | async-start | bytes 14155776 | tf_op jit(solution)/shard_map/all_gather | solution.py:1033
  10.0 197.8 %all-gather.15.cloned.1.call-start = ((), (), s32[]{:S(2)}) async-start(), calls=%async_computation.21 | async-start | bytes 4718592 | tf_op jit(solution)/shard_map/all_gather | solution.py:1033
  10.7 309.3 %all-gather.13.cloned.1.call-start = ((), (), s32[]{:S(2)}) async-start(), calls=%async_computation.11 | async-start | bytes 25952256 | tf_op jit(solution)/shard_map/all_gather | solution.py:1033
  14.7 331.3 %all-gather.17.cloned.1.call-start = ((), (), s32[]{:S(2)}) async-start(), calls=%async_computation.22 | async-start | bytes 12976128 | tf_op jit(solution)/shard_map/all_gather | solution.py:1033
  15.3 578.4 %all-gather.19.cloned.1.call-start = ((), (), s32[]{:S(2)}) async-start(), calls=%async_computation.23 | async-start | bytes 5242880 | tf_op jit(solution)/shard_map/all_gather | solution.py:1064
  356.9 113.8 %copy-start.25 = (bf16[2,1024,512]{2,1,0:T(8,128)(2,1)S(1)}, bf16[2,1024,512]{2,1,0:T(8,128)(2,1)}, u32[]{:S(2)}) copy-start(bf16[2,1024,512]{2,1,0:T(8,128)(2,1)} %param.11) | copy-start | bytes 6291460
  471.7 455.7 %reduce-scatter.13.cloned.1.call-start = ((), (), s32[]{:S(2)}) async-start(), calls=%async_computation.12 | async-start | bytes 14417920 | tf_op jit(solution)/shard_map/reduce_scatter | solution.py:1110
  593.7 130.5 %slice-start = ((s8[11534336]{0:T(1024)(128)(4,1)}), s8[3145728]{0:T(1024)(128)(4,1)S(1)}, s32[]{:S(2)}) async-start(s8[11534336]{0:T(1024)(128)(4,1)} %bitcast.201), calls=%async_computation.25 | async-start | bytes 6291456
  783.4 291.2 %reduce-scatter.15.cloned.1.call-start = ((), (), s32[]{:S(2)}) async-start(), calls=%async_computation.13 | async-start | bytes 5242880 | tf_op jit(solution)/shard_map/reduce_scatter | solution.py:1145
  786.4 115.9 %copy-start.17 = (f32[16,16,2048]{2,1,0:T(8,128)S(1)}, f32[16,16,2048]{2,1,0:T(8,128)}, u32[]{:S(2)}) copy-start(f32[16,16,2048]{2,1,0:T(8,128)} %get-tuple-element.80.refs_1_) | copy-start | bytes 6291460
  786.4 115.9 %copy-start.38 = (bf16[1024,1408]{1,0:T(8,128)(2,1)S(1)}, bf16[1024,1408]{1,0:T(8,128)(2,1)}, u32[]{:S(2)}) copy-start(bf16[1024,1408]{1,0:T(8,128)(2,1)} %get-tuple-element.156) | copy-start | bytes 8650756
  913.3 335.0 %reduce-scatter.17.cloned.1.call-start = ((), (), s32[]{:S(2)}) async-start(), calls=%async_computation.14 | async-start | bytes 2621440 | tf_op jit(solution)/shard_map/reduce_scatter | solution.py:1110
  926.6 321.7 %reduce-scatter.21.cloned.1.call-start = ((), (), s32[]{:S(2)}) async-start(), calls=%async_computation.16 | async-start | bytes 7208960 | tf_op jit(solution)/shard_map/reduce_scatter | solution.py:1110
  927.3 321.0 %reduce-scatter.19.cloned.1.call-start = ((), (), s32[]{:S(2)}) async-start(), calls=%async_computation.15 | async-start | bytes 7864320 | tf_op jit(solution)/shard_map/reduce_scatter | solution.py:1110
  1074.5 300.6 %reduce-scatter.23.cloned.1.call-start = ((), (), s32[]{:S(2)}) async-start(), calls=%async_computation.17 | async-start | bytes 14417920 | tf_op jit(solution)/shard_map/reduce_scatter | solution.py:1110
  1074.6 108.9 %copy-start.16 = (bf16[1024,1408]{1,0:T(8,128)(2,1)S(1)}, bf16[1024,1408]{1,0:T(8,128)(2,1)}, u32[]{:S(2)}) copy-start(bf16[1024,1408]{1,0:T(8,128)(2,1)} %multiply_convert_fusion.5) | copy-start | bytes 8650756
  1243.7 279.8 %reduce-scatter.31.cloned.1.call-start = ((), (), s32[]{:S(2)}) async-start(), calls=%async_computation.24 | async-start | bytes 1310720
  1361.8 189.9 %reduce-scatter.25.cloned.1.call-start = ((), (), s32[]{:S(2)}) async-start(), calls=%async_computation.18 | async-start | bytes 7208960 | tf_op jit(solution)/shard_map/reduce_scatter | solution.py:1110
  1362.6 189.1 %reduce-scatter.27.cloned.1.call-start = ((), (), s32[]{:S(2)}) async-start(), calls=%async_computation.19 | async-start | bytes 2621440 | tf_op jit(solution)/shard_map/reduce_scatter | solution.py:1110
  1375.1 287.6 %reduce-scatter.29.cloned.1.call-start = ((), (), s32[]{:S(2)}) async-start(), calls=%async_computation.20 | async-start | bytes 7864320 | tf_op jit(solution)/shard_map/reduce_scatter | solution.py:1110
  1551.7 113.2 %copy-start.18 = (bf16[512,512]{1,0:T(8,128)(2,1)S(1)}, bf16[512,512]{1,0:T(8,128)(2,1)}, u32[]{:S(2)}) copy-start(bf16[512,512]{1,0:T(8,128)(2,1)} %reduce-scatter.17.cloned.1.call-done.refs_6_) | copy-start | bytes 1572868
  1551.7 113.2 %copy-start.19 = (bf16[512,512]{1,0:T(8,128)(2,1)S(1)}, bf16[512,512]{1,0:T(8,128)(2,1)}, u32[]{:S(2)}) copy-start(bf16[512,512]{1,0:T(8,128)(2,1)} %reduce-scatter.27.cloned.1.call-done.refs_4_) | copy-start | bytes 1572868
  1551.7 113.2 %copy-start.26 = (bf16[512,512]{1,0:T(8,128)(2,1)S(1)}, bf16[512,512]{1,0:T(8,128)(2,1)}, u32[]{:S(2)}) copy-start(bf16[512,512]{1,0:T(8,128)(2,1)} %get-tuple-element.120) | copy-start | bytes 1572868
  1662.7 38.6 %collective-permute-start = (bf16[512,1536]{1,0:T(8,128)(2,1)}, bf16[512,1536]{1,0:T(8,128)(2,1)S(1)}, u32[]{:S(2)}, u32[]{:S(2)}) collective-permute-start(bf16[512,1536]{1,0:T(8,128)(2,1)} %reduce-scatter.29.cloned.1.call-done), channel_id=1, source_target_pairs={{16,0},{17,1},{18,2},{19,3},{20,4},{21,5},{22,6},{23,7},{24,8},{25... | collective-permute-start | bytes 4718600 | tf_op jit(solution)/shard_map/ppermute | solution.py:1194
  (38 other events, 536.8 us)
Sparse Core Ops, SparseCore 0:
  10.5 78.1 all-gather.10
  90.5 36.7 all-gather.14
  129.7 144.0 all-gather.12
  275.6 70.2 all-gather.16
  471.8 106.6 all-gather.18
  783.5 103.7 reduce-scatter.12
  913.4 82.1 reduce-scatter.14
  998.3 43.2 reduce-scatter.16
  1044.8 54.8 reduce-scatter.20
  1102.2 58.4 reduce-scatter.18
  1243.8 96.4 reduce-scatter.22
  1361.9 39.9 reduce-scatter.30
  1404.6 73.5 reduce-scatter.24
  1481.2 37.8 reduce-scatter.26
  1521.6 59.2 reduce-scatter.28

commit v5 on v4

--- a/solution.py
+++ b/solution.py
@@ -63,12 +63,14 @@
     return pl.ds(pl.multiple_of(which * size, size), size)
 
 
-def attend_kernel(
-    heads, n, bq, bk, bid_q, bid_k, qkv, cosines, sines,
-    spread, mixed, lse_ref, mix, vone, scores, leaving, qkv_sent, qkv_got, mix_sent, mix_got,
-):
+def attend_kernel(heads, n, bq, bk, given, bid_q, bid_k, *refs):
     me = lax.axis_index("row")
-    tokens = qkv.shape[0]
+    if given:
+        spread, mixed, lse_ref, mix, vone, scores, mix_sent, mix_got = refs
+    else:
+        qkv, cosines, sines, spread, mixed, lse_ref, mix, vone, scores, mix_sent, mix_got = refs[:11]
+        leaving, qkv_sent, qkv_got = refs[11:]
+    tokens = mix.shape[0]
     seq = n * tokens
     here = pl.ds(pl.multiple_of(me * tokens, tokens), tokens)
     low = jnp.bfloat16
@@ -84,18 +86,20 @@
         to = lax.rem(me + d, n)
         return remote(leaving.at[d - 1], spread.at[:, here], qkv_sent.at[d - 1], qkv_got.at[me], "row", to)
 
-    for d in range(1, n):
-        for k, part in enumerate(parts(lax.rem(me + d, n))):
-            leaving[d - 1, k] = part
-        leave(d).start()
-    for k, part in enumerate(parts(me)):
-        spread[k, here, :] = part
+    if not given:
+        for d in range(1, n):
+            for k, part in enumerate(parts(lax.rem(me + d, n))):
+                leaving[d - 1, k] = part
+            leave(d).start()
+        for k, part in enumerate(parts(me)):
+            spread[k, here, :] = part
 
     def come(row):
-        @pl.when(row != me)
-        def _():
-            there = pl.ds(row * tokens, tokens)
-            remote(leaving.at[0], spread.at[:, there], qkv_sent.at[0], qkv_got.at[row], "row", me).wait_recv()
+        if not given:
+            @pl.when(row != me)
+            def _():
+                there = pl.ds(row * tokens, tokens)
+                remote(leaving.at[0], spread.at[:, there], qkv_sent.at[0], qkv_got.at[row], "row", me).wait_recv()
 
         there = pl.ds(row * tokens, tokens)
         for h in range(heads):
@@ -180,8 +184,9 @@
 
         lax.fori_loop(0, per_row, run, 0)
 
-    for d in range(1, n):
-        leave(d).wait_send()
+    if not given:
+        for d in range(1, n):
+            leave(d).wait_send()
     for i in range(n * per_row):
         @pl.when(i // per_row != me)
         def _(i=i):
@@ -197,51 +202,56 @@
                 ).wait_recv()
 
 
-def attend(number, qkv, block_all, cosines, sines, heads, n, bq=512, bk=512):
-    tokens = qkv.shape[0]
+def attend(number, block_all, heads, n, tokens, qkv=None, cosines=None, sines=None, spread=None, bq=512, bk=512):
     bq, bk = min(bq, tokens), min(bk, tokens)
     seq = n * tokens
     vmem = pl.BlockSpec(memory_space=pltpu.VMEM)
     low = jnp.bfloat16
-    return pl.pallas_call(
-        functools.partial(attend_kernel, heads, n, bq, bk),
-        in_specs=[vmem] * 5,
-        out_specs=[vmem] * 4,
-        out_shape=[
-            jax.ShapeDtypeStruct((3, seq, LANES), low),
-            jax.ShapeDtypeStruct((seq, LANES), low),
-            jax.ShapeDtypeStruct((LANES, seq), jnp.float32),
-            jax.ShapeDtypeStruct((tokens, n * LANES), low),
-        ],
+    given = spread is not None
+    operands = [spread] if given else [qkv, cosines, sines]
+    out_shape = [
+        jax.ShapeDtypeStruct((3, seq, LANES), low),
+        jax.ShapeDtypeStruct((seq, LANES), low),
+        jax.ShapeDtypeStruct((LANES, seq), jnp.float32),
+        jax.ShapeDtypeStruct((tokens, n * LANES), low),
+    ][given:]
+    exchange = [
+        pltpu.VMEM((n - 1, 3, tokens, LANES), low),
+        pltpu.SemaphoreType.DMA((n - 1,)),
+        pltpu.SemaphoreType.DMA((n,)),
+    ]
+    found = pl.pallas_call(
+        functools.partial(attend_kernel, heads, n, bq, bk, given),
+        in_specs=[vmem] * (2 + len(operands)),
+        out_specs=[vmem] * len(out_shape),
+        out_shape=out_shape,
         scratch_shapes=[
             pltpu.VMEM((heads, seq, LANES), low),
             pltpu.VMEM((heads, bq, seq), jnp.float32),
-            pltpu.VMEM((n - 1, 3, tokens, LANES), low),
-            pltpu.SemaphoreType.DMA((n - 1,)),
-            pltpu.SemaphoreType.DMA((n,)),
             pltpu.SemaphoreType.DMA((seq // bq,)),
             pltpu.SemaphoreType.DMA((n, tokens // bq)),
-        ],
+        ]
+        + ([] if given else exchange),
         compiler_params=pltpu.CompilerParams(
             collective_id=number, has_side_effects=True, vmem_limit_bytes=58 * 2**20
         ),
         cost_estimate=pl.CostEstimate(flops=10**10, bytes_accessed=2 * 10**8, transcendentals=0),
-    )(block_all.reshape(seq, 1), block_all.reshape(1, seq), qkv, cosines, sines)
+    )(block_all.reshape(seq, 1), block_all.reshape(1, seq), *operands)
+    return [spread] + list(found) if given else found
 
 
 def attend_back_kernel(
-    heads, n, bq, bk, layer, bid_q, bid_k, d_mix, spread, mixed, lse_ref, cosines, sines, carry, *refs
+    heads, n, bq, bk, layer, bid_q, bid_k, grads, spread, mixed, lse_ref, cosines, sines, carry, *refs
 ):
-    d_qkv, carried, grads, kone, dk_acc, dv_acc, leaving, g_sent, g_got, back_sent, back_got, carry_sent, carry_got = refs
+    d_qkv, carried, kone, dk_acc, dv_acc, leaving, back_sent, back_got, carry_sent, carry_got = refs
     section = lax.axis_index("section")
     me = lax.axis_index("row")
-    tokens = d_mix.shape[0]
-    seq = n * tokens
+    seq = grads.shape[0]
+    tokens = seq // n
     per_row = tokens // bq
     blocks = n * per_row
     low = jnp.bfloat16
     zero = jnp.zeros((), low)
-    here = pl.ds(pl.multiple_of(me * tokens, tokens), tokens)
     barrier = pltpu.get_barrier_semaphore()
     pl.semaphore_signal(barrier, 1, device_id={"section": 1 - section}, device_id_type=pl.DeviceIdType.MESH)
     for d in range(1, n):
@@ -249,18 +259,10 @@
     pl.semaphore_wait(barrier, n)
     carry_copy = remote(carry, carried, carry_sent, carry_got, "section", layer)
 
-    def give(d):
-        to = lax.rem(me + d, n)
-        return remote(d_mix.at[:, columns(to)], grads.at[here], g_sent.at[d - 1], g_got.at[me], "row", to)
-
-    for d in range(1, n):
-        give(d).start()
-
     @pl.when(section != layer)
     def _():
         carry_copy.start()
 
-    grads[here, :] = d_mix[:, columns(me)]
     for h in range(heads):
         kone[h] = jnp.where(lanes_of(seq, h), spread[1], zero)
     dk_acc[...] = jnp.zeros_like(dk_acc)
@@ -335,11 +337,6 @@
         send(2, i, dv_acc[rows, :].astype(low))
 
     for row in range(n - 1, -1, -1):
-        @pl.when(row != me)
-        def _(row=row):
-            there = pl.ds(row * tokens, tokens)
-            remote(d_mix.at[:, columns(0)], grads.at[there], g_sent.at[0], g_got.at[row], "row", me).wait_recv()
-
         def run(step, carry, row=row):
             i = row * per_row + per_row - 1 - step
             send(0, i, block(i))
@@ -352,9 +349,6 @@
 
         lax.fori_loop(0, per_row, run, 0)
     keys_done(0)
-
-    for d in range(1, n):
-        give(d).wait_send()
 
     def settle(i, carry):
         @pl.when(i // per_row != me)
@@ -385,10 +379,10 @@
         carry_copy.wait_recv()
 
 
-def attend_back(number, d_mix, spread, mixed, lse, block_all, cosines, sines, heads, n, layer, carry, bq=512, bk=512):
-    tokens = d_mix.shape[0]
+def attend_back(number, grads, spread, mixed, lse, block_all, cosines, sines, heads, n, layer, carry, bq=512, bk=512):
+    seq = grads.shape[0]
+    tokens = seq // n
     bq, bk = min(bq, tokens), min(bk, tokens)
-    seq = n * tokens
     vmem = pl.BlockSpec(memory_space=pltpu.VMEM)
     low = jnp.bfloat16
     return pl.pallas_call(
@@ -397,13 +391,10 @@
         out_specs=[vmem, pl.BlockSpec(memory_space=pl.ANY)],
         out_shape=[jax.ShapeDtypeStruct((tokens, 3 * n * LANES), low), jax.ShapeDtypeStruct(carry.shape, carry.dtype)],
         scratch_shapes=[
-            pltpu.VMEM((seq, LANES), low),
             pltpu.VMEM((heads, seq, LANES), low),
             pltpu.VMEM((seq, LANES), jnp.float32),
             pltpu.VMEM((seq, LANES), jnp.float32),
             pltpu.VMEM((3, seq, LANES), low),
-            pltpu.SemaphoreType.DMA((n - 1,)),
-            pltpu.SemaphoreType.DMA((n,)),
             pltpu.SemaphoreType.DMA((3, seq // bq)),
             pltpu.SemaphoreType.DMA((3, n, tokens // bq)),
             pltpu.SemaphoreType.DMA,
@@ -413,7 +404,7 @@
             collective_id=number, has_side_effects=True, vmem_limit_bytes=58 * 2**20
         ),
         cost_estimate=pl.CostEstimate(flops=10**10, bytes_accessed=3 * 10**8, transcendentals=0),
-    )(block_all.reshape(1, seq), block_all.reshape(seq, 1), d_mix, spread, mixed, lse, cosines, sines, carry)
+    )(block_all.reshape(1, seq), block_all.reshape(seq, 1), grads, spread, mixed, lse, cosines, sines, carry)
 
 
 def norm_parts(values):
@@ -461,10 +452,16 @@
     return given.astype(jnp.bfloat16)
 
 
-def relay_kernel(middle, n_ins, n_outs, layers, n_after, polish, n, chunks, lag, spread, partial, *refs):
+def relay_kernel(
+    middle, n_ins, n_outs, layers, n_after, polish, parts, n_row, n, chunks, lag, spread, partial, *refs
+):
     ins, carry, refs = refs[:n_ins], refs[n_ins : n_ins + len(layers)], refs[n_ins + len(layers) + n_after :]
     whole, outs, refs = refs[0], refs[1 : 1 + n_outs], refs[1 + n_outs :]
     carried, refs = refs[: len(layers)], refs[len(layers) :]
+    if parts:
+        ins, (weight, bias, cosines, sines) = ins[:-4], ins[-4:]
+        outs, landed = outs[:-1], outs[-1]
+        *refs, projected, leaving, part_sent, part_got = refs
     if polish:
         ins, (gain, shift) = ins[:-2], ins[-2:]
         outs, polished = outs[:-1], outs[-1]
@@ -486,6 +483,10 @@
         pl.semaphore_wait(barrier, 2 * n - 1)
     else:
         greet(section=1 - section)
+        me = lax.axis_index("row")
+        row_peers = n_row - 1 if parts else 0
+        for d in range(1, row_peers + 1):
+            greet(row=lax.rem(me + d, n_row))
 
         @pl.when(i > 0)
         def _():
@@ -497,11 +498,11 @@
 
         @pl.when(first | last)
         def _():
-            pl.semaphore_wait(barrier, 2)
+            pl.semaphore_wait(barrier, 2 + row_peers)
 
         @pl.when((i > 0) & (i < n - 1))
         def _():
-            pl.semaphore_wait(barrier, 3)
+            pl.semaphore_wait(barrier, 3 + row_peers)
 
     def carry_copy(k):
         return remote(carry[k], carried[k], carry_sent.at[k], carry_got.at[k], "section", layers[k])
@@ -544,6 +545,46 @@
             mean, inverse = norm_parts(values)
             polished[c, o] = ((values - mean) * inverse * gain[...] + shift[...]).astype(jnp.bfloat16)
 
+    rows = whole.shape[-2]
+    per = max(1, min(chunks, LANES // (n * rows)))
+    many = per * n * rows
+    tokens = chunks * n * rows
+
+    def part_rows(source, b):
+        return pl.ds(pl.multiple_of(source * tokens + b * many, many), many)
+
+    def part_copy(b, d):
+        to = lax.rem(me + d, n_row)
+        return remote(
+            leaving.at[d - 1, :, part_rows(0, b)],
+            landed.at[:, part_rows(me, b)],
+            part_sent.at[d - 1, b],
+            part_got.at[me, b],
+            "row",
+            to,
+        )
+
+    def project(b):
+        values = (polished if polish else whole)[pl.ds(b * per, per)].reshape(many, whole.shape[-1])
+        projected[...] = jnp.dot(values, weight[...], preferred_element_type=jnp.float32) + bias[...]
+        here = part_rows(me, b)
+
+        def part(k, t):
+            found = projected[:, columns(k * n_row + t)]
+            if parts == 3 and k < 2:
+                found = spin(found, cosines[here, :], sines[here, :])
+            found = found.astype(jnp.bfloat16)
+            if parts == 3 and k == 0:
+                found = (found * jnp.asarray(HEAD_DIM**-0.5, jnp.bfloat16)).astype(jnp.bfloat16)
+            return found
+
+        for d in range(1, n_row):
+            for k in range(parts):
+                leaving[d - 1, k, part_rows(0, b), :] = part(k, lax.rem(me + d, n_row))
+            part_copy(b, d).start()
+        for k in range(parts):
+            landed[k, here, :] = part(k, me)
+
     def sums_copy(d):
         to = lax.rem(i + d, n)
         return pltpu.make_async_remote_copy(
@@ -685,6 +726,13 @@
             def _(c=c, o=o):
                 work(c, o)
 
+        if parts:
+            since = now - (n * (per - 1) + 2 * lag * (n - 1))
+
+            @pl.when((since >= 0) & (lax.rem(jnp.maximum(since, 0), n * per) == 0))
+            def _():
+                project(jnp.maximum(since, 0) // (n * per))
+
         return carry
 
     lax.fori_loop(0, n * (chunks - 1) + 2 * lag * (n - 1) + 1, step, 0)
@@ -762,6 +810,23 @@
                 def _(s=s, o=o):
                     sums_arrive(s, o).wait_recv()
 
+    if parts:
+        def settle_parts(b, carry):
+            for d in range(1, n_row):
+                part_copy(b, d).wait_send()
+                source = lax.rem(me + d, n_row)
+                remote(
+                    leaving.at[0, :, part_rows(0, b)],
+                    landed.at[:, part_rows(source, b)],
+                    part_sent.at[0, b],
+                    part_got.at[source, b],
+                    "row",
+                    source,
+                ).wait_recv()
+            return carry
+
+        lax.fori_loop(0, chunks // per, settle_parts, 0)
+
     for k, layer in enumerate(layers):
         @pl.when(section != layer)
         def _(k=k):
@@ -772,13 +837,15 @@
             carry_copy(k).wait_recv()
 
 
-def relay(middle, number, partial, ins, outs, n, spread=False, carry=(), behind=(), polish=(), lag=3, rows=RELAY_ROWS):
+def relay(middle, number, partial, ins, outs, n, spread=False, carry=(), behind=(), polish=(), project=(), n_row=1, lag=3, rows=RELAY_ROWS):
     tokens, features = partial.shape
     owned = tokens // n
     chunks = owned // rows
     blocks = lambda values: values.reshape(chunks, rows, features) if values.shape[0] == owned else values
-    ins = [blocks(values) for values in ins] + list(polish)
-    outs = list(outs) + ([(tokens, features)] if polish else []) + ([(2, n, 2, features // n)] if spread else [])
+    ins = [blocks(values) for values in ins] + list(polish) + list(project)
+    parts = project[0].shape[1] // (n_row * LANES) if project else 0
+    batches = chunks // max(1, min(chunks, LANES // (n * rows)))
+    outs = list(outs) + ([(tokens, features)] if polish else []) + ([(parts, n_row * tokens, LANES)] if parts else []) + ([(2, n, 2, features // n)] if spread else [])
     out_shapes = [
         jax.ShapeDtypeStruct(
             (2, chunks, n, rows, features // n) if spread else (chunks, n, rows, features), jnp.bfloat16
@@ -786,6 +853,8 @@
     ] + [
         jax.ShapeDtypeStruct((chunks, n, rows, features), jnp.bfloat16)
         if shape[0] == tokens
+        else jax.ShapeDtypeStruct(shape, jnp.bfloat16)
+        if shape[-1] == LANES
         else jax.ShapeDtypeStruct((chunks, rows, features) if shape[0] == owned else shape, jnp.float32)
         for shape in outs
     ]
@@ -793,7 +862,7 @@
     layers = tuple(layer for layer, _ in carry)
     carry = [values for _, values in carry]
     whole, *rest = pl.pallas_call(
-        functools.partial(relay_kernel, middle, len(ins), len(outs), layers, len(behind), bool(polish), n, chunks, lag, spread),
+        functools.partial(relay_kernel, middle, len(ins), len(outs), layers, len(behind), bool(polish), parts, n_row, n, chunks, lag, spread),
         in_specs=[vmem] * (1 + len(ins)) + [anywhere] * (len(carry) + len(behind)),
         out_specs=[vmem] * len(out_shapes) + [anywhere] * len(carry),
         out_shape=out_shapes + [jax.ShapeDtypeStruct(values.shape, values.dtype) for values in carry],
@@ -809,7 +878,17 @@
             pltpu.SemaphoreType.DMA((max(1, len(carry)),)),
             pltpu.SemaphoreType.DMA((n,)),
             pltpu.SemaphoreType.DMA((2, n)),
-        ],
+        ]
+        + (
+            [
+                pltpu.VMEM((tokens // batches, project[0].shape[1]), jnp.float32),
+                pltpu.VMEM((n_row - 1, parts, tokens, LANES), jnp.bfloat16),
+                pltpu.SemaphoreType.DMA((n_row - 1, batches)),
+                pltpu.SemaphoreType.DMA((n_row, batches)),
+            ]
+            if parts
+            else []
+        ),
         compiler_params=pltpu.CompilerParams(
             collective_id=number, has_side_effects=True, vmem_limit_bytes=56 * 2**20
         ),
@@ -1018,9 +1097,10 @@
     def expand(values):
         if whole_lanes:
             return values
-        values = values.reshape(tokens, -1, width // HEAD_DIM, HEAD_DIM)
+        rows = values.shape[0]
+        values = values.reshape(rows, -1, width // HEAD_DIM, HEAD_DIM)
         values = jnp.pad(jnp.repeat(values, copies, axis=2), ((0, 0), (0, 0), (0, 0), (0, LANES - HEAD_DIM)))
-        return values.reshape(tokens, -1)
+        return values.reshape(rows, -1)
 
     def contract(values):
         if whole_lanes:
@@ -1058,14 +1138,18 @@
     hidden_out = []
     waited = []
     for layer in range(2):
-        qkv = product(normed, qkv_w[layer]) + bias[layer]
-        if layer == 1:
+        if layer == 0:
+            qkv = expand(product(normed, qkv_w[0]) + bias[0])
+            spread, mixed, log_sums, attn_mix = attend(
+                8, ids, heads, rows_axis, tokens, qkv=qkv, cosines=cosines, sines=sines
+            )
+        else:
             here = section + jnp.where(hidden_out[0][0, 0] == hidden_out[0][0, 0], 0, 1)
             branch = lax.all_gather(
                 lax.dynamic_index_in_dim(cotangent, here, 0, keepdims=False), "col", axis=1, tiled=True
             )
             waited = [branch]
-        spread, mixed, log_sums, attn_mix = attend(8, expand(qkv), ids, cosines, sines, heads, rows_axis)
+            spread, mixed, log_sums, attn_mix = attend(9, ids, heads, rows_axis, tokens, spread=spread)
         attn_mix = contract(attn_mix)
         normed_two, after = relay(
             after_attention,
@@ -1082,7 +1166,7 @@
         kept.append((stream, normed, spread, mixed, log_sums, attn_mix, after, normed_two, gate_up, hidden))
         partial = product(hidden, down_w[layer].T)
         if layer == 0:
-            stream, normed = relay(
+            stream, normed, spread = relay(
                 after_hidden,
                 2,
                 partial.astype(jnp.bfloat16),
@@ -1090,6 +1174,8 @@
                 [],
                 cols_axis,
                 polish=(gains[1, :1], shifts[1, :1]),
+                project=(expand(qkv_w[1]), expand(bias[1:]), cosines, sines),
+                n_row=rows_axis,
             )
             hidden_out.append(my_features(stream))
         else:
@@ -1111,6 +1197,8 @@
         return weight_sums[layer][-1]
 
     arrived = [[None] * 4, [None] * 4]
+    no_table = jnp.zeros((8, LANES), jnp.float32)
+
     def together(*values):
         return lax.optimization_barrier(values)
 
@@ -1128,7 +1216,7 @@
             dot_first(normed_two, d_gate_up).astype(jnp.bfloat16),
         )
         down_sum, gate_up_sum = collect(layer, down_term), collect(layer, gate_up_term)
-        grad_attn, d_after, sums_two, *got = relay(
+        grad_attn, d_after, sums_two, spread_grad, *got = relay(
             behind_norm,
             3 + layer,
             partial,
@@ -1139,6 +1227,8 @@
             if layer == 1
             else [(0, hidden_out[0]), (1, hidden_out[1]), (1, input_out[1]), (1, weight_sums[1][2]), (1, weight_sums[1][3])],
             behind=[] if layer == 1 else [weight_sums[1][0]],
+            project=(expand(out_w[layer]), jnp.zeros((1, rows_axis * LANES), jnp.float32), no_table, no_table),
+            n_row=rows_axis,
         )
         if layer == 1:
             result = jnp.where(d_after[0, 0] == d_after[0, 0], result, 0)
@@ -1146,13 +1236,11 @@
         else:
             hidden_got[0], hidden_got[1], input_got[1], arrived[1][2], arrived[1][3] = got
         small_sums += [sums_two]
-        d_mix, out_term = together(
-            product(grad_attn, out_w[layer]).astype(jnp.bfloat16), dot_first(grad_attn, attn_mix).astype(jnp.bfloat16)
-        )
+        out_term = dot_first(grad_attn, attn_mix).astype(jnp.bfloat16)
         out_sum = collect(layer, out_term)
         d_qkv, arrived[layer][1] = attend_back(
-            9 + layer,
-            expand(d_mix),
+            10 + layer,
+            spread_grad[0],
             spread,
             mixed,
             log_sums,

time: 1720 us -> 1760 us (1.023)
  Pallas kernels: 1270 us -> 1300 us
  matrix products: 278 us -> 251 us
    pallas_call x7, Pallas kernels: 760 us -> 850 us  [relay(): pl.pallas_call(functools.partial(relay_kernel, middle, len(ins), len(outs...]
    pallas_call x2, Pallas kernels: 186 us -> 145 us  [attend(): pl.pallas_call(functools.partial(attend_kernel, heads, n, bq, bk, given),...]
    dot_general x12 -> x9, matrix products: 136 us -> 110 us  [product(): return jnp.dot(left, right, preferred_element_type=jnp.float32)]
    unnamed x101 -> x103, local copies, waits for them, and re-layouts: 35.8 us -> 37.1 us
  transfers between devices with their start and end apart: 16 -> 16, of which waited for: 2 -> 2; matrix products, arithmetic and copies ran while one was open for 15% -> 14% of each run, Pallas kernels for 61% -> 59%
where the time goes in v5:
time: 1760 us; the launch traced here: 1750 us
  Pallas kernels  1300 us (74%)
  matrix products  251 us (14%)
  local copies, waits for them, and re-layouts  80.7 us (5%)
  waiting for transfers between devices  44.7 us (3%)
  other arithmetic  35.1 us (2%)
    pallas_call x7, Pallas kernels, relay(): pl.pallas_call(functools.partial(relay_kernel, middle, len(ins), len(outs...  850 us
    pallas_call x2, Pallas kernels, attend_back(): pl.pallas_call(functools.partial(attend_back_kernel, heads, n, bq, bk, la...  226 us
    pallas_call x2, Pallas kernels, attend(): pl.pallas_call(functools.partial(attend_kernel, heads, n, bq, bk, given),...  145 us
    dot_general x9, matrix products, product(): return jnp.dot(left, right, preferred_element_type=jnp.float32)  110 us
    dot_general x8, matrix products, dot_first(): lax.dot_general(a, b, (((0,), (0,)), ((), ())), preferred_element_type=jn...  82.1 us
    pallas_call x1, Pallas kernels, gathered(): pl.pallas_call(functools.partial(gather_kernel, n, chunks, lag), in_specs...  81.9 us
    dot_general x4, matrix products, dot_last(): lax.dot_general(a, b, (((1,), (1,)), ((), ())), preferred_element_type=jn...  58.8 us
    unnamed x103, local copies, waits for them, and re-layouts  37.1 us
  transfers between devices with their start and end apart: 16, of which 2 were waited for; matrix products, arithmetic and copies ran while one was open for 14% of the time, Pallas kernels for 59%

profile of v5, /device:TPU:0, one launch (start us, length us, event | category | flops | bytes accessed | tf_op | source)
XLA Modules:
  0.0 1749.4 jit_solution(594042434948511699)
XLA Ops:
  19.2 81.9 %shard_map.169 = (bf16[1024,2048]{1,0:T(8,128)(2,1)S(1)}, f32[2,4,8,512]{3,2,1,0:T(8,128)S(1)}, bf16[1024,2048]{1,0:T(8,128)(2,1)S(1)}, f32[4096,128]{1,0:T(8,128)S(1)}, f32[4096,128]{1,0:T(8,128)S(1)}) custom-call(bf16[1024,512]{1,0:T(8,128)(2,1)S(1)} %dynamic-slice_bitcast_fusion.2.own, f32[8,512]{1,0:T(8,128)S(1)} %pad_maximum_fusion.8.small, ...), custom_call_target="tpu_custom_call" | custom-call | bytes 250000000 | tf_op jit(solution)/shard_map/pallas_call | solution.py:1036
  114.1 11.9 fusion.18.refs_0_
  126.0 87.5 %shard_map.170 = (bf16[3,4096,128]{2,1,0:T(8,128)(2,1)}, bf16[4096,128]{1,0:T(8,128)(2,1)}, f32[128,4096]{1,0:T(8,128)}, bf16[1024,512]{1,0:T(8,128)(2,1)}) custom-call(s32[4096,1]{1,0:T(8,128)} %copy.34.bid_q.bid_k, s32[1,4096]{1,0:T(1,128)} %constant_dynamic-slice_fusion.4.bid_k.bid_q, f32[1024,1536]{1,0:T(8,128)} %fusion.18.refs_0_, ...), custom_call_target="tpu_custom_call" | custom-call | flops 10000000000 | bytes 200000000 | tf_op jit(solution)/shard_map/pallas_call | solution.py:223
  219.8 103.4 %shard_map.171 = (bf16[16,4,16,2048]{3,2,1,0:T(8,128)(2,1)}, f32[16,16,2048]{2,1,0:T(8,128)}) custom-call(bf16[16,4,16,2048]{3,2,1,0:T(8,128)(2,1)} %bitcast.169, bf16[16,16,2048]{2,1,0:T(8,128)(2,1)} %dynamic-slice_bitcast_fusion.1.refs_0_.refs_1_, f32[1,2048]{1,0:T(1,128)} %get-tuple-element.161.refs_1_.refs_2_, f32[1,2048]{1,0:T(1,128)} %get-tuple-element.160.refs_2_), custom_call_target="tpu_custom_call" | custom-call | bytes 350000000 | tf_op jit(solution)/shard_map/pallas_call | solution.py:864
  329.0 17.4 fusion.6
  364.4 164.6 %shard_map.172 = (bf16[16,4,16,2048]{3,2,1,0:T(8,128)(2,1)}, bf16[16,4,16,2048]{3,2,1,0:T(8,128)(2,1)}, bf16[3,4096,128]{2,1,0:T(8,128)(2,1)}) custom-call(bf16[16,4,16,2048]{3,2,1,0:T(8,128)(2,1)} %bitcast.175, f32[16,16,2048]{2,1,0:T(8,128)} %get-tuple-element.72.refs_0_.refs_1_, f32[1,2048]{1,0:T(1,128)} %get-tuple-element.159.refs_1_.refs_2_, ...), custom_call_target="tpu_custom_call" | custom-call | bytes 350000000 | tf_op jit(solution)/shard_map/pallas_call | solution.py:864
  534.4 57.4 %shard_map.173 = (bf16[4096,128]{1,0:T(8,128)(2,1)}, f32[128,4096]{1,0:T(8,128)}, bf16[1024,512]{1,0:T(8,128)(2,1)}) custom-call(s32[4096,1]{1,0:T(8,128)} %copy.34.bid_q.bid_k, s32[1,4096]{1,0:T(1,128)} %constant_dynamic-slice_fusion.4.bid_k.bid_q, bf16[3,4096,128]{2,1,0:T(8,128)(2,1)} %get-tuple-element.74.refs_0_.spread), custom_call_target="tpu_custom_call" | custom-call | flops 10000000000 | bytes 200000000 | tf_op jit(solution)/shard_map/pallas_call | solution.py:223
  598.1 13.9 all-gather.19.cloned.1.call-done
  612.0 114.5 %shard_map.174 = (bf16[16,4,16,2048]{3,2,1,0:T(8,128)(2,1)}, f32[16,16,2048]{2,1,0:T(8,128)}) custom-call(bf16[16,4,16,2048]{3,2,1,0:T(8,128)(2,1)} %bitcast.173, bf16[16,16,2048]{2,1,0:T(8,128)(2,1)} %dynamic-slice_bitcast_fusion.refs_0_.refs_1_, f32[1,2048]{1,0:T(1,128)} %get-tuple-element.157.refs_1_.refs_2_, f32[1,2048]{1,0:T(1,128)} %get-tuple-element.156.refs_2_, ...), custom_call_target="tpu_custom_call" | custom-call | bytes 350000000 | tf_op jit(solution)/shard_map/pallas_call | solution.py:864
  726.5 18.8 %fusion.2 = f32[1024,2816]{1,0:T(8,128)} fusion(bf16[1024,2048]{1,0:T(8,128)(2,1)} %bitcast.204, bf16[4096,2816]{1,0:T(8,128)(2,1)} %all-gather.13.cloned.1.call-done), kind=kOutput, calls=%fused_computation.4 | convolution fusion | flops 11811160064 | bytes 27262976 | tf_op jit(solution)/shard_map/dot_general | solution.py:1068
  745.4 13.4 multiply_convert_fusion.4
  758.8 18.7 %convolution_convert_fusion.1 = bf16[2048,2816]{1,0:T(8,128)(2,1)} fusion(bf16[1024,2048]{1,0:T(8,128)(2,1)} %bitcast.205, bf16[1024,1408]{1,0:T(8,128)(2,1)} %get-tuple-element.151, bf16[1024,1408]{1,0:T(8,128)(2,1)} %get-tuple-element.150), kind=kOutput, calls=%fused_computation.1 | convolution fusion | flops 11828461568 | bytes 21495808 | tf_op jit(solution)/shard_map/dot_general | solution.py:27
  777.5 18.1 %fusion.25 = bf16[1024,2048]{1,0:T(8,128)(2,1)} fusion(bf16[4096,2816]{1,0:T(8,128)(2,1)} %all-gather.13.cloned.1.call-done, bf16[1024,1408]{1,0:T(8,128)(2,1)} %get-tuple-element.151, bf16[1024,1408]{1,0:T(8,128)(2,1)} %get-tuple-element.150), kind=kOutput, calls=%fused_computation.43 | convolution fusion | flops 11824791552 | bytes 21495808 | tf_op jit(solution)/shard_map/dot_general | solution.py:23
  813.0 121.2 %shard_map.175 = (bf16[16,4,16,2048]{3,2,1,0:T(8,128)(2,1)}, f32[16,16,2048]{2,1,0:T(8,128)}, f32[2,2048]{1,0:T(2,128)}, bf16[1,4096,128]{2,1,0:T(8,128)(2,1)}) custom-call(bf16[16,4,16,2048]{3,2,1,0:T(8,128)(2,1)} %bitcast.172, f32[16,16,2048]{2,1,0:T(8,128)} %bitcast_convert_fusion.refs_0_, f32[16,16,2048]{2,1,0:T(8,128)} %get-tuple-element.78.refs_1_, ...), custom_call_target="tpu_custom_call" | custom-call | bytes 350000000 | tf_op jit(solution)/shard_map/pallas_call | solution.py:864
  955.7 116.2 %shard_map.176 = (bf16[1024,1536]{1,0:T(8,128)(2,1)}, bf16[512,2816]{1,0:T(8,128)(2,1)}) custom-call(s32[1,4096]{1,0:T(1,128)} %constant_dynamic-slice_fusion.4.bid_k.bid_q, s32[4096,1]{1,0:T(8,128)} %copy.34.bid_q.bid_k, bf16[4096,128]{1,0:T(8,128)(2,1)} %bitcast.207, bf16[3,4096,128]{2,1,0:T(8,128)(2,1)} %get-tuple-element.74.refs_0_.spread, ...), custom_call_target="tpu_custom_call" | custom-call | flops 10000000000 | bytes 300000000 | tf_op jit(solution)/shard_map/pallas_call | solution.py:388
  1094.3 108.4 %shard_map.177 = (bf16[16,4,16,2048]{3,2,1,0:T(8,128)(2,1)}, f32[16,16,2048]{2,1,0:T(8,128)}, f32[2,2048]{1,0:T(2,128)}) custom-call(bf16[16,4,16,2048]{3,2,1,0:T(8,128)(2,1)} %bitcast.168, f32[16,16,2048]{2,1,0:T(8,128)} %get-tuple-element.86.refs_0_, bf16[16,16,2048]{2,1,0:T(8,128)(2,1)} %dynamic-slice_bitcast_fusion.refs_0_.refs_1_, ...), custom_call_target="tpu_custom_call" | custom-call | bytes 350000000 | tf_op jit(solution)/shard_map/pallas_call | solution.py:864
  1213.7 14.0 multiply_convert_fusion.1
  1230.2 14.6 convolution_convert_fusion
  1244.8 18.2 %fusion.22 = bf16[1024,2048]{1,0:T(8,128)(2,1)} fusion(bf16[4096,2816]{1,0:T(8,128)(2,1)} %all-gather.13.cloned.1.call-done, bf16[1024,1408]{1,0:T(8,128)(2,1)} %copy-done.42, bf16[1024,1408]{1,0:T(8,128)(2,1)} %copy-done.41), kind=kOutput, calls=%fused_computation.42 | convolution fusion | flops 11824791552 | bytes 21495808 | tf_op jit(solution)/shard_map/dot_general | solution.py:23
  1267.6 130.6 %shard_map.178 = (bf16[16,4,16,2048]{3,2,1,0:T(8,128)(2,1)}, f32[16,16,2048]{2,1,0:T(8,128)}, f32[2,2048]{1,0:T(2,128)}, bf16[1,4096,128]{2,1,0:T(8,128)(2,1)}, ...) custom-call(bf16[16,4,16,2048]{3,2,1,0:T(8,128)(2,1)} %bitcast.174, ...), custom_call_target="tpu_custom_call" | custom-call | bytes 350000000 | tf_op jit(solution)/shard_map/pallas_call | solution.py:864
  1414.5 109.9 %shard_map.179 = (bf16[1024,1536]{1,0:T(8,128)(2,1)}, bf16[512,2816]{1,0:T(8,128)(2,1)}) custom-call(s32[1,4096]{1,0:T(1,128)} %constant_dynamic-slice_fusion.4.bid_k.bid_q, s32[4096,1]{1,0:T(8,128)} %copy.34.bid_q.bid_k, bf16[4096,128]{1,0:T(8,128)(2,1)} %bitcast.206, bf16[3,4096,128]{2,1,0:T(8,128)(2,1)} %get-tuple-element.96.spread, ...), custom_call_target="tpu_custom_call" | custom-call | flops 10000000000 | bytes 300000000 | tf_op jit(solution)/shard_map/pallas_call | solution.py:388
  1526.9 11.3 fusion.29
  1580.4 107.1 %shard_map.180 = (bf16[2,16,4,16,512]{4,3,2,1,0:T(8,128)(2,1)}, f32[16,16,2048]{2,1,0:T(8,128)}, f32[2,2048]{1,0:T(2,128)}, f32[2,4,2,512]{3,2,1,0:T(2,128)}, bf...) custom-call(bf16[16,4,16,2048]{3,2,1,0:T(8,128)(2,1)} %bitcast.171, ...), custom_call_target="tpu_custom_call" | custom-call | bytes 350000000 | tf_op jit(solution)/shard_map/pallas_call | solution.py:864
  1705.2 27.8 %collective-permute-done = bf16[512,1536]{1,0:T(8,128)(2,1)S(1)} collective-permute-done((bf16[512,1536]{1,0:T(8,128)(2,1)}, bf16[512,1536]{1,0:T(8,128)(2,1)S(1)}, u32[]{:S(2)}, u32[]{:S(2)}) %collective-permute-start) | collective-permute-done | bytes 1572896 | tf_op jit(solution)/shard_map/ppermute | solution.py:1282
  (215 shorter events, 231.8 us)
Async XLA Ops:
  7.2 106.9 %all-gather.11.cloned.1.call-start = ((), (), s32[]{:S(2)}) async-start(), calls=%async_computation.10 | async-start | bytes 14155776 | tf_op jit(solution)/shard_map/all_gather | solution.py:1113
  12.6 200.9 %all-gather.15.cloned.1.call-start = ((), (), s32[]{:S(2)}) async-start(), calls=%async_computation.21 | async-start | bytes 4718592 | tf_op jit(solution)/shard_map/all_gather | solution.py:1113
  13.3 315.7 %all-gather.13.cloned.1.call-start = ((), (), s32[]{:S(2)}) async-start(), calls=%async_computation.11 | async-start | bytes 25952256 | tf_op jit(solution)/shard_map/all_gather | solution.py:1113
  17.3 336.2 %all-gather.17.cloned.1.call-start = ((), (), s32[]{:S(2)}) async-start(), calls=%async_computation.22 | async-start | bytes 12976128 | tf_op jit(solution)/shard_map/all_gather | solution.py:1113
  17.8 594.1 %all-gather.19.cloned.1.call-start = ((), (), s32[]{:S(2)}) async-start(), calls=%async_computation.23 | async-start | bytes 5242880 | tf_op jit(solution)/shard_map/all_gather | solution.py:1148
  364.4 166.5 %copy-start.25 = (bf16[2,1024,512]{2,1,0:T(8,128)(2,1)S(1)}, bf16[2,1024,512]{2,1,0:T(8,128)(2,1)}, u32[]{:S(2)}) copy-start(bf16[2,1024,512]{2,1,0:T(8,128)(2,1)} %param.11) | copy-start | bytes 6291460
  532.0 423.7 %reduce-scatter.13.cloned.1.call-start = ((), (), s32[]{:S(2)}) async-start(), calls=%async_computation.12 | async-start | bytes 14417920 | tf_op jit(solution)/shard_map/reduce_scatter | solution.py:1196
  612.0 133.3 %slice-start = ((s8[11534336]{0:T(1024)(128)(4,1)}), s8[3145728]{0:T(1024)(128)(4,1)S(1)}, s32[]{:S(2)}) async-start(s8[11534336]{0:T(1024)(128)(4,1)} %bitcast.197), calls=%async_computation.25 | async-start | bytes 6291456
  804.5 289.8 %reduce-scatter.15.cloned.1.call-start = ((), (), s32[]{:S(2)}) async-start(), calls=%async_computation.13 | async-start | bytes 5242880 | tf_op jit(solution)/shard_map/reduce_scatter | solution.py:1235
  813.0 123.7 %copy-start.18 = (f32[16,16,2048]{2,1,0:T(8,128)S(1)}, f32[16,16,2048]{2,1,0:T(8,128)}, u32[]{:S(2)}) copy-start(f32[16,16,2048]{2,1,0:T(8,128)} %get-tuple-element.78.refs_1_) | copy-start | bytes 6291460
  813.0 123.7 %copy-start.38 = (bf16[1024,1408]{1,0:T(8,128)(2,1)S(1)}, bf16[1024,1408]{1,0:T(8,128)(2,1)}, u32[]{:S(2)}) copy-start(bf16[1024,1408]{1,0:T(8,128)(2,1)} %get-tuple-element.152) | copy-start | bytes 8650756
  947.7 319.9 %reduce-scatter.17.cloned.1.call-start = ((), (), s32[]{:S(2)}) async-start(), calls=%async_computation.14 | async-start | bytes 2621440 | tf_op jit(solution)/shard_map/reduce_scatter | solution.py:1196
  954.8 312.8 %reduce-scatter.21.cloned.1.call-start = ((), (), s32[]{:S(2)}) async-start(), calls=%async_computation.16 | async-start | bytes 7208960 | tf_op jit(solution)/shard_map/reduce_scatter | solution.py:1196
  955.6 312.0 %reduce-scatter.19.cloned.1.call-start = ((), (), s32[]{:S(2)}) async-start(), calls=%async_computation.15 | async-start | bytes 7864320 | tf_op jit(solution)/shard_map/reduce_scatter | solution.py:1196
  1094.3 320.2 %reduce-scatter.23.cloned.1.call-start = ((), (), s32[]{:S(2)}) async-start(), calls=%async_computation.17 | async-start | bytes 14417920 | tf_op jit(solution)/shard_map/reduce_scatter | solution.py:1196
  1263.0 289.8 %reduce-scatter.31.cloned.1.call-start = ((), (), s32[]{:S(2)}) async-start(), calls=%async_computation.24 | async-start | bytes 1310720
  1267.6 130.6 %copy-start.30 = (f32[2,2048]{1,0:T(2,128)S(1)}, f32[2,2048]{1,0:T(2,128)}, u32[]{:S(2)}) copy-start(f32[2,2048]{1,0:T(2,128)} %get-tuple-element.105) | copy-start | bytes 49156
  1267.6 130.6 %copy-start.31 = (f32[2,2048]{1,0:T(2,128)S(1)}, f32[2,2048]{1,0:T(2,128)}, u32[]{:S(2)}) copy-start(f32[2,2048]{1,0:T(2,128)} %get-tuple-element.106) | copy-start | bytes 49156
  1407.3 173.0 %reduce-scatter.25.cloned.1.call-start = ((), (), s32[]{:S(2)}) async-start(), calls=%async_computation.18 | async-start | bytes 7208960 | tf_op jit(solution)/shard_map/reduce_scatter | solution.py:1196
  1408.1 172.3 %reduce-scatter.27.cloned.1.call-start = ((), (), s32[]{:S(2)}) async-start(), calls=%async_computation.19 | async-start | bytes 2621440 | tf_op jit(solution)/shard_map/reduce_scatter | solution.py:1196
  1414.4 280.2 %reduce-scatter.29.cloned.1.call-start = ((), (), s32[]{:S(2)}) async-start(), calls=%async_computation.20 | async-start | bytes 7864320 | tf_op jit(solution)/shard_map/reduce_scatter | solution.py:1196
  1580.4 116.5 %copy-start.17 = (bf16[512,512]{1,0:T(8,128)(2,1)S(1)}, bf16[512,512]{1,0:T(8,128)(2,1)}, u32[]{:S(2)}) copy-start(bf16[512,512]{1,0:T(8,128)(2,1)} %reduce-scatter.27.cloned.1.call-done.refs_4_) | copy-start | bytes 1572868
  1580.4 116.5 %copy-start.20 = (bf16[512,512]{1,0:T(8,128)(2,1)S(1)}, bf16[512,512]{1,0:T(8,128)(2,1)}, u32[]{:S(2)}) copy-start(bf16[512,512]{1,0:T(8,128)(2,1)} %reduce-scatter.17.cloned.1.call-done.refs_10_) | copy-start | bytes 1572868
  1694.6 38.4 %collective-permute-start = (bf16[512,1536]{1,0:T(8,128)(2,1)}, bf16[512,1536]{1,0:T(8,128)(2,1)S(1)}, u32[]{:S(2)}, u32[]{:S(2)}) collective-permute-start(bf16[512,1536]{1,0:T(8,128)(2,1)} %reduce-scatter.29.cloned.1.call-done), channel_id=1, source_target_pairs={{16,0},{17,1},{18,2},{19,3},{20,4},{21,5},{22,6},{23,7},{24,8},{25... | collective-permute-start | bytes 4718600 | tf_op jit(solution)/shard_map/ppermute | solution.py:1282
  (38 other events, 641.2 us)
Sparse Core Ops, SparseCore 0:
  12.7 75.4 all-gather.10
  90.0 36.7 all-gather.14
  129.3 145.5 all-gather.12
  276.6 70.3 all-gather.16
  532.1 79.8 all-gather.18
  804.6 97.6 reduce-scatter.12
  947.8 77.1 reduce-scatter.14
  1027.7 42.4 reduce-scatter.16
  1073.4 55.5 reduce-scatter.20
  1131.5 58.3 reduce-scatter.18
  1263.2 106.0 reduce-scatter.22
  1407.4 26.4 reduce-scatter.30
  1436.6 75.0 reduce-scatter.24
  1514.6 32.3 reduce-scatter.26
  1549.6 59.3 reduce-scatter.28

commit v6 on v5

--- a/solution.py
+++ b/solution.py
@@ -63,7 +63,7 @@
     return pl.ds(pl.multiple_of(which * size, size), size)
 
 
-def attend_kernel(heads, n, bq, bk, given, bid_q, bid_k, *refs):
+def attend_kernel(heads, n, bq, given, bid_q, bid_k, *refs):
     me = lax.axis_index("row")
     if given:
         spread, mixed, lse_ref, mix, vone, scores, mix_sent, mix_got = refs
@@ -115,12 +115,12 @@
         rows = pl.ds(pl.multiple_of(i * bq, bq), bq)
         q = spread[0, rows, :]
         bid = bid_q[rows, :]
-        free = i * (bq // bk)
-        last = jnp.minimum(((i + 1) * bq + REACH + bk - 1) // bk, seq // bk)
+        begin = i * bq
+        ahead = jnp.where(begin + bq < seq, 1, 0)
         qs = [jnp.where(lanes_of(bq, h), q, jnp.zeros((), low)) for h in range(heads)]
 
-        def score(t, tops, hide):
-            span = pl.ds(pl.multiple_of(t * bk, bk), bk)
+        def score(start, size, tops, hide):
+            span = pl.ds(pl.multiple_of(start, REACH), size)
             keys = spread[1, span, :]
             if hide:
                 visible = bid_k[:, span] <= bid
@@ -131,18 +131,20 @@
                     s = jnp.where(visible, s, -1e30)
                 scores[h, :, span] = s
                 top = tops[h]
-                for c in range(bk // LANES):
+                for c in range(size // LANES):
                     top = jnp.maximum(top, s[:, c * LANES : (c + 1) * LANES])
                 found.append(top)
             return tuple(found)
 
         tops = tuple(jnp.full((bq, LANES), -1e30, jnp.float32) for _ in range(heads))
-        tops = lax.fori_loop(0, free, lambda t, c: score(t, c, False), tops)
-        tops = lax.fori_loop(free, last, lambda t, c: score(t, c, True), tops)
+        tops = lax.fori_loop(0, i // 2, lambda t, c: score(2 * t * bq, 2 * bq, c, False), tops)
+        tops = lax.fori_loop(i // 2 * 2, i, lambda t, c: score(t * bq, bq, c, False), tops)
+        tops = score(begin, bq, tops, True)
+        tops = lax.fori_loop(0, ahead, lambda t, c: score(begin + bq, REACH, c, True), tops)
         tops = [jnp.max(top, axis=1, keepdims=True) for top in tops]
 
-        def gather(t, sums):
-            span = pl.ds(pl.multiple_of(t * bk, bk), bk)
+        def gather(start, size, sums):
+            span = pl.ds(pl.multiple_of(start, REACH), size)
             found = []
             for h in range(heads):
                 p = jnp.exp(scores[h, :, span] - tops[h]).astype(low)
@@ -150,7 +152,9 @@
             return tuple(found)
 
         sums = tuple(jnp.zeros((bq, LANES), jnp.float32) for _ in range(heads))
-        sums = lax.fori_loop(0, last, gather, sums)
+        sums = lax.fori_loop(0, (i + 1) // 2, lambda t, c: gather(2 * t * bq, 2 * bq, c), sums)
+        sums = lax.fori_loop((i + 1) // 2 * 2, i + 1, lambda t, c: gather(t * bq, bq, c), sums)
+        sums = lax.fori_loop(0, ahead, lambda t, c: gather(begin + bq, REACH, c), sums)
         outcome = jnp.zeros((bq, LANES), jnp.float32)
         lse = jnp.zeros((bq, LANES), jnp.float32)
         for h in range(heads):
@@ -202,8 +206,8 @@
                 ).wait_recv()
 
 
-def attend(number, block_all, heads, n, tokens, qkv=None, cosines=None, sines=None, spread=None, bq=512, bk=512):
-    bq, bk = min(bq, tokens), min(bk, tokens)
+def attend(number, block_all, heads, n, tokens, qkv=None, cosines=None, sines=None, spread=None, bq=512):
+    bq = min(bq, tokens)
     seq = n * tokens
     vmem = pl.BlockSpec(memory_space=pltpu.VMEM)
     low = jnp.bfloat16
@@ -221,7 +225,7 @@
         pltpu.SemaphoreType.DMA((n,)),
     ]
     found = pl.pallas_call(
-        functools.partial(attend_kernel, heads, n, bq, bk, given),
+        functools.partial(attend_kernel, heads, n, bq, given),
         in_specs=[vmem] * (2 + len(operands)),
         out_specs=[vmem] * len(out_shape),
         out_shape=out_shape,
@@ -241,17 +245,18 @@
 
 
 def attend_back_kernel(
-    heads, n, bq, bk, layer, bid_q, bid_k, grads, spread, mixed, lse_ref, cosines, sines, carry, *refs
+    heads, n, bq, layer, bid_q, bid_k, d_mix, spread, mixed, lse_ref, cosines, sines, carry, *refs
 ):
-    d_qkv, carried, kone, dk_acc, dv_acc, leaving, back_sent, back_got, carry_sent, carry_got = refs
+    d_qkv, carried, grads, kone, dk_acc, dv_acc, leaving, g_sent, g_got, back_sent, back_got, carry_sent, carry_got = refs
     section = lax.axis_index("section")
     me = lax.axis_index("row")
-    seq = grads.shape[0]
-    tokens = seq // n
+    tokens = d_mix.shape[0]
+    seq = n * tokens
     per_row = tokens // bq
     blocks = n * per_row
     low = jnp.bfloat16
     zero = jnp.zeros((), low)
+    here = pl.ds(pl.multiple_of(me * tokens, tokens), tokens)
     barrier = pltpu.get_barrier_semaphore()
     pl.semaphore_signal(barrier, 1, device_id={"section": 1 - section}, device_id_type=pl.DeviceIdType.MESH)
     for d in range(1, n):
@@ -259,18 +264,26 @@
     pl.semaphore_wait(barrier, n)
     carry_copy = remote(carry, carried, carry_sent, carry_got, "section", layer)
 
+    def give(d):
+        to = lax.rem(me + d, n)
+        return remote(d_mix.at[:, columns(to)], grads.at[here], g_sent.at[d - 1], g_got.at[me], "row", to)
+
+    for d in range(1, n):
+        give(d).start()
+
     @pl.when(section != layer)
     def _():
         carry_copy.start()
 
+    grads[here, :] = d_mix[:, columns(me)]
     for h in range(heads):
-        kone[h] = jnp.where(lanes_of(seq, h), spread[1], zero)
+        kone[h] = jnp.where(lanes_of(seq, h), spread[1], zero).T
     dk_acc[...] = jnp.zeros_like(dk_acc)
     dv_acc[...] = jnp.zeros_like(dv_acc)
 
-    def tile(t, dq, hide, stuff):
+    def tile(start, size, dq, hide, stuff):
         qs, gs, lses, deltas, bid = stuff
-        span = pl.ds(pl.multiple_of(t * bk, bk), bk)
+        span = pl.ds(pl.multiple_of(start, REACH), size)
         keys, values = spread[1, span, :], spread[2, span, :]
         dv, dk = dv_acc[span, :], dk_acc[span, :]
         if hide:
@@ -284,7 +297,7 @@
             ds = (p * (dp - deltas[h])).astype(low)
             dv = dv + jnp.dot(p.astype(low), gs[h], preferred_element_type=jnp.float32)
             dk = dk + jnp.dot(ds, qs[h], preferred_element_type=jnp.float32)
-            dq = dq + dot_first(ds, kone[h, span, :])
+            dq = dq + jnp.dot(kone[h, :, span], ds, preferred_element_type=jnp.float32)
         dv_acc[span, :] = dv
         dk_acc[span, :] = dk
         return dq
@@ -299,12 +312,13 @@
         qs = [jnp.where(lanes_of(bq, h), q, zero) for h in range(heads)]
         gs = [jnp.where(lanes_of(bq, h), g, zero) for h in range(heads)]
         stuff = (qs, gs, lses, deltas, bid_q[:, rows])
-        free = i * (bq // bk)
-        last = jnp.minimum(((i + 1) * bq + REACH + bk - 1) // bk, seq // bk)
-        dq = jnp.zeros((bq, LANES), jnp.float32)
-        dq = lax.fori_loop(0, free, lambda t, c: tile(t, c, False, stuff), dq)
-        dq = lax.fori_loop(free, last, lambda t, c: tile(t, c, True, stuff), dq)
-        return spin(dq * (HEAD_DIM**-0.5), cosines[rows, :], -sines[rows, :]).astype(low)
+        begin = i * bq
+        ahead = jnp.where(begin + bq < seq, 1, 0)
+        dq = jnp.zeros((LANES, bq), jnp.float32)
+        dq = lax.fori_loop(0, i, lambda t, c: tile(t * bq, bq, c, False, stuff), dq)
+        dq = tile(begin, bq, dq, True, stuff)
+        dq = lax.fori_loop(0, ahead, lambda t, c: tile(begin + bq, REACH, c, True, stuff), dq)
+        return spin(dq.T * (HEAD_DIM**-0.5), cosines[rows, :], -sines[rows, :]).astype(low)
 
     def back_copy(k, i, device):
         half = lax.rem(i, per_row)
@@ -337,6 +351,11 @@
         send(2, i, dv_acc[rows, :].astype(low))
 
     for row in range(n - 1, -1, -1):
+        @pl.when(row != me)
+        def _(row=row):
+            there = pl.ds(row * tokens, tokens)
+            remote(d_mix.at[:, columns(0)], grads.at[there], g_sent.at[0], g_got.at[row], "row", me).wait_recv()
+
         def run(step, carry, row=row):
             i = row * per_row + per_row - 1 - step
             send(0, i, block(i))
@@ -349,6 +368,9 @@
 
         lax.fori_loop(0, per_row, run, 0)
     keys_done(0)
+
+    for d in range(1, n):
+        give(d).wait_send()
 
     def settle(i, carry):
         @pl.when(i // per_row != me)
@@ -379,22 +401,25 @@
         carry_copy.wait_recv()
 
 
-def attend_back(number, grads, spread, mixed, lse, block_all, cosines, sines, heads, n, layer, carry, bq=512, bk=512):
-    seq = grads.shape[0]
-    tokens = seq // n
-    bq, bk = min(bq, tokens), min(bk, tokens)
+def attend_back(number, d_mix, spread, mixed, lse, block_all, cosines, sines, heads, n, layer, carry, bq=512):
+    tokens = d_mix.shape[0]
+    bq = min(bq, tokens)
+    seq = n * tokens
     vmem = pl.BlockSpec(memory_space=pltpu.VMEM)
     low = jnp.bfloat16
     return pl.pallas_call(
-        functools.partial(attend_back_kernel, heads, n, bq, bk, layer),
+        functools.partial(attend_back_kernel, heads, n, bq, layer),
         in_specs=[vmem] * 8 + [pl.BlockSpec(memory_space=pl.ANY)],
         out_specs=[vmem, pl.BlockSpec(memory_space=pl.ANY)],
         out_shape=[jax.ShapeDtypeStruct((tokens, 3 * n * LANES), low), jax.ShapeDtypeStruct(carry.shape, carry.dtype)],
         scratch_shapes=[
-            pltpu.VMEM((heads, seq, LANES), low),
+            pltpu.VMEM((seq, LANES), low),
+            pltpu.VMEM((heads, LANES, seq), low),
             pltpu.VMEM((seq, LANES), jnp.float32),
             pltpu.VMEM((seq, LANES), jnp.float32),
             pltpu.VMEM((3, seq, LANES), low),
+            pltpu.SemaphoreType.DMA((n - 1,)),
+            pltpu.SemaphoreType.DMA((n,)),
             pltpu.SemaphoreType.DMA((3, seq // bq)),
             pltpu.SemaphoreType.DMA((3, n, tokens // bq)),
             pltpu.SemaphoreType.DMA,
@@ -404,7 +429,7 @@
             collective_id=number, has_side_effects=True, vmem_limit_bytes=58 * 2**20
         ),
         cost_estimate=pl.CostEstimate(flops=10**10, bytes_accessed=3 * 10**8, transcendentals=0),
-    )(block_all.reshape(1, seq), block_all.reshape(seq, 1), grads, spread, mixed, lse, cosines, sines, carry)
+    )(block_all.reshape(1, seq), block_all.reshape(seq, 1), d_mix, spread, mixed, lse, cosines, sines, carry)
 
 
 def norm_parts(values):
@@ -459,9 +484,11 @@
     whole, outs, refs = refs[0], refs[1 : 1 + n_outs], refs[1 + n_outs :]
     carried, refs = refs[: len(layers)], refs[len(layers) :]
     if parts:
-        ins, (weight, bias, cosines, sines) = ins[:-4], ins[-4:]
+        ins, (weights, bias, cosines, sines) = ins[:-4], ins[-4:]
         outs, landed = outs[:-1], outs[-1]
-        *refs, projected, leaving, part_sent, part_got = refs
+        *refs, leaving, part_sent, part_got, weight, weight_got = refs
+        weight_copy = pltpu.make_async_copy(weights.at[pl.ds(weight.shape[0], weight.shape[0])], weight, weight_got)
+        weight_copy.start()
     if polish:
         ins, (gain, shift) = ins[:-2], ins[-2:]
         outs, polished = outs[:-1], outs[-1]
@@ -548,6 +575,7 @@
     rows = whole.shape[-2]
     per = max(1, min(chunks, LANES // (n * rows)))
     many = per * n * rows
+    unit = max(1, n * per // n_row)
     tokens = chunks * n * rows
 
     def part_rows(source, b):
@@ -564,26 +592,30 @@
             to,
         )
 
-    def project(b):
+    def project(b, d):
         values = (polished if polish else whole)[pl.ds(b * per, per)].reshape(many, whole.shape[-1])
-        projected[...] = jnp.dot(values, weight[...], preferred_element_type=jnp.float32) + bias[...]
-        here = part_rows(me, b)
-
-        def part(k, t):
-            found = projected[:, columns(k * n_row + t)]
+        here, there = part_rows(me, b), part_rows(0, b)
+        t = lax.rem(me + d, n_row)
+        for k in range(parts):
+            column = columns(k * n_row + t)
+            found = jnp.dot(values, weight[:, column], preferred_element_type=jnp.float32) + bias[:, column]
             if parts == 3 and k < 2:
                 found = spin(found, cosines[here, :], sines[here, :])
             found = found.astype(jnp.bfloat16)
             if parts == 3 and k == 0:
                 found = (found * jnp.asarray(HEAD_DIM**-0.5, jnp.bfloat16)).astype(jnp.bfloat16)
-            return found
-
-        for d in range(1, n_row):
-            for k in range(parts):
-                leaving[d - 1, k, part_rows(0, b), :] = part(k, lax.rem(me + d, n_row))
+
+            @pl.when(d > 0)
+            def _(k=k, found=found):
+                leaving[d - 1, k, there, :] = found
+
+            @pl.when(d == 0)
+            def _(k=k, found=found):
+                landed[k, here, :] = found
+
+        @pl.when(d > 0)
+        def _():
             part_copy(b, d).start()
-        for k in range(parts):
-            landed[k, here, :] = part(k, me)
 
     def sums_copy(d):
         to = lax.rem(i + d, n)
@@ -728,14 +760,21 @@
 
         if parts:
             since = now - (n * (per - 1) + 2 * lag * (n - 1))
-
-            @pl.when((since >= 0) & (lax.rem(jnp.maximum(since, 0), n * per) == 0))
+            given = jnp.maximum(since, 0)
+            turn = lax.rem(given, n * per) // unit
+
+            @pl.when(since == 0)
             def _():
-                project(jnp.maximum(since, 0) // (n * per))
+                weight_copy.wait()
+
+            @pl.when((since >= 0) & (lax.rem(given, unit) == 0) & (turn < n_row) & (given < n * chunks))
+            def _():
+                project(given // (n * per), lax.rem(turn + 1, n_row))
 
         return carry
 
-    lax.fori_loop(0, n * (chunks - 1) + 2 * lag * (n - 1) + 1, step, 0)
+    steps = n * (chunks - 1) + 2 * lag * (n - 1) + 1
+    lax.fori_loop(0, steps + (unit * (n_row - 1) if parts else 0), step, 0)
 
     if spread:
         for d in range(1, n):
@@ -859,11 +898,14 @@
         for shape in outs
     ]
     vmem, anywhere = pl.BlockSpec(memory_space=pltpu.VMEM), pl.BlockSpec(memory_space=pl.ANY)
+    specs = [vmem] * (1 + len(ins))
+    if project:
+        specs[-4] = anywhere
     layers = tuple(layer for layer, _ in carry)
     carry = [values for _, values in carry]
     whole, *rest = pl.pallas_call(
         functools.partial(relay_kernel, middle, len(ins), len(outs), layers, len(behind), bool(polish), parts, n_row, n, chunks, lag, spread),
-        in_specs=[vmem] * (1 + len(ins)) + [anywhere] * (len(carry) + len(behind)),
+        in_specs=specs + [anywhere] * (len(carry) + len(behind)),
         out_specs=[vmem] * len(out_shapes) + [anywhere] * len(carry),
         out_shape=out_shapes + [jax.ShapeDtypeStruct(values.shape, values.dtype) for values in carry],
         scratch_shapes=[
@@ -881,10 +923,11 @@
         ]
         + (
             [
-                pltpu.VMEM((tokens // batches, project[0].shape[1]), jnp.float32),
                 pltpu.VMEM((n_row - 1, parts, tokens, LANES), jnp.bfloat16),
                 pltpu.SemaphoreType.DMA((n_row - 1, batches)),
                 pltpu.SemaphoreType.DMA((n_row, batches)),
+                pltpu.VMEM((features, project[0].shape[1]), jnp.bfloat16),
+                pltpu.SemaphoreType.DMA,
             ]
             if parts
             else []
@@ -1174,7 +1217,7 @@
                 [],
                 cols_axis,
                 polish=(gains[1, :1], shifts[1, :1]),
-                project=(expand(qkv_w[1]), expand(bias[1:]), cosines, sines),
+                project=(expand(qkv_w.reshape(2 * D, -1)), expand(bias[1:]), cosines, sines),
                 n_row=rows_axis,
             )
             hidden_out.append(my_features(stream))
@@ -1197,8 +1240,6 @@
         return weight_sums[layer][-1]
 
     arrived = [[None] * 4, [None] * 4]
-    no_table = jnp.zeros((8, LANES), jnp.float32)
-
     def together(*values):
         return lax.optimization_barrier(values)
 
@@ -1216,7 +1257,7 @@
             dot_first(normed_two, d_gate_up).astype(jnp.bfloat16),
         )
         down_sum, gate_up_sum = collect(layer, down_term), collect(layer, gate_up_term)
-        grad_attn, d_after, sums_two, spread_grad, *got = relay(
+        grad_attn, d_after, sums_two, *got = relay(
             behind_norm,
             3 + layer,
             partial,
@@ -1227,8 +1268,6 @@
             if layer == 1
             else [(0, hidden_out[0]), (1, hidden_out[1]), (1, input_out[1]), (1, weight_sums[1][2]), (1, weight_sums[1][3])],
             behind=[] if layer == 1 else [weight_sums[1][0]],
-            project=(expand(out_w[layer]), jnp.zeros((1, rows_axis * LANES), jnp.float32), no_table, no_table),
-            n_row=rows_axis,
         )
         if layer == 1:
             result = jnp.where(d_after[0, 0] == d_after[0, 0], result, 0)
@@ -1236,11 +1275,13 @@
         else:
             hidden_got[0], hidden_got[1], input_got[1], arrived[1][2], arrived[1][3] = got
         small_sums += [sums_two]
-        out_term = dot_first(grad_attn, attn_mix).astype(jnp.bfloat16)
+        d_mix, out_term = together(
+            product(grad_attn, out_w[layer]).astype(jnp.bfloat16), dot_first(grad_attn, attn_mix).astype(jnp.bfloat16)
+        )
         out_sum = collect(layer, out_term)
         d_qkv, arrived[layer][1] = attend_back(
             10 + layer,
-            spread_grad[0],
+            expand(d_mix),
             spread,
             mixed,
             log_sums,

time: 1760 us -> 1720 us (0.977)
  Pallas kernels: 1300 us -> 1260 us
    pallas_call x7, Pallas kernels: 850 us -> 808 us  [relay(): pl.pallas_call(functools.partial(relay_kernel, middle, len(ins), len(outs...]
    dot_general x9 -> x11, matrix products: 110 us -> 122 us  [product(): return jnp.dot(left, right, preferred_element_type=jnp.float32)]
  transfers between devices with their start and end apart: 16 -> 16, of which waited for: 2 -> 2; matrix products, arithmetic and copies ran while one was open for 14% -> 14% of each run, Pallas kernels for 59% -> 58%
where the time goes in v6:
time: 1720 us; the launch traced here: 1710 us
  Pallas kernels  1260 us (73%)
  matrix products  264 us (15%)
  local copies, waits for them, and re-layouts  69.8 us (4%)
  waiting for transfers between devices  49.2 us (3%)
  other arithmetic  35 us (2%)
    pallas_call x7, Pallas kernels, relay(): pl.pallas_call(functools.partial(relay_kernel, middle, len(ins), len(outs...  808 us
    pallas_call x2, Pallas kernels, attend_back(): pl.pallas_call(functools.partial(attend_back_kernel, heads, n, bq, layer)...  231 us
    pallas_call x2, Pallas kernels, attend(): pl.pallas_call(functools.partial(attend_kernel, heads, n, bq, given), in_...  139 us
    dot_general x11, matrix products, product(): return jnp.dot(left, right, preferred_element_type=jnp.float32)  122 us
    dot_general x8, matrix products, dot_first(): lax.dot_general(a, b, (((0,), (0,)), ((), ())), preferred_element_type=jn...  82.1 us
    pallas_call x1, Pallas kernels, gathered(): pl.pallas_call(functools.partial(gather_kernel, n, chunks, lag), in_specs...  82 us
    dot_general x4, matrix products, dot_last(): lax.dot_general(a, b, (((1,), (1,)), ((), ())), preferred_element_type=jn...  59.6 us
    unnamed x103, local copies, waits for them, and re-layouts  36.5 us
  transfers between devices with their start and end apart: 16, of which 2 were waited for; matrix products, arithmetic and copies ran while one was open for 14% of the time, Pallas kernels for 58%

profile of v6, /device:TPU:0, one launch (start us, length us, event | category | flops | bytes accessed | tf_op | source)
XLA Modules:
  0.0 1713.0 jit_solution(14557081705841318575)
XLA Ops:
  20.8 82.0 %shard_map.169 = (bf16[1024,2048]{1,0:T(8,128)(2,1)S(1)}, f32[2,4,8,512]{3,2,1,0:T(8,128)S(1)}, bf16[1024,2048]{1,0:T(8,128)(2,1)S(1)}, f32[4096,128]{1,0:T(8,128)S(1)}, f32[4096,128]{1,0:T(8,128)S(1)}) custom-call(bf16[1024,512]{1,0:T(8,128)(2,1)S(1)} %dynamic-slice_bitcast_fusion.2.own, f32[8,512]{1,0:T(8,128)S(1)} %maximum_maximum_fusion.small, ...), custom_call_target="tpu_custom_call" | custom-call | bytes 250000000 | tf_op jit(solution)/shard_map/pallas_call | solution.py:1079
  113.6 11.7 fusion.20.refs_0_
  125.3 86.2 %shard_map.170 = (bf16[3,4096,128]{2,1,0:T(8,128)(2,1)}, bf16[4096,128]{1,0:T(8,128)(2,1)}, f32[128,4096]{1,0:T(8,128)}, bf16[1024,512]{1,0:T(8,128)(2,1)}) custom-call(s32[4096,1]{1,0:T(8,128)} %copy.34.bid_q.bid_k, s32[1,4096]{1,0:T(1,128)} %constant_dynamic-slice_fusion.4.bid_k.bid_q, f32[1024,1536]{1,0:T(8,128)} %fusion.20.refs_0_, ...), custom_call_target="tpu_custom_call" | custom-call | flops 10000000000 | bytes 200000000 | tf_op jit(solution)/shard_map/pallas_call | solution.py:227
  218.2 106.8 %shard_map.171 = (bf16[16,4,16,2048]{3,2,1,0:T(8,128)(2,1)}, f32[16,16,2048]{2,1,0:T(8,128)}) custom-call(bf16[16,4,16,2048]{3,2,1,0:T(8,128)(2,1)} %bitcast.178, bf16[16,16,2048]{2,1,0:T(8,128)(2,1)} %dynamic-slice_bitcast_fusion.1.refs_0_.refs_1_, f32[1,2048]{1,0:T(1,128)} %get-tuple-element.163.refs_1_.refs_2_, f32[1,2048]{1,0:T(1,128)} %get-tuple-element.162.refs_2_), custom_call_target="tpu_custom_call" | custom-call | bytes 350000000 | tf_op jit(solution)/shard_map/pallas_call | solution.py:906
  325.0 17.3 %fusion.6 = f32[1024,2816]{1,0:T(8,128)S(1)} fusion(bf16[1024,2048]{1,0:T(8,128)(2,1)} %bitcast.206, bf16[4096,2816]{1,0:T(8,128)(2,1)} %all-gather.13.cloned.1.call-done), kind=kOutput, calls=%fused_computation.8 | convolution fusion | flops 11811160064 | bytes 27262976 | tf_op jit(solution)/shard_map/dot_general | solution.py:1111
  360.3 157.3 %shard_map.172 = (bf16[16,4,16,2048]{3,2,1,0:T(8,128)(2,1)}, bf16[16,4,16,2048]{3,2,1,0:T(8,128)(2,1)}, bf16[3,4096,128]{2,1,0:T(8,128)(2,1)}) custom-call(bf16[16,4,16,2048]{3,2,1,0:T(8,128)(2,1)} %bitcast.182, f32[16,16,2048]{2,1,0:T(8,128)} %get-tuple-element.74.refs_0_.refs_1_, f32[1,2048]{1,0:T(1,128)} %get-tuple-element.161.refs_1_.refs_2_, ...), custom_call_target="tpu_custom_call" | custom-call | bytes 350000000 | tf_op jit(solution)/shard_map/pallas_call | solution.py:906
  522.9 53.3 %shard_map.173 = (bf16[4096,128]{1,0:T(8,128)(2,1)}, f32[128,4096]{1,0:T(8,128)}, bf16[1024,512]{1,0:T(8,128)(2,1)}) custom-call(s32[4096,1]{1,0:T(8,128)} %copy.34.bid_q.bid_k, s32[1,4096]{1,0:T(1,128)} %constant_dynamic-slice_fusion.4.bid_k.bid_q, bf16[3,4096,128]{2,1,0:T(8,128)(2,1)} %get-tuple-element.76.refs_0_.spread), custom_call_target="tpu_custom_call" | custom-call | flops 10000000000 | bytes 200000000 | tf_op jit(solution)/shard_map/pallas_call | solution.py:227
  582.5 18.8 %all-gather.19.cloned.1.call-done = bf16[1,1024,2048]{2,1,0:T(8,128)(2,1)} async-done(((bf16[1,1024,512]{2,1,0:T(8,128)(2,1)}), bf16[1,1024,2048]{2,1,0:T(8,128)(2,1)}) %all-gather.19.cloned.1.call-update) | async-done | bytes 4194320 | tf_op jit(solution)/shard_map/all_gather | solution.py:1191
  601.3 114.3 %shard_map.174 = (bf16[16,4,16,2048]{3,2,1,0:T(8,128)(2,1)}, f32[16,16,2048]{2,1,0:T(8,128)}) custom-call(bf16[16,4,16,2048]{3,2,1,0:T(8,128)(2,1)} %bitcast.181, bf16[16,16,2048]{2,1,0:T(8,128)(2,1)} %dynamic-slice_bitcast_fusion.refs_0_.refs_1_, f32[1,2048]{1,0:T(1,128)} %get-tuple-element.159.refs_1_.refs_2_, f32[1,2048]{1,0:T(1,128)} %get-tuple-element.158.refs_2_, ...), custom_call_target="tpu_custom_call" | custom-call | bytes 350000000 | tf_op jit(solution)/shard_map/pallas_call | solution.py:906
  715.6 18.8 %fusion.2 = f32[1024,2816]{1,0:T(8,128)} fusion(bf16[1024,2048]{1,0:T(8,128)(2,1)} %bitcast.213, bf16[4096,2816]{1,0:T(8,128)(2,1)} %all-gather.13.cloned.1.call-done), kind=kOutput, calls=%fused_computation.4 | convolution fusion | flops 11811160064 | bytes 27262976 | tf_op jit(solution)/shard_map/dot_general | solution.py:1111
  734.5 13.4 multiply_convert_fusion.4
  747.9 18.5 %convolution_convert_fusion.1 = bf16[2048,2816]{1,0:T(8,128)(2,1)} fusion(bf16[1024,2048]{1,0:T(8,128)(2,1)} %bitcast.214, bf16[1024,1408]{1,0:T(8,128)(2,1)} %get-tuple-element.155, bf16[1024,1408]{1,0:T(8,128)(2,1)} %get-tuple-element.154), kind=kOutput, calls=%fused_computation.1 | convolution fusion | flops 11828461568 | bytes 21495808 | tf_op jit(solution)/shard_map/dot_general | solution.py:27
  766.4 18.2 %fusion.27 = bf16[1024,2048]{1,0:T(8,128)(2,1)} fusion(bf16[4096,2816]{1,0:T(8,128)(2,1)} %all-gather.13.cloned.1.call-done, bf16[1024,1408]{1,0:T(8,128)(2,1)} %get-tuple-element.155, bf16[1024,1408]{1,0:T(8,128)(2,1)} %get-tuple-element.154), kind=kOutput, calls=%fused_computation.45 | convolution fusion | flops 11824791552 | bytes 21495808 | tf_op jit(solution)/shard_map/dot_general | solution.py:23
  796.7 113.4 %shard_map.175 = (bf16[16,4,16,2048]{3,2,1,0:T(8,128)(2,1)}, f32[16,16,2048]{2,1,0:T(8,128)}, f32[2,2048]{1,0:T(2,128)}) custom-call(bf16[16,4,16,2048]{3,2,1,0:T(8,128)(2,1)} %bitcast.176, f32[16,16,2048]{2,1,0:T(8,128)} %bitcast_convert_fusion.refs_0_, f32[16,16,2048]{2,1,0:T(8,128)} %get-tuple-element.80.refs_1_, f32[1,2048]{1,0:T(1,128)} %get-tuple-element.159.refs_1_.refs_2_), custom_call_target="tpu_custom_call" | custom-call | bytes 350000000 | tf_op jit(solution)/shard_map/pallas_call | solution.py:906
  937.6 108.5 %shard_map.176 = (bf16[1024,1536]{1,0:T(8,128)(2,1)}, bf16[512,2816]{1,0:T(8,128)(2,1)}) custom-call(s32[1,4096]{1,0:T(1,128)} %constant_dynamic-slice_fusion.4.bid_k.bid_q, s32[4096,1]{1,0:T(8,128)} %copy.34.bid_q.bid_k, bf16[1024,512]{1,0:T(8,128)(2,1)} %fusion.40.d_mix, bf16[3,4096,128]{2,1,0:T(8,128)(2,1)} %get-tuple-element.76.refs_0_.spread, ...), custom_call_target="tpu_custom_call" | custom-call | flops 10000000000 | bytes 300000000 | tf_op jit(solution)/shard_map/pallas_call | solution.py:410
  1049.1 11.7 fusion.34
  1069.5 107.4 %shard_map.177 = (bf16[16,4,16,2048]{3,2,1,0:T(8,128)(2,1)}, f32[16,16,2048]{2,1,0:T(8,128)}, f32[2,2048]{1,0:T(2,128)}) custom-call(bf16[16,4,16,2048]{3,2,1,0:T(8,128)(2,1)} %bitcast.177, f32[16,16,2048]{2,1,0:T(8,128)} %get-tuple-element.89.refs_0_, bf16[16,16,2048]{2,1,0:T(8,128)(2,1)} %dynamic-slice_bitcast_fusion.refs_0_.refs_1_, ...), custom_call_target="tpu_custom_call" | custom-call | bytes 350000000 | tf_op jit(solution)/shard_map/pallas_call | solution.py:906
  1187.8 14.0 multiply_convert_fusion.1
  1204.4 14.6 convolution_convert_fusion
  1219.0 18.2 %fusion.24 = bf16[1024,2048]{1,0:T(8,128)(2,1)} fusion(bf16[4096,2816]{1,0:T(8,128)(2,1)} %all-gather.13.cloned.1.call-done, bf16[1024,1408]{1,0:T(8,128)(2,1)} %copy-done.42, bf16[1024,1408]{1,0:T(8,128)(2,1)} %copy-done.41), kind=kOutput, calls=%fused_computation.44 | convolution fusion | flops 11824791552 | bytes 21495808 | tf_op jit(solution)/shard_map/dot_general | solution.py:23
  1241.8 101.9 %shard_map.178 = (bf16[16,4,16,2048]{3,2,1,0:T(8,128)(2,1)}, f32[16,16,2048]{2,1,0:T(8,128)}, f32[2,2048]{1,0:T(2,128)}, bf16[1024,512]{1,0:T(8,128)(2,1)}, bf16...) custom-call(bf16[16,4,16,2048]{3,2,1,0:T(8,128)(2,1)} %bitcast.175, ...), custom_call_target="tpu_custom_call" | custom-call | bytes 350000000 | tf_op jit(solution)/shard_map/pallas_call | solution.py:906
  1366.1 122.5 %shard_map.179 = (bf16[1024,1536]{1,0:T(8,128)(2,1)}, bf16[512,2816]{1,0:T(8,128)(2,1)}) custom-call(s32[1,4096]{1,0:T(1,128)} %constant_dynamic-slice_fusion.4.bid_k.bid_q, s32[4096,1]{1,0:T(8,128)} %copy.34.bid_q.bid_k, bf16[1024,512]{1,0:T(8,128)(2,1)} %fusion.41.d_mix, bf16[3,4096,128]{2,1,0:T(8,128)(2,1)} %get-tuple-element.100.spread, ...), custom_call_target="tpu_custom_call" | custom-call | flops 10000000000 | bytes 300000000 | tf_op jit(solution)/shard_map/pallas_call | solution.py:410
  1544.4 107.2 %shard_map.180 = (bf16[2,16,4,16,512]{4,3,2,1,0:T(8,128)(2,1)}, f32[16,16,2048]{2,1,0:T(8,128)}, f32[2,2048]{1,0:T(2,128)}, f32[2,4,2,512]{3,2,1,0:T(2,128)}, bf...) custom-call(bf16[16,4,16,2048]{3,2,1,0:T(8,128)(2,1)} %bitcast.180, ...), custom_call_target="tpu_custom_call" | custom-call | bytes 350000000 | tf_op jit(solution)/shard_map/pallas_call | solution.py:906
  1669.1 27.5 %collective-permute-done = bf16[512,1536]{1,0:T(8,128)(2,1)S(1)} collective-permute-done((bf16[512,1536]{1,0:T(8,128)(2,1)}, bf16[512,1536]{1,0:T(8,128)(2,1)S(1)}, u32[]{:S(2)}, u32[]{:S(2)}) %collective-permute-start) | collective-permute-done | bytes 1572896 | tf_op jit(solution)/shard_map/ppermute | solution.py:1323
  (214 shorter events, 232.9 us)
Async XLA Ops:
  7.2 106.4 %all-gather.11.cloned.1.call-start = ((), (), s32[]{:S(2)}) async-start(), calls=%async_computation.10 | async-start | bytes 14155776 | tf_op jit(solution)/shard_map/all_gather | solution.py:1156
  12.6 199.0 %all-gather.15.cloned.1.call-start = ((), (), s32[]{:S(2)}) async-start(), calls=%async_computation.21 | async-start | bytes 4718592 | tf_op jit(solution)/shard_map/all_gather | solution.py:1156
  13.3 311.7 %all-gather.13.cloned.1.call-start = ((), (), s32[]{:S(2)}) async-start(), calls=%async_computation.11 | async-start | bytes 25952256 | tf_op jit(solution)/shard_map/all_gather | solution.py:1156
  17.3 332.1 %all-gather.17.cloned.1.call-start = ((), (), s32[]{:S(2)}) async-start(), calls=%async_computation.22 | async-start | bytes 12976128 | tf_op jit(solution)/shard_map/all_gather | solution.py:1156
  17.8 583.4 %all-gather.19.cloned.1.call-start = ((), (), s32[]{:S(2)}) async-start(), calls=%async_computation.23 | async-start | bytes 5242880 | tf_op jit(solution)/shard_map/all_gather | solution.py:1191
  360.3 159.2 %copy-start.25 = (bf16[2,1024,512]{2,1,0:T(8,128)(2,1)S(1)}, bf16[2,1024,512]{2,1,0:T(8,128)(2,1)}, u32[]{:S(2)}) copy-start(bf16[2,1024,512]{2,1,0:T(8,128)(2,1)} %param.11) | copy-start | bytes 6291460
  520.5 417.1 %reduce-scatter.13.cloned.1.call-start = ((), (), s32[]{:S(2)}) async-start(), calls=%async_computation.12 | async-start | bytes 14417920 | tf_op jit(solution)/shard_map/reduce_scatter | solution.py:1239
  601.3 133.2 %slice-start = ((s8[11534336]{0:T(1024)(128)(4,1)}), s8[3145728]{0:T(1024)(128)(4,1)S(1)}, s32[]{:S(2)}) async-start(s8[11534336]{0:T(1024)(128)(4,1)} %bitcast.204), calls=%async_computation.25 | async-start | bytes 6291456
  793.7 275.9 %reduce-scatter.15.cloned.1.call-start = ((), (), s32[]{:S(2)}) async-start(), calls=%async_computation.13 | async-start | bytes 5242880 | tf_op jit(solution)/shard_map/reduce_scatter | solution.py:1274
  796.7 115.9 %copy-start.17 = (f32[16,16,2048]{2,1,0:T(8,128)S(1)}, f32[16,16,2048]{2,1,0:T(8,128)}, u32[]{:S(2)}) copy-start(f32[16,16,2048]{2,1,0:T(8,128)} %get-tuple-element.80.refs_1_) | copy-start | bytes 6291460
  796.7 115.9 %copy-start.38 = (bf16[1024,1408]{1,0:T(8,128)(2,1)S(1)}, bf16[1024,1408]{1,0:T(8,128)(2,1)}, u32[]{:S(2)}) copy-start(bf16[1024,1408]{1,0:T(8,128)(2,1)} %get-tuple-element.156) | copy-start | bytes 8650756
  923.5 318.2 %reduce-scatter.17.cloned.1.call-start = ((), (), s32[]{:S(2)}) async-start(), calls=%async_computation.14 | async-start | bytes 2621440 | tf_op jit(solution)/shard_map/reduce_scatter | solution.py:1239
  936.8 304.9 %reduce-scatter.21.cloned.1.call-start = ((), (), s32[]{:S(2)}) async-start(), calls=%async_computation.16 | async-start | bytes 7208960 | tf_op jit(solution)/shard_map/reduce_scatter | solution.py:1239
  937.5 304.2 %reduce-scatter.19.cloned.1.call-start = ((), (), s32[]{:S(2)}) async-start(), calls=%async_computation.15 | async-start | bytes 7864320 | tf_op jit(solution)/shard_map/reduce_scatter | solution.py:1239
  1069.5 296.7 %reduce-scatter.23.cloned.1.call-start = ((), (), s32[]{:S(2)}) async-start(), calls=%async_computation.17 | async-start | bytes 14417920 | tf_op jit(solution)/shard_map/reduce_scatter | solution.py:1239
  1069.5 107.4 %copy-start.16 = (bf16[1024,1408]{1,0:T(8,128)(2,1)S(1)}, bf16[1024,1408]{1,0:T(8,128)(2,1)}, u32[]{:S(2)}) copy-start(bf16[1024,1408]{1,0:T(8,128)(2,1)} %multiply_convert_fusion.5) | copy-start | bytes 8650756
  1237.2 280.2 %reduce-scatter.31.cloned.1.call-start = ((), (), s32[]{:S(2)}) async-start(), calls=%async_computation.24 | async-start | bytes 1310720
  1352.8 191.6 %reduce-scatter.25.cloned.1.call-start = ((), (), s32[]{:S(2)}) async-start(), calls=%async_computation.18 | async-start | bytes 7208960 | tf_op jit(solution)/shard_map/reduce_scatter | solution.py:1239
  1353.5 190.9 %reduce-scatter.27.cloned.1.call-start = ((), (), s32[]{:S(2)}) async-start(), calls=%async_computation.19 | async-start | bytes 2621440 | tf_op jit(solution)/shard_map/reduce_scatter | solution.py:1239
  1366.1 292.4 %reduce-scatter.29.cloned.1.call-start = ((), (), s32[]{:S(2)}) async-start(), calls=%async_computation.20 | async-start | bytes 7864320 | tf_op jit(solution)/shard_map/reduce_scatter | solution.py:1239
  1544.4 116.3 %copy-start.18 = (bf16[512,512]{1,0:T(8,128)(2,1)S(1)}, bf16[512,512]{1,0:T(8,128)(2,1)}, u32[]{:S(2)}) copy-start(bf16[512,512]{1,0:T(8,128)(2,1)} %reduce-scatter.17.cloned.1.call-done.refs_6_) | copy-start | bytes 1572868
  1544.4 116.3 %copy-start.19 = (bf16[512,512]{1,0:T(8,128)(2,1)S(1)}, bf16[512,512]{1,0:T(8,128)(2,1)}, u32[]{:S(2)}) copy-start(bf16[512,512]{1,0:T(8,128)(2,1)} %reduce-scatter.27.cloned.1.call-done.refs_4_) | copy-start | bytes 1572868
  1544.4 116.3 %copy-start.26 = (bf16[512,512]{1,0:T(8,128)(2,1)S(1)}, bf16[512,512]{1,0:T(8,128)(2,1)}, u32[]{:S(2)}) copy-start(bf16[512,512]{1,0:T(8,128)(2,1)} %get-tuple-element.120) | copy-start | bytes 1572868
  1658.5 38.1 %collective-permute-start = (bf16[512,1536]{1,0:T(8,128)(2,1)}, bf16[512,1536]{1,0:T(8,128)(2,1)S(1)}, u32[]{:S(2)}, u32[]{:S(2)}) collective-permute-start(bf16[512,1536]{1,0:T(8,128)(2,1)} %reduce-scatter.29.cloned.1.call-done), channel_id=1, source_target_pairs={{16,0},{17,1},{18,2},{19,3},{20,4},{21,5},{22,6},{23,7},{24,8},{25... | collective-permute-start | bytes 4718600 | tf_op jit(solution)/shard_map/ppermute | solution.py:1323
  (38 other events, 532.0 us)
Sparse Core Ops, SparseCore 0:
  12.7 76.0 all-gather.10
  90.6 36.7 all-gather.14
  129.9 145.2 all-gather.12
  276.9 70.5 all-gather.16
  520.7 80.5 all-gather.18
  793.8 90.8 reduce-scatter.12
  923.7 76.0 reduce-scatter.14
  1002.4 42.1 reduce-scatter.16
  1047.7 54.2 reduce-scatter.20
  1104.6 58.3 reduce-scatter.18
  1237.3 97.9 reduce-scatter.22
  1352.9 45.0 reduce-scatter.30
  1400.7 78.7 reduce-scatter.24
  1482.5 35.0 reduce-scatter.26
  1520.1 58.3 reduce-scatter.28

commit v7 on v6

--- a/solution.py
+++ b/solution.py
@@ -1107,6 +1107,17 @@
     return jnp.concatenate([jnp.cos(angles), jnp.sin(angles)])
 
 
+def hold(values, behind):
+    anywhere = pl.BlockSpec(memory_space=pl.ANY)
+    return pl.pallas_call(
+        lambda *refs: None,
+        in_specs=[anywhere] * (1 + len(behind)),
+        out_specs=anywhere,
+        out_shape=jax.ShapeDtypeStruct(values.shape, values.dtype),
+        input_output_aliases={0: 0},
+    )(values, *behind)
+
+
 def product(left, right):
     return jnp.dot(left, right, preferred_element_type=jnp.float32)
 
@@ -1179,7 +1190,14 @@
     ids = lax.dynamic_index_in_dim(block_ids, section, 0, keepdims=False)
     kept = []
     hidden_out = []
-    waited = []
+
+    def gathered_half(which, half):
+        values = lax.dynamic_index_in_dim(cotangent, which, 0, keepdims=False)
+        values = values[half * (tokens // 2) : (half + 1) * (tokens // 2)]
+        return lax.all_gather(values, "col", axis=1, tiled=True)
+
+    first_half = gathered_half(section, 0)
+    waited = [first_half]
     for layer in range(2):
         if layer == 0:
             qkv = expand(product(normed, qkv_w[0]) + bias[0])
@@ -1188,10 +1206,8 @@
             )
         else:
             here = section + jnp.where(hidden_out[0][0, 0] == hidden_out[0][0, 0], 0, 1)
-            branch = lax.all_gather(
-                lax.dynamic_index_in_dim(cotangent, here, 0, keepdims=False), "col", axis=1, tiled=True
-            )
-            waited = [branch]
+            second_half = gathered_half(here, 1)
+            waited = [second_half]
             spread, mixed, log_sums, attn_mix = attend(9, ids, heads, rows_axis, tokens, spread=spread)
         attn_mix = contract(attn_mix)
         normed_two, after = relay(
@@ -1227,6 +1243,7 @@
             blocks = blocks + jnp.where(owner, after.reshape(-1, 1, RELAY_ROWS, D), 0.0)
             result = blocks.reshape(tokens, D).astype(jnp.bfloat16)
 
+    branch = jnp.concatenate([first_half, second_half])
     grad = mine(branch).astype(jnp.float32)
     weight_sums = [[], []]
     small_sums = []
@@ -1239,7 +1256,7 @@
         weight_sums[layer].append(lax.psum_scatter(term, "row", scatter_dimension=0, tiled=True))
         return weight_sums[layer][-1]
 
-    arrived = [[None] * 4, [None] * 4]
+    arrived = [[None] * 3, [None] * 3]
     def together(*values):
         return lax.optimization_barrier(values)
 
@@ -1266,14 +1283,14 @@
             cols_axis,
             carry=[]
             if layer == 1
-            else [(0, hidden_out[0]), (1, hidden_out[1]), (1, input_out[1]), (1, weight_sums[1][2]), (1, weight_sums[1][3])],
+            else [(0, hidden_out[0]), (1, hidden_out[1]), (1, input_out[1]), (1, weight_sums[1][2])],
             behind=[] if layer == 1 else [weight_sums[1][0]],
         )
         if layer == 1:
             result = jnp.where(d_after[0, 0] == d_after[0, 0], result, 0)
             hidden_out.append(lax.psum_scatter(result, "col", scatter_dimension=1, tiled=True))
         else:
-            hidden_got[0], hidden_got[1], input_got[1], arrived[1][2], arrived[1][3] = got
+            hidden_got[0], hidden_got[1], input_got[1], arrived[1][2] = got
         small_sums += [sums_two]
         d_mix, out_term = together(
             product(grad_attn, out_w[layer]).astype(jnp.bfloat16), dot_first(grad_attn, attn_mix).astype(jnp.bfloat16)
@@ -1281,7 +1298,7 @@
         out_sum = collect(layer, out_term)
         d_qkv, arrived[layer][1] = attend_back(
             10 + layer,
-            expand(d_mix),
+            expand(d_mix) if layer == 1 else hold(expand(d_mix), [down_sum]),
             spread,
             mixed,
             log_sums,
@@ -1299,7 +1316,11 @@
             dot_first(normed, d_qkv).astype(jnp.bfloat16),
             jnp.sum(d_qkv.astype(jnp.float32), axis=0),
         )
-        qkv_sum = collect(layer, qkv_term)
+        if layer == 1:
+            qkv_terms = jnp.pad(qkv_term, ((D, 0), (0, 0)))
+        else:
+            qkv_terms = lax.dynamic_update_slice(qkv_terms, qkv_term, (0, 0))
+            qkv_grad = lax.psum_scatter(qkv_terms, both, scatter_dimension=0, tiled=True).astype(jnp.float32)
         if layer == 0:
             early_sums = lax.psum_scatter(jnp.stack(small_sums), "col", scatter_dimension=2, tiled=True)
             early = jnp.concatenate([early_sums.reshape(6, -1), bias_grads[1].reshape(3, -1), bias_grads[0].reshape(3, -1)])
@@ -1320,12 +1341,11 @@
         small_sums += [sums_one]
         input_out[layer] = my_features(branch) if layer == 1 else branch
 
-    arrived[0][3] = lax.ppermute(weight_sums[0][3], "section", [(1, 0)])
     hidden_states = jnp.where(
         section == 0, jnp.stack([hidden_out[0], hidden_got[0]]), jnp.stack([hidden_got[1], hidden_out[1]])
     )
     input_grads = jnp.where(section == 0, input_out[0], jnp.stack([input_got[1], input_out[1]])).astype(jnp.float32)
-    down_grad, gate_up_grad, out_grad, qkv_grad = (
+    down_grad, gate_up_grad, out_grad = (
         jnp.where(section == 0, first, second).astype(jnp.float32)
         + jnp.where(section == 0, first_got, second_got).astype(jnp.float32)
         for first, second, first_got, second_got in zip(*weight_sums, *arrived)

time: 1720 us -> 1680 us (0.977)
  Pallas kernels: 1260 us -> 1210 us
    reduce_scatter x8 -> x6, waiting for transfers between devices: 0.07 us -> 30 us  [collect(): lax.psum_scatter(term, 'row', scatter_dimension=0, tiled=True)]
    ppermute x1 -> x0, waiting for transfers between devices: 27.5 us -> none  [per_device(): arrived[0][3] = lax.ppermute(weight_sums[0][3], 'section', [(1, 0)])]
    pallas_call x2, Pallas kernels: 231 us -> 206 us  [attend_back(): pl.pallas_call(functools.partial(attend_back_kernel, heads, n, bq, layer)...]
    all_gather x4, waiting for transfers between devices: 0.05 us -> 24 us  [weights_of(): return lax.all_gather(block, both, axis=0, tiled=True).reshape(2, D, -1)]
    all_gather x1 -> x2, waiting for transfers between devices: 18.8 us -> 0.01 us  [gathered_half(): return lax.all_gather(values, 'col', axis=1, tiled=True)]
    unnamed x103 -> x91, local copies, waits for them, and re-layouts: 36.5 us -> 37.8 us
  transfers between devices with their start and end apart: 16 -> 15, of which waited for: 2 -> 2; matrix products, arithmetic and copies ran while one was open for 14% -> 15% of each run, Pallas kernels for 58% -> 58%
where the time goes in v7:
time: 1680 us
  Pallas kernels  1210 us (72%)
  matrix products  266 us (16%)
  local copies, waits for them, and re-layouts  73 us (4%)
  waiting for transfers between devices  56.5 us (3%)
  other arithmetic  37.1 us (2%)
  blocking collectives  17.1 us (1%)
    pallas_call x7, Pallas kernels, relay(): pl.pallas_call(functools.partial(relay_kernel, middle, len(ins), len(outs...  795 us
    pallas_call x2, Pallas kernels, attend_back(): pl.pallas_call(functools.partial(attend_back_kernel, heads, n, bq, layer)...  206 us
    pallas_call x2, Pallas kernels, attend(): pl.pallas_call(functools.partial(attend_kernel, heads, n, bq, given), in_...  127 us
    dot_general x11, matrix products, product(): return jnp.dot(left, right, preferred_element_type=jnp.float32)  125 us
    pallas_call x1, Pallas kernels, gathered(): pl.pallas_call(functools.partial(gather_kernel, n, chunks, lag), in_specs...  81.9 us
    dot_general x8, matrix products, dot_first(): lax.dot_general(a, b, (((0,), (0,)), ((), ())), preferred_element_type=jn...  81.3 us
    dot_general x4, matrix products, dot_last(): lax.dot_general(a, b, (((1,), (1,)), ((), ())), preferred_element_type=jn...  59.2 us
    unnamed x91, local copies, waits for them, and re-layouts  37.8 us
  transfers between devices with their start and end apart: 15, of which 2 were waited for; matrix products, arithmetic and copies ran while one was open for 15% of the time, Pallas kernels for 58%

profile of v7, /device:TPU:0, one launch (start us, length us, event | category | flops | bytes accessed | tf_op | source)
XLA Modules:
  0.0 1675.7 jit_solution(13616777318122710637)
XLA Ops:
  22.7 81.9 %shard_map.169 = (bf16[1024,2048]{1,0:T(8,128)(2,1)S(1)}, f32[2,4,8,512]{3,2,1,0:T(8,128)S(1)}, bf16[1024,2048]{1,0:T(8,128)(2,1)S(1)}, f32[4096,128]{1,0:T(8,128)S(1)}, f32[4096,128]{1,0:T(8,128)S(1)}) custom-call(bf16[1024,512]{1,0:T(8,128)(2,1)S(1)} %dynamic-slice_bitcast_fusion.2.own, f32[8,512]{1,0:T(8,128)S(1)} %maximum_maximum_fusion.small, ...), custom_call_target="tpu_custom_call" | custom-call | bytes 250000000 | tf_op jit(solution)/shard_map/pallas_call | solution.py:1079
  115.9 11.9 fusion.20.refs_0_
  127.8 73.3 %shard_map.170 = (bf16[3,4096,128]{2,1,0:T(8,128)(2,1)}, bf16[4096,128]{1,0:T(8,128)(2,1)}, f32[128,4096]{1,0:T(8,128)}, bf16[1024,512]{1,0:T(8,128)(2,1)}) custom-call(s32[4096,1]{1,0:T(8,128)} %copy.35.bid_q.bid_k, s32[1,4096]{1,0:T(1,128)} %constant_dynamic-slice_fusion.5.bid_k.bid_q, f32[1024,1536]{1,0:T(8,128)} %fusion.20.refs_0_, ...), custom_call_target="tpu_custom_call" | custom-call | flops 10000000000 | bytes 200000000 | tf_op jit(solution)/shard_map/pallas_call | solution.py:227
  207.4 111.6 %shard_map.171 = (bf16[16,4,16,2048]{3,2,1,0:T(8,128)(2,1)}, f32[16,16,2048]{2,1,0:T(8,128)}) custom-call(bf16[16,4,16,2048]{3,2,1,0:T(8,128)(2,1)} %bitcast.182, bf16[16,16,2048]{2,1,0:T(8,128)(2,1)} %dynamic-slice_bitcast_fusion.1.refs_0_.refs_1_, f32[1,2048]{1,0:T(1,128)} %get-tuple-element.161.refs_1_.refs_2_, f32[1,2048]{1,0:T(1,128)} %get-tuple-element.160.refs_2_, ...), custom_call_target="tpu_custom_call" | custom-call | bytes 350000000 | tf_op jit(solution)/shard_map/pallas_call | solution.py:906
  319.0 17.2 %fusion.6 = f32[1024,2816]{1,0:T(8,128)S(1)} fusion(bf16[1024,2048]{1,0:T(8,128)(2,1)} %bitcast.208, bf16[4096,2816]{1,0:T(8,128)(2,1)} %all-gather.15.cloned.1.call-done), kind=kOutput, calls=%fused_computation.9 | convolution fusion | flops 11811160064 | bytes 27262976 | tf_op jit(solution)/shard_map/dot_general | solution.py:1122
  343.3 24.0 %all-gather.21.cloned.1.call-done = bf16[1,4096,1408]{2,1,0:T(8,128)(2,1)} async-done(((bf16[1,512,1408]{2,1,0:T(8,128)(2,1)}), bf16[1,4096,1408]{2,1,0:T(8,128)(2,1)}) %all-gather.21.cloned.1.call-update) | async-done | bytes 11534352 | tf_op jit(solution)/shard_map/all_gather | solution.py:1167
  378.2 130.6 %shard_map.172 = (bf16[16,4,16,2048]{3,2,1,0:T(8,128)(2,1)}, bf16[16,4,16,2048]{3,2,1,0:T(8,128)(2,1)}, bf16[3,4096,128]{2,1,0:T(8,128)(2,1)}) custom-call(bf16[16,4,16,2048]{3,2,1,0:T(8,128)(2,1)} %bitcast.186, f32[16,16,2048]{2,1,0:T(8,128)} %get-tuple-element.73.refs_0_.refs_1_, f32[1,2048]{1,0:T(1,128)} %get-tuple-element.159.refs_1_.refs_2_, ...), custom_call_target="tpu_custom_call" | custom-call | bytes 350000000 | tf_op jit(solution)/shard_map/pallas_call | solution.py:906
  515.0 53.3 %shard_map.173 = (bf16[4096,128]{1,0:T(8,128)(2,1)}, f32[128,4096]{1,0:T(8,128)}, bf16[1024,512]{1,0:T(8,128)(2,1)}) custom-call(s32[4096,1]{1,0:T(8,128)} %copy.35.bid_q.bid_k, s32[1,4096]{1,0:T(1,128)} %constant_dynamic-slice_fusion.5.bid_k.bid_q, bf16[3,4096,128]{2,1,0:T(8,128)(2,1)} %get-tuple-element.75.refs_0_.spread), custom_call_target="tpu_custom_call" | custom-call | flops 10000000000 | bytes 200000000 | tf_op jit(solution)/shard_map/pallas_call | solution.py:227
  574.6 112.3 %shard_map.174 = (bf16[16,4,16,2048]{3,2,1,0:T(8,128)(2,1)}, f32[16,16,2048]{2,1,0:T(8,128)}) custom-call(bf16[16,4,16,2048]{3,2,1,0:T(8,128)(2,1)} %bitcast.183, bf16[16,16,2048]{2,1,0:T(8,128)(2,1)} %dynamic-slice_bitcast_fusion.refs_0_.refs_1_, f32[1,2048]{1,0:T(1,128)} %get-tuple-element.157.refs_1_.refs_2_, f32[1,2048]{1,0:T(1,128)} %get-tuple-element.156.refs_2_, ...), custom_call_target="tpu_custom_call" | custom-call | bytes 350000000 | tf_op jit(solution)/shard_map/pallas_call | solution.py:906
  686.9 18.8 %fusion.2 = f32[1024,2816]{1,0:T(8,128)} fusion(bf16[1024,2048]{1,0:T(8,128)(2,1)} %bitcast.215, bf16[4096,2816]{1,0:T(8,128)(2,1)} %all-gather.15.cloned.1.call-done), kind=kOutput, calls=%fused_computation.5 | convolution fusion | flops 11811160064 | bytes 27262976 | tf_op jit(solution)/shard_map/dot_general | solution.py:1122
  705.7 15.8 multiply_convert_fusion.4
  731.9 18.4 %convolution_convert_fusion.1 = bf16[2048,2816]{1,0:T(8,128)(2,1)} fusion(bf16[1024,2048]{1,0:T(8,128)(2,1)} %bitcast.216, bf16[1024,1408]{1,0:T(8,128)(2,1)} %get-tuple-element.153, bf16[1024,1408]{1,0:T(8,128)(2,1)} %get-tuple-element.152), kind=kOutput, calls=%fused_computation.2 | convolution fusion | flops 11828461568 | bytes 21495808 | tf_op jit(solution)/shard_map/dot_general | solution.py:27
  750.3 18.0 %fusion.27 = bf16[1024,2048]{1,0:T(8,128)(2,1)} fusion(bf16[4096,2816]{1,0:T(8,128)(2,1)} %all-gather.15.cloned.1.call-done, bf16[1024,1408]{1,0:T(8,128)(2,1)} %get-tuple-element.153, bf16[1024,1408]{1,0:T(8,128)(2,1)} %get-tuple-element.152), kind=kOutput, calls=%fused_computation.47 | convolution fusion | flops 11824791552 | bytes 21495808 | tf_op jit(solution)/shard_map/dot_general | solution.py:23
  772.3 115.4 %shard_map.175 = (bf16[16,4,16,2048]{3,2,1,0:T(8,128)(2,1)}, f32[16,16,2048]{2,1,0:T(8,128)}, f32[2,2048]{1,0:T(2,128)}) custom-call(bf16[16,4,16,2048]{3,2,1,0:T(8,128)(2,1)} %bitcast.180, f32[16,16,2048]{2,1,0:T(8,128)} %bitcast_convert_fusion.refs_0_, f32[16,16,2048]{2,1,0:T(8,128)} %get-tuple-element.79.refs_1_, f32[1,2048]{1,0:T(1,128)} %get-tuple-element.157.refs_1_.refs_2_), custom_call_target="tpu_custom_call" | custom-call | bytes 350000000 | tf_op jit(solution)/shard_map/pallas_call | solution.py:906
  915.1 108.4 %shard_map.176 = (bf16[1024,1536]{1,0:T(8,128)(2,1)}, bf16[512,2816]{1,0:T(8,128)(2,1)}) custom-call(s32[1,4096]{1,0:T(1,128)} %constant_dynamic-slice_fusion.5.bid_k.bid_q, s32[4096,1]{1,0:T(8,128)} %copy.35.bid_q.bid_k, bf16[1024,512]{1,0:T(8,128)(2,1)} %fusion.40.d_mix, bf16[3,4096,128]{2,1,0:T(8,128)(2,1)} %get-tuple-element.75.refs_0_.spread, ...), custom_call_target="tpu_custom_call" | custom-call | flops 10000000000 | bytes 300000000 | tf_op jit(solution)/shard_map/pallas_call | solution.py:410
  1046.9 106.2 %shard_map.177 = (bf16[16,4,16,2048]{3,2,1,0:T(8,128)(2,1)}, f32[16,16,2048]{2,1,0:T(8,128)}, f32[2,2048]{1,0:T(2,128)}) custom-call(bf16[16,4,16,2048]{3,2,1,0:T(8,128)(2,1)} %bitcast.181, f32[16,16,2048]{2,1,0:T(8,128)} %get-tuple-element.88.refs_0_, bf16[16,16,2048]{2,1,0:T(8,128)(2,1)} %dynamic-slice_bitcast_fusion.refs_0_.refs_1_, ...), custom_call_target="tpu_custom_call" | custom-call | bytes 350000000 | tf_op jit(solution)/shard_map/pallas_call | solution.py:906
  1164.1 14.0 multiply_convert_fusion.1
  1180.6 14.6 convolution_convert_fusion
  1195.2 18.1 %fusion.24 = bf16[1024,2048]{1,0:T(8,128)(2,1)} fusion(bf16[4096,2816]{1,0:T(8,128)(2,1)} %all-gather.15.cloned.1.call-done, bf16[1024,1408]{1,0:T(8,128)(2,1)} %copy-done.37, bf16[1024,1408]{1,0:T(8,128)(2,1)} %copy-done.36), kind=kOutput, calls=%fused_computation.46 | convolution fusion | flops 11824791552 | bytes 21495808 | tf_op jit(solution)/shard_map/dot_general | solution.py:23
  1218.6 102.3 %shard_map.178 = (bf16[16,4,16,2048]{3,2,1,0:T(8,128)(2,1)}, f32[16,16,2048]{2,1,0:T(8,128)}, f32[2,2048]{1,0:T(2,128)}, bf16[1024,512]{1,0:T(8,128)(2,1)}, bf16...) custom-call(bf16[16,4,16,2048]{3,2,1,0:T(8,128)(2,1)} %bitcast.179, ...), custom_call_target="tpu_custom_call" | custom-call | bytes 350000000 | tf_op jit(solution)/shard_map/pallas_call | solution.py:906
  1340.6 30.0 %reduce-scatter.22.cloned.1.call-done.carry = bf16[512,2816]{1,0:T(8,128)(2,1)} async-done(((bf16[2048,2816]{1,0:T(8,128)(2,1)}), bf16[512,2816]{1,0:T(8,128)(2,1)}) %reduce-scatter.22.cloned.1.call-update) | async-done | bytes 2883600 | tf_op jit(solution)/shard_map/reduce_scatter | solution.py:1256
  1370.5 97.5 %shard_map.180 = (bf16[1024,1536]{1,0:T(8,128)(2,1)}, bf16[512,2816]{1,0:T(8,128)(2,1)}) custom-call(s32[1,4096]{1,0:T(1,128)} %constant_dynamic-slice_fusion.5.bid_k.bid_q, s32[4096,1]{1,0:T(8,128)} %copy.35.bid_q.bid_k, bf16[1024,512]{1,0:T(8,128)(2,1)} %shard_map.179.d_mix, bf16[3,4096,128]{2,1,0:T(8,128)(2,1)} %get-tuple-element.99.spread, ...), custom_call_target="tpu_custom_call" | custom-call | flops 10000000000 | bytes 300000000 | tf_op jit(solution)/shard_map/pallas_call | solution.py:410
  1468.1 11.9 fusion.31
  1529.3 116.4 %shard_map.181 = (bf16[2,16,4,16,512]{4,3,2,1,0:T(8,128)(2,1)}, f32[16,16,2048]{2,1,0:T(8,128)}, f32[2,2048]{1,0:T(2,128)}, f32[2,4,2,512]{3,2,1,0:T(2,128)}, bf...) custom-call(bf16[16,4,16,2048]{3,2,1,0:T(8,128)(2,1)} %bitcast.185, ...), custom_call_target="tpu_custom_call" | custom-call | bytes 350000000 | tf_op jit(solution)/shard_map/pallas_call | solution.py:906
  (203 shorter events, 237.1 us)
Async XLA Ops:
  7.2 108.7 %all-gather.13.cloned.1.call-start = ((), (), s32[]{:S(2)}) async-start(), calls=%async_computation.9 | async-start | bytes 14155776 | tf_op jit(solution)/shard_map/all_gather | solution.py:1167
  12.6 188.5 %all-gather.17.cloned.1.call-start = ((), (), s32[]{:S(2)}) async-start(), calls=%async_computation.19 | async-start | bytes 4718592 | tf_op jit(solution)/shard_map/all_gather | solution.py:1167
  13.3 194.1 %all-gather.19.cloned.1.call-start = ((), (), s32[]{:S(2)}) async-start(), calls=%async_computation.20 | async-start | bytes 2621440 | tf_op jit(solution)/shard_map/all_gather | solution.py:1197
  15.3 303.7 %all-gather.15.cloned.1.call-start = ((), (), s32[]{:S(2)}) async-start(), calls=%async_computation.10 | async-start | bytes 25952256 | tf_op jit(solution)/shard_map/all_gather | solution.py:1167
  19.2 348.1 %all-gather.21.cloned.1.call-start = ((), (), s32[]{:S(2)}) async-start(), calls=%async_computation.21 | async-start | bytes 12976128 | tf_op jit(solution)/shard_map/all_gather | solution.py:1167
  19.8 554.8 %all-gather.23.cloned.1.call-start = ((), (), s32[]{:S(2)}) async-start(), calls=%async_computation.22 | async-start | bytes 2621440 | tf_op jit(solution)/shard_map/all_gather | solution.py:1197
  512.6 402.5 %reduce-scatter.12.cloned.1.call-start = ((), (), s32[]{:S(2)}) async-start(), calls=%async_computation.11 | async-start | bytes 14417920 | tf_op jit(solution)/shard_map/reduce_scatter | solution.py:1256
  768.3 278.5 %reduce-scatter.14.cloned.1.call-start = ((), (), s32[]{:S(2)}) async-start(), calls=%async_computation.12 | async-start | bytes 5242880 | tf_op jit(solution)/shard_map/reduce_scatter | solution.py:1291
  772.3 117.9 %copy-start.16 = (f32[16,16,2048]{2,1,0:T(8,128)S(1)}, f32[16,16,2048]{2,1,0:T(8,128)}, u32[]{:S(2)}) copy-start(f32[16,16,2048]{2,1,0:T(8,128)} %get-tuple-element.79.refs_1_) | copy-start | bytes 6291460
  772.3 117.9 %copy-start.33 = (bf16[1024,1408]{1,0:T(8,128)(2,1)S(1)}, bf16[1024,1408]{1,0:T(8,128)(2,1)}, u32[]{:S(2)}) copy-start(bf16[1024,1408]{1,0:T(8,128)(2,1)} %copy-done.32) | copy-start | bytes 8650756
  901.2 317.4 %reduce-scatter.16.cloned.1.call-start = ((), (), s32[]{:S(2)}) async-start(), calls=%async_computation.13 | async-start | bytes 2621440 | tf_op jit(solution)/shard_map/reduce_scatter | solution.py:1256
  914.5 304.1 %reduce-scatter.18.cloned.1.call-start = ((), (), s32[]{:S(2)}) async-start(), calls=%async_computation.14 | async-start | bytes 7208960 | tf_op jit(solution)/shard_map/reduce_scatter | solution.py:1256
  915.0 425.5 %reduce-scatter.20.cloned.1.call-start = ((), (), s32[]{:S(2)}) async-start(), calls=%async_computation.15 | async-start | bytes 7208960 | tf_op jit(solution)/shard_map/reduce_scatter | solution.py:1256
  1046.9 106.2 %copy-start.15 = (bf16[1024,1408]{1,0:T(8,128)(2,1)S(1)}, bf16[1024,1408]{1,0:T(8,128)(2,1)}, u32[]{:S(2)}) copy-start(bf16[1024,1408]{1,0:T(8,128)(2,1)} %multiply_convert_fusion.5) | copy-start | bytes 8650756
  1213.4 157.1 %reduce-scatter.22.cloned.1.call-start = ((), (), s32[]{:S(2)}) async-start(), calls=%async_computation.16 | async-start | bytes 14417920 | tf_op jit(solution)/shard_map/reduce_scatter | solution.py:1256
  1214.0 285.6 %reduce-scatter.28.cloned.1.call-start = ((), (), s32[]{:S(2)}) async-start(), calls=%async_computation.23 | async-start | bytes 1310720
  1218.6 102.3 %copy-start.25 = (f32[2,2048]{1,0:T(2,128)S(1)}, f32[2,2048]{1,0:T(2,128)}, u32[]{:S(2)}) copy-start(f32[2,2048]{1,0:T(2,128)} %get-tuple-element.107) | copy-start | bytes 49156
  1218.6 102.3 %copy-start.26 = (f32[2,2048]{1,0:T(2,128)S(1)}, f32[2,2048]{1,0:T(2,128)}, u32[]{:S(2)}) copy-start(f32[2,2048]{1,0:T(2,128)} %get-tuple-element.108) | copy-start | bytes 49156
  1330.0 199.3 %reduce-scatter.24.cloned.1.call-start = ((), (), s32[]{:S(2)}) async-start(), calls=%async_computation.17 | async-start | bytes 2621440 | tf_op jit(solution)/shard_map/reduce_scatter | solution.py:1256
  1340.5 321.8 %reduce-scatter.26.cloned.1.call-start = ((), (), s32[]{:S(2)}) async-start(), calls=%async_computation.18 | async-start | bytes 14155776 | tf_op jit(solution)/shard_map/reduce_scatter | solution.py:1323
  1468.0 19.8 %slice-start = ((s8[6291456]{0:T(1024)(128)(4,1)}), s8[4194304]{0:T(1024)(128)(4,1)S(1)}, s32[]{:S(2)}) async-start(s8[6291456]{0:T(1024)(128)(4,1)} %bitcast.177), calls=%async_computation.24 | async-start | bytes 8388608
  1529.3 124.7 %copy-start.17 = (bf16[512,512]{1,0:T(8,128)(2,1)S(1)}, bf16[512,512]{1,0:T(8,128)(2,1)}, u32[]{:S(2)}) copy-start(bf16[512,512]{1,0:T(8,128)(2,1)} %reduce-scatter.16.cloned.1.call-done.refs_6_) | copy-start | bytes 1572868
  1529.3 124.7 %copy-start.18 = (bf16[512,512]{1,0:T(8,128)(2,1)S(1)}, bf16[512,512]{1,0:T(8,128)(2,1)}, u32[]{:S(2)}) copy-start(bf16[512,512]{1,0:T(8,128)(2,1)} %reduce-scatter.24.cloned.1.call-done.refs_4_) | copy-start | bytes 1572868
  1529.3 124.7 %copy-start.22 = (bf16[512,512]{1,0:T(8,128)(2,1)S(1)}, bf16[512,512]{1,0:T(8,128)(2,1)}, u32[]{:S(2)}) copy-start(bf16[512,512]{1,0:T(8,128)(2,1)} %get-tuple-element.118) | copy-start | bytes 1572868
  (31 other events, 194.5 us)
Sparse Core Ops, SparseCore 0:
  12.7 76.2 all-gather.12
  90.8 36.7 all-gather.16
  129.1 45.9 all-gather.18
  177.4 120.3 all-gather.14
  299.6 67.6 all-gather.20
  512.8 44.7 all-gather.22
  768.5 91.5 reduce-scatter.11
  901.3 74.3 reduce-scatter.13
  978.4 43.2 reduce-scatter.15
  1024.7 53.1 reduce-scatter.17
  1213.5 62.2 reduce-scatter.19
  1278.3 92.2 reduce-scatter.21
  1372.8 27.1 reduce-scatter.27
  1403.1 36.5 reduce-scatter.23
  1493.6 148.2 reduce-scatter.25

commit v8 on v7

--- a/solution.py
+++ b/solution.py
@@ -1100,22 +1100,45 @@
     )(own, small, angles)
 
 
+def ffn_kernel(units, values, weight, down, gate_up, hidden, partial):
+    both = jnp.dot(values[...], weight[...], preferred_element_type=jnp.float32)
+    gate_up[...] = both
+    gate, up = both[:, :units], both[:, units:]
+    found = (gate * (1.0 / (1.0 + jnp.exp(-gate))) * up).astype(jnp.bfloat16)
+    hidden[...] = found
+    partial[...] = dot_last(found, down[...]).astype(partial.dtype)
+
+
+def ffn_back_kernel(units, branch, gate_up, weight, down, d_gate_up, partial):
+    d_hidden = jnp.dot(branch[...], down[...], preferred_element_type=jnp.float32)
+    gate, up = gate_up[:, :units], gate_up[:, units:]
+    sig = 1.0 / (1.0 + jnp.exp(-gate))
+    d_gate_up[:, :units] = (d_hidden * up * sig * (1.0 + gate * (1.0 - sig))).astype(jnp.bfloat16)
+    d_gate_up[:, units:] = (d_hidden * gate * sig).astype(jnp.bfloat16)
+    partial[...] = dot_last(d_gate_up[...], weight[...]).astype(partial.dtype)
+
+
+def ffn_call(kernel, layer, inputs, weight, down, outs, rows=256):
+    tokens = inputs[0].shape[0]
+    units = down.shape[1]
+    by_rows = lambda width: pl.BlockSpec((rows, width), lambda i: (i, 0))
+    once = lambda width: pl.BlockSpec((D, width), lambda i: (layer, 0), pipeline_mode=pl.Buffered(1))
+    return pl.pallas_call(
+        functools.partial(kernel, units),
+        grid=(tokens // rows,),
+        in_specs=[by_rows(values.shape[1]) for values in inputs] + [once(2 * units), once(units)],
+        out_specs=[by_rows(width) for width, _ in outs],
+        out_shape=[jax.ShapeDtypeStruct((tokens, width), kind) for width, kind in outs],
+        compiler_params=pltpu.CompilerParams(vmem_limit_bytes=58 * 2**20),
+        cost_estimate=pl.CostEstimate(flops=6 * tokens * D * units, bytes_accessed=4 * 10**7, transcendentals=0),
+    )(*inputs, weight, down)
+
+
 def rotary_angles(positions):
     half_dims = ROT // 2
     inverse_freq = 1.0 / 10000.0 ** (jnp.arange(half_dims, dtype=jnp.float32) * 2.0 / ROT)
     angles = positions.astype(jnp.float32)[None, :] * inverse_freq[:, None]
     return jnp.concatenate([jnp.cos(angles), jnp.sin(angles)])
-
-
-def hold(values, behind):
-    anywhere = pl.BlockSpec(memory_space=pl.ANY)
-    return pl.pallas_call(
-        lambda *refs: None,
-        in_specs=[anywhere] * (1 + len(behind)),
-        out_specs=anywhere,
-        out_shape=jax.ShapeDtypeStruct(values.shape, values.dtype),
-        input_output_aliases={0: 0},
-    )(values, *behind)
 
 
 def product(left, right):
@@ -1188,6 +1211,28 @@
     down_w = weights_of(down_weight)
 
     ids = lax.dynamic_index_in_dim(block_ids, section, 0, keepdims=False)
+    def feed_forward(layer, values):
+        kind = jnp.bfloat16 if layer == 0 else jnp.float32
+        if units % LANES == 0:
+            outs = [(2 * units, jnp.float32), (units, jnp.bfloat16), (D, kind)]
+            return ffn_call(ffn_kernel, layer, [values], all_gate_up, all_down, outs)
+        gate_up = product(values, gate_up_w[layer])
+        hidden = (jax.nn.silu(gate_up[:, :units]) * gate_up[:, units:]).astype(jnp.bfloat16)
+        return gate_up, hidden, dot_last(hidden, down_w[layer]).astype(kind)
+
+    def feed_back(layer, branch, gate_up):
+        if units % LANES == 0:
+            outs = [(2 * units, jnp.bfloat16), (D, jnp.bfloat16)]
+            return ffn_call(ffn_back_kernel, layer, [branch, gate_up], all_gate_up, all_down, outs)
+        gate, up = gate_up[:, :units], gate_up[:, units:]
+        d_hidden = product(branch, down_w[layer])
+        sig = jax.nn.sigmoid(gate)
+        d_gate = d_hidden * up * sig * (1.0 + gate * (1.0 - sig))
+        d_up = d_hidden * gate * sig
+        d_gate_up = jnp.concatenate([d_gate, d_up], axis=1).astype(jnp.bfloat16)
+        return d_gate_up, dot_last(d_gate_up, gate_up_w[layer]).astype(jnp.bfloat16)
+
+    all_gate_up, all_down = gate_up_w.reshape(2 * D, -1), down_w.reshape(2 * D, -1)
     kept = []
     hidden_out = []
 
@@ -1219,11 +1264,8 @@
             cols_axis,
             behind=waited,
         )
-        gate_up = product(normed_two, gate_up_w[layer])
-        gate, up = gate_up[:, :units], gate_up[:, units:]
-        hidden = (jax.nn.silu(gate) * up).astype(jnp.bfloat16)
+        gate_up, hidden, partial = feed_forward(layer, normed_two)
         kept.append((stream, normed, spread, mixed, log_sums, attn_mix, after, normed_two, gate_up, hidden))
-        partial = product(hidden, down_w[layer].T)
         if layer == 0:
             stream, normed, spread = relay(
                 after_hidden,
@@ -1262,14 +1304,9 @@
 
     for layer in (1, 0):
         stream, normed, spread, mixed, log_sums, attn_mix, after, normed_two, gate_up, hidden = kept[layer]
-        gate, up = gate_up[:, :units], gate_up[:, units:]
-        d_hidden = product(branch, down_w[layer])
-        sig = jax.nn.sigmoid(gate)
-        d_gate = d_hidden * up * sig * (1.0 + gate * (1.0 - sig))
-        d_up = d_hidden * gate * sig
-        d_gate_up = jnp.concatenate([d_gate, d_up], axis=1).astype(jnp.bfloat16)
+        d_gate_up, partial = feed_back(layer, branch, gate_up)
         partial, down_term, gate_up_term = together(
-            dot_last(d_gate_up, gate_up_w[layer]).astype(jnp.bfloat16),
+            partial,
             dot_first(branch, hidden).astype(jnp.bfloat16),
             dot_first(normed_two, d_gate_up).astype(jnp.bfloat16),
         )
@@ -1298,7 +1335,7 @@
         out_sum = collect(layer, out_term)
         d_qkv, arrived[layer][1] = attend_back(
             10 + layer,
-            expand(d_mix) if layer == 1 else hold(expand(d_mix), [down_sum]),
+            expand(d_mix),
             spread,
             mixed,
             log_sums,

time: 1680 us -> 1700 us (1.012)
  Pallas kernels: 1210 us -> 1360 us
  matrix products: 266 us -> 144 us
    pallas_call x1 -> x4, Pallas kernels: 0.01 us -> 115 us  [ffn_call(): pl.pallas_call(functools.partial(kernel, units), grid=(tokens // rows,),...]
    dot_general x11 -> x5, matrix products: 125 us -> 37 us  [product(): return jnp.dot(left, right, preferred_element_type=jnp.float32)]
    dot_general x4 -> x2, matrix products: 59.2 us -> 23.4 us  [dot_last(): lax.dot_general(a, b, (((1,), (1,)), ((), ())), preferred_element_type=jn...]
    pallas_call x2, Pallas kernels: 206 us -> 238 us  [attend_back(): pl.pallas_call(functools.partial(attend_back_kernel, heads, n, bq, layer)...]
    reduce_scatter x6, waiting for transfers between devices: 30 us -> 0.04 us  [collect(): lax.psum_scatter(term, 'row', scatter_dimension=0, tiled=True)]
    all_gather x4, waiting for transfers between devices: 24 us -> 46.3 us  [weights_of(): return lax.all_gather(block, both, axis=0, tiled=True).reshape(2, D, -1)]
    unnamed x91 -> x79, local copies, waits for them, and re-layouts: 37.8 us -> 29.5 us
  transfers between devices with their start and end apart: 15 -> 15, of which waited for: 2 -> 1; matrix products, arithmetic and copies ran while one was open for 15% -> 12% of each run, Pallas kernels for 58% -> 61%
where the time goes in v8:
time: 1700 us; the launch traced here: 1690 us
  Pallas kernels  1360 us (80%)
  matrix products  144 us (8%)
  local copies, waits for them, and re-layouts  64.6 us (4%)
  waiting for transfers between devices  48.8 us (3%)
  other arithmetic  45.7 us (3%)
    pallas_call x7, Pallas kernels, relay(): pl.pallas_call(functools.partial(relay_kernel, middle, len(ins), len(outs...  795 us
    pallas_call x2, Pallas kernels, attend_back(): pl.pallas_call(functools.partial(attend_back_kernel, heads, n, bq, layer)...  238 us
    pallas_call x2, Pallas kernels, attend(): pl.pallas_call(functools.partial(attend_kernel, heads, n, bq, given), in_...  126 us
    pallas_call x4, Pallas kernels, ffn_call(): pl.pallas_call(functools.partial(kernel, units), grid=(tokens // rows,),...  115 us
    dot_general x8, matrix products, dot_first(): lax.dot_general(a, b, (((0,), (0,)), ((), ())), preferred_element_type=jn...  83.7 us
    pallas_call x1, Pallas kernels, gathered(): pl.pallas_call(functools.partial(gather_kernel, n, chunks, lag), in_specs...  82.2 us
    all_gather x4, waiting for transfers between devices, weights_of(): return lax.all_gather(block, both, axis=0, tiled=True).reshape(2, D, -1)  46.3 us
    dot_general x5, matrix products, product(): return jnp.dot(left, right, preferred_element_type=jnp.float32)  37 us
  transfers between devices with their start and end apart: 15, of which 1 were waited for; matrix products, arithmetic and copies ran while one was open for 12% of the time, Pallas kernels for 61%

profile of v8, /device:TPU:0, one launch (start us, length us, event | category | flops | bytes accessed | tf_op | source)
XLA Modules:
  0.0 1692.5 jit_solution(6762790905237447512)
XLA Ops:
  22.7 82.2 %shard_map.169 = (bf16[1024,2048]{1,0:T(8,128)(2,1)S(1)}, f32[2,4,8,512]{3,2,1,0:T(8,128)S(1)}, bf16[1024,2048]{1,0:T(8,128)(2,1)S(1)}, f32[4096,128]{1,0:T(8,128)S(1)}, f32[4096,128]{1,0:T(8,128)S(1)}) custom-call(bf16[1024,512]{1,0:T(8,128)(2,1)S(1)} %dynamic-slice_bitcast_fusion.2.own, f32[8,512]{1,0:T(8,128)S(1)} %maximum_maximum_fusion.small, ...), custom_call_target="tpu_custom_call" | custom-call | bytes 250000000 | tf_op jit(solution)/shard_map/pallas_call | solution.py:1079
  116.0 11.8 fusion.8.refs_0_
  127.8 73.4 %shard_map.170 = (bf16[3,4096,128]{2,1,0:T(8,128)(2,1)}, bf16[4096,128]{1,0:T(8,128)(2,1)}, f32[128,4096]{1,0:T(8,128)}, bf16[1024,512]{1,0:T(8,128)(2,1)}) custom-call(s32[4096,1]{1,0:T(8,128)} %copy.34.bid_q.bid_k, s32[1,4096]{1,0:T(1,128)} %constant_dynamic-slice_fusion.5.bid_k.bid_q, f32[1024,1536]{1,0:T(8,128)} %fusion.8.refs_0_, ...), custom_call_target="tpu_custom_call" | custom-call | flops 10000000000 | bytes 200000000 | tf_op jit(solution)/shard_map/pallas_call | solution.py:227
  207.5 113.5 %shard_map.171 = (bf16[16,4,16,2048]{3,2,1,0:T(8,128)(2,1)}, f32[16,16,2048]{2,1,0:T(8,128)}) custom-call(bf16[16,4,16,2048]{3,2,1,0:T(8,128)(2,1)} %bitcast.163, bf16[16,16,2048]{2,1,0:T(8,128)(2,1)} %dynamic-slice_bitcast_fusion.1.refs_0_.refs_1_, f32[1,2048]{1,0:T(1,128)} %get-tuple-element.176.refs_1_.refs_2_, f32[1,2048]{1,0:T(1,128)} %get-tuple-element.175.refs_2_, ...), custom_call_target="tpu_custom_call" | custom-call | bytes 350000000 | tf_op jit(solution)/shard_map/pallas_call | solution.py:906
  321.0 46.3 %all-gather.15.cloned.1.call-done.weight = bf16[4096,2816]{1,0:T(8,128)(2,1)} async-done(((bf16[512,2816]{1,0:T(8,128)(2,1)}), bf16[4096,2816]{1,0:T(8,128)(2,1)}) %all-gather.15.cloned.1.call-update) | async-done | bytes 23068688 | tf_op jit(solution)/shard_map/all_gather | solution.py:1190
  367.3 28.8 %shard_map.172 = (f32[1024,2816]{1,0:T(8,128)}, bf16[1024,1408]{1,0:T(8,128)(2,1)}, bf16[1024,2048]{1,0:T(8,128)(2,1)}) custom-call(bf16[1024,2048]{1,0:T(8,128)(2,1)} %bitcast.192, bf16[4096,2816]{1,0:T(8,128)(2,1)} %all-gather.15.cloned.1.call-done.weight, bf16[4096,1408]{1,0:T(8,128)(2,1)} %bitcast.188), custom_call_target="tpu_custom_call" | custom-call | flops 17716740096 | bytes 40000000 | tf_op jit(solution)/shard_map/pallas_call | solution.py:1126
  396.1 131.3 %shard_map.173 = (bf16[16,4,16,2048]{3,2,1,0:T(8,128)(2,1)}, bf16[16,4,16,2048]{3,2,1,0:T(8,128)(2,1)}, bf16[3,4096,128]{2,1,0:T(8,128)(2,1)}) custom-call(bf16[16,4,16,2048]{3,2,1,0:T(8,128)(2,1)} %bitcast.166, f32[16,16,2048]{2,1,0:T(8,128)} %get-tuple-element.84.refs_0_.refs_1_, f32[1,2048]{1,0:T(1,128)} %get-tuple-element.174.refs_1_.refs_2_, ...), custom_call_target="tpu_custom_call" | custom-call | bytes 350000000 | tf_op jit(solution)/shard_map/pallas_call | solution.py:906
  533.6 52.8 %shard_map.174 = (bf16[4096,128]{1,0:T(8,128)(2,1)}, f32[128,4096]{1,0:T(8,128)}, bf16[1024,512]{1,0:T(8,128)(2,1)}) custom-call(s32[4096,1]{1,0:T(8,128)} %copy.34.bid_q.bid_k, s32[1,4096]{1,0:T(1,128)} %constant_dynamic-slice_fusion.5.bid_k.bid_q, bf16[3,4096,128]{2,1,0:T(8,128)(2,1)} %get-tuple-element.86.refs_0_.spread), custom_call_target="tpu_custom_call" | custom-call | flops 10000000000 | bytes 200000000 | tf_op jit(solution)/shard_map/pallas_call | solution.py:227
  597.0 112.1 %shard_map.175 = (bf16[16,4,16,2048]{3,2,1,0:T(8,128)(2,1)}, f32[16,16,2048]{2,1,0:T(8,128)}) custom-call(bf16[16,4,16,2048]{3,2,1,0:T(8,128)(2,1)} %bitcast.162, bf16[16,16,2048]{2,1,0:T(8,128)(2,1)} %dynamic-slice_bitcast_fusion.refs_0_.refs_1_, f32[1,2048]{1,0:T(1,128)} %get-tuple-element.172.refs_1_.refs_2_, f32[1,2048]{1,0:T(1,128)} %get-tuple-element.171.refs_2_, ...), custom_call_target="tpu_custom_call" | custom-call | bytes 350000000 | tf_op jit(solution)/shard_map/pallas_call | solution.py:906
  709.2 29.3 %shard_map.176 = (f32[1024,2816]{1,0:T(8,128)}, bf16[1024,1408]{1,0:T(8,128)(2,1)}, f32[1024,2048]{1,0:T(8,128)}) custom-call(bf16[1024,2048]{1,0:T(8,128)(2,1)} %bitcast.199, bf16[4096,2816]{1,0:T(8,128)(2,1)} %all-gather.15.cloned.1.call-done.weight, bf16[4096,1408]{1,0:T(8,128)(2,1)} %bitcast.189), custom_call_target="tpu_custom_call" | custom-call | flops 17716740096 | bytes 40000000 | tf_op jit(solution)/shard_map/pallas_call | solution.py:1126
  738.5 10.4 convolution_convert_fusion.5
  748.9 28.4 %shard_map.177 = (bf16[1024,2816]{1,0:T(8,128)(2,1)}, bf16[1024,2048]{1,0:T(8,128)(2,1)}) custom-call(bf16[1024,2048]{1,0:T(8,128)(2,1)} %pad_maximum_fusion.1.branch, f32[1024,2816]{1,0:T(8,128)} %get-tuple-element.89.gate_up, bf16[4096,2816]{1,0:T(8,128)(2,1)} %all-gather.15.cloned.1.call-done.weight, bf16[4096,1408]{1,0:T(8,128)(2,1)} %bitcast.190), custom_call_target="tpu_custom_call" | custom-call | flops 17716740096 | bytes 40000000 | tf_op jit(solution)/shard_map/pallas_call | solution.py:1126
  777.3 18.2 %convolution_convert_fusion.1 = bf16[2048,2816]{1,0:T(8,128)(2,1)} fusion(bf16[1024,2048]{1,0:T(8,128)(2,1)} %bitcast.200, bf16[1024,2816]{1,0:T(8,128)(2,1)} %get-tuple-element.92), kind=kOutput, calls=%fused_computation.2 | convolution fusion | flops 11816927232 | bytes 21495808 | tf_op jit(solution)/shard_map/dot_general | solution.py:27
  798.5 115.7 %shard_map.178 = (bf16[16,4,16,2048]{3,2,1,0:T(8,128)(2,1)}, f32[16,16,2048]{2,1,0:T(8,128)}, f32[2,2048]{1,0:T(2,128)}) custom-call(bf16[16,4,16,2048]{3,2,1,0:T(8,128)(2,1)} %bitcast.160, f32[16,16,2048]{2,1,0:T(8,128)} %bitcast_convert_fusion.refs_0_, f32[16,16,2048]{2,1,0:T(8,128)} %get-tuple-element.94.refs_1_, f32[1,2048]{1,0:T(1,128)} %get-tuple-element.172.refs_1_.refs_2_), custom_call_target="tpu_custom_call" | custom-call | bytes 350000000 | tf_op jit(solution)/shard_map/pallas_call | solution.py:906
  936.2 108.5 %shard_map.179 = (bf16[1024,1536]{1,0:T(8,128)(2,1)}, bf16[512,2816]{1,0:T(8,128)(2,1)}) custom-call(s32[1,4096]{1,0:T(1,128)} %constant_dynamic-slice_fusion.5.bid_k.bid_q, s32[4096,1]{1,0:T(8,128)} %copy.34.bid_q.bid_k, bf16[1024,512]{1,0:T(8,128)(2,1)} %fusion.21.d_mix, bf16[3,4096,128]{2,1,0:T(8,128)(2,1)} %get-tuple-element.86.refs_0_.spread, ...), custom_call_target="tpu_custom_call" | custom-call | flops 10000000000 | bytes 300000000 | tf_op jit(solution)/shard_map/pallas_call | solution.py:410
  1047.1 12.2 fusion.15
  1068.0 104.9 %shard_map.180 = (bf16[16,4,16,2048]{3,2,1,0:T(8,128)(2,1)}, f32[16,16,2048]{2,1,0:T(8,128)}, f32[2,2048]{1,0:T(2,128)}) custom-call(bf16[16,4,16,2048]{3,2,1,0:T(8,128)(2,1)} %bitcast.161, f32[16,16,2048]{2,1,0:T(8,128)} %get-tuple-element.103.refs_0_, bf16[16,16,2048]{2,1,0:T(8,128)(2,1)} %dynamic-slice_bitcast_fusion.refs_0_.refs_1_, ...), custom_call_target="tpu_custom_call" | custom-call | bytes 350000000 | tf_op jit(solution)/shard_map/pallas_call | solution.py:906
  1172.9 28.1 %shard_map.181 = (bf16[1024,2816]{1,0:T(8,128)(2,1)}, bf16[1024,2048]{1,0:T(8,128)(2,1)}) custom-call(bf16[1024,2048]{1,0:T(8,128)(2,1)} %bitcast.176, f32[1024,2816]{1,0:T(8,128)} %get-tuple-element.106.gate_up, bf16[4096,2816]{1,0:T(8,128)(2,1)} %all-gather.15.cloned.1.call-done.weight, bf16[4096,1408]{1,0:T(8,128)(2,1)} %bitcast.191), custom_call_target="tpu_custom_call" | custom-call | flops 17716740096 | bytes 40000000 | tf_op jit(solution)/shard_map/pallas_call | solution.py:1126
  1201.0 11.0 convolution_convert_fusion.3
  1212.0 18.4 %convolution_convert_fusion = bf16[2048,2816]{1,0:T(8,128)(2,1)} fusion(bf16[1024,2048]{1,0:T(8,128)(2,1)} %bitcast.193, bf16[1024,2816]{1,0:T(8,128)(2,1)} %get-tuple-element.109), kind=kOutput, calls=%fused_computation.1 | convolution fusion | flops 11816927232 | bytes 21495808 | tf_op jit(solution)/shard_map/dot_general | solution.py:27
  1235.0 102.6 %shard_map.182 = (bf16[16,4,16,2048]{3,2,1,0:T(8,128)(2,1)}, f32[16,16,2048]{2,1,0:T(8,128)}, f32[2,2048]{1,0:T(2,128)}, bf16[1024,512]{1,0:T(8,128)(2,1)}, bf16...) custom-call(bf16[16,4,16,2048]{3,2,1,0:T(8,128)(2,1)} %bitcast.159, ...), custom_call_target="tpu_custom_call" | custom-call | bytes 350000000 | tf_op jit(solution)/shard_map/pallas_call | solution.py:906
  1357.5 129.4 %shard_map.183 = (bf16[1024,1536]{1,0:T(8,128)(2,1)}, bf16[512,2816]{1,0:T(8,128)(2,1)}) custom-call(s32[1,4096]{1,0:T(1,128)} %constant_dynamic-slice_fusion.5.bid_k.bid_q, s32[4096,1]{1,0:T(8,128)} %copy.34.bid_q.bid_k, bf16[1024,512]{1,0:T(8,128)(2,1)} %fusion.22.d_mix, bf16[3,4096,128]{2,1,0:T(8,128)(2,1)} %get-tuple-element.118.spread, ...), custom_call_target="tpu_custom_call" | custom-call | flops 10000000000 | bytes 300000000 | tf_op jit(solution)/shard_map/pallas_call | solution.py:410
  1489.4 11.3 fusion.12
  1548.0 114.7 %shard_map.184 = (bf16[2,16,4,16,512]{4,3,2,1,0:T(8,128)(2,1)}, f32[16,16,2048]{2,1,0:T(8,128)}, f32[2,2048]{1,0:T(2,128)}, f32[2,4,2,512]{3,2,1,0:T(2,128)}, bf...) custom-call(bf16[16,4,16,2048]{3,2,1,0:T(8,128)(2,1)} %bitcast.165, ...), custom_call_target="tpu_custom_call" | custom-call | bytes 350000000 | tf_op jit(solution)/shard_map/pallas_call | solution.py:906
  (186 shorter events, 180.7 us)
Async XLA Ops:
  7.2 14.8 copy-start
  7.2 108.8 %all-gather.13.cloned.1.call-start = ((), (), s32[]{:S(2)}) async-start(), calls=%async_computation.9 | async-start | bytes 14155776 | tf_op jit(solution)/shard_map/all_gather | solution.py:1190
  12.6 188.6 %all-gather.17.cloned.1.call-start = ((), (), s32[]{:S(2)}) async-start(), calls=%async_computation.19 | async-start | bytes 4718592 | tf_op jit(solution)/shard_map/all_gather | solution.py:1190
  13.3 194.2 %all-gather.19.cloned.1.call-start = ((), (), s32[]{:S(2)}) async-start(), calls=%async_computation.20 | async-start | bytes 2621440 | tf_op jit(solution)/shard_map/all_gather | solution.py:1242
  15.3 305.7 %all-gather.21.cloned.1.call-start = ((), (), s32[]{:S(2)}) async-start(), calls=%async_computation.21 | async-start | bytes 12976128 | tf_op jit(solution)/shard_map/all_gather | solution.py:1190
  15.9 351.4 %all-gather.15.cloned.1.call-start = ((), (), s32[]{:S(2)}) async-start(), calls=%async_computation.10 | async-start | bytes 25952256 | tf_op jit(solution)/shard_map/all_gather | solution.py:1190
  19.8 573.1 %all-gather.23.cloned.1.call-start = ((), (), s32[]{:S(2)}) async-start(), calls=%async_computation.22 | async-start | bytes 2621440 | tf_op jit(solution)/shard_map/all_gather | solution.py:1242
  531.2 405.0 %reduce-scatter.12.cloned.1.call-start = ((), (), s32[]{:S(2)}) async-start(), calls=%async_computation.11 | async-start | bytes 14417920 | tf_op jit(solution)/shard_map/reduce_scatter | solution.py:1298
  709.2 29.3 %copy-start.11 = (bf16[1,512,2048]{2,1,0:T(8,128)(2,1)S(1)}, bf16[1,512,2048]{2,1,0:T(8,128)(2,1)}, u32[]{:S(2)}) copy-start(bf16[1,512,2048]{2,1,0:T(8,128)(2,1)} %all-gather.23.cloned.1.call-done) | copy-start | bytes 6291460
  795.5 272.5 %reduce-scatter.14.cloned.1.call-start = ((), (), s32[]{:S(2)}) async-start(), calls=%async_computation.12 | async-start | bytes 5242880 | tf_op jit(solution)/shard_map/reduce_scatter | solution.py:1328
  798.5 118.2 %copy-start.10 = (f32[16,16,2048]{2,1,0:T(8,128)S(1)}, f32[16,16,2048]{2,1,0:T(8,128)}, u32[]{:S(2)}) copy-start(f32[16,16,2048]{2,1,0:T(8,128)} %get-tuple-element.94.refs_1_) | copy-start | bytes 6291460
  922.3 312.7 %reduce-scatter.16.cloned.1.call-start = ((), (), s32[]{:S(2)}) async-start(), calls=%async_computation.13 | async-start | bytes 2621440 | tf_op jit(solution)/shard_map/reduce_scatter | solution.py:1298
  935.5 299.4 %reduce-scatter.18.cloned.1.call-start = ((), (), s32[]{:S(2)}) async-start(), calls=%async_computation.14 | async-start | bytes 7208960 | tf_op jit(solution)/shard_map/reduce_scatter | solution.py:1298
  936.1 421.4 %reduce-scatter.20.cloned.1.call-start = ((), (), s32[]{:S(2)}) async-start(), calls=%async_computation.15 | async-start | bytes 14417920 | tf_op jit(solution)/shard_map/reduce_scatter | solution.py:1298
  1230.4 289.7 %reduce-scatter.28.cloned.1.call-start = ((), (), s32[]{:S(2)}) async-start(), calls=%async_computation.23 | async-start | bytes 1310720
  1235.0 102.6 %copy-start.23 = (f32[2,2048]{1,0:T(2,128)S(1)}, f32[2,2048]{1,0:T(2,128)}, u32[]{:S(2)}) copy-start(f32[2,2048]{1,0:T(2,128)} %get-tuple-element.127) | copy-start | bytes 49156
  1235.0 102.6 %copy-start.24 = (f32[2,2048]{1,0:T(2,128)S(1)}, f32[2,2048]{1,0:T(2,128)}, u32[]{:S(2)}) copy-start(f32[2,2048]{1,0:T(2,128)} %get-tuple-element.128) | copy-start | bytes 49156
  1346.7 201.3 %reduce-scatter.24.cloned.1.call-start = ((), (), s32[]{:S(2)}) async-start(), calls=%async_computation.17 | async-start | bytes 2621440 | tf_op jit(solution)/shard_map/reduce_scatter | solution.py:1298
  1356.9 191.1 %reduce-scatter.22.cloned.1.call-start = ((), (), s32[]{:S(2)}) async-start(), calls=%async_computation.16 | async-start | bytes 7208960 | tf_op jit(solution)/shard_map/reduce_scatter | solution.py:1298
  1357.4 321.6 %reduce-scatter.26.cloned.1.call-start = ((), (), s32[]{:S(2)}) async-start(), calls=%async_computation.18 | async-start | bytes 14155776 | tf_op jit(solution)/shard_map/reduce_scatter | solution.py:1360
  1489.4 18.7 %slice-start = ((s8[6291456]{0:T(1024)(128)(4,1)}), s8[4194304]{0:T(1024)(128)(4,1)S(1)}, s32[]{:S(2)}) async-start(s8[6291456]{0:T(1024)(128)(4,1)} %bitcast.157), calls=%async_computation.24 | async-start | bytes 8388608
  1548.0 122.8 %copy-start.15 = (bf16[512,512]{1,0:T(8,128)(2,1)S(1)}, bf16[512,512]{1,0:T(8,128)(2,1)}, u32[]{:S(2)}) copy-start(bf16[512,512]{1,0:T(8,128)(2,1)} %reduce-scatter.16.cloned.1.call-done.refs_6_) | copy-start | bytes 1572868
  1548.0 122.8 %copy-start.16 = (bf16[512,512]{1,0:T(8,128)(2,1)S(1)}, bf16[512,512]{1,0:T(8,128)(2,1)}, u32[]{:S(2)}) copy-start(bf16[512,512]{1,0:T(8,128)(2,1)} %reduce-scatter.24.cloned.1.call-done.refs_4_) | copy-start | bytes 1572868
  1548.0 122.8 %copy-start.20 = (bf16[512,512]{1,0:T(8,128)(2,1)S(1)}, bf16[512,512]{1,0:T(8,128)(2,1)}, u32[]{:S(2)}) copy-start(bf16[512,512]{1,0:T(8,128)(2,1)} %get-tuple-element.138) | copy-start | bytes 1572868
  (25 other events, 129.5 us)
Sparse Core Ops, SparseCore 0:
  12.7 76.2 all-gather.12
  90.8 36.6 all-gather.16
  129.1 45.9 all-gather.18
  176.9 71.5 all-gather.20
  250.8 116.4 all-gather.14
  531.3 44.7 all-gather.22
  795.6 91.8 reduce-scatter.11
  922.4 74.3 reduce-scatter.13
  1000.0 43.0 reduce-scatter.15
  1045.5 52.9 reduce-scatter.17
  1230.5 98.8 reduce-scatter.19
  1346.8 44.7 reduce-scatter.27
  1394.7 32.9 reduce-scatter.23
  1430.3 73.6 reduce-scatter.21
  1513.9 142.1 reduce-scatter.25

commit v9 on v8

--- a/solution.py
+++ b/solution.py
@@ -493,7 +493,9 @@
         ins, (gain, shift) = ins[:-2], ins[-2:]
         outs, polished = outs[:-1], outs[-1]
     if spread:
-        outs, all_sums = outs[:-1], outs[-1]
+        ins, more = ins[:-1], ins[-1]
+        outs, all_sums, all_more = outs[:-2], outs[-2], outs[-1]
+        *refs, more_sent, more_got = refs
     arrived, outgoing, total, sum_sent, sum_got, block_sent, block_got, carry_sent, carry_got, last_sent, last_got = refs
     section, i = lax.axis_index("section"), lax.axis_index("col")
     width = whole.shape[-1]
@@ -533,6 +535,35 @@
 
     def carry_copy(k):
         return remote(carry[k], carried[k], carry_sent.at[k], carry_got.at[k], "section", layers[k])
+
+    others = [(s, d) for s in range(2) for d in range(n) if (s, d) != (0, 0)] if spread else []
+
+    def more_copy(s, d):
+        to = lax.rem(i + d, n)
+        return pltpu.make_async_remote_copy(
+            src_ref=more.at[:, pl.ds(pl.multiple_of(to * width, 128), width)],
+            dst_ref=all_more.at[section, i],
+            send_sem=more_sent.at[s, d],
+            recv_sem=more_got.at[section, i],
+            device_id={"section": lax.rem(section + s, 2), "col": to},
+            device_id_type=pl.DeviceIdType.MESH,
+        )
+
+    def more_arrives(s, d):
+        from_s, from_d = lax.rem(section + s, 2), lax.rem(i + d, n)
+        return pltpu.make_async_remote_copy(
+            src_ref=more.at[:, pl.ds(0, width)],
+            dst_ref=all_more.at[from_s, from_d],
+            send_sem=more_sent.at[s, d],
+            recv_sem=more_got.at[from_s, from_d],
+            device_id={"section": from_s, "col": from_d},
+            device_id_type=pl.DeviceIdType.MESH,
+        )
+
+    for s, d in others:
+        more_copy(s, d).start()
+    if spread:
+        all_more[section, i] = more[:, pl.ds(pl.multiple_of(i * width, 128), width)]
 
     for k, layer in enumerate(layers):
         @pl.when(section != layer)
@@ -848,6 +879,10 @@
                 @pl.when((section == 0) & ((s == 1) | (o != i)))
                 def _(s=s, o=o):
                     sums_arrive(s, o).wait_recv()
+
+    for s, d in others:
+        more_copy(s, d).wait_send()
+        more_arrives(s, d).wait_recv()
 
     if parts:
         def settle_parts(b, carry):
@@ -884,7 +919,7 @@
     ins = [blocks(values) for values in ins] + list(polish) + list(project)
     parts = project[0].shape[1] // (n_row * LANES) if project else 0
     batches = chunks // max(1, min(chunks, LANES // (n * rows)))
-    outs = list(outs) + ([(tokens, features)] if polish else []) + ([(parts, n_row * tokens, LANES)] if parts else []) + ([(2, n, 2, features // n)] if spread else [])
+    outs = list(outs) + ([(tokens, features)] if polish else []) + ([(parts, n_row * tokens, LANES)] if parts else []) + ([(2, n, 2, features // n), (2, n, 8, features // n)] if spread else [])
     out_shapes = [
         jax.ShapeDtypeStruct(
             (2, chunks, n, rows, features // n) if spread else (chunks, n, rows, features), jnp.bfloat16
@@ -931,7 +966,8 @@
             ]
             if parts
             else []
-        ),
+        )
+        + ([pltpu.SemaphoreType.DMA((2, n)), pltpu.SemaphoreType.DMA((2, n))] if spread else []),
         compiler_params=pltpu.CompilerParams(
             collective_id=number, has_side_effects=True, vmem_limit_bytes=56 * 2**20
         ),
@@ -1213,7 +1249,7 @@
     ids = lax.dynamic_index_in_dim(block_ids, section, 0, keepdims=False)
     def feed_forward(layer, values):
         kind = jnp.bfloat16 if layer == 0 else jnp.float32
-        if units % LANES == 0:
+        if layer == 1 and units % LANES == 0:
             outs = [(2 * units, jnp.float32), (units, jnp.bfloat16), (D, kind)]
             return ffn_call(ffn_kernel, layer, [values], all_gate_up, all_down, outs)
         gate_up = product(values, gate_up_w[layer])
@@ -1236,13 +1272,14 @@
     kept = []
     hidden_out = []
 
-    def gathered_half(which, half):
+    def gathered_part(which, half):
         values = lax.dynamic_index_in_dim(cotangent, which, 0, keepdims=False)
-        values = values[half * (tokens // 2) : (half + 1) * (tokens // 2)]
+        cut = tokens * 3 // 8
+        values = values[cut:] if half else values[:cut]
         return lax.all_gather(values, "col", axis=1, tiled=True)
 
-    first_half = gathered_half(section, 0)
-    waited = [first_half]
+    first_part = gathered_part(section, 0)
+    waited = [first_part]
     for layer in range(2):
         if layer == 0:
             qkv = expand(product(normed, qkv_w[0]) + bias[0])
@@ -1251,8 +1288,8 @@
             )
         else:
             here = section + jnp.where(hidden_out[0][0, 0] == hidden_out[0][0, 0], 0, 1)
-            second_half = gathered_half(here, 1)
-            waited = [second_half]
+            second_part = gathered_part(here, 1)
+            waited = [second_part]
             spread, mixed, log_sums, attn_mix = attend(9, ids, heads, rows_axis, tokens, spread=spread)
         attn_mix = contract(attn_mix)
         normed_two, after = relay(
@@ -1285,7 +1322,7 @@
             blocks = blocks + jnp.where(owner, after.reshape(-1, 1, RELAY_ROWS, D), 0.0)
             result = blocks.reshape(tokens, D).astype(jnp.bfloat16)
 
-    branch = jnp.concatenate([first_half, second_half])
+    branch = jnp.concatenate([first_part, second_part])
     grad = mine(branch).astype(jnp.float32)
     weight_sums = [[], []]
     small_sums = []
@@ -1358,23 +1395,20 @@
         else:
             qkv_terms = lax.dynamic_update_slice(qkv_terms, qkv_term, (0, 0))
             qkv_grad = lax.psum_scatter(qkv_terms, both, scatter_dimension=0, tiled=True).astype(jnp.float32)
-        if layer == 0:
-            early_sums = lax.psum_scatter(jnp.stack(small_sums), "col", scatter_dimension=2, tiled=True)
-            early = jnp.concatenate([early_sums.reshape(6, -1), bias_grads[1].reshape(3, -1), bias_grads[0].reshape(3, -1)])
-            early = jnp.sum(lax.all_gather(early, both, axis=0), axis=0)
         branch, grad, sums_one, *got = relay(
             behind_norm,
             5 + layer,
             partial,
-            [d_after, mine(stream), gains[layer, :1]],
+            [d_after, mine(stream), gains[layer, :1]]
+            + ([] if layer == 1 else [jnp.concatenate(small_sums + [jnp.zeros((2, D), jnp.float32)])]),
             [(owned, D), (2, D)],
             cols_axis,
             spread=layer == 0,
             carry=[] if layer == 1 else [(0, down_sum), (0, out_sum), (1, weight_sums[1][0])],
-            behind=[hidden_out[1]] if layer == 1 else [early_sums],
+            behind=[hidden_out[1]] if layer == 1 else [],
         )
         if layer == 0:
-            late_sums, arrived[0][0], arrived[0][2], arrived[1][0] = got
+            late_sums, early_sums, arrived[0][0], arrived[0][2], arrived[1][0] = got
         small_sums += [sums_one]
         input_out[layer] = my_features(branch) if layer == 1 else branch
 
@@ -1387,7 +1421,10 @@
         + jnp.where(section == 0, first_got, second_got).astype(jnp.float32)
         for first, second, first_got, second_got in zip(*weight_sums, *arrived)
     )
-    last = lax.psum(jnp.sum(late_sums, axis=(0, 1)), "row")
+    early = 0.5 * jnp.sum(early_sums, axis=(0, 1))[:6]
+    last = jnp.where(section == 0, jnp.sum(late_sums, axis=(0, 1)), 0.0)
+    sums = lax.psum(jnp.concatenate([early, bias_grads[1].reshape(3, -1), bias_grads[0].reshape(3, -1), last]), both)
+    early, last = sums[:12], sums[12:]
     norm_sums = jnp.where(section == 0, jnp.stack([last, early[4:6]]), jnp.stack([early[2:4], early[0:2]]))
     bias_sum = jnp.where(section == 0, early[9:12], early[6:9])
     return (

time: 1700 us -> 1690 us (level)
  Pallas kernels: 1360 us -> 1320 us
  matrix products: 144 us -> 175 us
  waiting for transfers between devices: 48.8 us -> 19.9 us
  blocking collectives: 16.3 us -> 42.8 us
    psum x1, blocking collectives: 6.67 us -> 42.8 us  [per_device(): lax.psum(jnp.concatenate([early, bias_grads[1].reshape(3, -1), bias_grads...]
    pallas_call x4 -> x3, Pallas kernels: 115 us -> 85.4 us  [ffn_call(): pl.pallas_call(functools.partial(kernel, units), grid=(tokens // rows,),...]
    all_gather x4, waiting for transfers between devices: 46.3 us -> 17.2 us  [weights_of(): return lax.all_gather(block, both, axis=0, tiled=True).reshape(2, D, -1)]
    pallas_call x7, Pallas kernels: 795 us -> 775 us  [relay(): pl.pallas_call(functools.partial(relay_kernel, middle, len(ins), len(outs...]
    dot_general x5 -> x6, matrix products: 37 us -> 54.4 us  [product(): return jnp.dot(left, right, preferred_element_type=jnp.float32)]
    dot_general x2 -> x3, matrix products: 23.4 us -> 34.3 us  [dot_last(): lax.dot_general(a, b, (((1,), (1,)), ((), ())), preferred_element_type=jn...]
  transfers between devices with their start and end apart: 15 -> 14, of which waited for: 1 -> 1; matrix products, arithmetic and copies ran while one was open for 12% -> 13% of each run, Pallas kernels for 61% -> 60%
where the time goes in v9:
time: 1690 us; the launch traced here: 1680 us
  Pallas kernels  1320 us (78%)
  matrix products  175 us (10%)
  local copies, waits for them, and re-layouts  58.3 us (3%)
  other arithmetic  51.6 us (3%)
  blocking collectives  42.8 us (3%)
  waiting for transfers between devices  19.9 us (1%)
    pallas_call x7, Pallas kernels, relay(): pl.pallas_call(functools.partial(relay_kernel, middle, len(ins), len(outs...  775 us
    pallas_call x2, Pallas kernels, attend_back(): pl.pallas_call(functools.partial(attend_back_kernel, heads, n, bq, layer)...  250 us
    pallas_call x2, Pallas kernels, attend(): pl.pallas_call(functools.partial(attend_kernel, heads, n, bq, given), in_...  126 us
    dot_general x8, matrix products, dot_first(): lax.dot_general(a, b, (((0,), (0,)), ((), ())), preferred_element_type=jn...  86.5 us
    pallas_call x3, Pallas kernels, ffn_call(): pl.pallas_call(functools.partial(kernel, units), grid=(tokens // rows,),...  85.4 us
    pallas_call x1, Pallas kernels, gathered(): pl.pallas_call(functools.partial(gather_kernel, n, chunks, lag), in_specs...  82.3 us
    dot_general x6, matrix products, product(): return jnp.dot(left, right, preferred_element_type=jnp.float32)  54.4 us
    psum x1, blocking collectives, per_device(): lax.psum(jnp.concatenate([early, bias_grads[1].reshape(3, -1), bias_grads...  42.8 us
  transfers between devices with their start and end apart: 14, of which 1 were waited for; matrix products, arithmetic and copies ran while one was open for 13% of the time, Pallas kernels for 60%

profile of v9, /device:TPU:0, one launch (start us, length us, event | category | flops | bytes accessed | tf_op | source)
XLA Modules:
  0.0 1684.9 jit_solution(7677068946360973209)
XLA Ops:
  20.6 82.3 %shard_map.169 = (bf16[1024,2048]{1,0:T(8,128)(2,1)S(1)}, f32[2,4,8,512]{3,2,1,0:T(8,128)S(1)}, bf16[1024,2048]{1,0:T(8,128)(2,1)S(1)}, f32[4096,128]{1,0:T(8,128)S(1)}, f32[4096,128]{1,0:T(8,128)S(1)}) custom-call(bf16[1024,512]{1,0:T(8,128)(2,1)S(1)} %dynamic-slice_bitcast_fusion.2.own, f32[8,512]{1,0:T(8,128)S(1)} %maximum_maximum_fusion.1.small, ...), custom_call_target="tpu_custom_call" | custom-call | bytes 250000000 | tf_op jit(solution)/shard_map/pallas_call | solution.py:1115
  115.8 12.0 fusion.12.refs_0_
  127.8 73.2 %shard_map.170 = (bf16[3,4096,128]{2,1,0:T(8,128)(2,1)}, bf16[4096,128]{1,0:T(8,128)(2,1)}, f32[128,4096]{1,0:T(8,128)}, bf16[1024,512]{1,0:T(8,128)(2,1)}) custom-call(s32[4096,1]{1,0:T(8,128)} %copy.24.bid_q.bid_k, s32[1,4096]{1,0:T(1,128)} %constant_dynamic-slice_fusion.5.bid_k.bid_q, f32[1024,1536]{1,0:T(8,128)} %fusion.12.refs_0_, ...), custom_call_target="tpu_custom_call" | custom-call | flops 10000000000 | bytes 200000000 | tf_op jit(solution)/shard_map/pallas_call | solution.py:227
  207.4 112.1 %shard_map.171 = (bf16[16,4,16,2048]{3,2,1,0:T(8,128)(2,1)}, f32[16,16,2048]{2,1,0:T(8,128)}) custom-call(bf16[16,4,16,2048]{3,2,1,0:T(8,128)(2,1)} %bitcast.164, bf16[16,16,2048]{2,1,0:T(8,128)(2,1)} %dynamic-slice_bitcast_fusion.1.refs_0_.refs_1_, f32[1,2048]{1,0:T(1,128)} %get-tuple-element.163.refs_1_.refs_2_, f32[1,2048]{1,0:T(1,128)} %get-tuple-element.162.refs_2_, ...), custom_call_target="tpu_custom_call" | custom-call | bytes 350000000 | tf_op jit(solution)/shard_map/pallas_call | solution.py:941
  319.5 17.3 %fusion.gate_up = f32[1024,2816]{1,0:T(8,128)S(1)} fusion(bf16[1024,2048]{1,0:T(8,128)(2,1)} %bitcast.186, bf16[4096,2816]{1,0:T(8,128)(2,1)} %all-gather.13.cloned.1.call-done.weight), kind=kOutput, calls=%fused_computation.1 | convolution fusion | flops 11811160064 | bytes 27262976 | tf_op jit(solution)/shard_map/dot_general | solution.py:1181
  343.9 17.2 %all-gather.19.cloned.1.call-done = bf16[1,4096,1408]{2,1,0:T(8,128)(2,1)} async-done(((bf16[1,512,1408]{2,1,0:T(8,128)(2,1)}), bf16[1,4096,1408]{2,1,0:T(8,128)(2,1)}) %all-gather.19.cloned.1.call-update) | async-done | bytes 11534352 | tf_op jit(solution)/shard_map/all_gather | solution.py:1226
  361.1 10.9 fusion.19
  372.0 130.8 %shard_map.172 = (bf16[16,4,16,2048]{3,2,1,0:T(8,128)(2,1)}, bf16[16,4,16,2048]{3,2,1,0:T(8,128)(2,1)}, bf16[3,4096,128]{2,1,0:T(8,128)(2,1)}) custom-call(bf16[16,4,16,2048]{3,2,1,0:T(8,128)(2,1)} %bitcast.165, f32[16,16,2048]{2,1,0:T(8,128)} %get-tuple-element.81.refs_0_.refs_1_, f32[1,2048]{1,0:T(1,128)} %get-tuple-element.161.refs_1_.refs_2_, ...), custom_call_target="tpu_custom_call" | custom-call | bytes 350000000 | tf_op jit(solution)/shard_map/pallas_call | solution.py:941
  509.1 53.2 %shard_map.173 = (bf16[4096,128]{1,0:T(8,128)(2,1)}, f32[128,4096]{1,0:T(8,128)}, bf16[1024,512]{1,0:T(8,128)(2,1)}) custom-call(s32[4096,1]{1,0:T(8,128)} %copy.24.bid_q.bid_k, s32[1,4096]{1,0:T(1,128)} %constant_dynamic-slice_fusion.5.bid_k.bid_q, bf16[3,4096,128]{2,1,0:T(8,128)(2,1)} %get-tuple-element.83.refs_0_.spread), custom_call_target="tpu_custom_call" | custom-call | flops 10000000000 | bytes 200000000 | tf_op jit(solution)/shard_map/pallas_call | solution.py:227
  573.0 113.0 %shard_map.174 = (bf16[16,4,16,2048]{3,2,1,0:T(8,128)(2,1)}, f32[16,16,2048]{2,1,0:T(8,128)}) custom-call(bf16[16,4,16,2048]{3,2,1,0:T(8,128)(2,1)} %bitcast.163, bf16[16,16,2048]{2,1,0:T(8,128)(2,1)} %dynamic-slice_bitcast_fusion.refs_0_.refs_1_, f32[1,2048]{1,0:T(1,128)} %get-tuple-element.159.refs_1_.refs_2_, f32[1,2048]{1,0:T(1,128)} %get-tuple-element.158.refs_2_, ...), custom_call_target="tpu_custom_call" | custom-call | bytes 350000000 | tf_op jit(solution)/shard_map/pallas_call | solution.py:941
  686.0 29.2 %shard_map.175 = (f32[1024,2816]{1,0:T(8,128)}, bf16[1024,1408]{1,0:T(8,128)(2,1)}, f32[1024,2048]{1,0:T(8,128)}) custom-call(bf16[1024,2048]{1,0:T(8,128)(2,1)} %bitcast.193, bf16[4096,2816]{1,0:T(8,128)(2,1)} %all-gather.13.cloned.1.call-done.weight, bf16[4096,1408]{1,0:T(8,128)(2,1)} %bitcast.183), custom_call_target="tpu_custom_call" | custom-call | flops 17716740096 | bytes 40000000 | tf_op jit(solution)/shard_map/pallas_call | solution.py:1162
  715.2 28.0 %shard_map.176 = (bf16[1024,2816]{1,0:T(8,128)(2,1)}, bf16[1024,2048]{1,0:T(8,128)(2,1)}) custom-call(bf16[1024,2048]{1,0:T(8,128)(2,1)} %pad_maximum_fusion.1.branch, f32[1024,2816]{1,0:T(8,128)} %get-tuple-element.86.gate_up, bf16[4096,2816]{1,0:T(8,128)(2,1)} %all-gather.13.cloned.1.call-done.weight, bf16[4096,1408]{1,0:T(8,128)(2,1)} %bitcast.184), custom_call_target="tpu_custom_call" | custom-call | flops 17716740096 | bytes 40000000 | tf_op jit(solution)/shard_map/pallas_call | solution.py:1162
  743.2 18.6 %convolution_convert_fusion.1 = bf16[2048,2816]{1,0:T(8,128)(2,1)} fusion(bf16[1024,2048]{1,0:T(8,128)(2,1)} %bitcast.194, bf16[1024,2816]{1,0:T(8,128)(2,1)} %get-tuple-element.89), kind=kOutput, calls=%fused_computation.4 | convolution fusion | flops 11816927232 | bytes 21495808 | tf_op jit(solution)/shard_map/dot_general | solution.py:27
  775.7 114.6 %shard_map.177 = (bf16[16,4,16,2048]{3,2,1,0:T(8,128)(2,1)}, f32[16,16,2048]{2,1,0:T(8,128)}, f32[2,2048]{1,0:T(2,128)}) custom-call(bf16[16,4,16,2048]{3,2,1,0:T(8,128)(2,1)} %bitcast.160, f32[16,16,2048]{2,1,0:T(8,128)} %bitcast_convert_fusion.refs_0_, f32[16,16,2048]{2,1,0:T(8,128)} %get-tuple-element.91.refs_1_, f32[1,2048]{1,0:T(1,128)} %get-tuple-element.159.refs_1_.refs_2_), custom_call_target="tpu_custom_call" | custom-call | bytes 350000000 | tf_op jit(solution)/shard_map/pallas_call | solution.py:941
  912.3 108.3 %shard_map.178 = (bf16[1024,1536]{1,0:T(8,128)(2,1)}, bf16[512,2816]{1,0:T(8,128)(2,1)}) custom-call(s32[1,4096]{1,0:T(1,128)} %constant_dynamic-slice_fusion.5.bid_k.bid_q, s32[4096,1]{1,0:T(8,128)} %copy.24.bid_q.bid_k, bf16[1024,512]{1,0:T(8,128)(2,1)} %fusion.26.d_mix, bf16[3,4096,128]{2,1,0:T(8,128)(2,1)} %get-tuple-element.83.refs_0_.spread, ...), custom_call_target="tpu_custom_call" | custom-call | flops 10000000000 | bytes 300000000 | tf_op jit(solution)/shard_map/pallas_call | solution.py:410
  1023.0 12.2 fusion.20
  1043.8 105.5 %shard_map.179 = (bf16[16,4,16,2048]{3,2,1,0:T(8,128)(2,1)}, f32[16,16,2048]{2,1,0:T(8,128)}, f32[2,2048]{1,0:T(2,128)}) custom-call(bf16[16,4,16,2048]{3,2,1,0:T(8,128)(2,1)} %bitcast.161, f32[16,16,2048]{2,1,0:T(8,128)} %get-tuple-element.100.refs_0_, bf16[16,16,2048]{2,1,0:T(8,128)(2,1)} %dynamic-slice_bitcast_fusion.refs_0_.refs_1_, ...), custom_call_target="tpu_custom_call" | custom-call | bytes 350000000 | tf_op jit(solution)/shard_map/pallas_call | solution.py:941
  1149.3 28.2 %shard_map.180 = (bf16[1024,2816]{1,0:T(8,128)(2,1)}, bf16[1024,2048]{1,0:T(8,128)(2,1)}) custom-call(bf16[1024,2048]{1,0:T(8,128)(2,1)} %bitcast.175, f32[1024,2816]{1,0:T(8,128)} %copy-done.8, bf16[4096,2816]{1,0:T(8,128)(2,1)} %all-gather.13.cloned.1.call-done.weight, bf16[4096,1408]{1,0:T(8,128)(2,1)} %bitcast.185), custom_call_target="tpu_custom_call" | custom-call | flops 17716740096 | bytes 40000000 | tf_op jit(solution)/shard_map/pallas_call | solution.py:1162
  1188.4 18.4 %convolution_convert_fusion = bf16[2048,2816]{1,0:T(8,128)(2,1)} fusion(bf16[1024,2048]{1,0:T(8,128)(2,1)} %bitcast.187, bf16[1024,2816]{1,0:T(8,128)(2,1)} %get-tuple-element.104), kind=kOutput, calls=%fused_computation.3 | convolution fusion | flops 11816927232 | bytes 21495808 | tf_op jit(solution)/shard_map/dot_general | solution.py:27
  1211.3 102.4 %shard_map.181 = (bf16[16,4,16,2048]{3,2,1,0:T(8,128)(2,1)}, f32[16,16,2048]{2,1,0:T(8,128)}, f32[2,2048]{1,0:T(2,128)}, bf16[1024,512]{1,0:T(8,128)(2,1)}, bf16...) custom-call(bf16[16,4,16,2048]{3,2,1,0:T(8,128)(2,1)} %bitcast.159, ...), custom_call_target="tpu_custom_call" | custom-call | bytes 350000000 | tf_op jit(solution)/shard_map/pallas_call | solution.py:941
  1327.0 142.0 %shard_map.182 = (bf16[1024,1536]{1,0:T(8,128)(2,1)}, bf16[512,2816]{1,0:T(8,128)(2,1)}) custom-call(s32[1,4096]{1,0:T(1,128)} %constant_dynamic-slice_fusion.5.bid_k.bid_q, s32[4096,1]{1,0:T(8,128)} %copy.24.bid_q.bid_k, bf16[1024,512]{1,0:T(8,128)(2,1)} %fusion.27.d_mix, bf16[3,4096,128]{2,1,0:T(8,128)(2,1)} %get-tuple-element.113.spread, ...), custom_call_target="tpu_custom_call" | custom-call | flops 10000000000 | bytes 300000000 | tf_op jit(solution)/shard_map/pallas_call | solution.py:410
  1471.4 11.3 fusion.16
  1520.7 96.6 %shard_map.183 = (bf16[2,16,4,16,512]{4,3,2,1,0:T(8,128)(2,1)}, f32[16,16,2048]{2,1,0:T(8,128)}, f32[2,2048]{1,0:T(2,128)}, f32[2,4,2,512]{3,2,1,0:T(2,128)}, f3...) custom-call(bf16[16,4,16,2048]{3,2,1,0:T(8,128)(2,1)} %bitcast.162, ...), custom_call_target="tpu_custom_call" | custom-call | bytes 350000000 | tf_op jit(solution)/shard_map/pallas_call | solution.py:941
  1619.0 42.8 %psum.7 = f32[14,512]{1,0:T(8,128)S(1)} all-reduce(f32[14,512]{1,0:T(8,128)S(1)} %pad_maximum_fusion.3), channel_id=1, replica_groups=mesh['section'=2,'row'=4,'col'=4] {'section','row'}, use_global_device_ids=true, to_apply=%region_11.12 | all-reduce | flops 7168 | bytes 57344 | tf_op jit(solution)/shard_map/psum | solution.py:1426
  (187 shorter events, 188.3 us)
Async XLA Ops:
  7.2 12.7 copy-start
  7.2 108.6 %all-gather.11.cloned.1.call-start = ((), (), s32[]{:S(2)}) async-start(), calls=%async_computation.8 | async-start | bytes 14155776 | tf_op jit(solution)/shard_map/all_gather | solution.py:1226
  12.6 188.5 %all-gather.15.cloned.1.call-start = ((), (), s32[]{:S(2)}) async-start(), calls=%async_computation.18 | async-start | bytes 4718592 | tf_op jit(solution)/shard_map/all_gather | solution.py:1226
  13.3 194.1 %all-gather.17.cloned.1.call-start = ((), (), s32[]{:S(2)}) async-start(), calls=%async_computation.19 | async-start | bytes 1966080 | tf_op jit(solution)/shard_map/all_gather | solution.py:1279
  15.2 304.4 %all-gather.13.cloned.1.call-start = ((), (), s32[]{:S(2)}) async-start(), calls=%async_computation.9 | async-start | bytes 25952256 | tf_op jit(solution)/shard_map/all_gather | solution.py:1226
  19.1 90.6 %copy-start.24 = (s32[2,4096]{1,0:T(2,128)S(1)}, s32[2,4096]{1,0:T(2,128)}, u32[]{:S(2)}) copy-start(s32[2,4096]{1,0:T(2,128)} %param.12) | copy-start | bytes 98308
  19.1 342.0 %all-gather.19.cloned.1.call-start = ((), (), s32[]{:S(2)}) async-start(), calls=%async_computation.20 | async-start | bytes 12976128 | tf_op jit(solution)/shard_map/all_gather | solution.py:1226
  19.7 549.0 %all-gather.21.cloned.1.call-start = ((), (), s32[]{:S(2)}) async-start(), calls=%async_computation.21 | async-start | bytes 3276800 | tf_op jit(solution)/shard_map/all_gather | solution.py:1279
  506.7 405.5 %reduce-scatter.9.cloned.1.call-start = ((), (), s32[]{:S(2)}) async-start(), calls=%async_computation.10 | async-start | bytes 14417920 | tf_op jit(solution)/shard_map/reduce_scatter | solution.py:1335
  772.7 271.2 %reduce-scatter.11.cloned.1.call-start = ((), (), s32[]{:S(2)}) async-start(), calls=%async_computation.11 | async-start | bytes 5242880 | tf_op jit(solution)/shard_map/reduce_scatter | solution.py:1365
  775.7 117.1 %copy-start.10 = (f32[16,16,2048]{2,1,0:T(8,128)S(1)}, f32[16,16,2048]{2,1,0:T(8,128)}, u32[]{:S(2)}) copy-start(f32[16,16,2048]{2,1,0:T(8,128)} %get-tuple-element.91.refs_1_) | copy-start | bytes 6291460
  898.3 313.0 %reduce-scatter.13.cloned.1.call-start = ((), (), s32[]{:S(2)}) async-start(), calls=%async_computation.12 | async-start | bytes 2621440 | tf_op jit(solution)/shard_map/reduce_scatter | solution.py:1335
  911.6 299.7 %reduce-scatter.15.cloned.1.call-start = ((), (), s32[]{:S(2)}) async-start(), calls=%async_computation.13 | async-start | bytes 7208960 | tf_op jit(solution)/shard_map/reduce_scatter | solution.py:1335
  912.2 414.8 %reduce-scatter.17.cloned.1.call-start = ((), (), s32[]{:S(2)}) async-start(), calls=%async_computation.14 | async-start | bytes 14417920 | tf_op jit(solution)/shard_map/reduce_scatter | solution.py:1335
  1023.0 12.2 copy-start.14
  1149.3 28.2 %copy-start.17 = (bf16[1024,1408]{1,0:T(8,128)(2,1)S(1)}, bf16[1024,1408]{1,0:T(8,128)(2,1)}, u32[]{:S(2)}) copy-start(bf16[1024,1408]{1,0:T(8,128)(2,1)} %fusion.7) | copy-start | bytes 8650756
  1206.8 313.9 %reduce-scatter.21.cloned.1.call-start = ((), (), s32[]{:S(2)}) async-start(), calls=%async_computation.16 | async-start | bytes 2621440 | tf_op jit(solution)/shard_map/reduce_scatter | solution.py:1335
  1211.3 102.4 %copy-start.32 = (bf16[1024,512]{1,0:T(8,128)(2,1)S(1)}, bf16[1024,512]{1,0:T(8,128)(2,1)}, u32[]{:S(2)}) copy-start(bf16[1024,512]{1,0:T(8,128)(2,1)} %get-tuple-element.78) | copy-start | bytes 3145732
  1325.8 194.9 %reduce-scatter.19.cloned.1.call-start = ((), (), s32[]{:S(2)}) async-start(), calls=%async_computation.15 | async-start | bytes 7208960 | tf_op jit(solution)/shard_map/reduce_scatter | solution.py:1335
  1326.5 344.9 %reduce-scatter.23.cloned.1.call-start = ((), (), s32[]{:S(2)}) async-start(), calls=%async_computation.17 | async-start | bytes 14155776 | tf_op jit(solution)/shard_map/reduce_scatter | solution.py:1397
  1471.4 18.7 %slice-start = ((s8[6291456]{0:T(1024)(128)(4,1)}), s8[4194304]{0:T(1024)(128)(4,1)S(1)}, s32[]{:S(2)}) async-start(s8[6291456]{0:T(1024)(128)(4,1)} %bitcast.154), calls=%async_computation.22 | async-start | bytes 8388608
  1520.7 142.5 %copy-start.18 = (bf16[512,512]{1,0:T(8,128)(2,1)S(1)}, bf16[512,512]{1,0:T(8,128)(2,1)}, u32[]{:S(2)}) copy-start(bf16[512,512]{1,0:T(8,128)(2,1)} %reduce-scatter.13.cloned.1.call-done.refs_6_) | copy-start | bytes 1572868
  1520.7 142.5 %copy-start.19 = (bf16[512,512]{1,0:T(8,128)(2,1)S(1)}, bf16[512,512]{1,0:T(8,128)(2,1)}, u32[]{:S(2)}) copy-start(bf16[512,512]{1,0:T(8,128)(2,1)} %reduce-scatter.21.cloned.1.call-done.refs_5_) | copy-start | bytes 1572868
  1520.7 142.5 %copy-start.23 = (bf16[512,512]{1,0:T(8,128)(2,1)S(1)}, bf16[512,512]{1,0:T(8,128)(2,1)}, u32[]{:S(2)}) copy-start(bf16[512,512]{1,0:T(8,128)(2,1)} %get-tuple-element.134) | copy-start | bytes 1572868
  (26 other events, 128.1 us)
Sparse Core Ops, SparseCore 0:
  12.7 75.9 all-gather.10
  90.5 36.7 all-gather.14
  128.8 37.0 all-gather.16
  168.3 123.3 all-gather.12
  293.4 67.6 all-gather.18
  506.8 53.5 all-gather.20
  772.8 90.8 reduce-scatter.8
  898.4 74.4 reduce-scatter.10
  976.2 42.8 reduce-scatter.12
  1021.5 52.8 reduce-scatter.14
  1206.9 98.3 reduce-scatter.16
  1325.9 52.0 reduce-scatter.20
  1380.5 82.3 reduce-scatter.18
  1495.9 140.3 reduce-scatter.22

commit v10 on v9

--- a/solution.py
+++ b/solution.py
@@ -919,7 +919,7 @@
     ins = [blocks(values) for values in ins] + list(polish) + list(project)
     parts = project[0].shape[1] // (n_row * LANES) if project else 0
     batches = chunks // max(1, min(chunks, LANES // (n * rows)))
-    outs = list(outs) + ([(tokens, features)] if polish else []) + ([(parts, n_row * tokens, LANES)] if parts else []) + ([(2, n, 2, features // n), (2, n, 8, features // n)] if spread else [])
+    outs = list(outs) + ([(tokens, features)] if polish else []) + ([(parts, n_row * tokens, LANES)] if parts else []) + ([(2, n, 2, features // n), (2, n, 16, features // n)] if spread else [])
     out_shapes = [
         jax.ShapeDtypeStruct(
             (2, chunks, n, rows, features // n) if spread else (chunks, n, rows, features), jnp.bfloat16
@@ -1274,7 +1274,7 @@
 
     def gathered_part(which, half):
         values = lax.dynamic_index_in_dim(cotangent, which, 0, keepdims=False)
-        cut = tokens * 3 // 8
+        cut = tokens // 4
         values = values[cut:] if half else values[:cut]
         return lax.all_gather(values, "col", axis=1, tiled=True)
 
@@ -1339,6 +1339,11 @@
     def together(*values):
         return lax.optimization_barrier(values)
 
+    def more_sums():
+        rows = jnp.concatenate([bias_grads[1].reshape(3, -1), bias_grads[0].reshape(3, -1)])
+        rows = lax.dynamic_update_slice(jnp.zeros((10, D), jnp.float32), rows, (0, col * width))
+        return jnp.concatenate(small_sums + [rows])
+
     for layer in (1, 0):
         stream, normed, spread, mixed, log_sums, attn_mix, after, normed_two, gate_up, hidden = kept[layer]
         d_gate_up, partial = feed_back(layer, branch, gate_up)
@@ -1400,7 +1405,7 @@
             5 + layer,
             partial,
             [d_after, mine(stream), gains[layer, :1]]
-            + ([] if layer == 1 else [jnp.concatenate(small_sums + [jnp.zeros((2, D), jnp.float32)])]),
+            + ([] if layer == 1 else [more_sums()]),
             [(owned, D), (2, D)],
             cols_axis,
             spread=layer == 0,
@@ -1421,9 +1426,7 @@
         + jnp.where(section == 0, first_got, second_got).astype(jnp.float32)
         for first, second, first_got, second_got in zip(*weight_sums, *arrived)
     )
-    early = 0.5 * jnp.sum(early_sums, axis=(0, 1))[:6]
-    last = jnp.where(section == 0, jnp.sum(late_sums, axis=(0, 1)), 0.0)
-    sums = lax.psum(jnp.concatenate([early, bias_grads[1].reshape(3, -1), bias_grads[0].reshape(3, -1), last]), both)
+    sums = lax.psum(jnp.concatenate([jnp.sum(early_sums, axis=(0, 1))[:12], jnp.sum(late_sums, axis=(0, 1))]), "row")
     early, last = sums[:12], sums[12:]
     norm_sums = jnp.where(section == 0, jnp.stack([last, early[4:6]]), jnp.stack([early[2:4], early[0:2]]))
     bias_sum = jnp.where(section == 0, early[9:12], early[6:9])

time: 1690 us -> 1680 us (level)
  transfers between devices with their start and end apart: 14 -> 14, of which waited for: 1 -> 2; matrix products, arithmetic and copies ran while one was open for 13% -> 13% of each run, Pallas kernels for 60% -> 61%
where the time goes in v10:
time: 1680 us; the launch traced here: 1670 us
  Pallas kernels  1320 us (79%)
  matrix products  177 us (11%)
  local copies, waits for them, and re-layouts  59.1 us (4%)
  other arithmetic  51 us (3%)
  blocking collectives  30.6 us (2%)
    pallas_call x7, Pallas kernels, relay(): pl.pallas_call(functools.partial(relay_kernel, middle, len(ins), len(outs...  778 us
    pallas_call x2, Pallas kernels, attend_back(): pl.pallas_call(functools.partial(attend_back_kernel, heads, n, bq, layer)...  251 us
    pallas_call x2, Pallas kernels, attend(): pl.pallas_call(functools.partial(attend_kernel, heads, n, bq, given), in_...  126 us
    dot_general x8, matrix products, dot_first(): lax.dot_general(a, b, (((0,), (0,)), ((), ())), preferred_element_type=jn...  86.6 us
    pallas_call x3, Pallas kernels, ffn_call(): pl.pallas_call(functools.partial(kernel, units), grid=(tokens // rows,),...  85.4 us
    pallas_call x1, Pallas kernels, gathered(): pl.pallas_call(functools.partial(gather_kernel, n, chunks, lag), in_specs...  82.3 us
    dot_general x6, matrix products, product(): return jnp.dot(left, right, preferred_element_type=jnp.float32)  55.9 us
    dot_general x3, matrix products, dot_last(): lax.dot_general(a, b, (((1,), (1,)), ((), ())), preferred_element_type=jn...  34 us
  transfers between devices with their start and end apart: 14, of which 2 were waited for; matrix products, arithmetic and copies ran while one was open for 13% of the time, Pallas kernels for 61%

profile of v10, /device:TPU:0, one launch (start us, length us, event | category | flops | bytes accessed | tf_op | source)
XLA Modules:
  0.0 1671.2 jit_solution(4893908163210872109)
XLA Ops:
  20.5 82.3 %shard_map.169 = (bf16[1024,2048]{1,0:T(8,128)(2,1)S(1)}, f32[2,4,8,512]{3,2,1,0:T(8,128)S(1)}, bf16[1024,2048]{1,0:T(8,128)(2,1)S(1)}, f32[4096,128]{1,0:T(8,128)S(1)}, f32[4096,128]{1,0:T(8,128)S(1)}) custom-call(bf16[1024,512]{1,0:T(8,128)(2,1)S(1)} %dynamic-slice_bitcast_fusion.2.own, f32[8,512]{1,0:T(8,128)S(1)} %maximum_maximum_fusion.small, ...), custom_call_target="tpu_custom_call" | custom-call | bytes 250000000 | tf_op jit(solution)/shard_map/pallas_call | solution.py:1115
  115.7 11.8 fusion.12.refs_0_
  127.5 73.2 %shard_map.170 = (bf16[3,4096,128]{2,1,0:T(8,128)(2,1)}, bf16[4096,128]{1,0:T(8,128)(2,1)}, f32[128,4096]{1,0:T(8,128)}, bf16[1024,512]{1,0:T(8,128)(2,1)}) custom-call(s32[4096,1]{1,0:T(8,128)} %copy.24.bid_q.bid_k, s32[1,4096]{1,0:T(1,128)} %constant_dynamic-slice_fusion.5.bid_k.bid_q, f32[1024,1536]{1,0:T(8,128)} %fusion.12.refs_0_, ...), custom_call_target="tpu_custom_call" | custom-call | flops 10000000000 | bytes 200000000 | tf_op jit(solution)/shard_map/pallas_call | solution.py:227
  207.0 111.4 %shard_map.171 = (bf16[16,4,16,2048]{3,2,1,0:T(8,128)(2,1)}, f32[16,16,2048]{2,1,0:T(8,128)}) custom-call(bf16[16,4,16,2048]{3,2,1,0:T(8,128)(2,1)} %bitcast.160, bf16[16,16,2048]{2,1,0:T(8,128)(2,1)} %dynamic-slice_bitcast_fusion.1.refs_0_.refs_1_, f32[1,2048]{1,0:T(1,128)} %get-tuple-element.163.refs_1_.refs_2_, f32[1,2048]{1,0:T(1,128)} %get-tuple-element.162.refs_2_, ...), custom_call_target="tpu_custom_call" | custom-call | bytes 350000000 | tf_op jit(solution)/shard_map/pallas_call | solution.py:941
  318.4 19.1 %fusion.gate_up = f32[1024,2816]{1,0:T(8,128)S(1)} fusion(bf16[1024,2048]{1,0:T(8,128)(2,1)} %bitcast.188, bf16[4096,2816]{1,0:T(8,128)(2,1)} %all-gather.13.cloned.1.call-done.weight), kind=kOutput, calls=%fused_computation.1 | convolution fusion | flops 11811160064 | bytes 27262976 | tf_op jit(solution)/shard_map/dot_general | solution.py:1181
  354.9 10.9 fusion.19
  365.8 130.8 %shard_map.172 = (bf16[16,4,16,2048]{3,2,1,0:T(8,128)(2,1)}, bf16[16,4,16,2048]{3,2,1,0:T(8,128)(2,1)}, bf16[3,4096,128]{2,1,0:T(8,128)(2,1)}) custom-call(bf16[16,4,16,2048]{3,2,1,0:T(8,128)(2,1)} %bitcast.163, f32[16,16,2048]{2,1,0:T(8,128)} %get-tuple-element.81.refs_0_.refs_1_, f32[1,2048]{1,0:T(1,128)} %get-tuple-element.161.refs_1_.refs_2_, ...), custom_call_target="tpu_custom_call" | custom-call | bytes 350000000 | tf_op jit(solution)/shard_map/pallas_call | solution.py:941
  503.0 53.2 %shard_map.173 = (bf16[4096,128]{1,0:T(8,128)(2,1)}, f32[128,4096]{1,0:T(8,128)}, bf16[1024,512]{1,0:T(8,128)(2,1)}) custom-call(s32[4096,1]{1,0:T(8,128)} %copy.24.bid_q.bid_k, s32[1,4096]{1,0:T(1,128)} %constant_dynamic-slice_fusion.5.bid_k.bid_q, bf16[3,4096,128]{2,1,0:T(8,128)(2,1)} %get-tuple-element.83.refs_0_.spread), custom_call_target="tpu_custom_call" | custom-call | flops 10000000000 | bytes 200000000 | tf_op jit(solution)/shard_map/pallas_call | solution.py:227
  567.5 114.3 %shard_map.174 = (bf16[16,4,16,2048]{3,2,1,0:T(8,128)(2,1)}, f32[16,16,2048]{2,1,0:T(8,128)}) custom-call(bf16[16,4,16,2048]{3,2,1,0:T(8,128)(2,1)} %bitcast.162, bf16[16,16,2048]{2,1,0:T(8,128)(2,1)} %dynamic-slice_bitcast_fusion.refs_0_.refs_1_, f32[1,2048]{1,0:T(1,128)} %get-tuple-element.159.refs_1_.refs_2_, f32[1,2048]{1,0:T(1,128)} %get-tuple-element.158.refs_2_, ...), custom_call_target="tpu_custom_call" | custom-call | bytes 350000000 | tf_op jit(solution)/shard_map/pallas_call | solution.py:941
  681.8 29.2 %shard_map.175 = (f32[1024,2816]{1,0:T(8,128)}, bf16[1024,1408]{1,0:T(8,128)(2,1)}, f32[1024,2048]{1,0:T(8,128)}) custom-call(bf16[1024,2048]{1,0:T(8,128)(2,1)} %bitcast.195, bf16[4096,2816]{1,0:T(8,128)(2,1)} %all-gather.13.cloned.1.call-done.weight, bf16[4096,1408]{1,0:T(8,128)(2,1)} %bitcast.185), custom_call_target="tpu_custom_call" | custom-call | flops 17716740096 | bytes 40000000 | tf_op jit(solution)/shard_map/pallas_call | solution.py:1162
  711.0 28.0 %shard_map.176 = (bf16[1024,2816]{1,0:T(8,128)(2,1)}, bf16[1024,2048]{1,0:T(8,128)(2,1)}) custom-call(bf16[1024,2048]{1,0:T(8,128)(2,1)} %pad_maximum_fusion.1.branch, f32[1024,2816]{1,0:T(8,128)} %get-tuple-element.86.gate_up, bf16[4096,2816]{1,0:T(8,128)(2,1)} %all-gather.13.cloned.1.call-done.weight, bf16[4096,1408]{1,0:T(8,128)(2,1)} %bitcast.186), custom_call_target="tpu_custom_call" | custom-call | flops 17716740096 | bytes 40000000 | tf_op jit(solution)/shard_map/pallas_call | solution.py:1162
  739.0 18.6 %convolution_convert_fusion.1 = bf16[2048,2816]{1,0:T(8,128)(2,1)} fusion(bf16[1024,2048]{1,0:T(8,128)(2,1)} %bitcast.196, bf16[1024,2816]{1,0:T(8,128)(2,1)} %get-tuple-element.89), kind=kOutput, calls=%fused_computation.4 | convolution fusion | flops 11816927232 | bytes 21495808 | tf_op jit(solution)/shard_map/dot_general | solution.py:27
  771.5 113.6 %shard_map.177 = (bf16[16,4,16,2048]{3,2,1,0:T(8,128)(2,1)}, f32[16,16,2048]{2,1,0:T(8,128)}, f32[2,2048]{1,0:T(2,128)}) custom-call(bf16[16,4,16,2048]{3,2,1,0:T(8,128)(2,1)} %bitcast.158, f32[16,16,2048]{2,1,0:T(8,128)} %bitcast_convert_fusion.refs_0_, f32[16,16,2048]{2,1,0:T(8,128)} %get-tuple-element.91.refs_1_, f32[1,2048]{1,0:T(1,128)} %get-tuple-element.159.refs_1_.refs_2_), custom_call_target="tpu_custom_call" | custom-call | bytes 350000000 | tf_op jit(solution)/shard_map/pallas_call | solution.py:941
  907.1 108.3 %shard_map.178 = (bf16[1024,1536]{1,0:T(8,128)(2,1)}, bf16[512,2816]{1,0:T(8,128)(2,1)}) custom-call(s32[1,4096]{1,0:T(1,128)} %constant_dynamic-slice_fusion.5.bid_k.bid_q, s32[4096,1]{1,0:T(8,128)} %copy.24.bid_q.bid_k, bf16[1024,512]{1,0:T(8,128)(2,1)} %fusion.26.d_mix, bf16[3,4096,128]{2,1,0:T(8,128)(2,1)} %get-tuple-element.83.refs_0_.spread, ...), custom_call_target="tpu_custom_call" | custom-call | flops 10000000000 | bytes 300000000 | tf_op jit(solution)/shard_map/pallas_call | solution.py:410
  1017.8 11.8 fusion.20
  1038.4 105.6 %shard_map.179 = (bf16[16,4,16,2048]{3,2,1,0:T(8,128)(2,1)}, f32[16,16,2048]{2,1,0:T(8,128)}, f32[2,2048]{1,0:T(2,128)}) custom-call(bf16[16,4,16,2048]{3,2,1,0:T(8,128)(2,1)} %bitcast.159, f32[16,16,2048]{2,1,0:T(8,128)} %get-tuple-element.100.refs_0_, bf16[16,16,2048]{2,1,0:T(8,128)(2,1)} %dynamic-slice_bitcast_fusion.refs_0_.refs_1_, ...), custom_call_target="tpu_custom_call" | custom-call | bytes 350000000 | tf_op jit(solution)/shard_map/pallas_call | solution.py:941
  1144.0 28.2 %shard_map.180 = (bf16[1024,2816]{1,0:T(8,128)(2,1)}, bf16[1024,2048]{1,0:T(8,128)(2,1)}) custom-call(bf16[1024,2048]{1,0:T(8,128)(2,1)} %bitcast.176, f32[1024,2816]{1,0:T(8,128)} %copy-done.8, bf16[4096,2816]{1,0:T(8,128)(2,1)} %all-gather.13.cloned.1.call-done.weight, bf16[4096,1408]{1,0:T(8,128)(2,1)} %bitcast.187), custom_call_target="tpu_custom_call" | custom-call | flops 17716740096 | bytes 40000000 | tf_op jit(solution)/shard_map/pallas_call | solution.py:1162
  1172.1 10.9 convolution_convert_fusion.3
  1183.0 18.4 %convolution_convert_fusion = bf16[2048,2816]{1,0:T(8,128)(2,1)} fusion(bf16[1024,2048]{1,0:T(8,128)(2,1)} %bitcast.189, bf16[1024,2816]{1,0:T(8,128)(2,1)} %get-tuple-element.104), kind=kOutput, calls=%fused_computation.3 | convolution fusion | flops 11816927232 | bytes 21495808 | tf_op jit(solution)/shard_map/dot_general | solution.py:27
  1206.0 102.5 %shard_map.181 = (bf16[16,4,16,2048]{3,2,1,0:T(8,128)(2,1)}, f32[16,16,2048]{2,1,0:T(8,128)}, f32[2,2048]{1,0:T(2,128)}, bf16[1024,512]{1,0:T(8,128)(2,1)}, bf16...) custom-call(bf16[16,4,16,2048]{3,2,1,0:T(8,128)(2,1)} %bitcast.157, ...), custom_call_target="tpu_custom_call" | custom-call | bytes 350000000 | tf_op jit(solution)/shard_map/pallas_call | solution.py:941
  1321.8 142.2 %shard_map.182 = (bf16[1024,1536]{1,0:T(8,128)(2,1)}, bf16[512,2816]{1,0:T(8,128)(2,1)}) custom-call(s32[1,4096]{1,0:T(1,128)} %constant_dynamic-slice_fusion.5.bid_k.bid_q, s32[4096,1]{1,0:T(8,128)} %copy.24.bid_q.bid_k, bf16[1024,512]{1,0:T(8,128)(2,1)} %fusion.27.d_mix, bf16[3,4096,128]{2,1,0:T(8,128)(2,1)} %get-tuple-element.113.spread, ...), custom_call_target="tpu_custom_call" | custom-call | flops 10000000000 | bytes 300000000 | tf_op jit(solution)/shard_map/pallas_call | solution.py:410
  1466.5 11.3 fusion.16
  1515.7 100.0 %shard_map.183 = (bf16[2,16,4,16,512]{4,3,2,1,0:T(8,128)(2,1)}, f32[16,16,2048]{2,1,0:T(8,128)}, f32[2,2048]{1,0:T(2,128)}, f32[2,4,2,512]{3,2,1,0:T(2,128)}, f3...) custom-call(bf16[16,4,16,2048]{3,2,1,0:T(8,128)(2,1)} %bitcast.161, ...), custom_call_target="tpu_custom_call" | custom-call | bytes 350000000 | tf_op jit(solution)/shard_map/pallas_call | solution.py:941
  1617.5 30.6 %psum.7 = f32[14,512]{1,0:T(8,128)S(1)} all-reduce(f32[14,512]{1,0:T(8,128)S(1)} %pad_maximum_fusion.4), channel_id=1, replica_groups=mesh['section'=2,'row'=4,'col'=4] {'row'}, use_global_device_ids=true, to_apply=%region_11.12 | all-reduce | flops 7168 | bytes 57344 | tf_op jit(solution)/shard_map/psum | solution.py:1429
  (182 shorter events, 188.4 us)
Async XLA Ops:
  7.2 12.6 copy-start
  7.2 108.5 %all-gather.11.cloned.1.call-start = ((), (), s32[]{:S(2)}) async-start(), calls=%async_computation.8 | async-start | bytes 14155776 | tf_op jit(solution)/shard_map/all_gather | solution.py:1226
  12.6 188.1 %all-gather.15.cloned.1.call-start = ((), (), s32[]{:S(2)}) async-start(), calls=%async_computation.18 | async-start | bytes 4718592 | tf_op jit(solution)/shard_map/all_gather | solution.py:1226
  13.3 193.7 %all-gather.17.cloned.1.call-start = ((), (), s32[]{:S(2)}) async-start(), calls=%async_computation.19 | async-start | bytes 1310720 | tf_op jit(solution)/shard_map/all_gather | solution.py:1279
  15.1 303.4 %all-gather.13.cloned.1.call-start = ((), (), s32[]{:S(2)}) async-start(), calls=%async_computation.9 | async-start | bytes 25952256 | tf_op jit(solution)/shard_map/all_gather | solution.py:1226
  19.0 90.6 %copy-start.22 = (s32[2,4096]{1,0:T(2,128)S(1)}, s32[2,4096]{1,0:T(2,128)}, u32[]{:S(2)}) copy-start(s32[2,4096]{1,0:T(2,128)} %param.12) | copy-start | bytes 98308
  19.0 335.9 %all-gather.19.cloned.1.call-start = ((), (), s32[]{:S(2)}) async-start(), calls=%async_computation.20 | async-start | bytes 12976128 | tf_op jit(solution)/shard_map/all_gather | solution.py:1226
  19.6 543.5 %all-gather.21.cloned.1.call-start = ((), (), s32[]{:S(2)}) async-start(), calls=%async_computation.21 | async-start | bytes 3932160 | tf_op jit(solution)/shard_map/all_gather | solution.py:1279
  500.6 406.5 %reduce-scatter.9.cloned.1.call-start = ((), (), s32[]{:S(2)}) async-start(), calls=%async_computation.10 | async-start | bytes 14417920 | tf_op jit(solution)/shard_map/reduce_scatter | solution.py:1335
  768.5 269.9 %reduce-scatter.11.cloned.1.call-start = ((), (), s32[]{:S(2)}) async-start(), calls=%async_computation.11 | async-start | bytes 5242880 | tf_op jit(solution)/shard_map/reduce_scatter | solution.py:1370
  771.5 116.1 %copy-start.10 = (f32[16,16,2048]{2,1,0:T(8,128)S(1)}, f32[16,16,2048]{2,1,0:T(8,128)}, u32[]{:S(2)}) copy-start(f32[16,16,2048]{2,1,0:T(8,128)} %get-tuple-element.91.refs_1_) | copy-start | bytes 6291460
  893.2 312.8 %reduce-scatter.13.cloned.1.call-start = ((), (), s32[]{:S(2)}) async-start(), calls=%async_computation.12 | async-start | bytes 2621440 | tf_op jit(solution)/shard_map/reduce_scatter | solution.py:1335
  906.5 299.5 %reduce-scatter.15.cloned.1.call-start = ((), (), s32[]{:S(2)}) async-start(), calls=%async_computation.13 | async-start | bytes 7208960 | tf_op jit(solution)/shard_map/reduce_scatter | solution.py:1335
  907.1 414.8 %reduce-scatter.17.cloned.1.call-start = ((), (), s32[]{:S(2)}) async-start(), calls=%async_computation.14 | async-start | bytes 14417920 | tf_op jit(solution)/shard_map/reduce_scatter | solution.py:1335
  1017.8 11.9 copy-start.14
  1144.0 28.2 %copy-start.15 = (bf16[1024,1408]{1,0:T(8,128)(2,1)S(1)}, bf16[1024,1408]{1,0:T(8,128)(2,1)}, u32[]{:S(2)}) copy-start(bf16[1024,1408]{1,0:T(8,128)(2,1)} %fusion.7) | copy-start | bytes 8650756
  1201.4 314.3 %reduce-scatter.21.cloned.1.call-start = ((), (), s32[]{:S(2)}) async-start(), calls=%async_computation.16 | async-start | bytes 2621440 | tf_op jit(solution)/shard_map/reduce_scatter | solution.py:1335
  1206.0 102.5 %copy-start.30 = (bf16[1024,512]{1,0:T(8,128)(2,1)S(1)}, bf16[1024,512]{1,0:T(8,128)(2,1)}, u32[]{:S(2)}) copy-start(bf16[1024,512]{1,0:T(8,128)(2,1)} %get-tuple-element.78) | copy-start | bytes 3145732
  1320.6 195.1 %reduce-scatter.19.cloned.1.call-start = ((), (), s32[]{:S(2)}) async-start(), calls=%async_computation.15 | async-start | bytes 7208960 | tf_op jit(solution)/shard_map/reduce_scatter | solution.py:1335
  1321.3 336.3 %reduce-scatter.23.cloned.1.call-start = ((), (), s32[]{:S(2)}) async-start(), calls=%async_computation.17 | async-start | bytes 14155776 | tf_op jit(solution)/shard_map/reduce_scatter | solution.py:1402
  1466.5 18.7 %slice-start = ((s8[6291456]{0:T(1024)(128)(4,1)}), s8[4194304]{0:T(1024)(128)(4,1)S(1)}, s32[]{:S(2)}) async-start(s8[6291456]{0:T(1024)(128)(4,1)} %bitcast.155), calls=%async_computation.22 | async-start | bytes 8388608
  1515.6 133.7 %copy-start.16 = (bf16[512,512]{1,0:T(8,128)(2,1)S(1)}, bf16[512,512]{1,0:T(8,128)(2,1)}, u32[]{:S(2)}) copy-start(bf16[512,512]{1,0:T(8,128)(2,1)} %reduce-scatter.13.cloned.1.call-done.refs_6_) | copy-start | bytes 1572868
  1515.7 133.7 %copy-start.17 = (bf16[512,512]{1,0:T(8,128)(2,1)S(1)}, bf16[512,512]{1,0:T(8,128)(2,1)}, u32[]{:S(2)}) copy-start(bf16[512,512]{1,0:T(8,128)(2,1)} %reduce-scatter.21.cloned.1.call-done.refs_5_) | copy-start | bytes 1572868
  1515.7 133.7 %copy-start.21 = (bf16[512,512]{1,0:T(8,128)(2,1)S(1)}, bf16[512,512]{1,0:T(8,128)(2,1)}, u32[]{:S(2)}) copy-start(bf16[512,512]{1,0:T(8,128)(2,1)} %get-tuple-element.134) | copy-start | bytes 1572868
  (24 other events, 122.0 us)
Sparse Core Ops, SparseCore 0:
  12.7 75.7 all-gather.10
  90.4 36.7 all-gather.14
  128.7 27.9 all-gather.16
  159.0 126.3 all-gather.12
  287.2 67.6 all-gather.18
  500.7 62.2 all-gather.20
  768.6 90.0 reduce-scatter.8
  893.3 75.0 reduce-scatter.10
  971.7 42.5 reduce-scatter.12
  1016.6 53.1 reduce-scatter.14
  1201.5 98.5 reduce-scatter.16
  1320.7 51.4 reduce-scatter.20
  1374.7 84.1 reduce-scatter.18
  1490.9 140.9 reduce-scatter.22
